TPU v7x, 32 devices: a whole 2x2x4 slice. The times are simulated.
32 devices in a mesh: section: 2 (over x), dp: 16 (over z, y, core).
Axes of the slice: x: 2, y: 2, z: 4, core: 2. Of those that a mesh axis runs over, the one named last changes fastest.
Arguments:
- boundary: bfloat16 [2, 32, 1024, 512], P('section', 'dp'), may hold values from -6 to 6
- segments: int32 [32, 1024], P('dp'), may hold values from 0 to 3, never falling along the last dimension, each value on 1 to 512 neighbouring positions
- code_index: int32 [32, 1024], P('dp'), may hold values from 0 to 8191
- attention_in: bfloat16 [2, 512, 1536], P('section'), may hold values from -0.25 to 0.25
- attention_out: bfloat16 [2, 512, 512], P('section'), may hold values from -2 to 2
- hidden_in: bfloat16 [2, 512, 2048], P('section'), may hold values from -0.25 to 0.25
- hidden_out: bfloat16 [2, 2048, 512], P('section'), may hold values from -0.125 to 0.125
- block_gains: float32 [2, 2, 512], P('section'), may hold values from 0.5 to 1.5
- block_biases: float32 [2, 6, 512], P('section'), may hold values from -2.5 to 2.5
- hidden_bias: float32 [2, 2048], P('section'), may hold values from -2.5 to 2.5
- output_gain: float32 [512], replicated, may hold values from 0.5 to 1.5
- head_bias: float32 [2, 512], replicated, may hold values from -2.5 to 2.5
- down_weight: float32 [512, 32], replicated, may hold values from -0.25 to 0.25
- down_bias: float32 [32], replicated, may hold values from -2.5 to 2.5
- up_weight: float32 [32, 512], replicated, may hold values from -3 to 3
- codebook: float32 [8192, 32], replicated, may hold values from -6 to 6
Outputs:
- edge_result: float32 [2, 32, 1024, 512], P('section', 'dp')
- attention_in_grad: float32 [2, 512, 1536], P('section')
- attention_out_grad: float32 [2, 512, 512], P('section')
- hidden_in_grad: float32 [2, 512, 2048], P('section')
- hidden_out_grad: float32 [2, 2048, 512], P('section')
- gains_grad: float32 [2, 2, 512], P('section')
- biases_grad: float32 [2, 6, 512], P('section')
- hidden_bias_grad: float32 [2, 2048], P('section')
- output_gain_grad: float32 [512], replicated
- head_bias_grad: float32 [2, 512], replicated
- down_weight_grad: float32 [512, 32], replicated
- down_bias_grad: float32 [32], replicated
- up_weight_grad: float32 [32, 512], replicated
- codebook_grad: float32 [8192, 32], replicated
Inputs may be any that keep to these rules, and one draw needn't show every extreme that they name: `segments`: within each packed row segment numbers never fall; each segment has 1 to 512 tokens, and one has exactly 512.
All inputs are finite; a program needn't handle non-finite values.
Results may differ from a plain program's by a relative error of at most 0.012.
Values sent between devices are 32-bit elements; how exact they have to be, the bound alone decides.
A program may use at most 320 MiB of HBM per device.

v0:
```python
import jax
import jax.numpy as jnp
from jax import lax
from jax.sharding import PartitionSpec as P

HEADS = 8
HEAD = 64


highest = lax.Precision.HIGHEST
norm_eps = 1e-06
masked_score = -1e30
commit_weight = 0.25
gelu_coef = 0.7978845608028654


def from_behind(value, axis, steps):
    count = lax.axis_size(axis)
    leading, last = (max(0, -steps), min(count, count - steps))
    return lax.ppermute(value, axis, [(source, source + steps) for source in range(leading, last)])


def layer_norm(values, gain, offset):
    center = values - jnp.mean(values, -1, keepdims=True)
    spread = jnp.mean(center * center, -1, keepdims=True)
    return center * lax.rsqrt(spread + norm_eps) * gain + offset


def gelu_tanh(values):
    return (
        0.5 * values * (1.0 + jnp.tanh(gelu_coef * (values + 0.044715 * values * values * values)))
    )


def unit_rows(values):
    return values * lax.rsqrt(jnp.sum(values * values, -1, keepdims=True) + norm_eps)


def encode_tail(hidden, gain, offset, weight, bias):
    normed = layer_norm(hidden, gain, offset)
    latent = jnp.dot(normed, weight, precision=highest) + bias
    return unit_rows(latent)


def attend(projected, segment):
    row_count = projected.shape[0]
    model_width = projected.shape[1] // 3
    block_rows = min(512, row_count)
    score_scale = HEAD ** (-0.5)
    key_rows = projected[:, model_width : 2 * model_width].reshape(row_count, HEADS, HEAD)
    value_rows = projected[:, 2 * model_width :].reshape(row_count, HEADS, HEAD)

    def one_block(number):
        offset = number * block_rows
        query_rows = lax.dynamic_slice_in_dim(projected, offset, block_rows, 0)[
            :, :model_width
        ].reshape(block_rows, HEADS, HEAD)
        own_segment = lax.dynamic_slice_in_dim(segment, offset, block_rows, 0)
        scores = (
            jnp.einsum("qhe,khe->hqk", query_rows, key_rows, preferred_element_type=jnp.float32)
            * score_scale
        )
        scores = jnp.where((own_segment[:, None] == segment[None, :])[None], scores, masked_score)
        row_max = jnp.max(scores, -1, keepdims=True)
        raised = jnp.exp(scores - row_max)
        denominator = jnp.sum(raised, -1, keepdims=True)
        attention = (raised / denominator).astype(jnp.bfloat16)
        context = jnp.einsum(
            "hqk,khe->qhe", attention, value_rows, preferred_element_type=jnp.float32
        )
        return (context.reshape(block_rows, model_width), (row_max + jnp.log(denominator))[..., 0])

    context, log_total = lax.map(one_block, jnp.arange(row_count // block_rows))
    return (
        context.reshape(row_count, model_width),
        jnp.transpose(log_total, (1, 0, 2)).reshape(HEADS, row_count),
    )


def attend_back(projected, segment, log_total, context_grad):
    row_count = projected.shape[0]
    model_width = projected.shape[1] // 3
    block_rows = min(512, row_count)
    score_scale = HEAD ** (-0.5)
    key_rows = projected[:, model_width : 2 * model_width].reshape(row_count, HEADS, HEAD)
    value_rows = projected[:, 2 * model_width :].reshape(row_count, HEADS, HEAD)

    def one_block(carry, number):
        key_grad, value_grad = carry
        offset = number * block_rows
        query_rows = lax.dynamic_slice_in_dim(projected, offset, block_rows, 0)[
            :, :model_width
        ].reshape(block_rows, HEADS, HEAD)
        own_segment = lax.dynamic_slice_in_dim(segment, offset, block_rows, 0)
        own_total = lax.dynamic_slice_in_dim(log_total, offset, block_rows, 1)
        own_context = lax.dynamic_slice_in_dim(context_grad, offset, block_rows, 0).reshape(
            block_rows, HEADS, HEAD
        )
        scores = (
            jnp.einsum("qhe,khe->hqk", query_rows, key_rows, preferred_element_type=jnp.float32)
            * score_scale
        )
        scores = jnp.where((own_segment[:, None] == segment[None, :])[None], scores, masked_score)
        attention = jnp.exp(scores - own_total[..., None])
        weight_grad = jnp.einsum(
            "qhe,khe->hqk", own_context, value_rows, preferred_element_type=jnp.float32
        )
        centre = jnp.sum(attention * weight_grad, -1, keepdims=True)
        score_grad = (attention * (weight_grad - centre)).astype(jnp.bfloat16)
        query_grad = (
            jnp.einsum("hqk,khe->qhe", score_grad, key_rows, preferred_element_type=jnp.float32)
            * score_scale
        )
        key_term = (
            jnp.einsum("hqk,qhe->khe", score_grad, query_rows, preferred_element_type=jnp.float32)
            * score_scale
        )
        value_term = jnp.einsum(
            "hqk,qhe->khe",
            attention.astype(jnp.bfloat16),
            own_context,
            preferred_element_type=jnp.float32,
        )
        key_grad = key_grad + key_term.reshape(row_count, model_width)
        value_grad = value_grad + value_term.reshape(row_count, model_width)
        return ((key_grad, value_grad), query_grad.reshape(block_rows, model_width))

    empty = jnp.zeros((row_count, model_width), jnp.float32)
    (key_grad, value_grad), query_grad = lax.scan(
        one_block, (empty, empty), jnp.arange(row_count // block_rows)
    )
    return (query_grad.reshape(row_count, model_width), key_grad, value_grad)


def block_forward(values, segment, weights):
    attention_in, attention_out, hidden_in, hidden_out, gains, biases, hidden_bias = weights
    model_width = values.shape[1]
    normed_first = layer_norm(values, gains[0], biases[3]).astype(jnp.bfloat16)
    bias_row = jnp.concatenate([biases[0], jnp.zeros((model_width,), jnp.float32), biases[1]])
    projected = (
        jnp.dot(normed_first, attention_in, preferred_element_type=jnp.float32) + bias_row
    ).astype(jnp.bfloat16)
    context, log_total = attend(projected, segment)
    context = context.astype(jnp.bfloat16)
    midway = values + (
        jnp.dot(context, attention_out, preferred_element_type=jnp.float32) + biases[2]
    )
    normed_second = layer_norm(midway, gains[1], biases[4]).astype(jnp.bfloat16)
    preact = jnp.dot(normed_second, hidden_in, preferred_element_type=jnp.float32) + hidden_bias
    activated = gelu_tanh(preact).astype(jnp.bfloat16)
    result = midway + (
        jnp.dot(activated, hidden_out, preferred_element_type=jnp.float32) + biases[5]
    )
    return (
        result,
        (
            values,
            normed_first,
            projected,
            log_total,
            context,
            midway,
            normed_second,
            preact,
            activated,
        ),
    )


def block_backward(kept_state, upstream, segment, weights):
    attention_in, attention_out, hidden_in, hidden_out, gains, biases, hidden_bias = weights
    (
        values,
        normed_first,
        projected,
        log_total,
        context,
        midway,
        normed_second,
        preact,
        activated,
    ) = kept_state
    model_width = values.shape[1]
    out_low = upstream.astype(jnp.bfloat16)
    hidden_out_grad = jnp.einsum(
        "nf,nd->fd", activated, out_low, preferred_element_type=jnp.float32
    )
    last_bias_grad = jnp.sum(out_low.astype(jnp.float32), 0)
    activated_grad = jnp.einsum(
        "nd,fd->nf", out_low, hidden_out, preferred_element_type=jnp.float32
    )
    unused, gelu_back = jax.vjp(gelu_tanh, preact)
    preact_low = gelu_back(activated_grad)[0].astype(jnp.bfloat16)
    hidden_in_grad = jnp.einsum(
        "nd,nf->df", normed_second, preact_low, preferred_element_type=jnp.float32
    )
    hidden_bias_grad = jnp.sum(preact_low.astype(jnp.float32), 0)
    normed_grad = jnp.einsum("nf,df->nd", preact_low, hidden_in, preferred_element_type=jnp.float32)
    unused, second_back = jax.vjp(layer_norm, midway, gains[1], biases[4])
    midway_term, second_gain, second_shift = second_back(normed_grad)
    midway_grad = upstream + midway_term
    branch_low = midway_grad.astype(jnp.bfloat16)
    attention_out_grad = jnp.einsum(
        "nc,nd->cd", context, branch_low, preferred_element_type=jnp.float32
    )
    out_bias_grad = jnp.sum(branch_low.astype(jnp.float32), 0)
    context_grad = jnp.einsum(
        "nd,cd->nc", branch_low, attention_out, preferred_element_type=jnp.float32
    ).astype(jnp.bfloat16)
    query_grad, key_grad, value_grad = attend_back(projected, segment, log_total, context_grad)
    projected_grad = jnp.concatenate([query_grad, key_grad, value_grad], 1).astype(jnp.bfloat16)
    attention_in_grad = jnp.einsum(
        "nd,ne->de", normed_first, projected_grad, preferred_element_type=jnp.float32
    )
    query_bias_grad = jnp.sum(projected_grad[:, :model_width].astype(jnp.float32), 0)
    value_bias_grad = jnp.sum(projected_grad[:, 2 * model_width :].astype(jnp.float32), 0)
    first_grad = jnp.einsum(
        "ne,de->nd", projected_grad, attention_in, preferred_element_type=jnp.float32
    )
    unused, first_back = jax.vjp(layer_norm, values, gains[0], biases[3])
    entry_term, first_gain, first_shift = first_back(first_grad)
    entry_grad = midway_grad + entry_term
    gain_grads = jnp.stack([first_gain, second_gain])
    bias_grads = jnp.stack(
        [query_bias_grad, value_bias_grad, out_bias_grad, first_shift, second_shift, last_bias_grad]
    )
    return (
        entry_grad,
        (
            attention_in_grad,
            attention_out_grad,
            hidden_in_grad,
            hidden_out_grad,
            gain_grads,
            bias_grads,
            hidden_bias_grad,
        ),
    )


def lookup(index_row, table):
    return jnp.take(table, index_row, axis=0)


def scatter_codes(index_row, rows_grad, code_count):
    return jax.ops.segment_sum(rows_grad, index_row, num_segments=code_count)


def pick(array, micro_index):
    return lax.dynamic_index_in_dim(array, micro_index, 0, False)


def on_device(
    boundary,
    segments,
    code_index,
    attention_in,
    attention_out,
    hidden_in,
    hidden_out,
    block_gains,
    block_biases,
    hidden_bias,
    output_gain,
    head_bias,
    down_weight,
    down_bias,
    up_weight,
    codebook,
):
    section_index = lax.axis_index("section")
    encoder_side = section_index == 0
    encoder_mask = encoder_side.astype(jnp.float32)
    decoder_mask = 1.0 - encoder_mask
    edges = boundary[0]
    micro_count = edges.shape[0]
    row_count = edges.shape[1]
    model_width = edges.shape[2]
    latent_width = up_weight.shape[0]
    weights = (
        attention_in[0],
        attention_out[0],
        hidden_in[0],
        hidden_out[0],
        block_gains[0],
        block_biases[0],
        hidden_bias[0],
    )
    unit_book, book_back = jax.vjp(unit_rows, codebook)
    block_total = tuple((jnp.zeros(weight.shape, jnp.float32) for weight in weights))
    head_total = (
        jnp.zeros(output_gain.shape, jnp.float32),
        jnp.zeros(head_bias.shape, jnp.float32),
        jnp.zeros(down_weight.shape, jnp.float32),
        jnp.zeros(down_bias.shape, jnp.float32),
        jnp.zeros(up_weight.shape, jnp.float32),
        jnp.zeros(codebook.shape, jnp.float32),
    )
    edge_store = jnp.zeros((micro_count, row_count, model_width), jnp.float32)
    outgoing = jnp.zeros((row_count, latent_width), jnp.float32)
    for rounds in range(micro_count + 1):
        position = rounds - 1 + section_index
        live_weight = ((position >= 0) & (position < micro_count)).astype(jnp.float32)
        micro_index = jnp.clip(position, 0, micro_count - 1)
        edge_in = pick(edges, micro_index).astype(jnp.float32)
        segment = pick(segments, micro_index)
        index_row = pick(code_index, micro_index)
        chosen_code = lookup(index_row, unit_book)
        decoder_in = jnp.dot(chosen_code, up_weight, precision=highest) + head_bias[1]
        block_in = jnp.where(encoder_side, edge_in, decoder_in)
        result, kept_state = block_forward(block_in, segment, weights)
        latent, tail_back = jax.vjp(
            encode_tail, result, output_gain, head_bias[0], down_weight, down_bias
        )
        encoder_weight = encoder_mask * live_weight
        decoder_weight = decoder_mask * live_weight
        if rounds > 0:
            latent_in = from_behind(outgoing, "section", -1)
        else:
            latent_in = jnp.zeros_like(outgoing)
        latent_grad = latent_in + 2.0 * commit_weight * (latent - chosen_code)
        result_grad, gain_term, shift_term, down_term, down_bias_term = tail_back(latent_grad)
        upstream = jnp.where(encoder_side, result_grad, edge_in)
        entry_grad, step_grads = block_backward(kept_state, upstream, segment, weights)
        up_weight_term = (
            jnp.einsum("nl,nd->ld", chosen_code, entry_grad, precision=highest) * decoder_weight
        )
        up_bias_term = jnp.sum(entry_grad, 0) * decoder_weight
        outgoing = jnp.einsum("nd,ld->nl", entry_grad, up_weight, precision=highest)
        book_rows = scatter_codes(
            index_row, 2.0 * (chosen_code - latent) * encoder_weight, codebook.shape[0]
        )
        head_step = (
            gain_term * encoder_weight,
            jnp.stack([shift_term * encoder_weight, up_bias_term]),
            down_term * encoder_weight,
            down_bias_term * encoder_weight,
            up_weight_term,
            book_rows,
        )
        head_total = tuple((total + term for total, term in zip(head_total, head_step)))
        step_grads = tuple((term * live_weight for term in step_grads))
        block_total = tuple((total + term for total, term in zip(block_total, step_grads)))
        written = jnp.where(encoder_side, entry_grad, result)
        current = pick(edge_store, micro_index)
        edge_store = lax.dynamic_update_index_in_dim(
            edge_store, jnp.where(live_weight > 0.0, written, current), micro_index, 0
        )
    block_total = lax.psum(block_total, "dp")
    book_grad = book_back(head_total[5])[0]
    head_sums = lax.psum(
        (head_total[0], head_total[1], head_total[2], head_total[3], head_total[4], book_grad),
        ("section", "dp"),
    )
    return (
        edge_store[None],
        block_total[0][None],
        block_total[1][None],
        block_total[2][None],
        block_total[3][None],
        block_total[4][None],
        block_total[5][None],
        block_total[6][None],
        head_sums[0],
        head_sums[1],
        head_sums[2],
        head_sums[3],
        head_sums[4],
        head_sums[5],
    )


def solution(mesh):
    return jax.shard_map(
        on_device,
        mesh=mesh,
        in_specs=(
            P("section", "dp", None, None),
            P("dp", None),
            P("dp", None),
            P("section", None, None),
            P("section", None, None),
            P("section", None, None),
            P("section", None, None),
            P("section", None, None),
            P("section", None, None),
            P("section", None),
            P(),
            P(),
            P(),
            P(),
            P(),
            P(),
        ),
        out_specs=(
            P("section", "dp", None, None),
            P("section", None, None),
            P("section", None, None),
            P("section", None, None),
            P("section", None, None),
            P("section", None, None),
            P("section", None, None),
            P("section", None),
            P(),
            P(),
            P(),
            P(),
            P(),
            P(),
        ),
        check_vma=False,
    )
```

profile of v0, /device:TPU:0, one launch (start us, length us, event | category | flops | bytes accessed | tf_op | source)
XLA Modules:
  0.0 1349.8 jit_solution(4308901802400367469)
XLA Ops:
  66.6 39.7 %while.82 = (s32[]{:T(128)}, bf16[2,512,512]{2,1,0:T(8,128)(2,1)}, f32[2,8,512]{2,1,0:T(8,128)S(1)}, s32[2]{0:T(128)S(1)}, s32[1024]{0:T(1024)S(1)}, /*index=5*/...) while((s32[]{:T(128)}, bf16[2,512,512]{2,1,0:T(8,128)(2,1)}, ...), condition=%wide.region_27.29_spmd, body=%wide.region_24.28_spmd.sunk | while | flops 1124593664 | bytes 63056596 | solution.py:73
  76.6 5.8 fusion.403
  96.5 5.8 fusion.403
  115.7 40.0 %while.81 = (s32[]{:T(128)}, bf16[2,512,512]{2,1,0:T(8,128)(2,1)}, f32[2,8,512]{2,1,0:T(8,128)S(1)}, s32[2]{0:T(128)S(1)}, s32[1024]{0:T(1024)S(1)}, /*index=5*/...) while((s32[]{:T(128)}, bf16[2,512,512]{2,1,0:T(8,128)(2,1)}, ...), condition=%wide.region_6.8_spmd, body=%wide.region_3.7_spmd.sunk | while | flops 1124593664 | bytes 63056596 | solution.py:73
  162.0 10.7 multiply_convert_fusion.4
  193.7 11.7 convert_reduce_fusion.2
  222.9 128.6 %while.84 = (s32[]{:T(128)}, f32[1024,512]{0,1:T(8,128)}, f32[1024,512]{0,1:T(8,128)}, bf16[2,512,512]{2,1,0:T(8,128)(2,1)}, s32[2]{0:T(128)S(1)}, /*index=5*/bf...) while((s32[]{:T(128)}, f32[1024,512]{0,1:T(8,128)}, ...), condition=%wide.region_19.21_spmd.clone, body=%wide.region_17.20_spmd.clone.sunk | while | flops 2725769216 | bytes 297364320 | solution.py:129
  227.8 9.4 fusion.420
  238.7 12.8 multiply_reduce_fusion.41
  251.5 11.5 multiply_convert_fusion.11
  273.6 5.8 bitcast_add_fusion.9
  291.2 9.4 fusion.420
  302.2 12.8 multiply_reduce_fusion.41
  315.0 11.5 multiply_convert_fusion.11
  337.1 7.0 bitcast_add_fusion.9
  356.0 6.1 fusion.240
  402.6 6.7 fusion.250
  418.8 40.1 %while.83 = (s32[]{:T(128)}, bf16[2,512,512]{2,1,0:T(8,128)(2,1)}, f32[2,8,512]{2,1,0:T(8,128)S(1)}, s32[2]{0:T(128)S(1)}, s32[1024]{0:T(1024)S(1)}, /*index=5*/...) while((s32[]{:T(128)}, bf16[2,512,512]{2,1,0:T(8,128)(2,1)}, ...), condition=%wide.region_48.50_spmd, body=%wide.region_45.49_spmd.sunk | while | flops 1124593664 | bytes 63056596 | solution.py:73
  429.3 5.8 fusion.409
  449.1 5.8 fusion.409
  509.9 10.0 convert_reduce_fusion.1
  540.8 120.3 %while.85 = (s32[]{:T(128)}, f32[1024,512]{0,1:T(8,128)}, f32[1024,512]{0,1:T(8,128)}, bf16[2,512,512]{2,1,0:T(8,128)(2,1)}, s32[2]{0:T(128)S(1)}, /*index=5*/bf...) while((s32[]{:T(128)}, f32[1024,512]{0,1:T(8,128)}, ...), condition=%wide.region_40.42_spmd.clone, body=%wide.region_38.41_spmd.clone.sunk | while | flops 2725769216 | bytes 297364320 | solution.py:129
  543.2 9.4 fusion.432
  554.2 12.7 multiply_reduce_fusion.42
  566.9 11.5 multiply_convert_fusion.12
  589.0 5.8 bitcast_add_fusion.10
  602.8 9.4 fusion.432
  613.7 12.7 multiply_reduce_fusion.42
  626.4 11.5 multiply_convert_fusion.12
  648.5 7.0 bitcast_add_fusion.10
  665.6 6.1 fusion.238
  703.0 19.5 %scatter_custom_fusion = f32[8192,32]{1,0:T(8,128)} fusion(s32[3072]{0:T(1024)} %bitcast.604, f32[3072,32]{1,0:T(8,128)} %copy.147, f32[]{:T(128)} %constant.249.clone.1), kind=kCustom, calls=%fused_computation.177 | custom fusion | flops 98304 | bytes 1049088 | tf_op jit(solution)/shard_map/add | solution.py:341
  728.5 5.8 add_add_fusion
  747.6 11.5 convert_reduce_fusion
  775.5 120.5 %while.86 = (s32[]{:T(128)}, f32[1024,512]{0,1:T(8,128)}, f32[1024,512]{0,1:T(8,128)}, bf16[2,512,512]{2,1,0:T(8,128)(2,1)}, s32[2]{0:T(128)S(1)}, /*index=5*/bf...) while((s32[]{:T(128)}, f32[1024,512]{0,1:T(8,128)}, ...), condition=%wide.region_61.63_spmd.clone, body=%wide.region_59.62_spmd.clone.sunk | while | flops 2725769216 | bytes 297364320 | solution.py:129
  778.2 9.4 fusion.444
  789.2 12.7 multiply_reduce_fusion.43
  801.9 11.5 multiply_convert_fusion.13
  837.8 9.4 fusion.444
  848.8 12.7 multiply_reduce_fusion.43
  861.4 11.5 multiply_convert_fusion.13
  883.5 7.0 bitcast_add_fusion.11
  922.5 8.9 add_bitcast_fusion
  931.4 8.2 add_bitcast_fusion.1
  943.0 6.8 fusion.41
  994.3 43.9 %all-reduce = (f32[512]{0:T(512)}, f32[2,512]{1,0:T(2,128)}, f32[32]{0:T(128)}) all-reduce(f32[512]{0:T(512)S(1)} %multiply_add_fusion.44, f32[2,512]{1,0:T(2,128)S(1)} %fusion.173, f32[32]{0:T(128)S(1)} %multiply_add_fusion.45), channel_id=1, replica_groups=mesh['section'=2,'dp'=16] {'section','dp'}, use_global_device_ids=true, to_apply=%region_101.103 | all-reduce | flops 1568 | bytes 12544 | tf_op jit(solution)/shard_map/psum | solution.py:351
  1038.4 60.0 %all-reduce.2 = (f32[1,2,512]{2,1,0:T(2,128)}, f32[1,6,512]{2,0,1:T(1,128)}, f32[1,2048]{1,0:T(1,128)}) all-reduce(f32[1,2,512]{2,1,0:T(2,128)S(1)} %fusion.172, f32[1,6,512]{2,0,1:T(1,128)S(1)} %broadcast_in_dim.300, f32[1,2048]{1,0:T(1,128)S(1)} %bitcast.603), channel_id=1, replica_groups=mesh['section'=2,'dp'=16] {'dp'}, use_global_device_ids=true, to_apply=%region_74.76 | all-reduce | flops 6144 | bytes 49152 | tf_op jit(solution)/shard_map/psum | solution.py:349
  1105.3 225.4 %all-reduce.9.cloned.1.call-done = (f32[1,512,1536]{2,1,0:T(8,128)}, f32[1,512,512]{2,1,0:T(8,128)}, f32[1,512,2048]{2,1,0:T(8,128)}, f32[1,2048,512]{2,1,0:T(8,128)}) async-done(((f32[1,512,1536]{2,1,0:T(8,128)}, f32[1,512,512]{2,1,0:T(8,128)}, f32[1,512,2048]{2,1,0:T(8,128)}, f32[1,2048,512]{2,1,0:T(8,128)}), (f32[1,512,1536]{2,1,0:T(8,128)}, f32[1,512,512]{2,1,0:T(8,128)}, f32[1,512,2048]{2,1,0:T(8,128)}, ...) | async-done | bytes 12582928 | tf_op jit(solution)/shard_map/psum | solution.py:349
  (1117 shorter events, 623.2 us)
Async XLA Ops:
  7.2 151.8 %copy-start = (bf16[1,512,2048]{2,1,0:T(8,128)(2,1)S(1)}, bf16[1,512,2048]{2,1,0:T(8,128)(2,1)}, u32[]{:S(2)}) copy-start(bf16[1,512,2048]{2,1,0:T(8,128)(2,1)} %param.35) | copy-start | bytes 6291460
  7.2 1094.3 %all-reduce.7.cloned.1.call-start = ((), (), s32[]{:S(2)}) async-start(), calls=%async_computation | async-start | bytes 8650752 | tf_op jit(solution)/shard_map/psum | solution.py:351
  12.5 16.9 %copy-start.264 = (pred[1024]{0:T(1024)(128)(4,1)}, pred[1024]{0:T(1024)(128)(4,1)S(1)}, u32[]{:S(2)}) copy-start(pred[1024]{0:T(1024)(128)(4,1)S(1)} %get-tuple-element.866) | copy-start | bytes 3076
  12.5 36.0 %copy-start.270 = (pred[1024]{0:T(1024)(128)(4,1)}, pred[1024]{0:T(1024)(128)(4,1)S(1)}, u32[]{:S(2)}) copy-start(pred[1024]{0:T(1024)(128)(4,1)S(1)} %get-tuple-element.867) | copy-start | bytes 3076
  16.9 31.6 %copy-start.262 = (f32[1,512]{1,0:T(1,128)}, f32[1,512]{1,0:T(1,128)S(1)}, u32[]{:S(2)}) copy-start(f32[1,512]{1,0:T(1,128)S(1)} %get-tuple-element.814) | copy-start | bytes 6148
  17.5 33.5 %copy-start.167 = (f32[1,1,512]{2,1,0:T(1,128)}, f32[1,1,512]{2,1,0:T(1,128)S(1)}, u32[]{:S(2)}) copy-start(f32[1,1,512]{2,1,0:T(1,128)S(1)} %get-tuple-element.816) | copy-start | bytes 6148
  18.1 32.9 %copy-start.309 = (f32[1,1,512]{2,0,1:T(1,128)}, f32[1,1,512]{2,0,1:T(1,128)S(1)}, u32[]{:S(2)}) copy-start(f32[1,1,512]{2,0,1:T(1,128)S(1)} %get-tuple-element.801) | copy-start | bytes 6148
  31.8 19.1 %copy-start.292 = (f32[1536]{0:T(1024)}, f32[1536]{0:T(1024)S(1)}, u32[]{:S(2)}) copy-start(f32[1536]{0:T(1024)S(1)} %pad_maximum_fusion.10) | copy-start | bytes 18436
  66.6 39.7 %copy-start.259 = (f32[1,1,512]{2,0,1:T(1,128)S(1)}, f32[1,1,512]{2,0,1:T(1,128)}, u32[]{:S(2)}) copy-start(f32[1,1,512]{2,0,1:T(1,128)} %get-tuple-element.798) | copy-start | bytes 6148
  115.7 40.0 %copy-start.260 = (f32[1,1,512]{2,0,1:T(1,128)S(1)}, f32[1,1,512]{2,0,1:T(1,128)}, u32[]{:S(2)}) copy-start(f32[1,1,512]{2,0,1:T(1,128)} %get-tuple-element.798) | copy-start | bytes 6148
  158.6 14.1 %copy-start.47 = (f32[1024,512]{0,1:T(8,128)}, f32[1024,512]{0,1:T(8,128)S(1)}, u32[]{:S(2)}) copy-start(f32[1024,512]{0,1:T(8,128)S(1)} %get-tuple-element.820) | copy-start | bytes 6291460
  158.6 57.7 %copy-start.222 = (f32[1024]{0:T(1024)}, f32[1024]{0:T(1024)S(1)}, u32[]{:S(2)}) copy-start(f32[1024]{0:T(1024)S(1)} %broadcast_multiply_fusion.9) | copy-start | bytes 12292
  158.9 57.4 %copy-start.257 = (f32[1024]{0:T(1024)}, f32[1024]{0:T(1024)S(1)}, u32[]{:S(2)}) copy-start(f32[1024]{0:T(1024)S(1)} %fusion.175) | copy-start | bytes 12292
  161.9 10.8 copy-start.337
  161.9 10.7 copy-start.317
  175.2 15.6 %copy-start.174 = (f32[1024]{0:T(1024)}, f32[1024]{0:T(1024)S(1)}, u32[]{:S(2)}) copy-start(f32[1024]{0:T(1024)S(1)} %broadcast_multiply_fusion.8) | copy-start | bytes 12292
  175.5 15.3 %copy-start.188 = (f32[1024]{0:T(1024)}, f32[1024]{0:T(1024)S(1)}, u32[]{:S(2)}) copy-start(f32[1024]{0:T(1024)S(1)} %fusion.176) | copy-start | bytes 12292
  191.4 25.5 %copy-start.206 = (f32[1024]{0:T(1024)}, f32[1024]{0:T(1024)S(1)}, u32[]{:S(2)}) copy-start(f32[1024]{0:T(1024)S(1)} %negate_multiply_fusion.8) | copy-start | bytes 12292
  193.1 12.4 copy-start.141
  251.5 19.1 %copy-start.1 = (f32[8,512,1024]{2,1,0:T(8,128)S(1)}, f32[8,512,1024]{2,1,0:T(8,128)}, u32[]{:S(2)}) copy-start(f32[8,512,1024]{2,1,0:T(8,128)} %get-tuple-element.1220) | copy-start | bytes 50331652 | tf_op jit(solution)/shard_map/while
  315.0 19.1 %copy-start.1 = (f32[8,512,1024]{2,1,0:T(8,128)S(1)}, f32[8,512,1024]{2,1,0:T(8,128)}, u32[]{:S(2)}) copy-start(f32[8,512,1024]{2,1,0:T(8,128)} %get-tuple-element.1220) | copy-start | bytes 50331652 | tf_op jit(solution)/shard_map/while
  377.3 111.0 %collective-permute-start = (f32[1024,32]{0,1:T(8,128)}, f32[1024,32]{0,1:T(8,128)}, u32[]{:S(2)}, u32[]{:S(2)}) collective-permute-start(f32[1024,32]{0,1:T(8,128)} %fusion.248), channel_id=1, source_target_pairs={{16,0},{17,1},{18,2},{19,3},{20,4},{21,5},{22,6},{23,7},{24,8},{25... | collective-permute-start | bytes 393224 | tf_op jit(solution)/shard_map/ppermute | solution.py:20
  418.8 40.1 %copy-start.261 = (f32[1,1,512]{2,0,1:T(1,128)S(1)}, f32[1,1,512]{2,0,1:T(1,128)}, u32[]{:S(2)}) copy-start(f32[1,1,512]{2,0,1:T(1,128)} %get-tuple-element.798) | copy-start | bytes 6148
  477.1 24.7 %copy-start.176 = (f32[1024]{0:T(1024)}, f32[1024]{0:T(1024)S(1)}, u32[]{:S(2)}) copy-start(f32[1024]{0:T(1024)S(1)} %broadcast_multiply_fusion.5) | copy-start | bytes 12292
  478.5 23.3 %copy-start.190 = (f32[1024]{0:T(1024)}, f32[1024]{0:T(1024)S(1)}, u32[]{:S(2)}) copy-start(f32[1024]{0:T(1024)S(1)} %fusion.179) | copy-start | bytes 12292
  502.4 33.3 %copy-start.202 = (f32[1024]{0:T(1024)}, f32[1024]{0:T(1024)S(1)}, u32[]{:S(2)}) copy-start(f32[1024]{0:T(1024)S(1)} %negate_multiply_fusion.5) | copy-start | bytes 12292
  566.9 19.1 %copy-start.2 = (f32[8,512,1024]{2,1,0:T(8,128)S(1)}, f32[8,512,1024]{2,1,0:T(8,128)}, u32[]{:S(2)}) copy-start(f32[8,512,1024]{2,1,0:T(8,128)} %get-tuple-element.1235) | copy-start | bytes 50331652 | tf_op jit(solution)/shard_map/while
  626.4 19.1 %copy-start.2 = (f32[8,512,1024]{2,1,0:T(8,128)S(1)}, f32[8,512,1024]{2,1,0:T(8,128)}, u32[]{:S(2)}) copy-start(f32[8,512,1024]{2,1,0:T(8,128)} %get-tuple-element.1235) | copy-start | bytes 50331652 | tf_op jit(solution)/shard_map/while
  665.6 23.9 %copy-start.99 = (bf16[1024,512]{1,0:T(8,128)(2,1)}, bf16[1024,512]{1,0:T(8,128)(2,1)S(1)}, u32[]{:S(2)}) copy-start(bf16[1024,512]{1,0:T(8,128)(2,1)S(1)} %copy.117) | copy-start | bytes 3145732
  683.5 14.2 %copy-start.51 = (f32[1024,512]{0,1:T(8,128)}, f32[1024,512]{0,1:T(8,128)S(1)}, u32[]{:S(2)}) copy-start(f32[1024,512]{0,1:T(8,128)S(1)} %get-tuple-element.740) | copy-start | bytes 6291460
  685.0 15.6 %collective-permute-start.1 = (f32[1024,32]{0,1:T(8,128)S(1)}, f32[1024,32]{0,1:T(8,128)S(1)}, u32[]{:S(2)}, u32[]{:S(2)}) collective-permute-start(f32[1024,32]{0,1:T(8,128)S(1)} %fusion.249), channel_id=1, source_target_pairs={{16,0},{17,1},{18,2},{19,3},{20,4},{21,5},{22,6},{23,7},{24,8},{25... | collective-permute-start | bytes 393224 | tf_op jit(solution)/shard_map/ppermute | solution.py:20
  701.3 33.0 %copy-start.130 = (f32[1024,32]{0,1:T(8,128)}, f32[1024,32]{0,1:T(8,128)S(1)}, u32[]{:S(2)}) copy-start(f32[1024,32]{0,1:T(8,128)S(1)} %get-tuple-element.736) | copy-start | bytes 393220
  703.0 24.3 %copy-start.157 = (f32[8192]{0:T(1024)S(1)}, f32[8192]{0:T(1024)}, u32[]{:S(2)}) copy-start(f32[8192]{0:T(1024)} %copy-done.156) | copy-start | bytes 98308
  745.3 25.2 %copy-start.204 = (f32[1024]{0:T(1024)}, f32[1024]{0:T(1024)S(1)}, u32[]{:S(2)}) copy-start(f32[1024]{0:T(1024)S(1)} %negate_multiply_fusion.2) | copy-start | bytes 12292
  746.9 12.2 copy-start.143
  801.9 19.1 %copy-start.3 = (f32[8,512,1024]{2,1,0:T(8,128)S(1)}, f32[8,512,1024]{2,1,0:T(8,128)}, u32[]{:S(2)}) copy-start(f32[8,512,1024]{2,1,0:T(8,128)} %get-tuple-element.1250) | copy-start | bytes 50331652 | tf_op jit(solution)/shard_map/while
  861.4 19.1 %copy-start.3 = (f32[8,512,1024]{2,1,0:T(8,128)S(1)}, f32[8,512,1024]{2,1,0:T(8,128)}, u32[]{:S(2)}) copy-start(f32[8,512,1024]{2,1,0:T(8,128)} %get-tuple-element.1250) | copy-start | bytes 50331652 | tf_op jit(solution)/shard_map/while
  900.6 41.8 %copy-start.101 = (bf16[1024,512]{1,0:T(8,128)(2,1)}, bf16[1024,512]{1,0:T(8,128)(2,1)S(1)}, u32[]{:S(2)}) copy-start(bf16[1024,512]{1,0:T(8,128)(2,1)S(1)} %copy.134) | copy-start | bytes 3145732
  917.6 22.1 %copy-start.74 = (f32[1024,512]{0,1:T(8,128)}, f32[1024,512]{0,1:T(8,128)S(1)}, u32[]{:S(2)}) copy-start(f32[1024,512]{0,1:T(8,128)S(1)} %get-tuple-element.738) | copy-start | bytes 6291460
  942.4 388.3 %all-reduce.9.cloned.1.call-start = ((), (), s32[]{:S(2)}) async-start(), calls=%async_computation.1 | async-start | bytes 25165824 | tf_op jit(solution)/shard_map/psum | solution.py:349
  991.2 47.1 %copy-start.276 = (f32[512]{0:T(512)S(1)}, f32[512]{0:T(512)}, u32[]{:S(2)}) copy-start(f32[512]{0:T(512)} %get-tuple-element.590) | copy-start | bytes 6148
  991.2 47.1 %copy-start.277 = (f32[512]{0:T(512)S(1)}, f32[512]{0:T(512)}, u32[]{:S(2)}) copy-start(f32[512]{0:T(512)} %get-tuple-element.588) | copy-start | bytes 6148
  991.2 47.1 %copy-start.285 = (f32[512]{0:T(512)S(1)}, f32[512]{0:T(512)}, u32[]{:S(2)}) copy-start(f32[512]{0:T(512)} %get-tuple-element.602) | copy-start | bytes 6148
  991.3 47.1 %copy-start.287 = (f32[512]{0:T(512)S(1)}, f32[512]{0:T(512)}, u32[]{:S(2)}) copy-start(f32[512]{0:T(512)} %get-tuple-element.600) | copy-start | bytes 6148
  991.3 47.1 %copy-start.289 = (f32[512]{0:T(512)S(1)}, f32[512]{0:T(512)}, u32[]{:S(2)}) copy-start(f32[512]{0:T(512)} %get-tuple-element.598) | copy-start | bytes 6148
  991.3 47.1 %copy-start.294 = (f32[2048]{0:T(1024)S(1)}, f32[2048]{0:T(1024)}, u32[]{:S(2)}) copy-start(f32[2048]{0:T(1024)} %get-tuple-element.858) | copy-start | bytes 24580
  991.3 47.1 %copy-start.295 = (f32[2048]{0:T(1024)S(1)}, f32[2048]{0:T(1024)}, u32[]{:S(2)}) copy-start(f32[2048]{0:T(1024)} %get-tuple-element.856) | copy-start | bytes 24580
  991.3 47.1 %copy-start.296 = (f32[2048]{0:T(1024)S(1)}, f32[2048]{0:T(1024)}, u32[]{:S(2)}) copy-start(f32[2048]{0:T(1024)} %get-tuple-element.854) | copy-start | bytes 24580
  (321 other events, 1079.6 us)
Sparse Core Ops, SparseCore 0:
  942.5 148.8 all-reduce.6
  1097.2 233.4 all-reduce.8
where the time goes:
time: 1360 us; the launch traced here: 1350 us
  matrix products  454 us (33%)
  local copies, waits for them, and re-layouts  281 us (21%)
  other arithmetic  254 us (19%)
  waiting for transfers between devices  225 us (17%)
  blocking collectives  104 us (8%)
  between operations  18.1 us (1%)
    psum x1, waiting for transfers between devices, on_device(): block_total = lax.psum(block_total, 'dp')  225 us
    dot_general x12, matrix products, one_block(): jnp.einsum('qhe,khe->hqk', query_rows, key_rows, preferred_element_type=j...  94.5 us
    convert_element_type x6, other arithmetic, one_block(): score_grad = (attention * (weight_grad - centre)).astype(jnp.bfloat16)  68.8 us
    psum x1, blocking collectives, on_device(): block_total = lax.psum(block_total, 'dp')  60 us
    dot_general x6, matrix products, one_block(): jnp.einsum('qhe,khe->hqk', own_context, value_rows, preferred_element_typ...  56.3 us
    unnamed x669, local copies, waits for them, and re-layouts  54.7 us
    psum x1, blocking collectives, on_device(): lax.psum((head_total[0], head_total[1], head_total[2], head_total[3], hea...  43.9 us
    dynamic_update_slice x24, local copies, waits for them, and re-layouts, attend(): context, log_total = lax.map(one_block, jnp.arange(row_count // block_rows))  39.8 us
  transfers between devices with their start and end apart: 4, of which 1 were waited for; matrix products, arithmetic and copies ran while one was open for 13% of the time, Pallas kernels for 0%

commit v1 on v0

v1 whole, which is shorter than its diff:
```python
import functools
import math

import jax
import jax.numpy as jnp
from jax import lax
from jax.experimental import pallas as pl
from jax.experimental.pallas import tpu as pltpu
from jax.sharding import PartitionSpec as P

HEAD = 64
BF = jnp.bfloat16
F32 = jnp.float32
LOG2E = math.log2(math.e)
NORM_EPS = 1e-06
MASKED = -1e30
GELU = 0.7978845608028654
CUBIC = 0.044715
NN = (((1,), (0,)), ((), ()))
NT = (((1,), (1,)), ((), ()))
TN = (((0,), (0,)), ((), ()))
TOKENS = 256
WINDOW = 256
PARAMS = pltpu.CompilerParams(vmem_limit_bytes=56 << 20)


def dot(a, b, dims):
    return lax.dot_general(a, b, dims, preferred_element_type=F32)


def lanes(shape):
    return lax.broadcasted_iota(jnp.int32, shape, 1)


def split(values):
    high = values.astype(BF)
    return high, (values - high.astype(F32)).astype(BF)


def dot3(left, right, dims):
    return dot(left[0], right[0], dims) + dot(left[0], right[1], dims) + dot(left[1], right[0], dims)


def norm_parts(values):
    center = values - jnp.mean(values, -1, keepdims=True)
    inverse = lax.rsqrt(jnp.mean(center * center, -1, keepdims=True) + NORM_EPS)
    return center * inverse, inverse


def norm_back(grad, gain, hat, inverse):
    scaled = grad * gain
    return inverse * (
        scaled
        - jnp.mean(scaled, -1, keepdims=True)
        - hat * jnp.mean(scaled * hat, -1, keepdims=True)
    )


def column_sum(values):
    return jnp.sum(values, 0, keepdims=True)


def code_kernel(index, table, unit, wide, raw):
    count = raw.shape[0]

    def some(step, carry):
        for inner in range(8):
            token = step * 8 + inner
            raw[pl.ds(token, 1), :] = table[pl.ds(index[token], 1), :]
        return carry

    lax.fori_loop(0, count // 8, some, 0)
    values = raw[...]
    values = values * lax.rsqrt(jnp.sum(values * values, -1, keepdims=True) + NORM_EPS)
    unit[...] = values
    high, low = split(values)
    wide[...] = jnp.concatenate([high, low, high, jnp.zeros_like(high)], 1)


def gather_codes(index, table):
    count, width = index.shape[0], table.shape[1]
    return pl.pallas_call(
        code_kernel,
        in_specs=[pl.BlockSpec(memory_space=pltpu.SMEM), pl.BlockSpec(memory_space=pltpu.VMEM)],
        out_specs=[pl.BlockSpec(memory_space=pltpu.VMEM)] * 2,
        out_shape=(
            jax.ShapeDtypeStruct((count, width), F32),
            jax.ShapeDtypeStruct((count, 4 * width), BF),
        ),
        scratch_shapes=[pltpu.VMEM((count, width), F32)],
        compiler_params=PARAMS,
        name="gather_codes",
    )(index, table)


def scatter_kernel(index, unit, latent, table, out, total, rows):
    count = rows.shape[0]
    width = unit.shape[1]
    total[...] = jnp.zeros_like(total)
    rows[...] = 2.0 * (unit[...] - latent[...])

    def some(step, carry):
        for inner in range(8):
            token = step * 8 + inner
            here = pl.ds(index[token], 1)
            total[here, :] = total[here, :] + rows[pl.ds(token, 1), :]
        return carry

    lax.fori_loop(0, count // 8, some, 0)
    block = 1024

    def back(step, carry):
        here = pl.ds(pl.multiple_of(step * block, block), block)
        values = table[here, :]
        grad = total[here, :]
        inverse = lax.rsqrt(jnp.sum(values * values, -1, keepdims=True) + NORM_EPS)
        book = values * inverse
        out[here, :] = inverse * (grad - book * jnp.sum(book * grad, -1, keepdims=True))
        return carry

    lax.fori_loop(0, total.shape[0] // block, back, 0)


def scatter_codes(index, unit, latent, table):
    return pl.pallas_call(
        scatter_kernel,
        in_specs=[pl.BlockSpec(memory_space=pltpu.SMEM)] + [pl.BlockSpec(memory_space=pltpu.VMEM)] * 3,
        out_specs=pl.BlockSpec(memory_space=pltpu.VMEM),
        out_shape=jax.ShapeDtypeStruct(table.shape, F32),
        scratch_shapes=[pltpu.VMEM(table.shape, F32), pltpu.VMEM(unit.shape, F32)],
        compiler_params=PARAMS,
        name="scatter_codes",
    )(index, unit, latent, table)


def entry_values(encoder, edge, wide, up, head_bias):
    return jnp.where(encoder, edge.astype(F32), dot(wide, up, NN) + head_bias[1:2, :])


def project_kernel(side, edge, wide, up, head_bias, gains, biases, weight, n1, query, key, value):
    width = edge.shape[1]
    encoder = side[0] == 0
    values = entry_values(encoder, edge[...], wide[...], up[...], head_bias[...])
    hat, unused = norm_parts(values)
    normed = (hat * gains[0:1, :] + biases[3:4, :]).astype(BF)
    n1[...] = normed
    query[...] = (
        (dot(normed, weight[:, :width], NN) + biases[0:1, :]) * (LOG2E * HEAD ** (-0.5))
    ).astype(BF)
    key[...] = dot(normed, weight[:, width : 2 * width], NN).astype(BF)
    value[...] = (dot(normed, weight[:, 2 * width :], NN) + biases[1:2, :]).astype(BF)


def merge(low_half, left, right):
    return jnp.where(low_half, left, right)


def attend_kernel(windows, query, key, value, query_mark, key_mark, context, marks, *, row):
    count = query.shape[0]
    size = TOKENS
    pairs = query.shape[1] // 128
    low_query = lanes((size, 128)) < 64
    mark_lane = lanes((size, 128)) & 63

    def block(number, start, extent):
        rows = pl.ds(pl.multiple_of(number * size, size), size)
        keys = pl.ds(pl.multiple_of(start, WINDOW), extent)
        low_key = lanes((extent, 128)) < 64
        query_aug, key_aug = query_mark[rows, :], key_mark[keys, :]
        ones = jnp.ones((extent, 128), BF)
        scores = []
        for pair in range(pairs):
            here = slice(pair * 128, pair * 128 + 128)
            query_pair, key_pair = query[rows, here], key[keys, here]
            scores.append(
                dot(merge(low_query, query_pair, query_aug), merge(low_key, key_pair, key_aug), NT)
            )
            scores.append(
                dot(merge(low_query, query_aug, query_pair), merge(low_key, key_aug, key_pair), NT)
            )
        tops = [jnp.max(score, -1, keepdims=True) for score in scores]
        raised = [jnp.exp2(score - top).astype(BF) for score, top in zip(scores, tops)]
        for pair in range(pairs):
            here = slice(pair * 128, pair * 128 + 128)
            value_pair = value[keys, here]
            even = dot(raised[2 * pair], merge(low_key, value_pair, ones), NN)
            odd = dot(raised[2 * pair + 1], merge(low_key, ones, value_pair), NN)
            total = merge(low_query, odd, even)
            context[rows, here] = (
                merge(low_query, even, odd) / pltpu.roll(total, 64, 1)
            ).astype(BF)
            level = -(merge(low_query, tops[2 * pair + 1], tops[2 * pair]) + jnp.log2(total))
            first = level.astype(BF)
            rest = level - first.astype(F32)
            second, third = split(rest)
            marks[rows, here] = merge(
                mark_lane == 4, first, merge(mark_lane == 5, second, merge(mark_lane == 6, third, query_aug))
            )

    def one(number, carry):
        base = (row * (count // size) + number) * 2
        for_windows(windows[base], windows[base + 1], count, functools.partial(block, number))
        return carry

    lax.fori_loop(0, count // size, one, 0)


def for_windows(start, steps, count, run):
    extents = list(range(2 * WINDOW, count + 1, WINDOW))
    for position, extent in enumerate(extents):
        take = steps * WINDOW <= extent
        if position:
            take = take & (steps * WINDOW > extents[position - 1])

        @pl.when(take)
        def _():
            run(jnp.minimum(start * WINDOW, count - extent), extent)


def gelu_parts(values):
    square = values * values
    half = 0.5 + 0.5 * jnp.tanh(values * (GELU + (GELU * CUBIC) * square))
    active = values * half
    slope = half + active * (1.0 - half) * (2.0 * GELU + (6.0 * GELU * CUBIC) * square)
    return active, slope


def hidden_kernel(
    side, edge, wide, up, head_bias, context, weight_out, gains, biases, weight_in, hidden_bias,
    weight_last, output_gain, down, down_bias,
    mid, n2, active_out, slope_out, result, latent_out,
):
    encoder = side[0] == 0
    width = edge.shape[1]
    values = entry_values(encoder, edge[...], wide[...], up[...], head_bias[...])
    midway = values + (dot(context[...], weight_out[...], NN) + biases[2:3, :])
    mid[...] = midway
    hat, unused = norm_parts(midway)
    normed = (hat * gains[1:2, :] + biases[4:5, :]).astype(BF)
    n2[...] = normed
    total = midway + biases[5:6, :]
    chunk = 512
    for start in range(0, weight_in.shape[1], chunk):
        here = slice(start, start + chunk)
        active, slope = gelu_parts(dot(normed, weight_in[:, here], NN) + hidden_bias[0:1, here])
        active = active.astype(BF)
        active_out[:, here] = active
        slope_out[:, here] = slope.astype(BF)
        total = total + dot(active, weight_last[here, :], NN)
    result[...] = total

    @pl.when(encoder)
    def _():
        last_hat, unused = norm_parts(total)
        code = last_hat * output_gain[0:1, :] + head_bias[0:1, :]
        latent = code_product(code, down[...]) + down_bias[0:1, :]
        scale = lax.rsqrt(jnp.sum(latent * latent, -1, keepdims=True) + NORM_EPS)
        latent_out[...] = latent * scale


def code_product(values, weight):
    narrow = weight.shape[1] // 2
    high, low = split(values)
    both = dot(high, weight, NN)
    return both[:, :narrow] + both[:, narrow:] + dot(low, weight[:, :narrow], NN)


def tail_back_kernel(
    side, result, cotangent, unit, latent_in, output_gain, head_bias, down, down_bias, down_turned,
    weight_last, slope, weight_in, mid, gains, biases, weight_out,
    out_low, preact_low, mid_grad, branch_low, context_grad, sums, head_weight,
    upstream,
):
    encoder = side[0] == 0
    width = result.shape[1]
    narrow = unit.shape[1]

    @pl.when(pl.program_id(0) == 0)
    def _():
        sums[...] = jnp.zeros_like(sums)
        head_weight[...] = jnp.zeros_like(head_weight)

    @pl.when(encoder)
    def _():
        hat, inverse = norm_parts(result[...])
        normed = hat * output_gain[0:1, :] + head_bias[0:1, :]
        latent = code_product(normed, down[...]) + down_bias[0:1, :]
        scale = lax.rsqrt(jnp.sum(latent * latent, -1, keepdims=True) + NORM_EPS)
        code = latent * scale
        code_grad = latent_in[...] + 0.5 * (code - unit[...])
        latent_grad = scale * (code_grad - code * jnp.sum(code * code_grad, -1, keepdims=True))
        pieces = split(latent_grad)
        normed_grad = dot3(pieces, (down_turned[:narrow, :], down_turned[narrow:, :]), NN)
        head_weight[...] += dot3(pieces, split(normed), TN)
        sums[2:3, :width] += column_sum(normed_grad * hat)
        sums[2:3, width : 2 * width] += column_sum(normed_grad)
        sums[3:4, :narrow] += column_sum(latent_grad)
        upstream[...] = norm_back(normed_grad, output_gain[0:1, :], hat, inverse)

    @pl.when(jnp.logical_not(encoder))
    def _():
        upstream[...] = cotangent[...].astype(F32)

    above = upstream[...]
    low = above.astype(BF)
    out_low[...] = low
    sums[1:2, :width] += column_sum(low.astype(F32))
    normed_grad = None
    chunk = 512
    for start in range(0, weight_in.shape[1], chunk):
        here = slice(start, start + chunk)
        active_grad = dot(low, weight_last[here, :], NT)
        inner = (active_grad * slope[:, here].astype(F32)).astype(BF)
        preact_low[:, here] = inner
        sums[0:1, here] += column_sum(inner.astype(F32))
        term = dot(inner, weight_in[:, here], NT)
        normed_grad = term if normed_grad is None else normed_grad + term
    hat, inverse = norm_parts(mid[...])
    sums[1:2, 2 * width : 3 * width] += column_sum(normed_grad * hat)
    sums[1:2, 3 * width :] += column_sum(normed_grad)
    middle = above + norm_back(normed_grad, gains[1:2, :], hat, inverse)
    mid_grad[...] = middle
    branch = middle.astype(BF)
    branch_low[...] = branch
    sums[1:2, width : 2 * width] += column_sum(branch.astype(F32))
    context_grad[...] = dot(branch, weight_out[...], NT).astype(BF)


def attend_back_kernel(
    windows, query, marks, key, value, context_grad, context, key_mark,
    query_grad, key_grad, value_grad, grad_mark, key_total, value_total, *, row
):
    count = query.shape[0]
    size = TOKENS
    pairs = query.shape[1] // 128
    low_all = lanes((count, 128)) < 64
    low_query = lanes((size, 128)) < 64
    lane_all = lanes((count, 128)) & 63
    across = (
        lax.broadcasted_iota(jnp.int32, (128, 128), 0) // 64 != lanes((128, 128)) // 64
    ).astype(BF)
    zero = jnp.zeros((count, 128), BF)
    for pair in range(pairs):
        here = slice(pair * 128, pair * 128 + 128)
        product = split(context_grad[:, here].astype(F32) * context[:, here].astype(F32))
        level = -(dot(product[0], across, NN) + dot(product[1], across, NN))
        first = level.astype(BF)
        second, third = split(level - first.astype(F32))
        grad_mark[:, here] = merge(
            lane_all == 0, first, merge(lane_all == 1, second, merge(lane_all == 2, third, zero))
        )
    key_total[...] = jnp.zeros_like(key_total)
    value_total[...] = jnp.zeros_like(value_total)

    def block(number, start, extent):
        rows = pl.ds(pl.multiple_of(number * size, size), size)
        keys = pl.ds(pl.multiple_of(start, WINDOW), extent)
        low_key = lanes((extent, 128)) < 64
        key_aug = key_mark[keys, :]
        ones = jnp.where((lanes((extent, 128)) & 63) < 3, 1.0, 0.0).astype(BF)
        none = jnp.zeros((extent, 128), BF)
        for pair in range(pairs):
            here = slice(pair * 128, pair * 128 + 128)
            query_pair, key_pair, value_pair = query[rows, here], key[keys, here], value[keys, here]
            grad_pair, query_aug, grad_aug = context_grad[rows, here], marks[rows, here], grad_mark[rows, here]
            found = []
            for swap in (False, True):

                def both(low, left, right):
                    return merge(low, right, left) if swap else merge(low, left, right)

                scores = dot(both(low_key, key_pair, key_aug), both(low_query, query_pair, query_aug), NT)
                rise = dot(both(low_key, value_pair, ones), both(low_query, grad_pair, grad_aug), NT)
                chance = jnp.exp2(scores)
                score_grad = (chance * rise).astype(BF)
                found.append(
                    (
                        dot(score_grad, query_pair, NN),
                        dot(chance.astype(BF), grad_pair, NN),
                        dot(score_grad, both(low_key, key_pair, none), TN),
                    )
                )
            key_total[keys, here] += merge(low_key, found[0][0], found[1][0])
            value_total[keys, here] += merge(low_key, found[0][1], found[1][1])
            query_grad[rows, here] = ((found[0][2] + found[1][2]) * HEAD ** (-0.5)).astype(BF)

    def one(number, carry):
        base = (row * (count // size) + number) * 2
        for_windows(windows[base], windows[base + 1], count, functools.partial(block, number))
        return carry

    lax.fori_loop(0, count // size, one, 0)
    key_grad[...] = (key_total[...] * (1.0 / LOG2E)).astype(BF)
    value_grad[...] = value_total[...].astype(BF)


def entry_back_kernel(
    side, edge, wide, up, head_bias, unit, query_grad, key_grad, value_grad, weight, gains, biases,
    mid_grad, up_turned,
    entry, latent_out, sums, head_weight,
):
    encoder = side[0] == 0
    width = edge.shape[1]
    narrow = unit.shape[1]

    @pl.when(pl.program_id(0) == 0)
    def _():
        sums[...] = jnp.zeros_like(sums)
        head_weight[...] = jnp.zeros_like(head_weight)

    values = entry_values(encoder, edge[...], wide[...], up[...], head_bias[...])
    normed_grad = (
        dot(query_grad[...], weight[:, :width], NT)
        + dot(key_grad[...], weight[:, width : 2 * width], NT)
        + dot(value_grad[...], weight[:, 2 * width :], NT)
    )
    hat, inverse = norm_parts(values)
    sums[0:1, :width] += column_sum(query_grad[...].astype(F32))
    sums[0:1, width : 2 * width] += column_sum(value_grad[...].astype(F32))
    sums[0:1, 2 * width : 3 * width] += column_sum(normed_grad * hat)
    sums[0:1, 3 * width :] += column_sum(normed_grad)
    total = mid_grad[...] + norm_back(normed_grad, gains[0:1, :], hat, inverse)
    entry[...] = total

    @pl.when(jnp.logical_not(encoder))
    def _():
        sums[1:2, :width] += column_sum(total)
        latent_out[...] = code_product(total, up_turned[...])
        head_weight[...] += dot3(split(unit[...]), split(total), TN)


def weight_kernel(*refs, turns, adding):
    operands, refs = refs[:10], refs[10:]
    if adding:
        before, refs = refs[:4], refs[4:]
    active, out_low, n2, preact_low, context, branch_low, n1 = operands[:7]
    step = pl.program_id(0)
    first, second, third = turns

    def put(number, value):
        if adding:
            value = value + before[number][...]
        refs[number][...] = value

    @pl.when(step < first)
    def _():
        put(3, dot(active[...], out_low[...], TN))

    @pl.when((step >= first) & (step < second))
    def _():
        put(2, dot(n2[...], preact_low[...], TN))

    @pl.when((step >= second) & (step < third))
    def _():
        put(1, dot(context[...], branch_low[...], TN))

    for place in range(3):

        @pl.when(step == third + place)
        def _():
            put(0, dot(n1[...], operands[7 + place][...], TN))


def weight_grads(kept, back, before=None):
    active, n2, context, n1 = kept["active"], kept["n2"], kept["context"], kept["n1"]
    out_low, preact_low, branch_low = back["out_low"], back["preact_low"], back["branch_low"]
    count, width = n1.shape
    hidden = active.shape[1]
    tile = 512
    first = hidden // tile
    second = 2 * first
    third = second + 1
    whole = lambda step: (0, 0)
    down_rows = lambda step: (jnp.minimum(step, first - 1), 0)
    active_columns = lambda step: (0, jnp.minimum(step, first - 1))
    hidden_columns = lambda step: (0, jnp.clip(step - first, 0, first - 1))
    last_columns = lambda step: (0, jnp.clip(step - third, 0, 2))
    full = pl.BlockSpec((count, width), whole)
    in_specs = [
        pl.BlockSpec((count, tile), active_columns),
        full,
        full,
        pl.BlockSpec((count, tile), hidden_columns),
        full,
        full,
        full,
        full,
        full,
        full,
    ]
    out_specs = [
        pl.BlockSpec((width, tile), last_columns),
        pl.BlockSpec((width, width), whole),
        pl.BlockSpec((width, tile), hidden_columns),
        pl.BlockSpec((tile, width), down_rows),
    ]
    shapes = ((width, 3 * width), (width, width), (width, hidden), (hidden, width))
    operands = [active, out_low, n2, preact_low, context, branch_low, n1]
    operands += [back["query_grad"], back["key_grad"], back["value_grad"]]
    adding = before is not None
    if adding:
        operands += list(before)
        in_specs = in_specs + out_specs
    return pl.pallas_call(
        functools.partial(weight_kernel, turns=(first, second, third), adding=adding),
        grid=(third + 3,),
        in_specs=in_specs,
        out_specs=out_specs,
        out_shape=tuple(jax.ShapeDtypeStruct(shape, F32) for shape in shapes),
        input_output_aliases={10 + number: number for number in range(4)} if adding else {},
        compiler_params=PARAMS,
        name="weight_grads",
    )(*operands)


def nothing_kernel(*refs):
    pass


def unwritten(shapes):
    return pl.pallas_call(
        nothing_kernel,
        out_specs=[pl.BlockSpec(memory_space=pl.ANY)] * len(shapes),
        out_shape=tuple(shapes),
        name="unwritten",
    )()


KEPT = ("n1", "query", "key", "value", "context", "marks", "mid", "n2", "active", "slope", "result", "latent")
BACK = (
    "out_low", "preact_low", "mid_grad", "branch_low", "query_grad", "key_grad", "value_grad",
    "entry", "latent_out", "sums_late", "sums_early", "head_late", "head_early",
)


class Rows:
    def __init__(self, side, edges, wide, unit, windows, query_mark, key_mark, weights, head):
        self.side, self.edges, self.wide, self.unit = side, edges, wide, unit
        self.windows, self.query_mark, self.key_mark = windows, query_mark, key_mark
        (
            self.attention_in, self.attention_out, self.hidden_in, self.hidden_out,
            self.gains, self.biases, self.hidden_bias,
        ) = weights
        (
            self.output_gain, self.head_bias, self.down, self.down_bias, self.down_turned,
            self.up, self.up_turned,
        ) = head
        self.rows, self.count, self.width = edges.shape
        self.hidden = self.hidden_in.shape[1]
        self.narrow = unit.shape[1]

    def kept_shapes(self):
        n, d, f = self.count, self.width, self.hidden
        table = dict(
            n1=(d, BF), query=(d, BF), key=(d, BF), value=(d, BF), context=(d, BF), marks=(d, BF),
            mid=(d, F32), n2=(d, BF), active=(f, BF), slope=(f, BF), result=(d, F32), latent=(self.narrow, F32),
        )
        return {name: jax.ShapeDtypeStruct((n, size), kind) for name, (size, kind) in table.items()}

    def back_shapes(self):
        n, d, f = self.count, self.width, self.hidden
        table = dict(
            out_low=(n, d, BF), preact_low=(n, f, BF), mid_grad=(n, d, F32), branch_low=(n, d, BF),
            query_grad=(n, d, BF), key_grad=(n, d, BF), value_grad=(n, d, BF), entry=(n, d, F32),
            latent_out=(n, self.narrow, F32), sums_late=(8, f, F32), sums_early=(8, f, F32),
            head_late=(self.narrow, d, F32), head_early=(self.narrow, d, F32),
        )
        return {name: jax.ShapeDtypeStruct((a, b), kind) for name, (a, b, kind) in table.items()}

    def side_spec(self):
        return pl.BlockSpec(memory_space=pltpu.SMEM)

    def tokens(self, array):
        return pl.BlockSpec((TOKENS, array.shape[1]), lambda step: (step, 0))

    def whole(self, array):
        return pl.BlockSpec(array.shape, lambda step: (0,) * len(array.shape))

    def entry_specs(self, row):
        steps = self.count // TOKENS
        return [
            pl.BlockSpec((None, TOKENS, self.width), lambda step: (row, step, 0)),
            pl.BlockSpec((TOKENS, self.wide.shape[1]), lambda step: (row * steps + step, 0)),
            self.whole(self.up),
            self.whole(self.head_bias),
        ]

    def unit_spec(self, row):
        steps = self.count // TOKENS
        return pl.BlockSpec((TOKENS, self.narrow), lambda step: (row * steps + step, 0))

    def call(self, kernel, in_specs, operands, outs, out_specs, name, scratch=()):
        return pl.pallas_call(
            kernel,
            grid=(self.count // TOKENS,),
            in_specs=in_specs,
            out_specs=out_specs,
            out_shape=tuple(outs),
            scratch_shapes=list(scratch),
            compiler_params=PARAMS,
            name=name,
        )(*operands)

    def attention_call(self, kernel, row, operands, outs, name, scratch=()):
        half = self.width // 2

        def spec(array):
            if array.ndim == 3:
                return pl.BlockSpec((None, self.count, array.shape[2]), lambda step, info: (row, 0, 0))
            return pl.BlockSpec((self.count, half), lambda step, info: (0, step))

        return pl.pallas_call(
            functools.partial(kernel, row=row),
            grid_spec=pltpu.PrefetchScalarGridSpec(
                num_scalar_prefetch=1,
                grid=(2,),
                in_specs=[spec(array) for array in operands],
                out_specs=[spec(array) for array in outs],
                scratch_shapes=list(scratch),
            ),
            out_shape=tuple(outs),
            compiler_params=PARAMS,
            name=name,
        )(self.windows, *operands)

    def forward(self, row):
        shapes = self.kept_shapes()
        entry = (self.edges, self.wide, self.up, self.head_bias)
        kept = {}
        names = ("n1", "query", "key", "value")
        outs = self.call(
            project_kernel,
            [self.side_spec()] + self.entry_specs(row)
            + [self.whole(self.gains), self.whole(self.biases), self.whole(self.attention_in)],
            (self.side,) + entry + (self.gains, self.biases, self.attention_in),
            [shapes[name] for name in names],
            [self.tokens(shapes[name]) for name in names],
            "project",
        )
        kept.update(zip(names, outs))
        names = ("context", "marks")
        outs = self.attention_call(
            attend_kernel, row,
            (kept["query"], kept["key"], kept["value"], self.query_mark, self.key_mark),
            [shapes[name] for name in names],
            "attend",
        )
        kept.update(zip(names, outs))
        names = ("mid", "n2", "active", "slope", "result", "latent")
        consts = (
            self.attention_out, self.gains, self.biases, self.hidden_in, self.hidden_bias, self.hidden_out,
            self.output_gain, self.down, self.down_bias,
        )
        outs = self.call(
            hidden_kernel,
            [self.side_spec()] + self.entry_specs(row) + [self.tokens(kept["context"])]
            + [self.whole(array) for array in consts],
            (self.side,) + entry + (kept["context"],) + consts,
            [shapes[name] for name in names],
            [self.tokens(shapes[name]) for name in names],
            "hidden",
        )
        kept.update(zip(names, outs))
        return kept

    def backward(self, row, kept, latent_in):
        shapes = self.back_shapes()
        back = {}
        names = ("out_low", "preact_low", "mid_grad", "branch_low", "context_grad", "sums_late", "head_late")
        shapes["context_grad"] = shapes["out_low"]
        consts = (self.output_gain, self.head_bias, self.down, self.down_bias, self.down_turned, self.hidden_out)
        late = (self.gains, self.biases, self.attention_out)
        outs = self.call(
            tail_back_kernel,
            [self.side_spec(), self.tokens(kept["result"]), self.entry_specs(row)[0], self.unit_spec(row),
             self.tokens(latent_in)]
            + [self.whole(array) for array in consts]
            + [self.tokens(kept["slope"]), self.whole(self.hidden_in), self.tokens(kept["mid"])]
            + [self.whole(array) for array in late],
            (self.side, kept["result"], self.edges, self.unit, latent_in) + consts
            + (kept["slope"], self.hidden_in, kept["mid"]) + late,
            [shapes[name] for name in names],
            [self.tokens(shapes[name]) for name in names[:5]] + [self.whole(shapes[name]) for name in names[5:]],
            "tail_back",
            scratch=[pltpu.VMEM((TOKENS, self.width), F32)],
        )
        back.update(zip(names, outs))
        names = ("query_grad", "key_grad", "value_grad")
        half = self.width // 2
        outs = self.attention_call(
            attend_back_kernel, row,
            (kept["query"], kept["marks"], kept["key"], kept["value"], back.pop("context_grad"), kept["context"],
             self.key_mark),
            [shapes[name] for name in names],
            "attend_back",
            scratch=[
                pltpu.VMEM((self.count, half), BF),
                pltpu.VMEM((self.count, half), F32),
                pltpu.VMEM((self.count, half), F32),
            ],
        )
        back.update(zip(names, outs))
        names = ("entry", "latent_out", "sums_early", "head_early")
        grads = (back["query_grad"], back["key_grad"], back["value_grad"])
        outs = self.call(
            entry_back_kernel,
            [self.side_spec()] + self.entry_specs(row) + [self.unit_spec(row)]
            + [self.tokens(array) for array in grads]
            + [self.whole(self.attention_in), self.whole(self.gains), self.whole(self.biases),
               self.tokens(back["mid_grad"]), self.whole(self.up_turned)],
            (self.side, self.edges, self.wide, self.up, self.head_bias, self.unit) + grads
            + (self.attention_in, self.gains, self.biases, back["mid_grad"], self.up_turned),
            [shapes[name] for name in names],
            [self.tokens(shapes[name]) for name in names[:2]] + [self.whole(shapes[name]) for name in names[2:]],
            "entry_back",
        )
        back.update(zip(names, outs))
        return back


def pair_of(values, axis):
    return jnp.concatenate(split(values), axis)


def as_list(table, names):
    return [table[name] for name in names]


def marks_of(segments):
    lane = jnp.arange(128) & 63
    same = segments[..., None] == lane
    inside = lane < 4
    query_mark = jnp.where(inside & ~same, MASKED, 0.0).astype(BF)
    key_mark = jnp.where((inside & same) | ((lane > 3) & (lane < 7)), 1.0, 0.0).astype(BF)
    return query_mark, key_mark


def windows_of(segments):
    rows, count = segments.shape
    steps = count // WINDOW
    blocks = segments.reshape(rows, steps, WINDOW)
    least, most = blocks[:, :, 0], blocks[:, :, -1]
    meets = (most[:, :, None] >= least[:, None, :]) & (least[:, :, None] <= most[:, None, :])
    place = jnp.arange(steps)
    start = jnp.min(jnp.where(meets, place, steps), -1)
    stop = jnp.max(jnp.where(meets, place, -1), -1) + 1
    return jnp.stack([start, stop - start], -1).reshape(-1).astype(jnp.int32)


def on_device(
    boundary, segments, code_index, attention_in, attention_out, hidden_in, hidden_out, block_gains,
    block_biases, hidden_bias, output_gain, head_bias, down_weight, down_bias, up_weight, codebook,
):
    section = lax.axis_index("section")
    encoder = section == 0
    side = section.astype(jnp.int32)[None]
    edges = boundary[0]
    rows, count, width = edges.shape
    hidden = hidden_in.shape[2]
    index = code_index.reshape(-1)
    unit, wide = gather_codes(index, codebook)
    query_mark, key_mark = marks_of(segments)
    up_high, up_low = split(up_weight)
    work = Rows(
        side, edges, wide, unit, windows_of(segments), query_mark, key_mark,
        (
            attention_in[0], attention_out[0], hidden_in[0], hidden_out[0], block_gains[0], block_biases[0],
            hidden_bias,
        ),
        (
            output_gain[None], head_bias, pair_of(down_weight, 1), down_bias[None], pair_of(down_weight.T, 0),
            jnp.concatenate([up_high, up_high, up_low, jnp.zeros_like(up_low)], 0), pair_of(up_weight.T, 1),
        ),
    )
    kept_shapes = as_list(work.kept_shapes(), KEPT)
    back_shapes = as_list(work.back_shapes(), BACK)
    book_shape = jax.ShapeDtypeStruct(codebook.shape, F32)
    weight_shapes = [
        jax.ShapeDtypeStruct(shape, F32)
        for shape in ((width, 3 * width), (width, width), (width, hidden), (hidden, width))
    ]
    quiet = jnp.zeros((count, unit.shape[1]), F32)
    first_kept = work.forward(0)

    def encoder_second():
        kept = work.forward(1)
        latent = jnp.concatenate([first_kept["latent"], kept["latent"]], 0)
        book = scatter_codes(index, unit, latent, codebook)
        return as_list(kept, KEPT), list(unwritten(back_shapes)), book

    def decoder_first():
        back = work.backward(0, first_kept, quiet)
        return list(unwritten(kept_shapes)), as_list(back, BACK), unwritten([book_shape])[0]

    kept_a, back_a, book = lax.cond(encoder, encoder_second, decoder_first)
    back_a = dict(zip(BACK, back_a))
    kept_a = dict(zip(KEPT, kept_a))
    latent_in = lax.ppermute(back_a["latent_out"], "section", [(1, 0)])

    def encoder_third():
        return list(unwritten(kept_shapes)), as_list(work.backward(0, first_kept, latent_in), BACK)

    def decoder_third():
        return as_list(work.forward(1), KEPT), list(unwritten(back_shapes))

    kept_b, back_b = lax.cond(encoder, encoder_third, decoder_third)
    kept_b, back_b = dict(zip(KEPT, kept_b)), dict(zip(BACK, back_b))

    def encoder_fourth():
        return list(unwritten(back_shapes)), list(weight_grads(first_kept, back_b))

    def decoder_fourth():
        return as_list(work.backward(1, kept_b, quiet), BACK), list(unwritten(weight_shapes))

    back_c, weights_c = lax.cond(encoder, encoder_fourth, decoder_fourth)
    back_c = dict(zip(BACK, back_c))
    latent_in_second = lax.ppermute(back_c["latent_out"], "section", [(1, 0)])

    def encoder_fifth():
        back = work.backward(1, kept_a, latent_in_second)
        total = weight_grads(kept_a, back, weights_c)
        sums = [back[name] + back_b[name] for name in BACK[-4:]]
        edge = jnp.stack([back_b["entry"], back["entry"]])
        return list(total), sums, edge

    def decoder_fifth():
        total = weight_grads(first_kept, back_a)
        total = weight_grads(kept_b, back_c, total)
        sums = [back_a[name] + back_c[name] for name in BACK[-4:]]
        edge = jnp.stack([first_kept["result"], kept_b["result"]])
        return list(total), sums, edge

    totals, sums, edge = lax.cond(encoder, encoder_fifth, decoder_fifth)
    head_weight = jnp.where(encoder, sums[2], sums[3])
    book = jnp.where(encoder, book, 0.0).reshape(-1, 128)
    totals, sums_late, sums_early, head_weight, book = lax.psum(
        (totals, sums[0], sums[1], head_weight, book), "dp"
    )
    from_encoder = jnp.where(
        encoder,
        jnp.concatenate([sums_late[2].reshape(-1, 128), sums_late[3].reshape(-1, 128)], 0), 0.0
    )
    from_decoder = jnp.where(encoder, 0.0, sums_early[1].reshape(-1, 128))
    empty = jnp.zeros_like(head_weight)
    book, head_sums, down_grad, up_grad = lax.psum(
        (
            book,
            jnp.concatenate([from_encoder, from_decoder], 0),
            jnp.where(encoder, head_weight, empty),
            jnp.where(encoder, empty, head_weight),
        ),
        "section",
    )
    head_sums = head_sums.reshape(3, -1)
    late, early = sums_late[1].reshape(4, width), sums_early[0].reshape(4, width)
    return (
        edge[None],
        totals[0][None],
        totals[1][None],
        totals[2][None],
        totals[3][None],
        jnp.stack([early[2], late[2]])[None],
        jnp.stack([early[0], early[1], late[1], early[3], late[3], late[0]])[None],
        sums_late[0][None],
        head_sums[0, :width],
        jnp.stack([head_sums[0, width : 2 * width], head_sums[2, :width]]),
        down_grad.T,
        head_sums[1, : unit.shape[1]],
        up_grad,
        book.reshape(codebook.shape),
    )


def solution(mesh):
    return jax.shard_map(
        on_device,
        mesh=mesh,
        in_specs=(
            P("section", "dp", None, None), P("dp", None), P("dp", None),
            P("section", None, None), P("section", None, None), P("section", None, None),
            P("section", None, None), P("section", None, None), P("section", None, None),
            P("section", None), P(), P(), P(), P(), P(), P(),
        ),
        out_specs=(
            P("section", "dp", None, None), P("section", None, None), P("section", None, None),
            P("section", None, None), P("section", None, None), P("section", None, None),
            P("section", None, None), P("section", None), P(), P(), P(), P(), P(), P(),
        ),
        check_vma=False,
    )
```

time: 1360 us -> 753 us (0.55)
  matrix products: 454 us -> 0 us
  local copies, waits for them, and re-layouts: 281 us -> 53.1 us
  other arithmetic: 254 us -> 26.2 us
  Pallas kernels: 0 us -> 214 us
  waiting for transfers between devices: 225 us -> 402 us
  blocking collectives: 104 us -> 9.07 us
    dot_general x95 -> x0, matrix products: 454 us -> none  [the longest x12 94.5 us: one_block(): jnp.einsum('qhe,khe->hqk', query_rows, key_rows, preferred_element_type=j...]
    pallas_call x0 -> x19, Pallas kernels: none -> 214 us  [the longest x8 98.8 us: call(): pl.pallas_call(kernel, grid=(self.count // TOKENS,), in_specs=in_specs, o...]
    psum x2, waiting for transfers between devices: 225 us -> 378 us  [the longest x1 279 us: on_device(): lax.psum((totals, sums[0], sums[1], head_weight, book), 'dp')]
    reduce_sum x56 -> x0, other arithmetic: 97.2 us -> none  [the longest x12 33.5 us: layer_norm(): return center * lax.rsqrt(spread + norm_eps) * gain + offset]
    psum x2 -> x1, blocking collectives: 104 us -> 9.07 us  [on_device(): lax.psum((book, jnp.concatenate([from_encoder, from_decoder], 0), jnp.whe...]
    convert_element_type x6, other arithmetic: 68.8 us -> 5.53 us  [the longest x4 3.27 us: split(): return (high, (values - high.astype(F32)).astype(BF))]
    while x81 -> x0, local copies, waits for them, and re-layouts: 55.7 us -> none
    add x12 -> x2, other arithmetic: 58.1 us -> 3.02 us  [decoder_fifth(): sums = [back_a[name] + back_c[name] for name in BACK[-4:]]]
  transfers between devices with their start and end apart: 4 -> 4, of which waited for: 1 -> 4; matrix products, arithmetic and copies ran while one was open for 13% -> 2% of each run, Pallas kernels for 0% -> 0%
where the time goes in v1:
time: 753 us; the launch traced here: 742 us
  waiting for transfers between devices  402 us (53%)
  Pallas kernels  214 us (28%)
  local copies, waits for them, and re-layouts  53.1 us (7%)
  other arithmetic  26.2 us (3%)
  loops' own time  20.7 us (3%)
  between operations  14.5 us (2%)
  blocking collectives  9.07 us (1%)
    psum x1, waiting for transfers between devices, on_device(): lax.psum((totals, sums[0], sums[1], head_weight, book), 'dp')  279 us
    psum x1, waiting for transfers between devices, on_device(): lax.psum((book, jnp.concatenate([from_encoder, from_decoder], 0), jnp.whe...  99 us
    pallas_call x8, Pallas kernels, call(): pl.pallas_call(kernel, grid=(self.count // TOKENS,), in_specs=in_specs, o...  98.8 us
    pallas_call x4, Pallas kernels, attention_call(): pl.pallas_call(functools.partial(kernel, row=row), grid_spec=pltpu.Prefet...  57 us
    pallas_call x2, Pallas kernels, weight_grads(): pl.pallas_call(functools.partial(weight_kernel, turns=(first, second, thi...  38.2 us
    unnamed x41, local copies, waits for them, and re-layouts  21.6 us
  transfers between devices with their start and end apart: 4, of which 4 were waited for; matrix products, arithmetic and copies ran while one was open for 2% of the time, Pallas kernels for 0%

profile of v1, /device:TPU:0, one launch (start us, length us, event | category | flops | bytes accessed | tf_op | source)
XLA Modules:
  0.0 742.2 jit_solution(760808639791694611)
XLA Ops:
  9.1 1.5 subtract_convert_fusion.1
  17.6 3.8 copy.81.table
  21.5 6.3 gather_codes.1
  29.4 6.0 project.5
  35.4 10.4 %attend.5 = (bf16[1024,512]{1,0:T(8,128)(2,1)}, bf16[1024,512]{1,0:T(8,128)(2,1)}) custom-call(s32[16]{0:T(128)} %reshape.90.windows, bf16[1024,512]{1,0:T(8,128)(2,1)} %get-tuple-element.905.query, bf16[1024,512]{1,0:T(8,128)(2,1)} %get-tuple-element.906.key, bf16[1024,512]{1,0:T(8,128)(2,1)} %get-tuple-element.907.value, ...), custom_call_target="tpu_custom_call" | custom-call | tf_op jit(solution)/shard_map/attend/pallas_call | solution.py:612
  45.9 18.2 %hidden.5 = (f32[1024,512]{1,0:T(8,128)}, bf16[1024,512]{1,0:T(8,128)(2,1)}, bf16[1024,2048]{1,0:T(8,128)(2,1)}, bf16[1024,2048]{1,0:T(8,128)(2,1)}, f32[1024,512]{1,0:T(8,128)}, /*index=5*/f32[1024,32]{1,0:T(8,128)}) custom-call(s32[1]{0:T(128)} %bitcast.6.side, bf16[2,1024,512]{2,1,0:T(8,128)(2,1)S(1)} %bitcast.57, ...), custom_call_target="tpu_custom_call" | custom-call | tf_op jit(solution)/shard_map/hidden/pallas_call | solution.py:593
  64.1 71.4 %conditional.4 = (bf16[1024,512]{1,0:T(8,128)(2,1)}, bf16[1024,512]{1,0:T(8,128)(2,1)}, bf16[1024,512]{1,0:T(8,128)(2,1)}, bf16[1024,512]{1,0:T(8,128)(2,1)}, bf...) conditional(s32[]{:T(128)} %convert_element_type.48, ...), branch_computations={%region_2.3_spmd, %region_3.4_spmd} | conditional | flops 65536 | bytes 20447528 | solution.py:795
  76.0 1.9 copy.89
  77.9 3.7 copy.90.table
  81.5 5.8 project.3
  87.4 10.0 %attend.3 = (bf16[1024,512]{1,0:T(8,128)(2,1)S(1)}, bf16[1024,512]{1,0:T(8,128)(2,1)}) custom-call(s32[16]{0:T(128)} %get-tuple-element.514.windows, bf16[1024,512]{1,0:T(8,128)(2,1)S(1)} %get-tuple-element.1344.query, bf16[1024,512]{1,0:T(8,128)(2,1)S(1)} %get-tuple-element.1345.key, bf16[1024,512]{1,0:T(8,128)(2,1)S(1)} %get-tuple-element.1346.value, ...), custom_call_target="tpu_custom_call" | custom-call | tf_op jit(solution)/shard_map/cond/branch_1_fun/attend/pallas_call | solution.py:612
  97.4 18.7 %hidden.3 = (f32[1024,512]{1,0:T(8,128)}, bf16[1024,512]{1,0:T(8,128)(2,1)}, bf16[1024,2048]{1,0:T(8,128)(2,1)}, bf16[1024,2048]{1,0:T(8,128)(2,1)}, f32[1024,512]{1,0:T(8,128)}, /*index=5*/f32[1024,32]{1,0:T(8,128)}) custom-call(s32[1]{0:T(128)} %get-tuple-element.502.side, bf16[2,1024,512]{2,1,0:T(8,128)(2,1)S(1)} %get-tuple-element.503.edge, ...), custom_call_target="tpu_custom_call" | custom-call | tf_op jit(solution)/shard_map/cond/branch_1_fun/hidden/pallas_call | solution.py:593
  116.2 1.9 copy.79
  118.0 1.7 pad_maximum_fusion
  119.7 2.3 copy.80.latent
  122.0 13.5 %scatter_codes.1 = f32[8192,32]{1,0:T(8,128)} custom-call(s32[2048]{0:T(1024)} %get-tuple-element.542.index, f32[2048,32]{1,0:T(8,128)S(1)} %get-tuple-element.543.unit, f32[2048,32]{1,0:T(8,128)} %copy.80.latent, f32[8192,32]{1,0:T(8,128)} %copy.90.table), custom_call_target="tpu_custom_call" | custom-call | tf_op jit(solution)/shard_map/cond/branch_1_fun/scatter_codes/pallas_call | solution.py:125
  136.8 13.1 %collective-permute-done = f32[1024,32]{1,0:T(8,128)} collective-permute-done((f32[1024,32]{1,0:T(8,128)}, f32[1024,32]{1,0:T(8,128)}, u32[]{:S(2)}, u32[]{:S(2)}) %collective-permute-start) | collective-permute-done | bytes 131104 | tf_op jit(solution)/shard_map/ppermute | solution.py:798
  149.9 43.1 %conditional.5 = (bf16[1024,512]{1,0:T(8,128)(2,1)}, bf16[1024,512]{1,0:T(8,128)(2,1)}, bf16[1024,512]{1,0:T(8,128)(2,1)}, bf16[1024,512]{1,0:T(8,128)(2,1)}, bf...) conditional(s32[]{:T(128)} %convert_element_type.48, ...), branch_computations={%region_4.5_spmd, %region_5.6_spmd} | conditional | bytes 16908576 | solution.py:806
  151.1 16.9 %tail_back.6 = (bf16[1024,512]{1,0:T(8,128)(2,1)}, bf16[1024,2048]{1,0:T(8,128)(2,1)}, f32[1024,512]{1,0:T(8,128)}, bf16[1024,512]{1,0:T(8,128)(2,1)}, bf16[1024...) custom-call(s32[1]{0:T(128)} %get-tuple-element.598.side, f32[1024,512]{1,0:T(8,128)} %get-tuple-element.599.result, ...), custom_call_target="tpu_custom_call" | custom-call | tf_op jit(solution)/shard_map/cond/branch_1_fun/tail_back/pallas_call | solution.py:593
  168.0 17.3 %attend_back.6 = (bf16[1024,512]{1,0:T(8,128)(2,1)S(1)}, bf16[1024,512]{1,0:T(8,128)(2,1)S(1)}, bf16[1024,512]{1,0:T(8,128)(2,1)S(1)}) custom-call(s32[16]{0:T(128)} %get-tuple-element.618.windows, bf16[1024,512]{1,0:T(8,128)(2,1)} %get-tuple-element.619.query, bf16[1024,512]{1,0:T(8,128)(2,1)S(1)} %copy-done.26, bf16[1024,512]{1,0:T(8,128)(2,1)} %get-tuple-element.621.key, ...), custom_call_target="tpu_custom_call" | custom-call | tf_op jit(solution)/shard_map/cond/branch_1_fun/attend_back/pallas_call | solution.py:612
  185.4 7.6 %entry_back.6 = (f32[1024,512]{1,0:T(8,128)}, f32[1024,32]{1,0:T(8,128)}, f32[8,2048]{1,0:T(8,128)}, f32[32,512]{1,0:T(8,128)}) custom-call(s32[1]{0:T(128)} %get-tuple-element.598.side, bf16[2,1024,512]{2,1,0:T(8,128)(2,1)S(1)} %get-tuple-element.600.cotangent.edge, bf16[2048,128]{1,0:T(8,128)(2,1)} %get-tuple-element.629.wide, ...), custom_call_target="tpu_custom_call" | custom-call | tf_op jit(solution)/shard_map/cond/branch_1_fun/entry_back/pallas_call | solution.py:593
  193.0 25.8 %conditional.6 = (bf16[1024,512]{1,0:T(8,128)(2,1)}, bf16[1024,2048]{1,0:T(8,128)(2,1)}, bf16[1024,512]{1,0:T(8,128)(2,1)}, bf16[1024,512]{1,0:T(8,128)(2,1)}, b...) conditional(s32[]{:T(128)} %convert_element_type.48, ...), branch_computations={%region_6.7_spmd, %region_7.8_spmd} | conditional | bytes 17039596 | solution.py:815
  200.7 18.1 %weight_grads.7 = (f32[512,1536]{1,0:T(8,128)}, f32[512,512]{1,0:T(8,128)}, f32[512,2048]{1,0:T(8,128)}, f32[2048,512]{1,0:T(8,128)}) custom-call(bf16[1024,2048]{1,0:T(8,128)(2,1)} %get-tuple-element.694.refs_0_, bf16[1024,512]{1,0:T(8,128)(2,1)} %get-tuple-element.695.refs_1_, bf16[1024,512]{1,0:T(8,128)(2,1)} %get-tuple-element.696.refs_2_, ...), custom_call_target="tpu_custom_call" | custom-call | tf_op jit(solution)/shard_map/cond/branch_1_fun/weight_grads/pallas_call | solution.py:504
  220.1 4.5 broadcast_select_fusion
  224.6 4.1 reshape.92
  228.7 10.8 %collective-permute-done.1 = f32[1024,32]{1,0:T(8,128)} collective-permute-done((f32[1024,32]{1,0:T(8,128)}, f32[1024,32]{1,0:T(8,128)}, u32[]{:S(2)}, u32[]{:S(2)}) %collective-permute-start.1) | collective-permute-done | bytes 131104 | tf_op jit(solution)/shard_map/ppermute | solution.py:817
  239.5 76.7 %conditional.7 = (f32[512,1536]{1,0:T(8,128)}, f32[512,512]{1,0:T(8,128)}, f32[512,2048]{1,0:T(8,128)}, f32[2048,512]{1,0:T(8,128)}, f32[8,2048]{1,0:T(8,128)}, ...) conditional(s32[]{:T(128)} %convert_element_type.48, ...), branch_computations={%region_8.9_spmd, %region_9.10_spmd} | conditional | flops 1048576 | bytes 42598560 | solution.py:833
  239.9 1.5 copy.255
  244.3 1.5 copy.249
  246.5 16.8 %tail_back.8 = (bf16[1024,512]{1,0:T(8,128)(2,1)}, bf16[1024,2048]{1,0:T(8,128)(2,1)}, f32[1024,512]{1,0:T(8,128)}, bf16[1024,512]{1,0:T(8,128)(2,1)}, bf16[1024...) custom-call(s32[1]{0:T(128)} %get-tuple-element.747.side, f32[1024,512]{1,0:T(8,128)} %get-tuple-element.748.result, ...), custom_call_target="tpu_custom_call" | custom-call | tf_op jit(solution)/shard_map/cond/branch_1_fun/tail_back/pallas_call | solution.py:593
  263.3 19.2 %attend_back.8 = (bf16[1024,512]{1,0:T(8,128)(2,1)}, bf16[1024,512]{1,0:T(8,128)(2,1)}, bf16[1024,512]{1,0:T(8,128)(2,1)}) custom-call(s32[16]{0:T(128)} %get-tuple-element.770.windows, bf16[1024,512]{1,0:T(8,128)(2,1)} %get-tuple-element.771.query, bf16[1024,512]{1,0:T(8,128)(2,1)} %get-tuple-element.772.marks, bf16[1024,512]{1,0:T(8,128)(2,1)} %get-tuple-element.773.key, ...), custom_call_target="tpu_custom_call" | custom-call | tf_op jit(solution)/shard_map/cond/branch_1_fun/attend_back/pallas_call | solution.py:612
  282.5 20.1 %weight_grads.10 = (f32[512,1536]{1,0:T(8,128)}, f32[512,512]{1,0:T(8,128)}, f32[512,2048]{1,0:T(8,128)S(1)}, f32[2048,512]{1,0:T(8,128)}) custom-call(bf16[1024,2048]{1,0:T(8,128)(2,1)} %get-tuple-element.746.refs_0_, bf16[1024,512]{1,0:T(8,128)(2,1)} %get-tuple-element.764.refs_1_, ...), custom_call_target="tpu_custom_call", output_to_operand_aliasing={{0}: (10, {}), {1}: (11, {}), {2}: (12, {}), {3}: (13, {})} | custom-call | tf_op jit(solution)/shard_map/cond/branch_1_fun/weight_grads/pallas_call | solution.py:504
  302.7 8.6 %entry_back.8 = (f32[1024,512]{1,0:T(8,128)}, f32[1024,32]{1,0:T(8,128)}, f32[8,2048]{1,0:T(8,128)}, f32[32,512]{1,0:T(8,128)}) custom-call(s32[1]{0:T(128)} %get-tuple-element.747.side, bf16[2,1024,512]{2,1,0:T(8,128)(2,1)S(1)} %get-tuple-element.749.cotangent.edge, bf16[2048,128]{1,0:T(8,128)(2,1)} %get-tuple-element.790.wide, ...), custom_call_target="tpu_custom_call" | custom-call | tf_op jit(solution)/shard_map/cond/branch_1_fun/entry_back/pallas_call | solution.py:593
  311.3 4.7 maximum_bitcast_fusion.1
  316.2 1.5 add.59
  317.7 1.5 add.60
  319.2 1.6 add_select_fusion
  320.9 279.2 %all-reduce.5.cloned.1.call-done = (f32[1,512,1536]{2,1,0:T(8,128)}, f32[1,512,512]{2,1,0:T(8,128)}, f32[1,512,2048]{2,1,0:T(8,128)}, f32[1,2048,512]{2,1,0:T(8,...) async-done(((f32[1,512,1536]{2,1,0:T(8,128)}, f32[1,512,512]{2,1,0:T(8,128)}, f32[1,512,2048]{2,1,0:T(8,128)}, ...) | async-done | bytes 13828112 | tf_op jit(solution)/shard_map/psum | solution.py:836
  600.9 1.6 fusion.4
  603.9 1.5 broadcast_select_fusion.1
  605.4 3.7 reshape.93
  610.1 9.1 %psum.90 = f32[3,2048]{1,0:T(4,128)S(1)} all-reduce(f32[3,2048]{1,0:T(4,128)S(1)} %reshape.91), channel_id=1, replica_groups=mesh['section'=2,'dp'=16] {'section'}, use_global_device_ids=true, to_apply=%region_16.17 | all-reduce | flops 6144 | bytes 49152 | tf_op jit(solution)/shard_map/psum | solution.py:845
  621.5 99.0 %all-reduce.7.cloned.1.call-done = (f32[512,32]{0,1:T(8,128)}, f32[32,512]{1,0:T(8,128)}, f32[8192,32]{1,0:T(8,128)}) async-done(((f32[512,32]{0,1:T(8,128)}, f32[32,512]{1,0:T(8,128)}, f32[8192,32]{1,0:T(8,128)}), (f32[512,32]{0,1:T(8,128)}, f32[32,512]{1,0:T(8,128)}, f32[8192,32]{1,0:T(8,128)})) %all-reduce.7.cloned.1.call-update) | async-done | bytes 1179664 | tf_op jit(solution)/shard_map/psum | solution.py:845
  720.5 3.6 copy.94
  724.1 1.7 copy.268
  728.1 2.1 copy.270
  730.3 1.6 copy-done.17
  731.8 2.0 copy.271
  (101 shorter events, 26.6 us)
Async XLA Ops:
  7.2 592.9 %all-reduce.5.cloned.1.call-start = ((), (), s32[]{:S(2)}) async-start(), calls=%async_computation | async-start | bytes 27656192 | tf_op jit(solution)/shard_map/psum | solution.py:836
  17.5 4.0 copy-start.31
  17.6 11.8 %copy-start = (bf16[1,2,1024,512]{3,2,1,0:T(8,128)(2,1)S(1)}, bf16[1,2,1024,512]{3,2,1,0:T(8,128)(2,1)}, u32[]{:S(2)}) copy-start(bf16[1,2,1024,512]{3,2,1,0:T(8,128)(2,1)} %param.24) | copy-start | bytes 6291460
  21.4 6.5 copy-start.29
  21.4 6.5 copy-start.30
  21.4 6.6 copy-start.34
  21.4 6.6 copy-start.35
  21.4 6.6 copy-start.36
  21.4 6.6 copy-start.37
  87.4 28.7 %copy-start.22 = (bf16[1024,512]{1,0:T(8,128)(2,1)}, bf16[1024,512]{1,0:T(8,128)(2,1)S(1)}, u32[]{:S(2)}) copy-start(bf16[1024,512]{1,0:T(8,128)(2,1)S(1)} %get-tuple-element.1344.query) | copy-start | bytes 3145732 | tf_op jit(solution)/shard_map/cond
  87.4 28.7 %copy-start.23 = (bf16[1024,512]{1,0:T(8,128)(2,1)}, bf16[1024,512]{1,0:T(8,128)(2,1)S(1)}, u32[]{:S(2)}) copy-start(bf16[1024,512]{1,0:T(8,128)(2,1)S(1)} %get-tuple-element.1345.key) | copy-start | bytes 3145732 | tf_op jit(solution)/shard_map/cond
  87.4 28.7 %copy-start.24 = (bf16[1024,512]{1,0:T(8,128)(2,1)}, bf16[1024,512]{1,0:T(8,128)(2,1)S(1)}, u32[]{:S(2)}) copy-start(bf16[1024,512]{1,0:T(8,128)(2,1)S(1)} %get-tuple-element.1346.value) | copy-start | bytes 3145732 | tf_op jit(solution)/shard_map/cond
  97.4 18.8 %copy-start.7 = (bf16[1024,512]{1,0:T(8,128)(2,1)}, bf16[1024,512]{1,0:T(8,128)(2,1)S(1)}, u32[]{:S(2)}) copy-start(bf16[1024,512]{1,0:T(8,128)(2,1)S(1)} %get-tuple-element.1347.context) | copy-start | bytes 3145732 | tf_op jit(solution)/shard_map/cond
  135.5 14.4 %collective-permute-start = (f32[1024,32]{1,0:T(8,128)}, f32[1024,32]{1,0:T(8,128)}, u32[]{:S(2)}, u32[]{:S(2)}) collective-permute-start(f32[1024,32]{1,0:T(8,128)} %get-tuple-element.924), channel_id=1, source_target_pairs={{16,0},{17,1},{18,2},{19,3},{20,4},{21,5},{22,6},{23,7},{24,8},{25... | collective-permute-start | bytes 393224 | tf_op jit(solution)/shard_map/ppermute | solution.py:798
  151.1 16.9 %copy-start.26 = (bf16[1024,512]{1,0:T(8,128)(2,1)S(1)}, bf16[1024,512]{1,0:T(8,128)(2,1)}, u32[]{:S(2)}) copy-start(bf16[1024,512]{1,0:T(8,128)(2,1)} %get-tuple-element.620.marks) | copy-start | bytes 3145732 | tf_op jit(solution)/shard_map/cond
  185.3 7.6 %copy-start.14 = (bf16[1024,512]{1,0:T(8,128)(2,1)}, bf16[1024,512]{1,0:T(8,128)(2,1)S(1)}, u32[]{:S(2)}) copy-start(bf16[1024,512]{1,0:T(8,128)(2,1)S(1)} %get-tuple-element.1402.query_grad) | copy-start | bytes 3145732 | tf_op jit(solution)/shard_map/cond
  185.3 7.6 %copy-start.15 = (bf16[1024,512]{1,0:T(8,128)(2,1)}, bf16[1024,512]{1,0:T(8,128)(2,1)S(1)}, u32[]{:S(2)}) copy-start(bf16[1024,512]{1,0:T(8,128)(2,1)S(1)} %get-tuple-element.1403.key_grad) | copy-start | bytes 3145732 | tf_op jit(solution)/shard_map/cond
  185.4 7.6 %copy-start.16 = (bf16[1024,512]{1,0:T(8,128)(2,1)}, bf16[1024,512]{1,0:T(8,128)(2,1)S(1)}, u32[]{:S(2)}) copy-start(bf16[1024,512]{1,0:T(8,128)(2,1)S(1)} %get-tuple-element.1404.value_grad) | copy-start | bytes 3145732 | tf_op jit(solution)/shard_map/cond
  218.8 20.7 %collective-permute-start.1 = (f32[1024,32]{1,0:T(8,128)}, f32[1024,32]{1,0:T(8,128)}, u32[]{:S(2)}, u32[]{:S(2)}) collective-permute-start(f32[1024,32]{1,0:T(8,128)} %get-tuple-element.957), channel_id=1, source_target_pairs={{16,0},{17,1},{18,2},{19,3},{20,4},{21,5},{22,6},{23,7},{24,8},{25... | collective-permute-start | bytes 393224 | tf_op jit(solution)/shard_map/ppermute | solution.py:817
  263.3 19.2 %copy-start.1 = (f32[512,2048]{1,0:T(8,128)S(1)}, f32[512,2048]{1,0:T(8,128)}, u32[]{:S(2)}) copy-start(f32[512,2048]{1,0:T(8,128)} %get-tuple-element.782.refs_12_) | copy-start | bytes 12582916 | tf_op jit(solution)/shard_map/cond
  302.7 13.3 %copy-start.3 = (f32[512,2048]{1,0:T(8,128)}, f32[512,2048]{1,0:T(8,128)S(1)}, u32[]{:S(2)}) copy-start(f32[512,2048]{1,0:T(8,128)S(1)} %get-tuple-element.1455) | copy-start | bytes 12582916 | tf_op jit(solution)/shard_map/cond
  320.8 399.7 %all-reduce.7.cloned.1.call-start = ((), (), s32[]{:S(2)}) async-start(), calls=%async_computation.1 | async-start | bytes 8650752 | tf_op jit(solution)/shard_map/psum | solution.py:845
  609.1 115.0 %copy-start.27 = (f32[1,512,1536]{2,1,0:T(8,128)S(1)}, f32[1,512,1536]{2,1,0:T(8,128)}, u32[]{:S(2)}) copy-start(f32[1,512,1536]{2,1,0:T(8,128)} %get-tuple-element.1467) | copy-start | bytes 9437188
  724.1 1.9 copy-start.28
  724.1 4.0 copy-start.18
  728.1 3.7 copy-start.17
  731.8 2.0 copy-start.33
  731.8 2.6 copy-start.32
Sparse Core Ops, SparseCore 0:
  320.9 279.1 all-reduce.4
  609.2 111.2 all-reduce.6

commit v2 on v1

--- a/solution.py
+++ b/solution.py
@@ -60,8 +60,16 @@
     return jnp.sum(values, 0, keepdims=True)
 
 
-def code_kernel(index, table, unit, wide, raw):
+def code_kernel(index, table_turned, unit, wide, table, raw):
     count = raw.shape[0]
+    block = 512
+
+    def turn(step, carry):
+        start = pl.multiple_of(step * block, block)
+        table[pl.ds(start, block), :] = table_turned[:, pl.ds(start, block)].T
+        return carry
+
+    lax.fori_loop(0, table.shape[0] // block, turn, 0)
 
     def some(step, carry):
         for inner in range(8):
@@ -77,8 +85,8 @@
     wide[...] = jnp.concatenate([high, low, high, jnp.zeros_like(high)], 1)
 
 
-def gather_codes(index, table):
-    count, width = index.shape[0], table.shape[1]
+def gather_codes(index, table_turned):
+    count, width = index.shape[0], table_turned.shape[0]
     return pl.pallas_call(
         code_kernel,
         in_specs=[pl.BlockSpec(memory_space=pltpu.SMEM), pl.BlockSpec(memory_space=pltpu.VMEM)],
@@ -87,17 +95,19 @@
             jax.ShapeDtypeStruct((count, width), F32),
             jax.ShapeDtypeStruct((count, 4 * width), BF),
         ),
-        scratch_shapes=[pltpu.VMEM((count, width), F32)],
+        scratch_shapes=[pltpu.VMEM(table_turned.shape[::-1], F32), pltpu.VMEM((count, width), F32)],
         compiler_params=PARAMS,
         name="gather_codes",
-    )(index, table)
-
-
-def scatter_kernel(index, unit, latent, table, out, total, rows):
+    )(index, table_turned)
+
+
+def scatter_kernel(index, unit, latent_first, latent_second, table_turned, out, total, rows):
     count = rows.shape[0]
     width = unit.shape[1]
+    half = count // 2
     total[...] = jnp.zeros_like(total)
-    rows[...] = 2.0 * (unit[...] - latent[...])
+    rows[:half, :] = 2.0 * (unit[:half, :] - latent_first[...])
+    rows[half:, :] = 2.0 * (unit[half:, :] - latent_second[...])
 
     def some(step, carry):
         for inner in range(8):
@@ -107,30 +117,36 @@
         return carry
 
     lax.fori_loop(0, count // 8, some, 0)
-    block = 1024
+    block = out.shape[1]
 
     def back(step, carry):
-        here = pl.ds(pl.multiple_of(step * block, block), block)
-        values = table[here, :]
-        grad = total[here, :]
-        inverse = lax.rsqrt(jnp.sum(values * values, -1, keepdims=True) + NORM_EPS)
+        start = pl.multiple_of(step * block, block)
+        values = table_turned[:, pl.ds(start, block)]
+        grad = total[pl.ds(start, block), :].T
+        inverse = lax.rsqrt(jnp.sum(values * values, 0, keepdims=True) + NORM_EPS)
         book = values * inverse
-        out[here, :] = inverse * (grad - book * jnp.sum(book * grad, -1, keepdims=True))
+        out[pl.ds(pl.multiple_of(step * width, width), width), :] = inverse * (
+            grad - book * jnp.sum(book * grad, 0, keepdims=True)
+        )
         return carry
 
     lax.fori_loop(0, total.shape[0] // block, back, 0)
 
 
-def scatter_codes(index, unit, latent, table):
+def book_shape(table_turned, width):
+    return jax.ShapeDtypeStruct((table_turned.size // width, width), F32)
+
+
+def scatter_codes(index, unit, latents, table_turned, width):
     return pl.pallas_call(
         scatter_kernel,
-        in_specs=[pl.BlockSpec(memory_space=pltpu.SMEM)] + [pl.BlockSpec(memory_space=pltpu.VMEM)] * 3,
+        in_specs=[pl.BlockSpec(memory_space=pltpu.SMEM)] + [pl.BlockSpec(memory_space=pltpu.VMEM)] * 4,
         out_specs=pl.BlockSpec(memory_space=pltpu.VMEM),
-        out_shape=jax.ShapeDtypeStruct(table.shape, F32),
-        scratch_shapes=[pltpu.VMEM(table.shape, F32), pltpu.VMEM(unit.shape, F32)],
+        out_shape=book_shape(table_turned, width),
+        scratch_shapes=[pltpu.VMEM(table_turned.shape[::-1], F32), pltpu.VMEM(unit.shape, F32)],
         compiler_params=PARAMS,
         name="scatter_codes",
-    )(index, unit, latent, table)
+    )(index, unit, *latents, table_turned)
 
 
 def entry_values(encoder, edge, wide, up, head_bias):
@@ -292,9 +308,9 @@
         pieces = split(latent_grad)
         normed_grad = dot3(pieces, (down_turned[:narrow, :], down_turned[narrow:, :]), NN)
         head_weight[...] += dot3(pieces, split(normed), TN)
-        sums[2:3, :width] += column_sum(normed_grad * hat)
-        sums[2:3, width : 2 * width] += column_sum(normed_grad)
-        sums[3:4, :narrow] += column_sum(latent_grad)
+        sums[8:9, :] += column_sum(normed_grad * hat)
+        sums[9:10, :] += column_sum(normed_grad)
+        sums[10:11, :narrow] += column_sum(latent_grad)
         upstream[...] = norm_back(normed_grad, output_gain[0:1, :], hat, inverse)
 
     @pl.when(jnp.logical_not(encoder))
@@ -304,7 +320,7 @@
     above = upstream[...]
     low = above.astype(BF)
     out_low[...] = low
-    sums[1:2, :width] += column_sum(low.astype(F32))
+    sums[4:5, :] += column_sum(low.astype(F32))
     normed_grad = None
     chunk = 512
     for start in range(0, weight_in.shape[1], chunk):
@@ -312,17 +328,17 @@
         active_grad = dot(low, weight_last[here, :], NT)
         inner = (active_grad * slope[:, here].astype(F32)).astype(BF)
         preact_low[:, here] = inner
-        sums[0:1, here] += column_sum(inner.astype(F32))
+        sums[start // chunk : start // chunk + 1, :] += column_sum(inner.astype(F32))
         term = dot(inner, weight_in[:, here], NT)
         normed_grad = term if normed_grad is None else normed_grad + term
     hat, inverse = norm_parts(mid[...])
-    sums[1:2, 2 * width : 3 * width] += column_sum(normed_grad * hat)
-    sums[1:2, 3 * width :] += column_sum(normed_grad)
+    sums[6:7, :] += column_sum(normed_grad * hat)
+    sums[7:8, :] += column_sum(normed_grad)
     middle = above + norm_back(normed_grad, gains[1:2, :], hat, inverse)
     mid_grad[...] = middle
     branch = middle.astype(BF)
     branch_low[...] = branch
-    sums[1:2, width : 2 * width] += column_sum(branch.astype(F32))
+    sums[5:6, :] += column_sum(branch.astype(F32))
     context_grad[...] = dot(branch, weight_out[...], NT).astype(BF)
 
 
@@ -415,102 +431,303 @@
         + dot(value_grad[...], weight[:, 2 * width :], NT)
     )
     hat, inverse = norm_parts(values)
-    sums[0:1, :width] += column_sum(query_grad[...].astype(F32))
-    sums[0:1, width : 2 * width] += column_sum(value_grad[...].astype(F32))
-    sums[0:1, 2 * width : 3 * width] += column_sum(normed_grad * hat)
-    sums[0:1, 3 * width :] += column_sum(normed_grad)
+    sums[0:1, :] += column_sum(query_grad[...].astype(F32))
+    sums[1:2, :] += column_sum(value_grad[...].astype(F32))
+    sums[2:3, :] += column_sum(normed_grad * hat)
+    sums[3:4, :] += column_sum(normed_grad)
     total = mid_grad[...] + norm_back(normed_grad, gains[0:1, :], hat, inverse)
     entry[...] = total
 
     @pl.when(jnp.logical_not(encoder))
     def _():
-        sums[1:2, :width] += column_sum(total)
+        sums[4:5, :] += column_sum(total)
         latent_out[...] = code_product(total, up_turned[...])
         head_weight[...] += dot3(split(unit[...]), split(total), TN)
 
 
 def weight_kernel(*refs, turns, adding):
-    operands, refs = refs[:10], refs[10:]
-    if adding:
-        before, refs = refs[:4], refs[4:]
+    operands, out = refs[:10], refs[-1]
     active, out_low, n2, preact_low, context, branch_low, n1 = operands[:7]
     step = pl.program_id(0)
     first, second, third = turns
 
-    def put(number, value):
-        if adding:
-            value = value + before[number][...]
-        refs[number][...] = value
+    def put(left, right):
+        value = dot(left[...], right[...], TN)
+        out[...] = value + refs[10][...] if adding else value
 
     @pl.when(step < first)
     def _():
-        put(3, dot(active[...], out_low[...], TN))
+        put(active, out_low)
 
     @pl.when((step >= first) & (step < second))
     def _():
-        put(2, dot(n2[...], preact_low[...], TN))
+        put(n2, preact_low)
 
     @pl.when((step >= second) & (step < third))
     def _():
-        put(1, dot(context[...], branch_low[...], TN))
+        put(context, branch_low)
 
     for place in range(3):
 
         @pl.when(step == third + place)
         def _():
-            put(0, dot(n1[...], operands[7 + place][...], TN))
+            put(n1, operands[7 + place])
 
 
 def weight_grads(kept, back, before=None):
     active, n2, context, n1 = kept["active"], kept["n2"], kept["context"], kept["n1"]
     out_low, preact_low, branch_low = back["out_low"], back["preact_low"], back["branch_low"]
     count, width = n1.shape
-    hidden = active.shape[1]
-    tile = 512
-    first = hidden // tile
+    first = active.shape[1] // width
     second = 2 * first
     third = second + 1
     whole = lambda step: (0, 0)
-    down_rows = lambda step: (jnp.minimum(step, first - 1), 0)
-    active_columns = lambda step: (0, jnp.minimum(step, first - 1))
-    hidden_columns = lambda step: (0, jnp.clip(step - first, 0, first - 1))
-    last_columns = lambda step: (0, jnp.clip(step - third, 0, 2))
     full = pl.BlockSpec((count, width), whole)
-    in_specs = [
-        pl.BlockSpec((count, tile), active_columns),
-        full,
-        full,
-        pl.BlockSpec((count, tile), hidden_columns),
-        full,
-        full,
-        full,
-        full,
-        full,
-        full,
-    ]
-    out_specs = [
-        pl.BlockSpec((width, tile), last_columns),
-        pl.BlockSpec((width, width), whole),
-        pl.BlockSpec((width, tile), hidden_columns),
-        pl.BlockSpec((tile, width), down_rows),
-    ]
-    shapes = ((width, 3 * width), (width, width), (width, hidden), (hidden, width))
+    in_specs = [full] * 10
+    in_specs[0] = pl.BlockSpec((count, width), lambda step: (0, jnp.minimum(step, first - 1)))
+    in_specs[3] = pl.BlockSpec((count, width), lambda step: (0, jnp.clip(step - first, 0, first - 1)))
+    out_spec = pl.BlockSpec((width, width), lambda step: (step, 0))
     operands = [active, out_low, n2, preact_low, context, branch_low, n1]
     operands += [back["query_grad"], back["key_grad"], back["value_grad"]]
     adding = before is not None
     if adding:
-        operands += list(before)
-        in_specs = in_specs + out_specs
+        operands.append(before)
+        in_specs.append(out_spec)
     return pl.pallas_call(
         functools.partial(weight_kernel, turns=(first, second, third), adding=adding),
         grid=(third + 3,),
         in_specs=in_specs,
-        out_specs=out_specs,
-        out_shape=tuple(jax.ShapeDtypeStruct(shape, F32) for shape in shapes),
-        input_output_aliases={10 + number: number for number in range(4)} if adding else {},
+        out_specs=out_spec,
+        out_shape=jax.ShapeDtypeStruct(((third + 3) * width, width), F32),
+        input_output_aliases={10: 0} if adding else {},
         compiler_params=PARAMS,
         name="weight_grads",
     )(*operands)
+
+
+MESH = pl.DeviceIdType.MESH
+
+
+def ring_chip(position, chips):
+    odd = position // (chips // 2)
+    return (1 - odd) * (2 * position) + odd * (2 * (chips - 1 - position) + 1)
+
+
+def sum_kernel(
+    chips, main, misc, main_out, misc_out,
+    own_main, own_misc, pair_main, pair_misc, run_main, run_misc, far_misc,
+    load_sems, pair_send, pair_recv, run_send, run_recv, far_send, far_recv,
+    keep_sems, spread_send, spread_recv, side_send, side_recv,
+):
+    place = lax.axis_index("dp")
+    section = lax.axis_index("section")
+    chip, core = place // 2, place % 2
+    column, odd = chip // 2, chip % 2
+    position = (1 - odd) * column + odd * (chips - 1 - column)
+    other = {"dp": chip * 2 + (1 - core)}
+    far = {"section": 1 - section}
+    ahead = {"dp": ring_chip((position + 1) % chips, chips) * 2 + core}
+    behind = {"dp": ring_chip((position + chips - 1) % chips, chips) * 2 + core}
+    targets = (ahead, behind)
+    sizes = (main.shape[0] // (4 * chips), misc.shape[0] // (4 * chips))
+    sources, results = (main, misc), (main_out, misc_out)
+    own, pair, run = (own_main, own_misc), (pair_main, pair_misc), (run_main, run_misc)
+
+    barrier = pltpu.get_barrier_semaphore()
+    for device in (other, far, ahead, behind):
+        pl.semaphore_signal(barrier, inc=1, device_id=device, device_id_type=MESH)
+
+    def piece(step, way):
+        return (position + (2 * chips - step if way == 0 else step)) % chips
+
+    def rows(which, half, way, number):
+        size = sizes[which]
+        return pl.ds(pl.multiple_of(((half * 2 + way) * chips + number) * size, 8), size)
+
+    def load(which, way, step):
+        return pltpu.make_async_copy(
+            sources[which].at[rows(which, core, way, piece(step, way))],
+            own[which].at[way, step],
+            load_sems.at[which, way, step],
+        )
+
+    def swap(which, way, step):
+        return pltpu.make_async_remote_copy(
+            src_ref=sources[which].at[rows(which, 1 - core, way, piece(step, way))],
+            dst_ref=pair[which].at[way, step],
+            send_sem=pair_send.at[which, way, step],
+            recv_sem=pair_recv.at[which, way, step],
+            device_id=other,
+            device_id_type=MESH,
+        )
+
+    def pass_on(which, way, step):
+        return pltpu.make_async_remote_copy(
+            src_ref=run[which].at[way, step],
+            dst_ref=run[which].at[way, step + 1],
+            send_sem=run_send.at[which, way, step],
+            recv_sem=run_recv.at[which, way, step + 1],
+            device_id=targets[way],
+            device_id_type=MESH,
+        )
+
+    def cross(way):
+        return pltpu.make_async_remote_copy(
+            src_ref=run_misc.at[way, chips - 1],
+            dst_ref=far_misc.at[way],
+            send_sem=far_send.at[way],
+            recv_sem=far_recv.at[way],
+            device_id=far,
+            device_id_type=MESH,
+        )
+
+    def final_rows(which, way, step):
+        return rows(which, core, way, piece(step + chips - 1, way))
+
+    def keep(which, way):
+        return pltpu.make_async_copy(
+            run[which].at[way, chips - 1], results[which].at[final_rows(which, way, 0)], keep_sems.at[which, way]
+        )
+
+    def spread(which, way, step, first=False):
+        here = results[which].at[final_rows(which, way, step)]
+        return pltpu.make_async_remote_copy(
+            src_ref=run[which].at[way, chips - 1] if first else here,
+            dst_ref=here,
+            send_sem=spread_send.at[which, way, step],
+            recv_sem=spread_recv.at[which, way, step],
+            device_id=targets[way],
+            device_id_type=MESH,
+        )
+
+    def aside(which, way, step, first=False):
+        here = results[which].at[final_rows(which, way, step)]
+        return pltpu.make_async_remote_copy(
+            src_ref=run[which].at[way, chips - 1] if first else here,
+            dst_ref=here,
+            send_sem=side_send.at[which, way, step],
+            recv_sem=side_recv.at[which, way, step],
+            device_id=other,
+            device_id_type=MESH,
+        )
+
+    def beside(which, way, step):
+        here = results[which].at[rows(which, 1 - core, way, piece(step + chips - 1, way))]
+        return pltpu.make_async_remote_copy(
+            src_ref=here, dst_ref=here, send_sem=side_send.at[which, way, step],
+            recv_sem=side_recv.at[which, way, step], device_id=other, device_id_type=MESH,
+        )
+
+    def incoming(which, way, step):
+        here = results[which].at[final_rows(which, way, step)]
+        return pltpu.make_async_remote_copy(
+            src_ref=here, dst_ref=here, send_sem=spread_send.at[which, way, step],
+            recv_sem=spread_recv.at[which, way, step - 1], device_id=targets[way], device_id_type=MESH,
+        )
+
+    both = [(which, way) for way in range(2) for which in range(2)]
+
+    def begin(step, carry):
+        for which, way in both:
+            load(which, way, step).start()
+        return carry
+
+    lax.fori_loop(0, chips, begin, 0)
+    pl.semaphore_wait(barrier, 4)
+
+    def begin_swap(step, carry):
+        for which, way in both:
+            swap(which, way, step).start()
+        return carry
+
+    lax.fori_loop(0, chips, begin_swap, 0)
+
+    for which, way in both:
+        load(which, way, 0).wait()
+        swap(which, way, 0).wait_recv()
+        run[which][way, 0] = own[which][way, 0] + pair[which][way, 0]
+        pass_on(which, way, 0).start()
+
+    def gather_step(step, carry):
+        for which, way in both:
+            load(which, way, step).wait()
+            swap(which, way, step).wait_recv()
+            pass_on(which, way, step - 1).wait_recv()
+            run[which][way, step] = run[which][way, step] + own[which][way, step] + pair[which][way, step]
+
+            @pl.when(step < chips - 1)
+            def _():
+                pass_on(which, way, step).start()
+
+        return carry
+
+    lax.fori_loop(1, chips, gather_step, 0)
+
+    for way in range(2):
+        cross(way).start()
+        keep(0, way).start()
+        spread(0, way, 0, True).start()
+        aside(0, way, 0, True).start()
+    for way in range(2):
+        cross(way).wait()
+        run_misc[way, chips - 1] = run_misc[way, chips - 1] + far_misc[way]
+        keep(1, way).start()
+        spread(1, way, 0, True).start()
+        aside(1, way, 0, True).start()
+
+    def spread_step(step, carry):
+        for which, way in both:
+            incoming(which, way, step).wait_recv()
+
+            @pl.when(step < chips - 1)
+            def _():
+                spread(which, way, step).start()
+
+            aside(which, way, step).start()
+        return carry
+
+    lax.fori_loop(1, chips, spread_step, 0)
+
+    def finish(step, carry):
+        for which, way in both:
+            swap(which, way, step).wait_send()
+            beside(which, way, step).wait_recv()
+            aside(which, way, step).wait_send()
+
+            @pl.when(step < chips - 1)
+            def _():
+                pass_on(which, way, step).wait_send()
+                spread(which, way, step).wait_send()
+
+        return carry
+
+    lax.fori_loop(0, chips, finish, 0)
+    for which, way in both:
+        keep(which, way).wait()
+
+
+def sum_over_dp(main, misc):
+    chips = lax.axis_size("dp") // 2
+    width = main.shape[1]
+    sizes = (main.shape[0] // (4 * chips), misc.shape[0] // (4 * chips))
+    slots = lambda which: pltpu.VMEM((2, chips, sizes[which], width), F32)
+    sems = lambda *shape: pltpu.SemaphoreType.DMA(shape)
+    return pl.pallas_call(
+        functools.partial(sum_kernel, chips),
+        in_specs=[pl.BlockSpec(memory_space=pl.ANY)] * 2,
+        out_specs=[pl.BlockSpec(memory_space=pl.ANY)] * 2,
+        out_shape=(jax.ShapeDtypeStruct(main.shape, F32), jax.ShapeDtypeStruct(misc.shape, F32)),
+        scratch_shapes=[slots(0), slots(1)] * 3
+        + [pltpu.VMEM((2, sizes[1], width), F32)]
+        + [sems(2, 2, chips)] * 5
+        + [sems(2)] * 2
+        + [sems(2, 2)]
+        + [sems(2, 2, chips)] * 4,
+        compiler_params=pltpu.CompilerParams(
+            collective_id=0, has_side_effects=True, vmem_limit_bytes=48 << 20
+        ),
+        name="sum_over_dp",
+    )(main, misc)
 
 
 def nothing_kernel(*refs):
@@ -553,19 +770,23 @@
         n, d, f = self.count, self.width, self.hidden
         table = dict(
             n1=(d, BF), query=(d, BF), key=(d, BF), value=(d, BF), context=(d, BF), marks=(d, BF),
-            mid=(d, F32), n2=(d, BF), active=(f, BF), slope=(f, BF), result=(d, F32), latent=(self.narrow, F32),
-        )
-        return {name: jax.ShapeDtypeStruct((n, size), kind) for name, (size, kind) in table.items()}
+            mid=(d, F32), n2=(d, BF), active=(f, BF), slope=(f, BF), latent=(self.narrow, F32),
+        )
+        shapes = {name: jax.ShapeDtypeStruct((n, size), kind) for name, (size, kind) in table.items()}
+        shapes["result"] = jax.ShapeDtypeStruct((self.rows, n, d), F32)
+        return shapes
 
     def back_shapes(self):
         n, d, f = self.count, self.width, self.hidden
         table = dict(
             out_low=(n, d, BF), preact_low=(n, f, BF), mid_grad=(n, d, F32), branch_low=(n, d, BF),
-            query_grad=(n, d, BF), key_grad=(n, d, BF), value_grad=(n, d, BF), entry=(n, d, F32),
-            latent_out=(n, self.narrow, F32), sums_late=(8, f, F32), sums_early=(8, f, F32),
+            query_grad=(n, d, BF), key_grad=(n, d, BF), value_grad=(n, d, BF),
+            latent_out=(n, self.narrow, F32), sums_late=(16, d, F32), sums_early=(16, d, F32),
             head_late=(self.narrow, d, F32), head_early=(self.narrow, d, F32),
         )
-        return {name: jax.ShapeDtypeStruct((a, b), kind) for name, (a, b, kind) in table.items()}
+        shapes = {name: jax.ShapeDtypeStruct((a, b), kind) for name, (a, b, kind) in table.items()}
+        shapes["entry"] = jax.ShapeDtypeStruct((self.rows, n, d), F32)
+        return shapes
 
     def side_spec(self):
         return pl.BlockSpec(memory_space=pltpu.SMEM)
@@ -585,13 +806,26 @@
             self.whole(self.head_bias),
         ]
 
+    def row_spec(self, row):
+        return pl.BlockSpec((None, TOKENS, self.width), lambda step: (row, step, 0))
+
     def unit_spec(self, row):
         steps = self.count // TOKENS
         return pl.BlockSpec((TOKENS, self.narrow), lambda step: (row * steps + step, 0))
 
-    def call(self, kernel, in_specs, operands, outs, out_specs, name, scratch=()):
+    def call(self, kernel, in_specs, operands, outs, out_specs, name, scratch=(), rest=None, place=0):
+        aliases = {}
+        if rest is not None:
+            inner, number = kernel, len(operands)
+
+            def kernel(*refs):
+                inner(*refs[:number], *refs[number + 1 :])
+
+            in_specs, operands = in_specs + [pl.BlockSpec(memory_space=pl.ANY)], operands + (rest,)
+            aliases = {number: place}
         return pl.pallas_call(
             kernel,
+            input_output_aliases=aliases,
             grid=(self.count // TOKENS,),
             in_specs=in_specs,
             out_specs=out_specs,
@@ -623,7 +857,7 @@
             name=name,
         )(self.windows, *operands)
 
-    def forward(self, row):
+    def forward(self, row, rest=None):
         shapes = self.kept_shapes()
         entry = (self.edges, self.wide, self.up, self.head_bias)
         kept = {}
@@ -657,13 +891,15 @@
             + [self.whole(array) for array in consts],
             (self.side,) + entry + (kept["context"],) + consts,
             [shapes[name] for name in names],
-            [self.tokens(shapes[name]) for name in names],
+            [self.row_spec(row) if name == "result" else self.tokens(shapes[name]) for name in names],
             "hidden",
+            rest=rest,
+            place=names.index("result"),
         )
         kept.update(zip(names, outs))
         return kept
 
-    def backward(self, row, kept, latent_in):
+    def backward(self, row, kept, latent_in, rest=None):
         shapes = self.back_shapes()
         back = {}
         names = ("out_low", "preact_low", "mid_grad", "branch_low", "context_grad", "sums_late", "head_late")
@@ -672,7 +908,7 @@
         late = (self.gains, self.biases, self.attention_out)
         outs = self.call(
             tail_back_kernel,
-            [self.side_spec(), self.tokens(kept["result"]), self.entry_specs(row)[0], self.unit_spec(row),
+            [self.side_spec(), self.row_spec(row), self.entry_specs(row)[0], self.unit_spec(row),
              self.tokens(latent_in)]
             + [self.whole(array) for array in consts]
             + [self.tokens(kept["slope"]), self.whole(self.hidden_in), self.tokens(kept["mid"])]
@@ -711,8 +947,9 @@
             (self.side, self.edges, self.wide, self.up, self.head_bias, self.unit) + grads
             + (self.attention_in, self.gains, self.biases, back["mid_grad"], self.up_turned),
             [shapes[name] for name in names],
-            [self.tokens(shapes[name]) for name in names[:2]] + [self.whole(shapes[name]) for name in names[2:]],
+            [self.row_spec(row), self.tokens(shapes["latent_out"])] + [self.whole(shapes[name]) for name in names[2:]],
             "entry_back",
+            rest=rest,
         )
         back.update(zip(names, outs))
         return back
@@ -758,7 +995,8 @@
     rows, count, width = edges.shape
     hidden = hidden_in.shape[2]
     index = code_index.reshape(-1)
-    unit, wide = gather_codes(index, codebook)
+    table_turned = codebook.T
+    unit, wide = gather_codes(index, table_turned)
     query_mark, key_mark = marks_of(segments)
     up_high, up_low = split(up_weight)
     work = Rows(
@@ -774,25 +1012,18 @@
     )
     kept_shapes = as_list(work.kept_shapes(), KEPT)
     back_shapes = as_list(work.back_shapes(), BACK)
-    book_shape = jax.ShapeDtypeStruct(codebook.shape, F32)
-    weight_shapes = [
-        jax.ShapeDtypeStruct(shape, F32)
-        for shape in ((width, 3 * width), (width, width), (width, hidden), (hidden, width))
-    ]
+    book_out = book_shape(table_turned, width)
+    weight_out = jax.ShapeDtypeStruct((2 * hidden + 4 * width, width), F32)
     quiet = jnp.zeros((count, unit.shape[1]), F32)
     first_kept = work.forward(0)
 
     def encoder_second():
-        kept = work.forward(1)
-        latent = jnp.concatenate([first_kept["latent"], kept["latent"]], 0)
-        book = scatter_codes(index, unit, latent, codebook)
-        return as_list(kept, KEPT), list(unwritten(back_shapes)), book
+        return as_list(work.forward(1), KEPT), list(unwritten(back_shapes))
 
     def decoder_first():
-        back = work.backward(0, first_kept, quiet)
-        return list(unwritten(kept_shapes)), as_list(back, BACK), unwritten([book_shape])[0]
-
-    kept_a, back_a, book = lax.cond(encoder, encoder_second, decoder_first)
+        return list(unwritten(kept_shapes)), as_list(work.backward(0, first_kept, quiet), BACK)
+
+    kept_a, back_a = lax.cond(encoder, encoder_second, decoder_first)
     back_a = dict(zip(BACK, back_a))
     kept_a = dict(zip(KEPT, kept_a))
     latent_in = lax.ppermute(back_a["latent_out"], "section", [(1, 0)])
@@ -801,74 +1032,81 @@
         return list(unwritten(kept_shapes)), as_list(work.backward(0, first_kept, latent_in), BACK)
 
     def decoder_third():
-        return as_list(work.forward(1), KEPT), list(unwritten(back_shapes))
+        return as_list(work.forward(1, first_kept["result"]), KEPT), list(unwritten(back_shapes))
 
     kept_b, back_b = lax.cond(encoder, encoder_third, decoder_third)
     kept_b, back_b = dict(zip(KEPT, kept_b)), dict(zip(BACK, back_b))
 
     def encoder_fourth():
-        return list(unwritten(back_shapes)), list(weight_grads(first_kept, back_b))
+        book = scatter_codes(index, unit, (first_kept["latent"], kept_a["latent"]), table_turned, width)
+        return list(unwritten(back_shapes)), weight_grads(first_kept, back_b), book
 
     def decoder_fourth():
-        return as_list(work.backward(1, kept_b, quiet), BACK), list(unwritten(weight_shapes))
-
-    back_c, weights_c = lax.cond(encoder, encoder_fourth, decoder_fourth)
+        weights, book = unwritten([weight_out, book_out])
+        return as_list(work.backward(1, kept_b, quiet), BACK), weights, book
+
+    back_c, weights_c, book = lax.cond(encoder, encoder_fourth, decoder_fourth)
     back_c = dict(zip(BACK, back_c))
     latent_in_second = lax.ppermute(back_c["latent_out"], "section", [(1, 0)])
 
     def encoder_fifth():
-        back = work.backward(1, kept_a, latent_in_second)
+        back = work.backward(1, kept_a, latent_in_second, back_b["entry"])
         total = weight_grads(kept_a, back, weights_c)
-        sums = [back[name] + back_b[name] for name in BACK[-4:]]
-        edge = jnp.stack([back_b["entry"], back["entry"]])
-        return list(total), sums, edge
+        late, early, down, unused = [back[name] + back_b[name] for name in BACK[-4:]]
+        empty = jnp.zeros_like(down)
+        none = jnp.zeros_like(jnp.concatenate([late, early]))
+        return total, jnp.concatenate([book, down, empty, late, early, none]), back["entry"]
 
     def decoder_fifth():
         total = weight_grads(first_kept, back_a)
         total = weight_grads(kept_b, back_c, total)
-        sums = [back_a[name] + back_c[name] for name in BACK[-4:]]
-        edge = jnp.stack([first_kept["result"], kept_b["result"]])
-        return list(total), sums, edge
-
-    totals, sums, edge = lax.cond(encoder, encoder_fifth, decoder_fifth)
-    head_weight = jnp.where(encoder, sums[2], sums[3])
-    book = jnp.where(encoder, book, 0.0).reshape(-1, 128)
-    totals, sums_late, sums_early, head_weight, book = lax.psum(
-        (totals, sums[0], sums[1], head_weight, book), "dp"
-    )
-    from_encoder = jnp.where(
-        encoder,
-        jnp.concatenate([sums_late[2].reshape(-1, 128), sums_late[3].reshape(-1, 128)], 0), 0.0
-    )
-    from_decoder = jnp.where(encoder, 0.0, sums_early[1].reshape(-1, 128))
-    empty = jnp.zeros_like(head_weight)
-    book, head_sums, down_grad, up_grad = lax.psum(
-        (
-            book,
-            jnp.concatenate([from_encoder, from_decoder], 0),
-            jnp.where(encoder, head_weight, empty),
-            jnp.where(encoder, empty, head_weight),
-        ),
-        "section",
-    )
-    head_sums = head_sums.reshape(3, -1)
-    late, early = sums_late[1].reshape(4, width), sums_early[0].reshape(4, width)
+        late, early, unused, up = [back_a[name] + back_c[name] for name in BACK[-4:]]
+        empty = jnp.zeros_like(up)
+        none = jnp.zeros_like(jnp.concatenate([late, early]))
+        return total, jnp.concatenate([jnp.zeros(book.shape, F32), empty, up, none, late, early]), kept_b["result"]
+
+    totals, misc, edge = lax.cond(encoder, encoder_fifth, decoder_fifth)
+    totals, misc = sum_all(totals, misc)
+    pieces, at = [], 0
+    for size in (book_out.shape[0], unit.shape[1], unit.shape[1], 16, 16, 16, 16):
+        pieces.append(misc[at : at + size])
+        at += size
+    book, down_grad, up_grad, first_late, first_early, second_late, second_early = pieces
+    late = jnp.where(encoder, first_late, second_late)
+    early = jnp.where(encoder, first_early, second_early)
+    steps = hidden // width
+    narrow = unit.shape[1]
+    book = book.reshape(-1, narrow, width).transpose(1, 0, 2).reshape(table_turned.shape)
+    tiles = totals.reshape(-1, width, width)
+
+    def columns(part):
+        return part.transpose(1, 0, 2).reshape(1, width, -1)
+
     return (
         edge[None],
-        totals[0][None],
-        totals[1][None],
-        totals[2][None],
-        totals[3][None],
-        jnp.stack([early[2], late[2]])[None],
-        jnp.stack([early[0], early[1], late[1], early[3], late[3], late[0]])[None],
-        sums_late[0][None],
-        head_sums[0, :width],
-        jnp.stack([head_sums[0, width : 2 * width], head_sums[2, :width]]),
+        columns(tiles[2 * steps + 1 :]),
+        tiles[2 * steps][None],
+        columns(tiles[steps : 2 * steps]),
+        totals[None, :hidden],
+        jnp.stack([early[2], late[6]])[None],
+        jnp.stack([early[0], early[1], late[5], early[3], late[7], late[4]])[None],
+        late[:steps].reshape(1, hidden),
+        first_late[8],
+        jnp.stack([first_late[9], second_early[4]]),
         down_grad.T,
-        head_sums[1, : unit.shape[1]],
+        first_late[10, :narrow],
         up_grad,
-        book.reshape(codebook.shape),
+        book.T,
     )
+
+
+def sum_all(main, misc):
+    devices = lax.axis_size("dp")
+    if devices < 4:
+        return main, lax.psum(misc, "section")
+    unit = 16 * devices
+    extra = -misc.shape[0] % unit
+    return sum_over_dp(main, jnp.pad(misc, ((0, extra), (0, 0))))
 
 
 def solution(mesh):

time: 753 us -> 500 us (0.66)
  waiting for transfers between devices: 402 us -> 28.4 us
  Pallas kernels: 214 us -> 379 us
  other arithmetic: 26.2 us -> 11.3 us
  between operations: 14.5 us -> 1.2 us
  blocking collectives: 9.07 us -> 0 us
    psum x2 -> x0, waiting for transfers between devices: 378 us -> none  [the longest x1 279 us: on_device(): lax.psum((totals, sums[0], sums[1], head_weight, book), 'dp')]
    pallas_call x8 -> x9, Pallas kernels: 98.8 us -> 252 us  [the longest x1 154 us: sum_over_dp(): pl.pallas_call(functools.partial(sum_kernel, chips), in_specs=[pl.BlockSp...]
    pallas_call x4, Pallas kernels: 57 us -> 73.2 us  [attention_call(): pl.pallas_call(functools.partial(kernel, row=row), grid_spec=pltpu.Prefet...]
    unnamed x41 -> x39, local copies, waits for them, and re-layouts: 21.6 us -> 8.55 us
    psum x1 -> x0, blocking collectives: 9.07 us -> none  [on_device(): lax.psum((book, jnp.concatenate([from_encoder, from_decoder], 0), jnp.whe...]
    select_n x5 -> x1, other arithmetic: 8.57 us -> 0.01 us  [on_device(): early = jnp.where(encoder, first_early, second_early)]
  transfers between devices with their start and end apart: 4 -> 2, of which waited for: 4 -> 2; matrix products, arithmetic and copies ran while one was open for 2% -> 0% of each run, Pallas kernels for 0% -> 0%
where the time goes in v2:
time: 500 us; the launch traced here: 493 us
  Pallas kernels  379 us (76%)
  local copies, waits for them, and re-layouts  51.3 us (10%)
  waiting for transfers between devices  28.4 us (6%)
  loops' own time  18.8 us (4%)
  other arithmetic  11.3 us (2%)
    pallas_call x1, Pallas kernels, sum_over_dp(): pl.pallas_call(functools.partial(sum_kernel, chips), in_specs=[pl.BlockSp...  154 us
    pallas_call x8, Pallas kernels, call(): pl.pallas_call(kernel, input_output_aliases=aliases, grid=(self.count //...  97.2 us
    pallas_call x4, Pallas kernels, attention_call(): pl.pallas_call(functools.partial(kernel, row=row), grid_spec=pltpu.Prefet...  73.2 us
    pallas_call x2, Pallas kernels, weight_grads(): pl.pallas_call(functools.partial(weight_kernel, turns=(first, second, thi...  37 us
    ppermute x1, waiting for transfers between devices, on_device(): latent_in_second = lax.ppermute(back_c['latent_out'], 'section', [(1, 0)])  16.3 us
    ppermute x1, waiting for transfers between devices, on_device(): latent_in = lax.ppermute(back_a['latent_out'], 'section', [(1, 0)])  12.1 us
    another operation x1, loops' own time, on_device(): kept_a, back_a = lax.cond(encoder, encoder_second, decoder_first)  10.7 us
  transfers between devices with their start and end apart: 2, of which 2 were waited for; matrix products, arithmetic and copies ran while one was open for 0% of the time, Pallas kernels for 0%

profile of v2, /device:TPU:0, one launch (start us, length us, event | category | flops | bytes accessed | tf_op | source)
XLA Modules:
  0.0 492.9 jit_solution(1049045890784243936)
XLA Ops:
  1.2 1.5 fusion.2
  2.7 1.0 subtract_convert_fusion.1
  3.7 0.8 convert_element_type.56
  4.5 1.5 fusion.3
  6.0 1.0 copy.70
  10.2 7.6 %gather_codes.1 = (f32[2048,32]{1,0:T(8,128)S(1)}, bf16[2048,128]{1,0:T(8,128)(2,1)}) custom-call(s32[2048]{0:T(1024)S(1)} %bitcast.105, f32[32,8192]{1,0:T(8,128)} %bitcast.79), custom_call_target="tpu_custom_call" | custom-call | tf_op jit(solution)/shard_map/gather_codes/pallas_call | solution.py:90
  18.0 1.3 select_convert_fusion
  19.3 6.1 %project.5 = (bf16[1024,512]{1,0:T(8,128)(2,1)}, bf16[1024,512]{1,0:T(8,128)(2,1)}, bf16[1024,512]{1,0:T(8,128)(2,1)}, bf16[1024,512]{1,0:T(8,128)(2,1)}) custom-call(s32[1]{0:T(128)} %bitcast.side, bf16[2,1024,512]{2,1,0:T(8,128)(2,1)S(1)} %bitcast.66, bf16[2048,128]{1,0:T(8,128)(2,1)} %get-tuple-element.809.wide, ...), custom_call_target="tpu_custom_call" | custom-call | tf_op jit(solution)/shard_map/project/pallas_call | solution.py:826
  25.5 13.4 %attend.5 = (bf16[1024,512]{1,0:T(8,128)(2,1)}, bf16[1024,512]{1,0:T(8,128)(2,1)}) custom-call(s32[16]{0:T(128)S(1)} %reshape.89.windows, bf16[1024,512]{1,0:T(8,128)(2,1)} %get-tuple-element.810.query, bf16[1024,512]{1,0:T(8,128)(2,1)} %get-tuple-element.811.key, bf16[1024,512]{1,0:T(8,128)(2,1)} %get-tuple-element.812.value, ...), custom_call_target="tpu_custom_call" | custom-call | tf_op jit(solution)/shard_map/attend/pallas_call | solution.py:846
  38.9 18.3 %hidden.5 = (f32[1024,512]{1,0:T(8,128)}, bf16[1024,512]{1,0:T(8,128)(2,1)}, bf16[1024,2048]{1,0:T(8,128)(2,1)}, bf16[1024,2048]{1,0:T(8,128)(2,1)}, f32[2,1024,512]{2,1,0:T(8,128)}, /*index=5*/f32[1024,32]{1,0:T(8,128)}) custom-call(s32[1]{0:T(128)} %bitcast.side, bf16[2,1024,512]{2,1,0:T(8,128)(2,1)S(1)} %bitcast.67, ...), custom_call_target="tpu_custom_call" | custom-call | tf_op jit(solution)/shard_map/hidden/pallas_call | solution.py:826
  57.3 48.3 %conditional.4 = (bf16[1024,512]{1,0:T(8,128)(2,1)}, bf16[1024,512]{1,0:T(8,128)(2,1)}, bf16[1024,512]{1,0:T(8,128)(2,1)}, bf16[1024,512]{1,0:T(8,128)(2,1)}, bf...) conditional(s32[]{:T(128)} %convert_element_type.50, ...), branch_computations={%region_2.3_spmd, %region_3.4_spmd} | conditional | bytes 18982144 | solution.py:1026
  67.8 6.0 %project.3 = (bf16[1024,512]{1,0:T(8,128)(2,1)}, bf16[1024,512]{1,0:T(8,128)(2,1)S(1)}, bf16[1024,512]{1,0:T(8,128)(2,1)S(1)}, bf16[1024,512]{1,0:T(8,128)(2,1)S(1)}) custom-call(s32[1]{0:T(128)} %get-tuple-element.448.side, bf16[2,1024,512]{2,1,0:T(8,128)(2,1)S(1)} %get-tuple-element.449.edge, bf16[2048,128]{1,0:T(8,128)(2,1)} %get-tuple-element.450.wide, ...), custom_call_target="tpu_custom_call" | custom-call | tf_op jit(solution)/shard_map/cond/branch_1_fun/project/pallas_call | solution.py:826
  74.0 13.1 %attend.3 = (bf16[1024,512]{1,0:T(8,128)(2,1)S(1)}, bf16[1024,512]{1,0:T(8,128)(2,1)}) custom-call(s32[16]{0:T(128)S(1)} %copy-done.63, bf16[1024,512]{1,0:T(8,128)(2,1)S(1)} %get-tuple-element.1110.query, bf16[1024,512]{1,0:T(8,128)(2,1)S(1)} %get-tuple-element.1111.key, bf16[1024,512]{1,0:T(8,128)(2,1)S(1)} %get-tuple-element.1112.value, ...), custom_call_target="tpu_custom_call" | custom-call | tf_op jit(solution)/shard_map/cond/branch_1_fun/attend/pallas_call | solution.py:846
  87.2 18.5 %hidden.3 = (f32[1024,512]{1,0:T(8,128)}, bf16[1024,512]{1,0:T(8,128)(2,1)}, bf16[1024,2048]{1,0:T(8,128)(2,1)}, bf16[1024,2048]{1,0:T(8,128)(2,1)}, f32[2,1024,512]{2,1,0:T(8,128)}, /*index=5*/f32[1024,32]{1,0:T(8,128)}) custom-call(s32[1]{0:T(128)} %get-tuple-element.448.side, bf16[2,1024,512]{2,1,0:T(8,128)(2,1)S(1)} %get-tuple-element.449.edge, ...), custom_call_target="tpu_custom_call" | custom-call | tf_op jit(solution)/shard_map/cond/branch_1_fun/hidden/pallas_call | solution.py:826
  105.6 1.3 collective-permute-start
  106.9 12.1 %collective-permute-done = f32[1024,32]{1,0:T(8,128)} collective-permute-done((f32[1024,32]{1,0:T(8,128)}, f32[1024,32]{1,0:T(8,128)}, u32[]{:S(2)}, u32[]{:S(2)}) %collective-permute-start) | collective-permute-done | bytes 131104 | tf_op jit(solution)/shard_map/ppermute | solution.py:1029
  119.1 48.2 %conditional.5 = (bf16[1024,512]{1,0:T(8,128)(2,1)}, bf16[1024,512]{1,0:T(8,128)(2,1)}, bf16[1024,512]{1,0:T(8,128)(2,1)}, bf16[1024,512]{1,0:T(8,128)(2,1)}, bf...) conditional(s32[]{:T(128)} %convert_element_type.50, ...), branch_computations={%region_4.5_spmd, %region_5.6_spmd} | conditional | bytes 35726500 | solution.py:1037
  120.0 17.0 %tail_back.5 = (bf16[1024,512]{1,0:T(8,128)(2,1)}, bf16[1024,2048]{1,0:T(8,128)(2,1)}, f32[1024,512]{1,0:T(8,128)}, bf16[1024,512]{1,0:T(8,128)(2,1)}, bf16[1024...) custom-call(s32[1]{0:T(128)} %get-tuple-element.539.side, f32[2,1024,512]{2,1,0:T(8,128)} %get-tuple-element.540.result, ...), custom_call_target="tpu_custom_call" | custom-call | tf_op jit(solution)/shard_map/cond/branch_1_fun/tail_back/pallas_call | solution.py:826
  137.0 22.6 %attend_back.5 = (bf16[1024,512]{1,0:T(8,128)(2,1)S(1)}, bf16[1024,512]{1,0:T(8,128)(2,1)S(1)}, bf16[1024,512]{1,0:T(8,128)(2,1)S(1)}) custom-call(s32[16]{0:T(128)S(1)} %copy-done.65, bf16[1024,512]{1,0:T(8,128)(2,1)} %get-tuple-element.560.query, bf16[1024,512]{1,0:T(8,128)(2,1)S(1)} %copy-done.29, bf16[1024,512]{1,0:T(8,128)(2,1)} %get-tuple-element.562.key, ...), custom_call_target="tpu_custom_call" | custom-call | tf_op jit(solution)/shard_map/cond/branch_1_fun/attend_back/pallas_call | solution.py:846
  159.7 7.6 %entry_back.5 = (f32[2,1024,512]{2,1,0:T(8,128)}, f32[1024,32]{1,0:T(8,128)}, f32[16,512]{1,0:T(8,128)}, f32[32,512]{1,0:T(8,128)}) custom-call(s32[1]{0:T(128)} %get-tuple-element.539.side, bf16[2,1024,512]{2,1,0:T(8,128)(2,1)S(1)} %get-tuple-element.541.cotangent.edge, bf16[2048,128]{1,0:T(8,128)(2,1)} %get-tuple-element.570.wide, ...), custom_call_target="tpu_custom_call" | custom-call | tf_op jit(solution)/shard_map/cond/branch_1_fun/entry_back/pallas_call | solution.py:826
  167.3 34.6 %conditional.6 = (bf16[1024,512]{1,0:T(8,128)(2,1)}, bf16[1024,2048]{1,0:T(8,128)(2,1)}, bf16[1024,512]{1,0:T(8,128)(2,1)}, bf16[1024,512]{1,0:T(8,128)(2,1)}, b...) conditional(s32[]{:T(128)} %convert_element_type.50, ...), branch_computations={%region_6.7_spmd, %region_7.8_spmd} | conditional | bytes 17072680 | solution.py:1048
  174.7 17.3 %weight_grads.4 = f32[6144,512]{1,0:T(8,128)} custom-call(bf16[1024,2048]{1,0:T(8,128)(2,1)} %get-tuple-element.630.refs_0_, bf16[1024,512]{1,0:T(8,128)(2,1)} %get-tuple-element.631.refs_1_, bf16[1024,512]{1,0:T(8,128)(2,1)} %get-tuple-element.632.refs_2_, bf16[1024,2048]{1,0:T(8,128)(2,1)} %get-tuple-element.633.refs_3_, ...), custom_call_target="tpu_custom_call" | custom-call | tf_op jit(solution)/shard_map/cond/branch_1_fun/weight_grads/pallas_call | solution.py:496
  192.1 9.8 %scatter_codes.1 = f32[512,512]{1,0:T(8,128)} custom-call(s32[2048]{0:T(1024)S(1)} %copy-done.55, f32[2048,32]{1,0:T(8,128)S(1)} %get-tuple-element.641.unit, f32[1024,32]{1,0:T(8,128)S(1)} %copy-done.47, f32[1024,32]{1,0:T(8,128)S(1)} %copy-done.48, f32[32,8192]{1,0:T(8,128)S(1)} %copy-done.27), custom_call_target="tpu_custom_call" | custom-call | tf_op jit(solution)/shard_map/cond/branch_1_fun/scatter_codes/pallas_call | solution.py:141
  201.9 1.3 collective-permute-start.1
  203.1 16.3 %collective-permute-done.1 = f32[1024,32]{1,0:T(8,128)} collective-permute-done((f32[1024,32]{1,0:T(8,128)}, f32[1024,32]{1,0:T(8,128)}, u32[]{:S(2)}, u32[]{:S(2)}) %collective-permute-start.1) | collective-permute-done | bytes 131104 | tf_op jit(solution)/shard_map/ppermute | solution.py:1050
  219.4 78.8 %conditional.7 = (f32[6144,512]{1,0:T(8,128)}, f32[2,1024,512]{2,1,0:T(8,128)}, f32[768,512]{1,0:T(8,128)S(1)}) conditional(s32[]{:T(128)} %convert_element_type.50, (bf16[1024,2048]{1,0:T(8,128)(2,1)}, bf16[1024,512]{1,0:T(8,128)(2,1)}, bf16[1024,512]{1,0:T(8,128)(2,1)}, bf16[1024,2048]{1,0:T(8,128)(2,1)}, bf16[1024,512]{1,0:T(8,128)(2,1)}, ...), branch_computations={%region_8.9_spmd, %region_9.10_spmd} | conditional | flops 32768 | bytes 62816904 | solution.py:1068
  220.4 1.4 constant_dynamic-update-slice_fusion
  222.3 16.8 %tail_back.7 = (bf16[1024,512]{1,0:T(8,128)(2,1)}, bf16[1024,2048]{1,0:T(8,128)(2,1)}, f32[1024,512]{1,0:T(8,128)}, bf16[1024,512]{1,0:T(8,128)(2,1)}, bf16[1024...) custom-call(s32[1]{0:T(128)} %get-tuple-element.673.side.refs_0_, ...), custom_call_target="tpu_custom_call" | custom-call | tf_op jit(solution)/shard_map/cond/branch_1_fun/tail_back/pallas_call | solution.py:826
  239.1 0.9 add_dynamic-update-slice_fusion.3
  240.0 0.8 add_dynamic-update-slice_fusion.5
  240.7 1.1 copy-done.13
  241.8 24.1 %attend_back.7 = (bf16[1024,512]{1,0:T(8,128)(2,1)}, bf16[1024,512]{1,0:T(8,128)(2,1)}, bf16[1024,512]{1,0:T(8,128)(2,1)}) custom-call(s32[16]{0:T(128)S(1)} %copy-done.67, bf16[1024,512]{1,0:T(8,128)(2,1)} %get-tuple-element.697.query, bf16[1024,512]{1,0:T(8,128)(2,1)} %get-tuple-element.698.marks, bf16[1024,512]{1,0:T(8,128)(2,1)} %get-tuple-element.699.key, ...), custom_call_target="tpu_custom_call" | custom-call | tf_op jit(solution)/shard_map/cond/branch_1_fun/attend_back/pallas_call | solution.py:846
  266.0 6.8 %entry_back.7 = (f32[2,1024,512]{2,1,0:T(8,128)S(1)}, f32[1024,32]{1,0:T(8,128)}, f32[16,512]{1,0:T(8,128)}, f32[32,512]{1,0:T(8,128)}) custom-call(s32[1]{0:T(128)} %get-tuple-element.673.side.refs_0_, bf16[2,1024,512]{2,1,0:T(8,128)(2,1)S(1)} %get-tuple-element.675.cotangent.refs_1_, ...), custom_call_target="tpu_custom_call", output_to_operand_aliasing={{0}: (14, {})} | custom-call | tf_op jit(solution)/shard_map/cond/branch_1_fun/entry_back/pallas_call | solution.py:826
  272.8 1.4 add_dynamic-update-slice_fusion.4
  274.8 2.1 copy.219
  277.0 0.9 copy-done.31
  278.2 19.7 %weight_grads.7 = f32[6144,512]{1,0:T(8,128)} custom-call(bf16[1024,2048]{1,0:T(8,128)(2,1)} %get-tuple-element.672.refs_0_, bf16[1024,512]{1,0:T(8,128)(2,1)} %get-tuple-element.690.refs_1_, bf16[1024,512]{1,0:T(8,128)(2,1)S(1)} %copy-done.32, bf16[1024,2048]{1,0:T(8,128)(2,1)} %get-tuple-element.692.refs_3_, ...), custom_call_target="tpu_custom_call", output_to_operand_aliasing={{}: (10, {})} | custom-call | tf_op jit(solution)/shard_map/cond/branch_1_fun/weight_grads/pallas_call | solution.py:496
  298.3 1.1 copy-done.12
  299.4 154.4 %sum_over_dp.1 = (f32[6144,512]{1,0:T(8,128)}, f32[768,512]{1,0:T(8,128)S(1)}) custom-call(f32[6144,512]{1,0:T(8,128)} %get-tuple-element.879.main, f32[768,512]{1,0:T(8,128)} %copy-done.12), custom_call_target="tpu_custom_call" | custom-call | tf_op jit(solution)/shard_map/sum_over_dp/pallas_call | solution.py:715
  455.7 1.0 slice.117
  456.7 2.3 slice_bitcast_fusion.1
  459.0 2.2 slice.92
  461.2 7.8 %slice_bitcast_fusion = (f32[1,2048,512]{2,1,0:T(8,128)}, f32[2048,512]{1,0:T(8,128)}) fusion(f32[6144,512]{1,0:T(8,128)} %get-tuple-element.881), kind=kLoop, calls=%fused_computation.12 | loop fusion | bytes 16777216 | tf_op jit(solution)/shard_map/broadcast_in_dim | solution.py:1090
  470.3 2.3 copy.84
  472.6 6.9 %copy.77 = f32[512,4,512]{2,1,0:T(4,128)} copy(f32[512,4,512]{2,0,1:T(8,128)} %bitcast.75) | data formatting | bytes 8388608 | tf_op jit(solution)/shard_map/transpose | solution.py:1083
  479.5 6.0 %reshape.91 = f32[1,512,2048]{2,1,0:T(8,128)} reshape(f32[512,4,512]{2,1,0:T(4,128)} %copy.77) | data formatting | bytes 8388608 | tf_op jit(solution)/shard_map/reshape | solution.py:1083
  485.5 2.4 copy.76
  487.9 3.5 copy.79
  (141 shorter events, 11.4 us)
Async XLA Ops:
  0.6 17.3 %copy-start.68 = (s32[2,1024]{1,0:T(2,128)S(1)}, s32[2,1024]{1,0:T(2,128)}, u32[]{:S(2)}) copy-start(s32[2,1024]{1,0:T(2,128)} %param.25) | copy-start | bytes 24580
  2.7 16.6 %copy-start = (bf16[1,2,1024,512]{3,2,1,0:T(8,128)(2,1)S(1)}, bf16[1,2,1024,512]{3,2,1,0:T(8,128)(2,1)}, u32[]{:S(2)}) copy-start(bf16[1,2,1024,512]{3,2,1,0:T(8,128)(2,1)} %param.24) | copy-start | bytes 6291460
  2.7 16.6 %copy-start.33 = (f32[2,512]{1,0:T(2,128)S(1)}, f32[2,512]{1,0:T(2,128)}, u32[]{:S(2)}) copy-start(f32[2,512]{1,0:T(2,128)} %head_bias.3) | copy-start | bytes 12292
  2.7 16.6 %copy-start.40 = (f32[1,2,512]{2,1,0:T(2,128)S(1)}, f32[1,2,512]{2,1,0:T(2,128)}, u32[]{:S(2)}) copy-start(f32[1,2,512]{2,1,0:T(2,128)} %param.31) | copy-start | bytes 12292
  7.7 17.8 %copy-start.54 = (s32[1,8,2,128]{3,1,2,0:T(8,128)}, s32[1,8,2,128]{3,1,2,0:T(8,128)S(1)}, u32[]{:S(2)}) copy-start(s32[1,8,2,128]{3,1,2,0:T(8,128)S(1)} %copy.90) | copy-start | bytes 24580
  9.1 16.3 %copy-start.61 = (s32[16]{0:T(128)}, s32[16]{0:T(128)S(1)}, u32[]{:S(2)}) copy-start(s32[16]{0:T(128)S(1)} %reshape.89.windows) | copy-start | bytes 196
  10.0 8.0 %copy-start.74 = (pred[128]{0:T(512)(128)(4,1)S(1)}, pred[128]{0:T(512)(128)(4,1)}, u32[]{:S(2)}) copy-start(pred[128]{0:T(512)(128)(4,1)} %get-tuple-element.1085) | copy-start | bytes 388
  10.0 8.0 %copy-start.75 = (pred[128]{0:T(512)(128)(4,1)S(1)}, pred[128]{0:T(512)(128)(4,1)}, u32[]{:S(2)}) copy-start(pred[128]{0:T(512)(128)(4,1)} %get-tuple-element.1086) | copy-start | bytes 388
  19.3 38.0 %copy-start.9 = (bf16[2,1024,128]{2,1,0:T(8,128)(2,1)}, bf16[2,1024,128]{2,1,0:T(8,128)(2,1)S(1)}, u32[]{:S(2)}) copy-start(bf16[2,1024,128]{2,1,0:T(8,128)(2,1)S(1)} %get-tuple-element.1082.query_mark) | copy-start | bytes 1572868
  25.5 13.4 %copy-start.56 = (f32[1,2048]{1,0:T(1,128)S(1)}, f32[1,2048]{1,0:T(1,128)}, u32[]{:S(2)}) copy-start(f32[1,2048]{1,0:T(1,128)} %hidden_bias.1) | copy-start | bytes 24580
  25.5 13.4 %copy-start.71 = (f32[32]{0:T(128)S(1)}, f32[32]{0:T(128)}, u32[]{:S(2)}) copy-start(f32[32]{0:T(128)} %param.37) | copy-start | bytes 388
  38.9 18.3 %copy-start.49 = (bf16[512,32]{0,1:T(8,128)(2,1)S(1)}, bf16[512,32]{0,1:T(8,128)(2,1)}, u32[]{:S(2)}) copy-start(bf16[512,32]{0,1:T(8,128)(2,1)} %get-tuple-element.1061) | copy-start | bytes 98308
  38.9 18.3 %copy-start.50 = (bf16[32,512]{1,0:T(8,128)(2,1)S(1)}, bf16[32,512]{1,0:T(8,128)(2,1)}, u32[]{:S(2)}) copy-start(bf16[32,512]{1,0:T(8,128)(2,1)} %get-tuple-element.1062) | copy-start | bytes 98308
  38.9 18.3 %copy-start.51 = (bf16[32,512]{1,0:T(8,128)(2,1)S(1)}, bf16[32,512]{1,0:T(8,128)(2,1)}, u32[]{:S(2)}) copy-start(bf16[32,512]{1,0:T(8,128)(2,1)} %get-tuple-element.1063) | copy-start | bytes 98308
  67.8 6.1 %copy-start.10 = (bf16[2,1024,128]{2,1,0:T(8,128)(2,1)}, bf16[2,1024,128]{2,1,0:T(8,128)(2,1)S(1)}, u32[]{:S(2)}) copy-start(bf16[2,1024,128]{2,1,0:T(8,128)(2,1)S(1)} %get-tuple-element.461.query_mark) | copy-start | bytes 1572868 | tf_op jit(solution)/shard_map/cond
  67.8 6.1 %copy-start.57 = (f32[1,2048]{1,0:T(1,128)}, f32[1,2048]{1,0:T(1,128)S(1)}, u32[]{:S(2)}) copy-start(f32[1,2048]{1,0:T(1,128)S(1)} %get-tuple-element.467.hidden_bias) | copy-start | bytes 24580 | tf_op jit(solution)/shard_map/cond
  67.8 6.1 %copy-start.63 = (s32[16]{0:T(128)S(1)}, s32[16]{0:T(128)}, u32[]{:S(2)}) copy-start(s32[16]{0:T(128)} %get-tuple-element.460.windows) | copy-start | bytes 196 | tf_op jit(solution)/shard_map/cond
  73.9 13.2 %copy-start.24 = (bf16[1024,512]{1,0:T(8,128)(2,1)}, bf16[1024,512]{1,0:T(8,128)(2,1)S(1)}, u32[]{:S(2)}) copy-start(bf16[1024,512]{1,0:T(8,128)(2,1)S(1)} %get-tuple-element.1110.query) | copy-start | bytes 3145732 | tf_op jit(solution)/shard_map/cond
  73.9 13.2 %copy-start.25 = (bf16[1024,512]{1,0:T(8,128)(2,1)}, bf16[1024,512]{1,0:T(8,128)(2,1)S(1)}, u32[]{:S(2)}) copy-start(bf16[1024,512]{1,0:T(8,128)(2,1)S(1)} %get-tuple-element.1111.key) | copy-start | bytes 3145732 | tf_op jit(solution)/shard_map/cond
  73.9 13.2 %copy-start.26 = (bf16[1024,512]{1,0:T(8,128)(2,1)}, bf16[1024,512]{1,0:T(8,128)(2,1)S(1)}, u32[]{:S(2)}) copy-start(bf16[1024,512]{1,0:T(8,128)(2,1)S(1)} %get-tuple-element.1112.value) | copy-start | bytes 3145732 | tf_op jit(solution)/shard_map/cond
  73.9 13.2 %copy-start.35 = (f32[2,512]{1,0:T(2,128)S(1)}, f32[2,512]{1,0:T(2,128)}, u32[]{:S(2)}) copy-start(f32[2,512]{1,0:T(2,128)} %get-tuple-element.452.head_bias) | copy-start | bytes 12292 | tf_op jit(solution)/shard_map/cond
  73.9 13.2 %copy-start.42 = (f32[2,512]{1,0:T(2,128)S(1)}, f32[2,512]{1,0:T(2,128)}, u32[]{:S(2)}) copy-start(f32[2,512]{1,0:T(2,128)} %get-tuple-element.453.gains) | copy-start | bytes 12292 | tf_op jit(solution)/shard_map/cond
  74.0 13.2 %copy-start.52 = (f32[1,512]{1,0:T(1,128)S(1)}, f32[1,512]{1,0:T(1,128)}, u32[]{:S(2)}) copy-start(f32[1,512]{1,0:T(1,128)} %get-tuple-element.469.output_gain) | copy-start | bytes 6148 | tf_op jit(solution)/shard_map/cond
  74.0 13.2 %copy-start.58 = (f32[1,2048]{1,0:T(1,128)S(1)}, f32[1,2048]{1,0:T(1,128)}, u32[]{:S(2)}) copy-start(f32[1,2048]{1,0:T(1,128)} %copy-done.57) | copy-start | bytes 24580 | tf_op jit(solution)/shard_map/cond
  74.0 13.2 %copy-start.72 = (f32[1,32]{1,0:T(1,128)S(1)}, f32[1,32]{1,0:T(1,128)}, u32[]{:S(2)}) copy-start(f32[1,32]{1,0:T(1,128)} %get-tuple-element.471.down_bias) | copy-start | bytes 388 | tf_op jit(solution)/shard_map/cond
  87.1 18.5 %copy-start.5 = (bf16[1024,512]{1,0:T(8,128)(2,1)}, bf16[1024,512]{1,0:T(8,128)(2,1)S(1)}, u32[]{:S(2)}) copy-start(bf16[1024,512]{1,0:T(8,128)(2,1)S(1)} %get-tuple-element.1113.context) | copy-start | bytes 3145732 | tf_op jit(solution)/shard_map/cond
  105.6 13.4 %collective-permute-start = (f32[1024,32]{1,0:T(8,128)}, f32[1024,32]{1,0:T(8,128)}, u32[]{:S(2)}, u32[]{:S(2)}) collective-permute-start(f32[1024,32]{1,0:T(8,128)} %get-tuple-element.828), channel_id=1, source_target_pairs={{16,0},{17,1},{18,2},{19,3},{20,4},{21,5},{22,6},{23,7},{24,8},{25... | collective-permute-start | bytes 393224 | tf_op jit(solution)/shard_map/ppermute | solution.py:1029
  120.0 17.0 %copy-start.29 = (bf16[1024,512]{1,0:T(8,128)(2,1)S(1)}, bf16[1024,512]{1,0:T(8,128)(2,1)}, u32[]{:S(2)}) copy-start(bf16[1024,512]{1,0:T(8,128)(2,1)} %get-tuple-element.561.marks) | copy-start | bytes 3145732 | tf_op jit(solution)/shard_map/cond
  120.0 17.0 %copy-start.65 = (s32[16]{0:T(128)S(1)}, s32[16]{0:T(128)}, u32[]{:S(2)}) copy-start(s32[16]{0:T(128)} %get-tuple-element.559.windows) | copy-start | bytes 196 | tf_op jit(solution)/shard_map/cond
  137.0 22.6 %copy-start.37 = (f32[2,512]{1,0:T(2,128)S(1)}, f32[2,512]{1,0:T(2,128)}, u32[]{:S(2)}) copy-start(f32[2,512]{1,0:T(2,128)} %get-tuple-element.545.head_bias) | copy-start | bytes 12292 | tf_op jit(solution)/shard_map/cond
  137.0 22.6 %copy-start.44 = (f32[2,512]{1,0:T(2,128)S(1)}, f32[2,512]{1,0:T(2,128)}, u32[]{:S(2)}) copy-start(f32[2,512]{1,0:T(2,128)} %get-tuple-element.553.gains) | copy-start | bytes 12292 | tf_op jit(solution)/shard_map/cond
  159.6 7.6 %copy-start.18 = (bf16[1024,512]{1,0:T(8,128)(2,1)}, bf16[1024,512]{1,0:T(8,128)(2,1)S(1)}, u32[]{:S(2)}) copy-start(bf16[1024,512]{1,0:T(8,128)(2,1)S(1)} %get-tuple-element.1166.query_grad) | copy-start | bytes 3145732 | tf_op jit(solution)/shard_map/cond
  159.6 7.6 %copy-start.19 = (bf16[1024,512]{1,0:T(8,128)(2,1)}, bf16[1024,512]{1,0:T(8,128)(2,1)S(1)}, u32[]{:S(2)}) copy-start(bf16[1024,512]{1,0:T(8,128)(2,1)S(1)} %get-tuple-element.1167.key_grad) | copy-start | bytes 3145732 | tf_op jit(solution)/shard_map/cond
  159.6 7.6 %copy-start.20 = (bf16[1024,512]{1,0:T(8,128)(2,1)}, bf16[1024,512]{1,0:T(8,128)(2,1)S(1)}, u32[]{:S(2)}) copy-start(bf16[1024,512]{1,0:T(8,128)(2,1)S(1)} %get-tuple-element.1168.value_grad) | copy-start | bytes 3145732 | tf_op jit(solution)/shard_map/cond
  174.6 17.4 %copy-start.27 = (f32[32,8192]{1,0:T(8,128)S(1)}, f32[32,8192]{1,0:T(8,128)}, u32[]{:S(2)}) copy-start(f32[32,8192]{1,0:T(8,128)} %get-tuple-element.644.table_turned) | copy-start | bytes 3145732 | tf_op jit(solution)/shard_map/cond
  174.7 17.4 %copy-start.47 = (f32[1024,32]{1,0:T(8,128)S(1)}, f32[1024,32]{1,0:T(8,128)}, u32[]{:S(2)}) copy-start(f32[1024,32]{1,0:T(8,128)} %get-tuple-element.642.latent_first) | copy-start | bytes 393220 | tf_op jit(solution)/shard_map/cond
  174.7 17.4 %copy-start.48 = (f32[1024,32]{1,0:T(8,128)S(1)}, f32[1024,32]{1,0:T(8,128)}, u32[]{:S(2)}) copy-start(f32[1024,32]{1,0:T(8,128)} %get-tuple-element.643.latent_second) | copy-start | bytes 393220 | tf_op jit(solution)/shard_map/cond
  174.7 17.4 %copy-start.55 = (s32[2048]{0:T(1024)S(1)}, s32[2048]{0:T(1024)}, u32[]{:S(2)}) copy-start(s32[2048]{0:T(1024)} %get-tuple-element.640.index) | copy-start | bytes 24580 | tf_op jit(solution)/shard_map/cond
  201.9 17.6 %collective-permute-start.1 = (f32[1024,32]{1,0:T(8,128)}, f32[1024,32]{1,0:T(8,128)}, u32[]{:S(2)}, u32[]{:S(2)}) collective-permute-start(f32[1024,32]{1,0:T(8,128)} %get-tuple-element.861), channel_id=1, source_target_pairs={{16,0},{17,1},{18,2},{19,3},{20,4},{21,5},{22,6},{23,7},{24,8},{25... | collective-permute-start | bytes 393224 | tf_op jit(solution)/shard_map/ppermute | solution.py:1050
  222.3 16.8 %copy-start.60 = (f32[32,512]{1,0:T(8,128)S(1)}, f32[32,512]{1,0:T(8,128)}, u32[]{:S(2)}) copy-start(f32[32,512]{1,0:T(8,128)} %get-tuple-element.716) | copy-start | bytes 196612 | tf_op jit(solution)/shard_map/cond
  222.3 17.7 %copy-start.69 = (f32[16,512]{1,0:T(8,128)S(1)}, f32[16,512]{1,0:T(8,128)}, u32[]{:S(2)}) copy-start(f32[16,512]{1,0:T(8,128)} %get-tuple-element.718) | copy-start | bytes 98308 | tf_op jit(solution)/shard_map/cond
  222.3 19.5 %copy-start.67 = (s32[16]{0:T(128)S(1)}, s32[16]{0:T(128)}, u32[]{:S(2)}) copy-start(s32[16]{0:T(128)} %get-tuple-element.696.windows) | copy-start | bytes 196 | tf_op jit(solution)/shard_map/cond
  241.8 24.2 %copy-start.4 = (f32[2,1024,512]{2,1,0:T(8,128)S(1)}, f32[2,1024,512]{2,1,0:T(8,128)}, u32[]{:S(2)}) copy-start(f32[2,1024,512]{2,1,0:T(8,128)} %get-tuple-element.712.refs_14_) | copy-start | bytes 12582916 | tf_op jit(solution)/shard_map/cond
  241.8 24.2 %copy-start.39 = (f32[2,512]{1,0:T(2,128)S(1)}, f32[2,512]{1,0:T(2,128)}, u32[]{:S(2)}) copy-start(f32[2,512]{1,0:T(2,128)} %get-tuple-element.679.head_bias.refs_4_) | copy-start | bytes 12292 | tf_op jit(solution)/shard_map/cond
  241.8 24.2 %copy-start.46 = (f32[2,512]{1,0:T(2,128)S(1)}, f32[2,512]{1,0:T(2,128)}, u32[]{:S(2)}) copy-start(f32[2,512]{1,0:T(2,128)} %get-tuple-element.687.gains.refs_10_) | copy-start | bytes 12292 | tf_op jit(solution)/shard_map/cond
  266.0 6.8 %copy-start.70 = (f32[16,512]{1,0:T(8,128)S(1)}, f32[16,512]{1,0:T(8,128)}, u32[]{:S(2)}) copy-start(f32[16,512]{1,0:T(8,128)} %get-tuple-element.720) | copy-start | bytes 98308 | tf_op jit(solution)/shard_map/cond
  274.8 3.4 copy-start.32
  278.2 19.7 %copy-start.14 = (f32[640,512]{1,0:T(8,128)S(1)}, f32[640,512]{1,0:T(8,128)}, u32[]{:S(2)}) copy-start(f32[640,512]{1,0:T(8,128)} %broadcast_dynamic-update-slice_fusion.4) | copy-start | bytes 3932164 | tf_op jit(solution)/shard_map/cond
  (5 other events, 9.3 us)

commit v3 on v2

--- a/solution.py
+++ b/solution.py
@@ -60,7 +60,7 @@
     return jnp.sum(values, 0, keepdims=True)
 
 
-def code_kernel(index, table_turned, unit, wide, table, raw):
+def code_kernel(index, table_turned, segments, unit, wide, query_mark, key_mark, table, raw):
     count = raw.shape[0]
     block = 512
 
@@ -72,33 +72,44 @@
     lax.fori_loop(0, table.shape[0] // block, turn, 0)
 
     def some(step, carry):
-        for inner in range(8):
-            token = step * 8 + inner
+        for inner in range(16):
+            token = step * 16 + inner
             raw[pl.ds(token, 1), :] = table[pl.ds(index[token], 1), :]
         return carry
 
-    lax.fori_loop(0, count // 8, some, 0)
+    lax.fori_loop(0, count // 16, some, 0)
     values = raw[...]
     values = values * lax.rsqrt(jnp.sum(values * values, -1, keepdims=True) + NORM_EPS)
     unit[...] = values
     high, low = split(values)
     wide[...] = jnp.concatenate([high, low, high, jnp.zeros_like(high)], 1)
-
-
-def gather_codes(index, table_turned):
+    length = segments.shape[1]
+    lane = lanes((length, 128)) & 63
+    for row in range(segments.shape[0]):
+        owner = jnp.broadcast_to(segments[row : row + 1, :], (128, length)).T
+        same = owner == lane
+        query_mark[row] = jnp.where((lane < 4) & jnp.logical_not(same), MASKED, 0.0).astype(BF)
+        key_mark[row] = jnp.where(((lane < 4) & same) | ((lane > 3) & (lane < 7)), 1.0, 0.0).astype(BF)
+
+
+def gather_codes(index, table_turned, segments):
     count, width = index.shape[0], table_turned.shape[0]
+    vmem = pl.BlockSpec(memory_space=pltpu.VMEM)
+    mark = jax.ShapeDtypeStruct(segments.shape + (128,), BF)
     return pl.pallas_call(
         code_kernel,
-        in_specs=[pl.BlockSpec(memory_space=pltpu.SMEM), pl.BlockSpec(memory_space=pltpu.VMEM)],
-        out_specs=[pl.BlockSpec(memory_space=pltpu.VMEM)] * 2,
+        in_specs=[pl.BlockSpec(memory_space=pltpu.SMEM), vmem, vmem],
+        out_specs=[vmem] * 4,
         out_shape=(
             jax.ShapeDtypeStruct((count, width), F32),
             jax.ShapeDtypeStruct((count, 4 * width), BF),
+            mark,
+            mark,
         ),
         scratch_shapes=[pltpu.VMEM(table_turned.shape[::-1], F32), pltpu.VMEM((count, width), F32)],
         compiler_params=PARAMS,
         name="gather_codes",
-    )(index, table_turned)
+    )(index, table_turned, segments)
 
 
 def scatter_kernel(index, unit, latent_first, latent_second, table_turned, out, total, rows):
@@ -150,7 +161,9 @@
 
 
 def entry_values(encoder, edge, wide, up, head_bias):
-    return jnp.where(encoder, edge.astype(F32), dot(wide, up, NN) + head_bias[1:2, :])
+    high, low = split(up)
+    parts = jnp.concatenate([high, high, low, jnp.zeros_like(low)], 0)
+    return jnp.where(encoder, edge.astype(F32), dot(wide, parts, NN) + head_bias[1:2, :])
 
 
 def project_kernel(side, edge, wide, up, head_bias, gains, biases, weight, n1, query, key, value):
@@ -255,7 +268,7 @@
     normed = (hat * gains[1:2, :] + biases[4:5, :]).astype(BF)
     n2[...] = normed
     total = midway + biases[5:6, :]
-    chunk = 512
+    chunk = 256
     for start in range(0, weight_in.shape[1], chunk):
         here = slice(start, start + chunk)
         active, slope = gelu_parts(dot(normed, weight_in[:, here], NN) + hidden_bias[0:1, here])
@@ -275,26 +288,23 @@
 
 
 def code_product(values, weight):
-    narrow = weight.shape[1] // 2
-    high, low = split(values)
-    both = dot(high, weight, NN)
-    return both[:, :narrow] + both[:, narrow:] + dot(low, weight[:, :narrow], NN)
+    return dot3(split(values), split(weight), NT)
 
 
 def tail_back_kernel(
-    side, result, cotangent, unit, latent_in, output_gain, head_bias, down, down_bias, down_turned,
-    weight_last, slope, weight_in, mid, gains, biases, weight_out,
-    out_low, preact_low, mid_grad, branch_low, context_grad, sums, head_weight,
-    upstream,
+    side, result, cotangent, unit, latent_in, output_gain, head_bias, down, down_bias,
+    weight_last, slope, weight_in, mid, gains, biases, weight_out, *refs, adding
 ):
+    before, refs = refs[: 2 * adding], refs[2 * adding :]
+    out_low, preact_low, mid_grad, branch_low, context_grad, sums, head_weight, upstream = refs
     encoder = side[0] == 0
     width = result.shape[1]
     narrow = unit.shape[1]
 
     @pl.when(pl.program_id(0) == 0)
     def _():
-        sums[...] = jnp.zeros_like(sums)
-        head_weight[...] = jnp.zeros_like(head_weight)
+        sums[...] = before[0][...] if adding else jnp.zeros_like(sums)
+        head_weight[...] = before[1][...] if adding else jnp.zeros_like(head_weight)
 
     @pl.when(encoder)
     def _():
@@ -303,10 +313,10 @@
         latent = code_product(normed, down[...]) + down_bias[0:1, :]
         scale = lax.rsqrt(jnp.sum(latent * latent, -1, keepdims=True) + NORM_EPS)
         code = latent * scale
-        code_grad = latent_in[...] + 0.5 * (code - unit[...])
+        code_grad = latent_in[...].T + 0.5 * (code - unit[...])
         latent_grad = scale * (code_grad - code * jnp.sum(code * code_grad, -1, keepdims=True))
         pieces = split(latent_grad)
-        normed_grad = dot3(pieces, (down_turned[:narrow, :], down_turned[narrow:, :]), NN)
+        normed_grad = dot3(pieces, split(down[...]), NN)
         head_weight[...] += dot3(pieces, split(normed), TN)
         sums[8:9, :] += column_sum(normed_grad * hat)
         sums[9:10, :] += column_sum(normed_grad)
@@ -322,13 +332,17 @@
     out_low[...] = low
     sums[4:5, :] += column_sum(low.astype(F32))
     normed_grad = None
-    chunk = 512
+    chunk = 1024
     for start in range(0, weight_in.shape[1], chunk):
         here = slice(start, start + chunk)
         active_grad = dot(low, weight_last[here, :], NT)
         inner = (active_grad * slope[:, here].astype(F32)).astype(BF)
         preact_low[:, here] = inner
-        sums[start // chunk : start // chunk + 1, :] += column_sum(inner.astype(F32))
+        part = column_sum(inner.astype(F32))
+        for at in range(0, chunk, min(chunk, width)):
+            row, lane = (start + at) // width, (start + at) % width
+            size = min(chunk, width)
+            sums[row : row + 1, lane : lane + size] += part[:, at : at + size]
         term = dot(inner, weight_in[:, here], NT)
         normed_grad = term if normed_grad is None else normed_grad + term
     hat, inverse = norm_parts(mid[...])
@@ -412,17 +426,18 @@
 
 def entry_back_kernel(
     side, edge, wide, up, head_bias, unit, query_grad, key_grad, value_grad, weight, gains, biases,
-    mid_grad, up_turned,
-    entry, latent_out, sums, head_weight,
+    mid_grad, *refs, adding
 ):
+    before, refs = refs[: 2 * adding], refs[2 * adding :]
+    entry, latent_out, sums, head_weight = refs
     encoder = side[0] == 0
     width = edge.shape[1]
     narrow = unit.shape[1]
 
     @pl.when(pl.program_id(0) == 0)
     def _():
-        sums[...] = jnp.zeros_like(sums)
-        head_weight[...] = jnp.zeros_like(head_weight)
+        sums[...] = before[0][...] if adding else jnp.zeros_like(sums)
+        head_weight[...] = before[1][...] if adding else jnp.zeros_like(head_weight)
 
     values = entry_values(encoder, edge[...], wide[...], up[...], head_bias[...])
     normed_grad = (
@@ -441,7 +456,7 @@
     @pl.when(jnp.logical_not(encoder))
     def _():
         sums[4:5, :] += column_sum(total)
-        latent_out[...] = code_product(total, up_turned[...])
+        latent_out[...] = code_product(total, up[...]).T
         head_weight[...] += dot3(split(unit[...]), split(total), TN)
 
 
@@ -706,6 +721,75 @@
         keep(which, way).wait()
 
 
+def head_kernel(side, book, down, up, late, early, out):
+    encoder = side[0] == 0
+    out[...] = jnp.zeros_like(out)
+    size = book.shape[0]
+    narrow = down.shape[0]
+    at = size + 2 * narrow
+
+    @pl.when(encoder)
+    def _():
+        out[:size, :] = book[...]
+        out[size : size + narrow, :] = down[...]
+        out[at : at + 16, :] = late[...]
+        out[at + 16 : at + 32, :] = early[...]
+
+    @pl.when(jnp.logical_not(encoder))
+    def _():
+        out[size + narrow : at, :] = up[...]
+        out[at + 32 : at + 48, :] = late[...]
+        out[at + 48 : at + 64, :] = early[...]
+
+
+def gather_head(side, book, down, up, late, early):
+    rows = book.shape[0] + 2 * down.shape[0] + 64
+    unit = 16 * lax.axis_size("dp")
+    vmem = pl.BlockSpec(memory_space=pltpu.VMEM)
+    return pl.pallas_call(
+        head_kernel,
+        in_specs=[pl.BlockSpec(memory_space=pltpu.SMEM)] + [vmem] * 5,
+        out_specs=vmem,
+        out_shape=jax.ShapeDtypeStruct((rows + (-rows % unit), book.shape[1]), F32),
+        compiler_params=PARAMS,
+        name="gather_head",
+    )(side, book, down, up, late, early)
+
+
+def unpack_kernel(main, misc, hidden_out, hidden_in, attention_out, attention_in, book, sems):
+    width = main.shape[1]
+    narrow = book.shape[0]
+    steps = hidden_out.shape[0] // width
+    copies = [(main.at[pl.ds(0, steps * width)], hidden_out)]
+    at = steps
+    for out, count in ((hidden_in, steps), (attention_out, 1), (attention_in, 3)):
+        for number in range(count):
+            copies.append((main.at[pl.ds((at + number) * width, width)], out.at[:, pl.ds(number * width, width)]))
+        at += count
+    for number in range(book.shape[1] // width):
+        copies.append((misc.at[pl.ds(number * narrow, narrow)], book.at[:, pl.ds(number * width, width)]))
+    copies = [pltpu.make_async_copy(*pair, sems.at[number]) for number, pair in enumerate(copies)]
+    for copy in copies:
+        copy.start()
+    for copy in copies:
+        copy.wait()
+
+
+def unpack(main, misc, hidden, table_turned):
+    width = main.shape[1]
+    shapes = ((hidden, width), (width, hidden), (width, width), (width, 3 * width), table_turned.shape)
+    count = 5 + hidden // width + table_turned.shape[1] // width
+    return pl.pallas_call(
+        unpack_kernel,
+        in_specs=[pl.BlockSpec(memory_space=pl.ANY)] * 2,
+        out_specs=[pl.BlockSpec(memory_space=pl.ANY)] * 5,
+        out_shape=tuple(jax.ShapeDtypeStruct(shape, F32) for shape in shapes),
+        scratch_shapes=[pltpu.SemaphoreType.DMA((count,))],
+        compiler_params=PARAMS,
+        name="unpack",
+    )(main, misc)
+
+
 def sum_over_dp(main, misc):
     chips = lax.axis_size("dp") // 2
     width = main.shape[1]
@@ -759,8 +843,7 @@
             self.gains, self.biases, self.hidden_bias,
         ) = weights
         (
-            self.output_gain, self.head_bias, self.down, self.down_bias, self.down_turned,
-            self.up, self.up_turned,
+            self.output_gain, self.head_bias, self.down, self.down_bias, self.up,
         ) = head
         self.rows, self.count, self.width = edges.shape
         self.hidden = self.hidden_in.shape[1]
@@ -781,12 +864,15 @@
         table = dict(
             out_low=(n, d, BF), preact_low=(n, f, BF), mid_grad=(n, d, F32), branch_low=(n, d, BF),
             query_grad=(n, d, BF), key_grad=(n, d, BF), value_grad=(n, d, BF),
-            latent_out=(n, self.narrow, F32), sums_late=(16, d, F32), sums_early=(16, d, F32),
+            latent_out=(self.narrow, n, F32), sums_late=(16, d, F32), sums_early=(16, d, F32),
             head_late=(self.narrow, d, F32), head_early=(self.narrow, d, F32),
         )
         shapes = {name: jax.ShapeDtypeStruct((a, b), kind) for name, (a, b, kind) in table.items()}
         shapes["entry"] = jax.ShapeDtypeStruct((self.rows, n, d), F32)
         return shapes
+
+    def turned(self, array):
+        return pl.BlockSpec((array.shape[0], TOKENS), lambda step: (0, step))
 
     def side_spec(self):
         return pl.BlockSpec(memory_space=pltpu.SMEM)
@@ -899,22 +985,24 @@
         kept.update(zip(names, outs))
         return kept
 
-    def backward(self, row, kept, latent_in, rest=None):
+    def backward(self, row, kept, latent_in, former=None, rest=None):
         shapes = self.back_shapes()
+        prior = () if former is None else (former["sums_late"], former["head_late"])
+        adding = int(former is not None)
         back = {}
         names = ("out_low", "preact_low", "mid_grad", "branch_low", "context_grad", "sums_late", "head_late")
         shapes["context_grad"] = shapes["out_low"]
-        consts = (self.output_gain, self.head_bias, self.down, self.down_bias, self.down_turned, self.hidden_out)
+        consts = (self.output_gain, self.head_bias, self.down, self.down_bias, self.hidden_out)
         late = (self.gains, self.biases, self.attention_out)
         outs = self.call(
-            tail_back_kernel,
+            functools.partial(tail_back_kernel, adding=adding),
             [self.side_spec(), self.row_spec(row), self.entry_specs(row)[0], self.unit_spec(row),
-             self.tokens(latent_in)]
+             self.turned(latent_in)]
             + [self.whole(array) for array in consts]
             + [self.tokens(kept["slope"]), self.whole(self.hidden_in), self.tokens(kept["mid"])]
-            + [self.whole(array) for array in late],
+            + [self.whole(array) for array in late + prior],
             (self.side, kept["result"], self.edges, self.unit, latent_in) + consts
-            + (kept["slope"], self.hidden_in, kept["mid"]) + late,
+            + (kept["slope"], self.hidden_in, kept["mid"]) + late + prior,
             [shapes[name] for name in names],
             [self.tokens(shapes[name]) for name in names[:5]] + [self.whole(shapes[name]) for name in names[5:]],
             "tail_back",
@@ -937,17 +1025,18 @@
         )
         back.update(zip(names, outs))
         names = ("entry", "latent_out", "sums_early", "head_early")
+        prior = () if former is None else (former["sums_early"], former["head_early"])
         grads = (back["query_grad"], back["key_grad"], back["value_grad"])
         outs = self.call(
-            entry_back_kernel,
+            functools.partial(entry_back_kernel, adding=adding),
             [self.side_spec()] + self.entry_specs(row) + [self.unit_spec(row)]
             + [self.tokens(array) for array in grads]
             + [self.whole(self.attention_in), self.whole(self.gains), self.whole(self.biases),
-               self.tokens(back["mid_grad"]), self.whole(self.up_turned)],
+               self.tokens(back["mid_grad"])] + [self.whole(array) for array in prior],
             (self.side, self.edges, self.wide, self.up, self.head_bias, self.unit) + grads
-            + (self.attention_in, self.gains, self.biases, back["mid_grad"], self.up_turned),
+            + (self.attention_in, self.gains, self.biases, back["mid_grad"]) + prior,
             [shapes[name] for name in names],
-            [self.row_spec(row), self.tokens(shapes["latent_out"])] + [self.whole(shapes[name]) for name in names[2:]],
+            [self.row_spec(row), self.turned(shapes["latent_out"])] + [self.whole(shapes[name]) for name in names[2:]],
             "entry_back",
             rest=rest,
         )
@@ -955,21 +1044,8 @@
         return back
 
 
-def pair_of(values, axis):
-    return jnp.concatenate(split(values), axis)
-
-
 def as_list(table, names):
     return [table[name] for name in names]
-
-
-def marks_of(segments):
-    lane = jnp.arange(128) & 63
-    same = segments[..., None] == lane
-    inside = lane < 4
-    query_mark = jnp.where(inside & ~same, MASKED, 0.0).astype(BF)
-    key_mark = jnp.where((inside & same) | ((lane > 3) & (lane < 7)), 1.0, 0.0).astype(BF)
-    return query_mark, key_mark
 
 
 def windows_of(segments):
@@ -996,9 +1072,7 @@
     hidden = hidden_in.shape[2]
     index = code_index.reshape(-1)
     table_turned = codebook.T
-    unit, wide = gather_codes(index, table_turned)
-    query_mark, key_mark = marks_of(segments)
-    up_high, up_low = split(up_weight)
+    unit, wide, query_mark, key_mark = gather_codes(index, table_turned, segments)
     work = Rows(
         side, edges, wide, unit, windows_of(segments), query_mark, key_mark,
         (
@@ -1006,15 +1080,14 @@
             hidden_bias,
         ),
         (
-            output_gain[None], head_bias, pair_of(down_weight, 1), down_bias[None], pair_of(down_weight.T, 0),
-            jnp.concatenate([up_high, up_high, up_low, jnp.zeros_like(up_low)], 0), pair_of(up_weight.T, 1),
+            output_gain[None], head_bias, down_weight.T, down_bias[None], up_weight,
         ),
     )
     kept_shapes = as_list(work.kept_shapes(), KEPT)
     back_shapes = as_list(work.back_shapes(), BACK)
     book_out = book_shape(table_turned, width)
     weight_out = jax.ShapeDtypeStruct((2 * hidden + 4 * width, width), F32)
-    quiet = jnp.zeros((count, unit.shape[1]), F32)
+    quiet = jnp.zeros((unit.shape[1], count), F32)
     first_kept = work.forward(0)
 
     def encoder_second():
@@ -1043,54 +1116,44 @@
 
     def decoder_fourth():
         weights, book = unwritten([weight_out, book_out])
-        return as_list(work.backward(1, kept_b, quiet), BACK), weights, book
+        return as_list(work.backward(1, kept_b, quiet, back_a), BACK), weights, book
 
     back_c, weights_c, book = lax.cond(encoder, encoder_fourth, decoder_fourth)
     back_c = dict(zip(BACK, back_c))
     latent_in_second = lax.ppermute(back_c["latent_out"], "section", [(1, 0)])
 
     def encoder_fifth():
-        back = work.backward(1, kept_a, latent_in_second, back_b["entry"])
+        back = work.backward(1, kept_a, latent_in_second, back_b, back_b["entry"])
         total = weight_grads(kept_a, back, weights_c)
-        late, early, down, unused = [back[name] + back_b[name] for name in BACK[-4:]]
-        empty = jnp.zeros_like(down)
-        none = jnp.zeros_like(jnp.concatenate([late, early]))
-        return total, jnp.concatenate([book, down, empty, late, early, none]), back["entry"]
+        return total, as_list(back, BACK[-4:]), back["entry"]
 
     def decoder_fifth():
         total = weight_grads(first_kept, back_a)
         total = weight_grads(kept_b, back_c, total)
-        late, early, unused, up = [back_a[name] + back_c[name] for name in BACK[-4:]]
-        empty = jnp.zeros_like(up)
-        none = jnp.zeros_like(jnp.concatenate([late, early]))
-        return total, jnp.concatenate([jnp.zeros(book.shape, F32), empty, up, none, late, early]), kept_b["result"]
-
-    totals, misc, edge = lax.cond(encoder, encoder_fifth, decoder_fifth)
-    totals, misc = sum_all(totals, misc)
-    pieces, at = [], 0
-    for size in (book_out.shape[0], unit.shape[1], unit.shape[1], 16, 16, 16, 16):
+        return total, as_list(back_c, BACK[-4:]), kept_b["result"]
+
+    totals, (late, early, down, up), edge = lax.cond(encoder, encoder_fifth, decoder_fifth)
+    totals, misc = sum_all(totals, gather_head(side, book, down, up, late, early))
+    hidden_out_grad, hidden_in_grad, attention_out_grad, attention_in_grad, book = unpack(
+        totals, misc, hidden, table_turned
+    )
+    narrow = unit.shape[1]
+    pieces, at = [], book_out.shape[0]
+    for size in (narrow, narrow, 16, 16, 16, 16):
         pieces.append(misc[at : at + size])
         at += size
-    book, down_grad, up_grad, first_late, first_early, second_late, second_early = pieces
+    down_grad, up_grad, first_late, first_early, second_late, second_early = pieces
     late = jnp.where(encoder, first_late, second_late)
     early = jnp.where(encoder, first_early, second_early)
-    steps = hidden // width
-    narrow = unit.shape[1]
-    book = book.reshape(-1, narrow, width).transpose(1, 0, 2).reshape(table_turned.shape)
-    tiles = totals.reshape(-1, width, width)
-
-    def columns(part):
-        return part.transpose(1, 0, 2).reshape(1, width, -1)
-
     return (
         edge[None],
-        columns(tiles[2 * steps + 1 :]),
-        tiles[2 * steps][None],
-        columns(tiles[steps : 2 * steps]),
-        totals[None, :hidden],
+        attention_in_grad[None],
+        attention_out_grad[None],
+        hidden_in_grad[None],
+        hidden_out_grad[None],
         jnp.stack([early[2], late[6]])[None],
         jnp.stack([early[0], early[1], late[5], early[3], late[7], late[4]])[None],
-        late[:steps].reshape(1, hidden),
+        late[: hidden // width].reshape(1, hidden),
         first_late[8],
         jnp.stack([first_late[9], second_early[4]]),
         down_grad.T,
@@ -1101,12 +1164,9 @@
 
 
 def sum_all(main, misc):
-    devices = lax.axis_size("dp")
-    if devices < 4:
+    if lax.axis_size("dp") < 4:
         return main, lax.psum(misc, "section")
-    unit = 16 * devices
-    extra = -misc.shape[0] % unit
-    return sum_over_dp(main, jnp.pad(misc, ((0, extra), (0, 0))))
+    return sum_over_dp(main, misc)
 
 
 def solution(mesh):

time: 500 us -> 843 us (1.69)
  Pallas kernels: 379 us -> 784 us
  local copies, waits for them, and re-layouts: 51.3 us -> 9.2 us
  waiting for transfers between devices: 28.4 us -> 16.5 us
  other arithmetic: 11.3 us -> 1.44 us
    pallas_call x0 -> x2, Pallas kernels: none -> 417 us  [the longest x1 414 us: unpack(): pl.pallas_call(unpack_kernel, in_specs=[pl.BlockSpec(memory_space=pl.ANY)...]
    pallas_call x8, Pallas kernels: 97.2 us -> 88.1 us  [call(): pl.pallas_call(kernel, input_output_aliases=aliases, grid=(self.count //...]
where the time goes in v3:
time: 843 us; the launch traced here: 833 us
  Pallas kernels  784 us (93%)
  loops' own time  18.2 us (2%)
  waiting for transfers between devices  16.5 us (2%)
  local copies, waits for them, and re-layouts  9.2 us (1%)
    pallas_call x1, Pallas kernels, unpack(): pl.pallas_call(unpack_kernel, in_specs=[pl.BlockSpec(memory_space=pl.ANY)...  414 us
    pallas_call x1, Pallas kernels, sum_over_dp(): pl.pallas_call(functools.partial(sum_kernel, chips), in_specs=[pl.BlockSp...  158 us
    pallas_call x8, Pallas kernels, call(): pl.pallas_call(kernel, input_output_aliases=aliases, grid=(self.count //...  88.1 us
    pallas_call x4, Pallas kernels, attention_call(): pl.pallas_call(functools.partial(kernel, row=row), grid_spec=pltpu.Prefet...  64.9 us
    pallas_call x2, Pallas kernels, weight_grads(): pl.pallas_call(functools.partial(weight_kernel, turns=(first, second, thi...  38.4 us
  transfers between devices with their start and end apart: 2, of which 2 were waited for; matrix products, arithmetic and copies ran while one was open for 0% of the time, Pallas kernels for 0%

profile of v3, /device:TPU:0, one launch (start us, length us, event | category | flops | bytes accessed | tf_op | source)
XLA Modules:
  0.0 832.7 jit_solution(8004106434036233370)
XLA Ops:
  0.7 0.7 copy.54
  1.4 0.7 reshape.59
  2.1 0.1 fusion.4
  2.1 0.1 copy.48
  2.2 0.1 copy.47
  2.3 0.2 select_reduce_fusion.1
  2.6 0.1 copy.44
  2.7 0.1 reshape.60.windows
  2.8 0.7 copy.53
  3.5 7.6 gather_codes.1
  11.1 0.0 copy-start.5
  11.1 0.0 copy-start.34
  11.1 0.0 copy-start.35
  11.2 6.6 project.5
  17.8 10.3 %attend.5 = (bf16[1024,512]{1,0:T(8,128)(2,1)}, bf16[1024,512]{1,0:T(8,128)(2,1)}) custom-call(s32[16]{0:T(128)S(1)} %reshape.60.windows, bf16[1024,512]{1,0:T(8,128)(2,1)} %get-tuple-element.811.query, bf16[1024,512]{1,0:T(8,128)(2,1)} %get-tuple-element.812.key, bf16[1024,512]{1,0:T(8,128)(2,1)} %get-tuple-element.813.value, ...), custom_call_target="tpu_custom_call" | custom-call | tf_op jit(solution)/shard_map/attend/pallas_call | solution.py:932
  28.2 14.6 %hidden.5 = (f32[1024,512]{1,0:T(8,128)}, bf16[1024,512]{1,0:T(8,128)(2,1)}, bf16[1024,2048]{1,0:T(8,128)(2,1)}, bf16[1024,2048]{1,0:T(8,128)(2,1)}, f32[2,1024,512]{2,1,0:T(8,128)}, /*index=5*/f32[1024,32]{1,0:T(8,128)}) custom-call(s32[1]{0:T(128)} %bitcast.side, bf16[2,1024,512]{2,1,0:T(8,128)(2,1)S(1)} %bitcast.43, ...), custom_call_target="tpu_custom_call" | custom-call | tf_op jit(solution)/shard_map/hidden/pallas_call | solution.py:912
  42.8 44.2 %conditional.4 = (bf16[1024,512]{1,0:T(8,128)(2,1)}, bf16[1024,512]{1,0:T(8,128)(2,1)}, bf16[1024,512]{1,0:T(8,128)(2,1)}, bf16[1024,512]{1,0:T(8,128)(2,1)}, bf...) conditional(s32[]{:T(128)} %convert_element_type.2, ...), branch_computations={%region_2.3_spmd, %region_3.4_spmd} | conditional | bytes 14811408 | solution.py:1099
  53.1 6.0 project.3
  59.1 13.3 %attend.3 = (bf16[1024,512]{1,0:T(8,128)(2,1)}, bf16[1024,512]{1,0:T(8,128)(2,1)}) custom-call(s32[16]{0:T(128)S(1)} %get-tuple-element.446.windows, bf16[1024,512]{1,0:T(8,128)(2,1)} %get-tuple-element.982.query, bf16[1024,512]{1,0:T(8,128)(2,1)} %get-tuple-element.983.key, bf16[1024,512]{1,0:T(8,128)(2,1)} %get-tuple-element.984.value, ...), custom_call_target="tpu_custom_call" | custom-call | tf_op jit(solution)/shard_map/cond/branch_1_fun/attend/pallas_call | solution.py:932
  72.4 14.6 %hidden.3 = (f32[1024,512]{1,0:T(8,128)}, bf16[1024,512]{1,0:T(8,128)(2,1)}, bf16[1024,2048]{1,0:T(8,128)(2,1)}, bf16[1024,2048]{1,0:T(8,128)(2,1)}, f32[2,1024,512]{2,1,0:T(8,128)}, /*index=5*/f32[1024,32]{1,0:T(8,128)}) custom-call(s32[1]{0:T(128)} %get-tuple-element.434.side, bf16[2,1024,512]{2,1,0:T(8,128)(2,1)S(1)} %get-tuple-element.435.edge, ...), custom_call_target="tpu_custom_call" | custom-call | tf_op jit(solution)/shard_map/cond/branch_1_fun/hidden/pallas_call | solution.py:912
  87.1 1.3 collective-permute-start
  88.4 5.8 collective-permute-done
  94.1 41.4 %conditional.5 = (bf16[1024,512]{1,0:T(8,128)(2,1)}, bf16[1024,512]{1,0:T(8,128)(2,1)}, bf16[1024,512]{1,0:T(8,128)(2,1)}, bf16[1024,512]{1,0:T(8,128)(2,1)}, bf...) conditional(s32[]{:T(128)} %convert_element_type.2, ...), branch_computations={%region_4.5_spmd, %region_5.6_spmd} | conditional | bytes 18875168 | solution.py:1110
  94.3 16.7 %tail_back.5 = (bf16[1024,512]{1,0:T(8,128)(2,1)}, bf16[1024,2048]{1,0:T(8,128)(2,1)}, f32[1024,512]{1,0:T(8,128)}, bf16[1024,512]{1,0:T(8,128)(2,1)}, bf16[1024...) custom-call(s32[1]{0:T(128)} %get-tuple-element.527.side, f32[2,1024,512]{2,1,0:T(8,128)} %get-tuple-element.528.result, ...), custom_call_target="tpu_custom_call" | custom-call | tf_op jit(solution)/shard_map/cond/branch_1_fun/tail_back/pallas_call | solution.py:912
  111.1 18.0 %attend_back.5 = (bf16[1024,512]{1,0:T(8,128)(2,1)}, bf16[1024,512]{1,0:T(8,128)(2,1)}, bf16[1024,512]{1,0:T(8,128)(2,1)}) custom-call(s32[16]{0:T(128)S(1)} %get-tuple-element.546.windows, bf16[1024,512]{1,0:T(8,128)(2,1)S(1)} %copy-done.22, bf16[1024,512]{1,0:T(8,128)(2,1)} %get-tuple-element.548.marks, bf16[1024,512]{1,0:T(8,128)(2,1)} %get-tuple-element.549.key, ...), custom_call_target="tpu_custom_call" | custom-call | tf_op jit(solution)/shard_map/cond/branch_1_fun/attend_back/pallas_call | solution.py:932
  129.1 6.4 entry_back.5
  135.5 34.5 %conditional.6 = (bf16[1024,512]{1,0:T(8,128)(2,1)}, bf16[1024,2048]{1,0:T(8,128)(2,1)}, bf16[1024,512]{1,0:T(8,128)(2,1)}, bf16[1024,512]{1,0:T(8,128)(2,1)}, b...) conditional(s32[]{:T(128)} %convert_element_type.2, ...), branch_computations={%region_6.7_spmd, %region_7.8_spmd} | conditional | bytes 19398960 | solution.py:1121
  142.7 17.5 %weight_grads.4 = f32[6144,512]{1,0:T(8,128)} custom-call(bf16[1024,2048]{1,0:T(8,128)(2,1)} %get-tuple-element.621.refs_0_, bf16[1024,512]{1,0:T(8,128)(2,1)} %get-tuple-element.622.refs_1_, bf16[1024,512]{1,0:T(8,128)(2,1)} %get-tuple-element.623.refs_2_, bf16[1024,2048]{1,0:T(8,128)(2,1)} %get-tuple-element.624.refs_3_, ...), custom_call_target="tpu_custom_call" | custom-call | tf_op jit(solution)/shard_map/cond/branch_1_fun/weight_grads/pallas_call | solution.py:511
  160.2 9.8 %scatter_codes.1 = f32[512,512]{1,0:T(8,128)} custom-call(s32[2048]{0:T(1024)S(1)} %get-tuple-element.631.index, f32[2048,32]{1,0:T(8,128)S(1)} %get-tuple-element.632.unit, f32[1024,32]{1,0:T(8,128)S(1)} %copy-done.37, f32[1024,32]{1,0:T(8,128)S(1)} %copy-done.38, f32[32,8192]{1,0:T(8,128)S(1)} %copy-done.33), custom_call_target="tpu_custom_call" | custom-call | tf_op jit(solution)/shard_map/cond/branch_1_fun/scatter_codes/pallas_call | solution.py:152
  170.0 1.3 collective-permute-start.1
  171.3 10.7 %collective-permute-done.1 = f32[32,1024]{1,0:T(8,128)S(1)} collective-permute-done((f32[32,1024]{1,0:T(8,128)}, f32[32,1024]{1,0:T(8,128)S(1)}, u32[]{:S(2)}, u32[]{:S(2)}) %collective-permute-start.1) | collective-permute-done | bytes 131104 | tf_op jit(solution)/shard_map/ppermute | solution.py:1123
  182.0 69.7 %conditional.7 = (f32[6144,512]{1,0:T(8,128)}, f32[16,512]{1,0:T(8,128)}, f32[16,512]{1,0:T(8,128)S(1)}, f32[32,512]{1,0:T(8,128)}, f32[32,512]{1,0:T(8,128)S(1)}, /*index=5*/f32[2,1024,512]{2,1,0:T(8,128)}) conditional(s32[]{:T(128)} %convert_element_type.2, (bf16[1024,2048]{1,0:T(8,128)(2,1)}, bf16[1024,512]{1,0:T(8,128)(2,1)}, ...), branch_computations={%region_8.9_spmd, %region_9.10_spmd} | conditional | bytes 44433680 | solution.py:1135
  182.2 16.7 %tail_back.7 = (bf16[1024,512]{1,0:T(8,128)(2,1)}, bf16[1024,2048]{1,0:T(8,128)(2,1)}, f32[1024,512]{1,0:T(8,128)}, bf16[1024,512]{1,0:T(8,128)(2,1)}, bf16[1024...) custom-call(s32[1]{0:T(128)} %get-tuple-element.662.side.refs_0_, ...), custom_call_target="tpu_custom_call" | custom-call | tf_op jit(solution)/shard_map/cond/branch_1_fun/tail_back/pallas_call | solution.py:912
  199.0 23.2 %attend_back.7 = (bf16[1024,512]{1,0:T(8,128)(2,1)}, bf16[1024,512]{1,0:T(8,128)(2,1)}, bf16[1024,512]{1,0:T(8,128)(2,1)}) custom-call(s32[16]{0:T(128)S(1)} %get-tuple-element.686.windows, bf16[1024,512]{1,0:T(8,128)(2,1)S(1)} %copy-done.32, bf16[1024,512]{1,0:T(8,128)(2,1)} %get-tuple-element.688.marks, bf16[1024,512]{1,0:T(8,128)(2,1)} %get-tuple-element.689.key, ...), custom_call_target="tpu_custom_call" | custom-call | tf_op jit(solution)/shard_map/cond/branch_1_fun/attend_back/pallas_call | solution.py:932
  222.3 6.4 entry_back.7
  228.6 20.9 %weight_grads.7 = f32[6144,512]{1,0:T(8,128)} custom-call(bf16[1024,2048]{1,0:T(8,128)(2,1)} %get-tuple-element.661.refs_0_, bf16[1024,512]{1,0:T(8,128)(2,1)} %get-tuple-element.680.refs_1_, bf16[1024,512]{1,0:T(8,128)(2,1)} %get-tuple-element.681.refs_2_, bf16[1024,2048]{1,0:T(8,128)(2,1)} %get-tuple-element.682.refs_3_, ...), custom_call_target="tpu_custom_call", output_to_operand_aliasing={{}: (10, {})} | custom-call | tf_op jit(solution)/shard_map/cond/branch_1_fun/weight_grads/pallas_call | solution.py:511
  249.5 2.0 copy.186
  251.8 2.6 gather_head.1.misc
  254.3 1.4 copy-done
  255.8 158.0 %sum_over_dp.1 = (f32[6144,512]{1,0:T(8,128)}, f32[768,512]{1,0:T(8,128)S(1)}) custom-call(f32[6144,512]{1,0:T(8,128)} %get-tuple-element.884.main, f32[768,512]{1,0:T(8,128)S(1)} %copy-done), custom_call_target="tpu_custom_call" | custom-call | tf_op jit(solution)/shard_map/sum_over_dp/pallas_call | solution.py:799
  413.8 0.6 slice_bitcast_fusion.2
  414.4 0.6 fusion.1
  415.0 0.7 fusion
  415.7 0.6 copy.50
  416.3 0.6 copy.45
  416.9 414.3 %unpack.1 = (f32[2048,512]{1,0:T(8,128)}, f32[512,2048]{1,0:T(8,128)}, f32[512,512]{1,0:T(8,128)}, f32[512,1536]{1,0:T(8,128)}, f32[32,8192]{1,0:T(8,128)}) custom-call(f32[6144,512]{1,0:T(8,128)} %get-tuple-element.890.main, f32[768,512]{1,0:T(8,128)} %copy-done.1), custom_call_target="tpu_custom_call" | custom-call | tf_op jit(solution)/shard_map/unpack/pallas_call | solution.py:782
  831.2 0.6 pad_maximum_fusion
  831.8 0.6 maximum_bitcast_fusion
  (64 shorter events, 0.2 us)
Async XLA Ops:
  11.0 31.8 %copy-start.11 = (bf16[2048,128]{1,0:T(8,128)(2,1)}, bf16[2048,128]{1,0:T(8,128)(2,1)S(1)}, u32[]{:S(2)}) copy-start(bf16[2048,128]{1,0:T(8,128)(2,1)S(1)} %get-tuple-element.810.wide) | copy-start | bytes 1572868
  11.0 17.1 %copy-start.2 = (bf16[1,2,1024,512]{3,2,1,0:T(8,128)(2,1)S(1)}, bf16[1,2,1024,512]{3,2,1,0:T(8,128)(2,1)}, u32[]{:S(2)}) copy-start(bf16[1,2,1024,512]{3,2,1,0:T(8,128)(2,1)} %param.24) | copy-start | bytes 6291460
  11.1 17.1 %copy-start.3 = (bf16[1,512,2048]{2,1,0:T(8,128)(2,1)S(1)}, bf16[1,512,2048]{2,1,0:T(8,128)(2,1)}, u32[]{:S(2)}) copy-start(bf16[1,512,2048]{2,1,0:T(8,128)(2,1)} %param.29) | copy-start | bytes 6291460
  11.1 17.1 %copy-start.5 = (bf16[1,2048,512]{2,1,0:T(8,128)(2,1)S(1)}, bf16[1,2048,512]{2,1,0:T(8,128)(2,1)}, u32[]{:S(2)}) copy-start(bf16[1,2048,512]{2,1,0:T(8,128)(2,1)} %param.30) | copy-start | bytes 6291460
  11.1 17.1 %copy-start.25 = (f32[32,512]{1,0:T(8,128)S(1)}, f32[32,512]{1,0:T(8,128)}, u32[]{:S(2)}) copy-start(f32[32,512]{1,0:T(8,128)} %up.3) | copy-start | bytes 196612
  11.1 17.1 %copy-start.34 = (f32[512,32]{0,1:T(8,128)S(1)}, f32[512,32]{0,1:T(8,128)}, u32[]{:S(2)}) copy-start(f32[512,32]{0,1:T(8,128)} %param.36) | copy-start | bytes 196612
  11.1 17.1 %copy-start.35 = (f32[2,512]{1,0:T(2,128)S(1)}, f32[2,512]{1,0:T(2,128)}, u32[]{:S(2)}) copy-start(f32[2,512]{1,0:T(2,128)} %head_bias.3) | copy-start | bytes 12292
  11.1 17.1 %copy-start.36 = (f32[1,2,512]{2,1,0:T(2,128)S(1)}, f32[1,2,512]{2,1,0:T(2,128)}, u32[]{:S(2)}) copy-start(f32[1,2,512]{2,1,0:T(2,128)} %param.31) | copy-start | bytes 12292
  11.1 17.1 %copy-start.39 = (f32[512]{0:T(512)S(1)}, f32[512]{0:T(512)}, u32[]{:S(2)}) copy-start(f32[512]{0:T(512)} %param.34) | copy-start | bytes 6148
  11.1 17.1 %copy-start.40 = (f32[1,2048]{1,0:T(1,128)S(1)}, f32[1,2048]{1,0:T(1,128)}, u32[]{:S(2)}) copy-start(f32[1,2048]{1,0:T(1,128)} %hidden_bias.1) | copy-start | bytes 24580
  11.1 17.1 %copy-start.45 = (f32[32]{0:T(128)S(1)}, f32[32]{0:T(128)}, u32[]{:S(2)}) copy-start(f32[32]{0:T(128)} %param.37) | copy-start | bytes 388
  87.1 7.1 collective-permute-start
  94.3 16.8 %copy-start.16 = (bf16[1024,512]{1,0:T(8,128)(2,1)S(1)}, bf16[1024,512]{1,0:T(8,128)(2,1)}, u32[]{:S(2)}) copy-start(bf16[1024,512]{1,0:T(8,128)(2,1)} %get-tuple-element.552.context) | copy-start | bytes 3145732 | tf_op jit(solution)/shard_map/cond
  94.3 16.8 %copy-start.17 = (bf16[2,1024,128]{2,1,0:T(8,128)(2,1)S(1)}, bf16[2,1024,128]{2,1,0:T(8,128)(2,1)}, u32[]{:S(2)}) copy-start(bf16[2,1024,128]{2,1,0:T(8,128)(2,1)} %get-tuple-element.553.key_mark) | copy-start | bytes 1572868 | tf_op jit(solution)/shard_map/cond
  94.3 16.8 %copy-start.22 = (bf16[1024,512]{1,0:T(8,128)(2,1)S(1)}, bf16[1024,512]{1,0:T(8,128)(2,1)}, u32[]{:S(2)}) copy-start(bf16[1024,512]{1,0:T(8,128)(2,1)} %get-tuple-element.547.query) | copy-start | bytes 3145732 | tf_op jit(solution)/shard_map/cond
  111.0 18.1 %copy-start.8 = (bf16[512,1536]{1,0:T(8,128)(2,1)S(1)}, bf16[512,1536]{1,0:T(8,128)(2,1)}, u32[]{:S(2)}) copy-start(bf16[512,1536]{1,0:T(8,128)(2,1)} %get-tuple-element.559.weight) | copy-start | bytes 4718596 | tf_op jit(solution)/shard_map/cond
  111.0 18.1 %copy-start.13 = (bf16[2048,128]{1,0:T(8,128)(2,1)S(1)}, bf16[2048,128]{1,0:T(8,128)(2,1)}, u32[]{:S(2)}) copy-start(bf16[2048,128]{1,0:T(8,128)(2,1)} %get-tuple-element.557.wide) | copy-start | bytes 1572868 | tf_op jit(solution)/shard_map/cond
  142.7 17.5 %copy-start.33 = (f32[32,8192]{1,0:T(8,128)S(1)}, f32[32,8192]{1,0:T(8,128)}, u32[]{:S(2)}) copy-start(f32[32,8192]{1,0:T(8,128)} %get-tuple-element.635.table_turned) | copy-start | bytes 3145732 | tf_op jit(solution)/shard_map/cond
  142.7 17.5 %copy-start.37 = (f32[1024,32]{1,0:T(8,128)S(1)}, f32[1024,32]{1,0:T(8,128)}, u32[]{:S(2)}) copy-start(f32[1024,32]{1,0:T(8,128)} %get-tuple-element.633.latent_first) | copy-start | bytes 393220 | tf_op jit(solution)/shard_map/cond
  142.7 17.5 %copy-start.38 = (f32[1024,32]{1,0:T(8,128)S(1)}, f32[1024,32]{1,0:T(8,128)}, u32[]{:S(2)}) copy-start(f32[1024,32]{1,0:T(8,128)} %get-tuple-element.634.latent_second) | copy-start | bytes 393220 | tf_op jit(solution)/shard_map/cond
  170.0 12.0 %collective-permute-start.1 = (f32[32,1024]{1,0:T(8,128)}, f32[32,1024]{1,0:T(8,128)S(1)}, u32[]{:S(2)}, u32[]{:S(2)}) collective-permute-start(f32[32,1024]{1,0:T(8,128)} %get-tuple-element.866), channel_id=1, source_target_pairs={{16,0},{17,1},{18,2},{19,3},{20,4},{21,5},{22,6},{23,7},{24,8},{25... | collective-permute-start | bytes 393224 | tf_op jit(solution)/shard_map/ppermute | solution.py:1123
  182.2 16.8 %copy-start.19 = (bf16[2,1024,128]{2,1,0:T(8,128)(2,1)S(1)}, bf16[2,1024,128]{2,1,0:T(8,128)(2,1)}, u32[]{:S(2)}) copy-start(bf16[2,1024,128]{2,1,0:T(8,128)(2,1)} %get-tuple-element.692.key_mark) | copy-start | bytes 1572868 | tf_op jit(solution)/shard_map/cond
  182.2 16.8 %copy-start.21 = (bf16[1024,512]{1,0:T(8,128)(2,1)S(1)}, bf16[1024,512]{1,0:T(8,128)(2,1)}, u32[]{:S(2)}) copy-start(bf16[1024,512]{1,0:T(8,128)(2,1)} %get-tuple-element.683.context.refs_4_) | copy-start | bytes 3145732 | tf_op jit(solution)/shard_map/cond
  182.2 16.8 %copy-start.32 = (bf16[1024,512]{1,0:T(8,128)(2,1)S(1)}, bf16[1024,512]{1,0:T(8,128)(2,1)}, u32[]{:S(2)}) copy-start(bf16[1024,512]{1,0:T(8,128)(2,1)} %get-tuple-element.687.query) | copy-start | bytes 3145732 | tf_op jit(solution)/shard_map/cond
  198.9 23.3 %copy-start.10 = (bf16[512,1536]{1,0:T(8,128)(2,1)S(1)}, bf16[512,1536]{1,0:T(8,128)(2,1)}, u32[]{:S(2)}) copy-start(bf16[512,1536]{1,0:T(8,128)(2,1)} %get-tuple-element.700.refs_9_) | copy-start | bytes 4718596 | tf_op jit(solution)/shard_map/cond
  198.9 23.3 %copy-start.15 = (bf16[2048,128]{1,0:T(8,128)(2,1)S(1)}, bf16[2048,128]{1,0:T(8,128)(2,1)}, u32[]{:S(2)}) copy-start(bf16[2048,128]{1,0:T(8,128)(2,1)} %get-tuple-element.698.refs_2_) | copy-start | bytes 1572868 | tf_op jit(solution)/shard_map/cond
  199.0 23.3 %copy-start.42 = (f32[32,512]{1,0:T(8,128)S(1)}, f32[32,512]{1,0:T(8,128)}, u32[]{:S(2)}) copy-start(f32[32,512]{1,0:T(8,128)} %get-tuple-element.703.refs_14_) | copy-start | bytes 196612 | tf_op jit(solution)/shard_map/cond
  199.0 23.3 %copy-start.44 = (f32[16,512]{1,0:T(8,128)S(1)}, f32[16,512]{1,0:T(8,128)}, u32[]{:S(2)}) copy-start(f32[16,512]{1,0:T(8,128)} %get-tuple-element.702.refs_13_) | copy-start | bytes 98308 | tf_op jit(solution)/shard_map/cond
  228.6 20.9 %copy-start.20 = (f32[2,1024,512]{2,1,0:T(8,128)S(1)}, f32[2,1024,512]{2,1,0:T(8,128)}, u32[]{:S(2)}) copy-start(f32[2,1024,512]{2,1,0:T(8,128)} %get-tuple-element.1085) | copy-start | bytes 12582916 | tf_op jit(solution)/shard_map/cond
  254.3 1.4 copy-start
  413.8 3.1 copy-start.1

commit v4 on v3

--- a/solution.py
+++ b/solution.py
@@ -356,21 +356,14 @@
     context_grad[...] = dot(branch, weight_out[...], NT).astype(BF)
 
 
-def attend_back_kernel(
-    windows, query, marks, key, value, context_grad, context, key_mark,
-    query_grad, key_grad, value_grad, grad_mark, key_total, value_total, *, row
-):
-    count = query.shape[0]
-    size = TOKENS
-    pairs = query.shape[1] // 128
-    low_all = lanes((count, 128)) < 64
-    low_query = lanes((size, 128)) < 64
+def mark_grads(context_grad, context, grad_mark):
+    count = context_grad.shape[0]
     lane_all = lanes((count, 128)) & 63
     across = (
         lax.broadcasted_iota(jnp.int32, (128, 128), 0) // 64 != lanes((128, 128)) // 64
     ).astype(BF)
     zero = jnp.zeros((count, 128), BF)
-    for pair in range(pairs):
+    for pair in range(context_grad.shape[1] // 128):
         here = slice(pair * 128, pair * 128 + 128)
         product = split(context_grad[:, here].astype(F32) * context[:, here].astype(F32))
         level = -(dot(product[0], across, NN) + dot(product[1], across, NN))
@@ -379,47 +372,71 @@
         grad_mark[:, here] = merge(
             lane_all == 0, first, merge(lane_all == 1, second, merge(lane_all == 2, third, zero))
         )
+
+
+def attend_back_block(
+    number, start, extent, base, pairs,
+    query, marks, key, value, context_grad, key_mark, grad_mark, query_grad, key_total, value_total,
+):
+    size = TOKENS
+    low_query = lanes((size, 128)) < 64
+    rows = pl.ds(pl.multiple_of(number * size, size), size)
+    keys = pl.ds(pl.multiple_of(start, WINDOW), extent)
+    low_key = lanes((extent, 128)) < 64
+    key_aug = key_mark[keys, :]
+    ones = jnp.where((lanes((extent, 128)) & 63) < 3, 1.0, 0.0).astype(BF)
+    none = jnp.zeros((extent, 128), BF)
+    for pair in range(pairs):
+        here = pl.ds(pl.multiple_of(base + pair * 128, 128), 128)
+        query_pair, key_pair, value_pair = query[rows, here], key[keys, here], value[keys, here]
+        grad_pair, query_aug, grad_aug = context_grad[rows, here], marks[rows, here], grad_mark[rows, here]
+        found = []
+        for swap in (False, True):
+
+            def both(low, left, right):
+                return merge(low, right, left) if swap else merge(low, left, right)
+
+            scores = dot(both(low_key, key_pair, key_aug), both(low_query, query_pair, query_aug), NT)
+            rise = dot(both(low_key, value_pair, ones), both(low_query, grad_pair, grad_aug), NT)
+            chance = jnp.exp2(scores)
+            score_grad = (chance * rise).astype(BF)
+            found.append(
+                (
+                    dot(score_grad, query_pair, NN),
+                    dot(chance.astype(BF), grad_pair, NN),
+                    dot(score_grad, both(low_key, key_pair, none), TN),
+                )
+            )
+        key_total[keys, here] += merge(low_key, found[0][0], found[1][0])
+        value_total[keys, here] += merge(low_key, found[0][1], found[1][1])
+        query_grad[rows, here] = ((found[0][2] + found[1][2]) * HEAD ** (-0.5)).astype(BF)
+
+
+def attend_back_kernel(
+    windows, query, marks, key, value, context_grad, context, key_mark,
+    query_grad, key_grad, value_grad, grad_mark, key_total, value_total, *, row
+):
+    count = query.shape[0]
+    steps = count // TOKENS
+    pairs = query.shape[1] // 128
+    mark_grads(context_grad, context, grad_mark)
     key_total[...] = jnp.zeros_like(key_total)
     value_total[...] = jnp.zeros_like(value_total)
 
-    def block(number, start, extent):
-        rows = pl.ds(pl.multiple_of(number * size, size), size)
-        keys = pl.ds(pl.multiple_of(start, WINDOW), extent)
-        low_key = lanes((extent, 128)) < 64
-        key_aug = key_mark[keys, :]
-        ones = jnp.where((lanes((extent, 128)) & 63) < 3, 1.0, 0.0).astype(BF)
-        none = jnp.zeros((extent, 128), BF)
-        for pair in range(pairs):
-            here = slice(pair * 128, pair * 128 + 128)
-            query_pair, key_pair, value_pair = query[rows, here], key[keys, here], value[keys, here]
-            grad_pair, query_aug, grad_aug = context_grad[rows, here], marks[rows, here], grad_mark[rows, here]
-            found = []
-            for swap in (False, True):
-
-                def both(low, left, right):
-                    return merge(low, right, left) if swap else merge(low, left, right)
-
-                scores = dot(both(low_key, key_pair, key_aug), both(low_query, query_pair, query_aug), NT)
-                rise = dot(both(low_key, value_pair, ones), both(low_query, grad_pair, grad_aug), NT)
-                chance = jnp.exp2(scores)
-                score_grad = (chance * rise).astype(BF)
-                found.append(
-                    (
-                        dot(score_grad, query_pair, NN),
-                        dot(chance.astype(BF), grad_pair, NN),
-                        dot(score_grad, both(low_key, key_pair, none), TN),
-                    )
-                )
-            key_total[keys, here] += merge(low_key, found[0][0], found[1][0])
-            value_total[keys, here] += merge(low_key, found[0][1], found[1][1])
-            query_grad[rows, here] = ((found[0][2] + found[1][2]) * HEAD ** (-0.5)).astype(BF)
-
-    def one(number, carry):
-        base = (row * (count // size) + number) * 2
-        for_windows(windows[base], windows[base + 1], count, functools.partial(block, number))
+    def one(turn, carry):
+        number, pair = turn // pairs, turn % pairs
+        at = (row * steps + number) * 2
+
+        def run(start, extent):
+            attend_back_block(
+                number, start, extent, pair * 128, 1,
+                query, marks, key, value, context_grad, key_mark, grad_mark, query_grad, key_total, value_total,
+            )
+
+        for_windows(windows[at], windows[at + 1], count, run)
         return carry
 
-    lax.fori_loop(0, count // size, one, 0)
+    lax.fori_loop(0, steps * pairs, one, 0)
     key_grad[...] = (key_total[...] * (1.0 / LOG2E)).astype(BF)
     value_grad[...] = value_total[...].astype(BF)
 
@@ -460,67 +477,90 @@
         head_weight[...] += dot3(split(unit[...]), split(total), TN)
 
 
-def weight_kernel(*refs, turns, adding):
-    operands, out = refs[:10], refs[-1]
-    active, out_low, n2, preact_low, context, branch_low, n1 = operands[:7]
+def hidden_weight_kernel(active, out_low, n2, preact_low, *refs):
+    out = refs[-1]
+    before = refs[0] if len(refs) > 1 else None
     step = pl.program_id(0)
-    first, second, third = turns
-
-    def put(left, right):
-        value = dot(left[...], right[...], TN)
-        out[...] = value + refs[10][...] if adding else value
+    first = pl.num_programs(0) // 2
+    width = n2.shape[1]
+
+    def put(value, rows):
+        out[rows, :] = value if before is None else value + before[rows, :]
 
     @pl.when(step < first)
     def _():
-        put(active, out_low)
-
-    @pl.when((step >= first) & (step < second))
-    def _():
-        put(n2, preact_low)
-
-    @pl.when((step >= second) & (step < third))
-    def _():
-        put(context, branch_low)
-
-    for place in range(3):
-
-        @pl.when(step == third + place)
-        def _():
-            put(n1, operands[7 + place])
-
-
-def weight_grads(kept, back, before=None):
-    active, n2, context, n1 = kept["active"], kept["n2"], kept["context"], kept["n1"]
-    out_low, preact_low, branch_low = back["out_low"], back["preact_low"], back["branch_low"]
-    count, width = n1.shape
-    first = active.shape[1] // width
-    second = 2 * first
-    third = second + 1
-    whole = lambda step: (0, 0)
-    full = pl.BlockSpec((count, width), whole)
-    in_specs = [full] * 10
-    in_specs[0] = pl.BlockSpec((count, width), lambda step: (0, jnp.minimum(step, first - 1)))
-    in_specs[3] = pl.BlockSpec((count, width), lambda step: (0, jnp.clip(step - first, 0, first - 1)))
-    out_spec = pl.BlockSpec((width, width), lambda step: (step, 0))
-    operands = [active, out_low, n2, preact_low, context, branch_low, n1]
-    operands += [back["query_grad"], back["key_grad"], back["value_grad"]]
-    adding = before is not None
-    if adding:
-        operands.append(before)
-        in_specs.append(out_spec)
+        put(dot(active[...], out_low[...], TN), slice(0, 2 * width))
+
+    @pl.when(step >= first)
+    def _():
+        value = dot(n2[...], preact_low[...], TN)
+        put(value[:, :width], slice(0, width))
+        put(value[:, width:], slice(width, 2 * width))
+
+
+def attention_weight_kernel(context, branch_low, n1, query_grad, key_grad, value_grad, *refs):
+    out = refs[-1]
+    before = refs[0] if len(refs) > 1 else None
+    step = pl.program_id(0)
+    width = n1.shape[1]
+
+    def put(value, number):
+        rows = slice(number * width, (number + 1) * width)
+        out[rows, :] = value if before is None else value + before[rows, :]
+
+    @pl.when(step == 0)
+    def _():
+        put(dot(context[...], branch_low[...], TN), 0)
+        put(dot(n1[...], query_grad[...], TN), 1)
+
+    @pl.when(step == 1)
+    def _():
+        put(dot(n1[...], key_grad[...], TN), 0)
+        put(dot(n1[...], value_grad[...], TN), 1)
+
+
+def weight_call(kernel, operands, in_specs, steps, before, name):
+    width = operands[1].shape[1]
+    out_spec = pl.BlockSpec((2 * width, width), lambda step: (step, 0))
+    aliases = {}
+    if before is not None:
+        aliases = {len(operands): 0}
+        operands, in_specs = operands + [before], in_specs + [out_spec]
     return pl.pallas_call(
-        functools.partial(weight_kernel, turns=(first, second, third), adding=adding),
-        grid=(third + 3,),
+        kernel,
+        grid=(steps,),
         in_specs=in_specs,
         out_specs=out_spec,
-        out_shape=jax.ShapeDtypeStruct(((third + 3) * width, width), F32),
-        input_output_aliases={10: 0} if adding else {},
+        out_shape=jax.ShapeDtypeStruct((2 * steps * width, width), F32),
+        input_output_aliases=aliases,
         compiler_params=PARAMS,
-        name="weight_grads",
+        name=name,
     )(*operands)
 
 
+def hidden_weights(kept, back, before=None):
+    operands = [kept["active"], back["out_low"], kept["n2"], back["preact_low"]]
+    count, width = kept["n2"].shape
+    first = kept["active"].shape[1] // (2 * width)
+    full = pl.BlockSpec((count, width), lambda step: (0, 0))
+    in_specs = [
+        pl.BlockSpec((count, 2 * width), lambda step: (0, jnp.minimum(step, first - 1))),
+        full,
+        full,
+        pl.BlockSpec((count, 2 * width), lambda step: (0, jnp.maximum(step - first, 0))),
+    ]
+    return weight_call(hidden_weight_kernel, operands, in_specs, 2 * first, before, "hidden_weights")
+
+
+def attention_weights(kept, back, before=None):
+    operands = [kept["context"], back["branch_low"], kept["n1"]]
+    operands += [back["query_grad"], back["key_grad"], back["value_grad"]]
+    full = pl.BlockSpec(kept["n1"].shape, lambda step: (0, 0))
+    return weight_call(attention_weight_kernel, operands, [full] * 6, 2, before, "attention_weights")
+
+
 MESH = pl.DeviceIdType.MESH
+LEAST_DEVICES = 4
 
 
 def ring_chip(position, chips):
@@ -528,290 +568,501 @@
     return (1 - odd) * (2 * position) + odd * (2 * (chips - 1 - position) + 1)
 
 
-def sum_kernel(
-    chips, main, misc, main_out, misc_out,
-    own_main, own_misc, pair_main, pair_misc, run_main, run_misc, far_misc,
-    load_sems, pair_send, pair_recv, run_send, run_recv, far_send, far_recv,
-    keep_sems, spread_send, spread_recv, side_send, side_recv,
+class Ring:
+    @staticmethod
+    def scratch(arrays, ways, crossing):
+        chips = lax.axis_size("dp") // 2
+        sizes = [array.shape[0] // (2 * count * chips) for array, count in zip(arrays, ways)]
+        shapes = [(count, chips, size, array.shape[1]) for array, count, size in zip(arrays, ways, sizes)]
+        buffers = [pltpu.VMEM(shape, F32) for shape in shapes] * 3
+        sems = [pltpu.SemaphoreType.DMA(shape[:2]) for shape in shapes] * 10
+        far = []
+        if crossing is not None:
+            count, unused, size, width = shapes[crossing]
+            far = [pltpu.VMEM((count, size, width), F32)] + [pltpu.SemaphoreType.DMA((count,))] * 2
+        return buffers + sems + far
+
+    def __init__(self, sources, results, ways, crossing, scratch):
+        number = len(sources)
+        take = lambda at: scratch[at * number : (at + 1) * number]
+        self.chips = lax.axis_size("dp") // 2
+        self.sources, self.results, self.ways, self.crossing = sources, results, ways, crossing
+        self.own, self.pair, self.run = take(0), take(1), take(2)
+        (
+            self.load_sems, self.pair_send, self.pair_recv, self.run_send, self.run_recv,
+            self.keep_sems, self.spread_send, self.spread_recv, self.side_send, self.side_recv,
+        ) = (take(at) for at in range(3, 13))
+        self.far = scratch[13 * number :]
+        self.sizes = [run.shape[2] for run in self.run]
+        self.lanes = [(which, way) for way in range(max(ways)) for which in range(number) if way < ways[which]]
+        place = lax.axis_index("dp")
+        chip, self.core = place // 2, place % 2
+        column, odd = chip // 2, chip % 2
+        chips = self.chips
+        self.position = (1 - odd) * column + odd * (chips - 1 - column)
+        self.other = {"dp": chip * 2 + (1 - self.core)}
+        self.across = {"section": 1 - lax.axis_index("section")}
+        self.targets = (
+            {"dp": ring_chip((self.position + 1) % chips, chips) * 2 + self.core},
+            {"dp": ring_chip((self.position + chips - 1) % chips, chips) * 2 + self.core},
+        )
+
+    def greet(self):
+        self.barrier = pltpu.get_barrier_semaphore()
+        devices = (self.other,) + self.targets + (() if self.crossing is None else (self.across,))
+        for device in devices:
+            pl.semaphore_signal(self.barrier, inc=1, device_id=device, device_id_type=MESH)
+        self.greeted = len(devices)
+
+    def piece(self, step, way):
+        return (self.position + (2 * self.chips - step if way % 2 == 0 else step)) % self.chips
+
+    def rows(self, which, half, way, number):
+        size = self.sizes[which]
+        return pl.ds(pl.multiple_of(((half * self.ways[which] + way) * self.chips + number) * size, 8), size)
+
+    def final(self, which, half, way, step):
+        return self.results[which].at[self.rows(which, half, way, self.piece(step + self.chips - 1, way))]
+
+    def load(self, which, way, step):
+        return pltpu.make_async_copy(
+            self.sources[which].at[self.rows(which, self.core, way, self.piece(step, way))],
+            self.own[which].at[way, step],
+            self.load_sems[which].at[way, step],
+        )
+
+    def remote(self, source, target, send, recv, device):
+        return pltpu.make_async_remote_copy(
+            src_ref=source, dst_ref=target, send_sem=send, recv_sem=recv, device_id=device, device_id_type=MESH
+        )
+
+    def swap(self, which, way, step):
+        return self.remote(
+            self.sources[which].at[self.rows(which, 1 - self.core, way, self.piece(step, way))],
+            self.pair[which].at[way, step],
+            self.pair_send[which].at[way, step],
+            self.pair_recv[which].at[way, step],
+            self.other,
+        )
+
+    def pass_on(self, which, way, step):
+        return self.remote(
+            self.run[which].at[way, step],
+            self.run[which].at[way, step + 1],
+            self.run_send[which].at[way, step],
+            self.run_recv[which].at[way, step + 1],
+            self.targets[way % 2],
+        )
+
+    def cross(self, way):
+        return self.remote(
+            self.run[self.crossing].at[way, self.chips - 1],
+            self.far[0].at[way],
+            self.far[1].at[way],
+            self.far[2].at[way],
+            self.across,
+        )
+
+    def keep(self, which, way):
+        return pltpu.make_async_copy(
+            self.run[which].at[way, self.chips - 1], self.final(which, self.core, way, 0), self.keep_sems[which].at[way, 0]
+        )
+
+    def spread(self, which, way, step, first=False):
+        here = self.final(which, self.core, way, step)
+        return self.remote(
+            self.run[which].at[way, self.chips - 1] if first else here,
+            here,
+            self.spread_send[which].at[way, step],
+            self.spread_recv[which].at[way, step],
+            self.targets[way % 2],
+        )
+
+    def incoming(self, which, way, step):
+        here = self.final(which, self.core, way, step)
+        return self.remote(
+            here, here, self.spread_send[which].at[way, step], self.spread_recv[which].at[way, step - 1],
+            self.targets[way % 2],
+        )
+
+    def aside(self, which, way, step, first=False):
+        here = self.final(which, self.core, way, step)
+        return self.remote(
+            self.run[which].at[way, self.chips - 1] if first else here,
+            here,
+            self.side_send[which].at[way, step],
+            self.side_recv[which].at[way, step],
+            self.other,
+        )
+
+    def beside(self, which, way, step):
+        here = self.final(which, 1 - self.core, way, step)
+        return self.remote(
+            here, here, self.side_send[which].at[way, step], self.side_recv[which].at[way, step], self.other
+        )
+
+    def begin(self):
+        def load(step, carry):
+            for which, way in self.lanes:
+                self.load(which, way, step).start()
+            return carry
+
+        def swap(step, carry):
+            for which, way in self.lanes:
+                self.swap(which, way, step).start()
+            return carry
+
+        lax.fori_loop(0, self.chips, load, 0)
+        pl.semaphore_wait(self.barrier, self.greeted)
+        lax.fori_loop(0, self.chips, swap, 0)
+        for which, way in self.lanes:
+            self.load(which, way, 0).wait()
+            self.swap(which, way, 0).wait_recv()
+            self.run[which][way, 0] = self.own[which][way, 0] + self.pair[which][way, 0]
+            self.pass_on(which, way, 0).start()
+
+    def gather(self, step):
+        for which, way in self.lanes:
+            run, own, pair = self.run[which], self.own[which], self.pair[which]
+            self.load(which, way, step).wait()
+            self.swap(which, way, step).wait_recv()
+            self.pass_on(which, way, step - 1).wait_recv()
+            run[way, step] = run[way, step] + own[way, step] + pair[way, step]
+
+            @pl.when(step < self.chips - 1)
+            def _():
+                self.pass_on(which, way, step).start()
+
+    def turn(self):
+        for which, way in self.lanes:
+            if which == self.crossing:
+                self.cross(way).start()
+        for which, way in self.lanes:
+            if which != self.crossing:
+                self.hand_out(which, way)
+        for which, way in self.lanes:
+            if which == self.crossing:
+                run = self.run[which]
+                self.cross(way).wait()
+                run[way, self.chips - 1] = run[way, self.chips - 1] + self.far[0][way]
+                self.hand_out(which, way)
+
+    def hand_out(self, which, way):
+        self.spread(which, way, 0, True).start()
+        self.aside(which, way, 0, True).start()
+        self.keep(which, way).start()
+
+    def pass_out(self, step):
+        for which, way in self.lanes:
+            self.incoming(which, way, step).wait_recv()
+
+            @pl.when(step < self.chips - 1)
+            def _():
+                self.spread(which, way, step).start()
+
+            self.aside(which, way, step).start()
+
+    def finish(self):
+        def one(step, carry):
+            for which, way in self.lanes:
+                self.swap(which, way, step).wait_send()
+                self.beside(which, way, step).wait_recv()
+                self.aside(which, way, step).wait_send()
+
+                @pl.when(step < self.chips - 1)
+                def _():
+                    self.pass_on(which, way, step).wait_send()
+                    self.spread(which, way, step).wait_send()
+
+            return carry
+
+        lax.fori_loop(0, self.chips, one, 0)
+        for which, way in self.lanes:
+            self.keep(which, way).wait()
+
+
+def loop(start, stop, run):
+    def one(step, carry):
+        run(step)
+        return carry
+
+    lax.fori_loop(start, stop, one, 0)
+
+
+SUM_WAYS = (4, 2)
+
+
+def sum_kernel(main, misc, main_out, misc_out, *scratch):
+    ring = Ring((main, misc), (main_out, misc_out), SUM_WAYS, 1, scratch)
+    ring.greet()
+    ring.begin()
+    loop(1, ring.chips, ring.gather)
+    ring.turn()
+    loop(1, ring.chips, ring.pass_out)
+    ring.finish()
+
+
+def sum_all(main, misc):
+    if lax.axis_size("dp") < LEAST_DEVICES:
+        return main, lax.psum(misc, "section")
+    arrays = (main, misc)
+    return pl.pallas_call(
+        sum_kernel,
+        in_specs=[pl.BlockSpec(memory_space=pl.ANY)] * 2,
+        out_specs=[pl.BlockSpec(memory_space=pl.ANY)] * 2,
+        out_shape=tuple(jax.ShapeDtypeStruct(array.shape, F32) for array in arrays),
+        scratch_shapes=Ring.scratch(arrays, SUM_WAYS, 1),
+        compiler_params=pltpu.CompilerParams(collective_id=0, has_side_effects=True, vmem_limit_bytes=40 << 20),
+        name="sum_all",
+    )(*arrays)
+
+
+FINISH_WAYS = (4,)
+
+
+def finish_kernel(
+    hidden, attention, query, marks, key, value, context_grad, context, key_mark, edges, mid_grad, weight, branch_low, n1,
+    gains, book, down, up, late, early,
+    hidden_out, attention_out, misc, entry,
+    query_in, marks_in, key_in, value_in, grad_in, context_in, key_mark_in, edge_in, mid_in, weight_in, branch_in, n1_in,
+    part, grad_mark, query_grad, key_total, value_total, key_grad, value_grad, in_sems, part_sem, out_sems,
+    *scratch,
 ):
-    place = lax.axis_index("dp")
-    section = lax.axis_index("section")
-    chip, core = place // 2, place % 2
-    column, odd = chip // 2, chip % 2
-    position = (1 - odd) * column + odd * (chips - 1 - column)
-    other = {"dp": chip * 2 + (1 - core)}
-    far = {"section": 1 - section}
-    ahead = {"dp": ring_chip((position + 1) % chips, chips) * 2 + core}
-    behind = {"dp": ring_chip((position + chips - 1) % chips, chips) * 2 + core}
-    targets = (ahead, behind)
-    sizes = (main.shape[0] // (4 * chips), misc.shape[0] // (4 * chips))
-    sources, results = (main, misc), (main_out, misc_out)
-    own, pair, run = (own_main, own_misc), (pair_main, pair_misc), (run_main, run_misc)
-
-    barrier = pltpu.get_barrier_semaphore()
-    for device in (other, far, ahead, behind):
-        pl.semaphore_signal(barrier, inc=1, device_id=device, device_id_type=MESH)
-
-    def piece(step, way):
-        return (position + (2 * chips - step if way == 0 else step)) % chips
-
-    def rows(which, half, way, number):
-        size = sizes[which]
-        return pl.ds(pl.multiple_of(((half * 2 + way) * chips + number) * size, 8), size)
-
-    def load(which, way, step):
-        return pltpu.make_async_copy(
-            sources[which].at[rows(which, core, way, piece(step, way))],
-            own[which].at[way, step],
-            load_sems.at[which, way, step],
-        )
-
-    def swap(which, way, step):
-        return pltpu.make_async_remote_copy(
-            src_ref=sources[which].at[rows(which, 1 - core, way, piece(step, way))],
-            dst_ref=pair[which].at[way, step],
-            send_sem=pair_send.at[which, way, step],
-            recv_sem=pair_recv.at[which, way, step],
-            device_id=other,
-            device_id_type=MESH,
-        )
-
-    def pass_on(which, way, step):
-        return pltpu.make_async_remote_copy(
-            src_ref=run[which].at[way, step],
-            dst_ref=run[which].at[way, step + 1],
-            send_sem=run_send.at[which, way, step],
-            recv_sem=run_recv.at[which, way, step + 1],
-            device_id=targets[way],
-            device_id_type=MESH,
-        )
-
-    def cross(way):
-        return pltpu.make_async_remote_copy(
-            src_ref=run_misc.at[way, chips - 1],
-            dst_ref=far_misc.at[way],
-            send_sem=far_send.at[way],
-            recv_sem=far_recv.at[way],
-            device_id=far,
-            device_id_type=MESH,
-        )
-
-    def final_rows(which, way, step):
-        return rows(which, core, way, piece(step + chips - 1, way))
-
-    def keep(which, way):
-        return pltpu.make_async_copy(
-            run[which].at[way, chips - 1], results[which].at[final_rows(which, way, 0)], keep_sems.at[which, way]
-        )
-
-    def spread(which, way, step, first=False):
-        here = results[which].at[final_rows(which, way, step)]
-        return pltpu.make_async_remote_copy(
-            src_ref=run[which].at[way, chips - 1] if first else here,
-            dst_ref=here,
-            send_sem=spread_send.at[which, way, step],
-            recv_sem=spread_recv.at[which, way, step],
-            device_id=targets[way],
-            device_id_type=MESH,
-        )
-
-    def aside(which, way, step, first=False):
-        here = results[which].at[final_rows(which, way, step)]
-        return pltpu.make_async_remote_copy(
-            src_ref=run[which].at[way, chips - 1] if first else here,
-            dst_ref=here,
-            send_sem=side_send.at[which, way, step],
-            recv_sem=side_recv.at[which, way, step],
-            device_id=other,
-            device_id_type=MESH,
-        )
-
-    def beside(which, way, step):
-        here = results[which].at[rows(which, 1 - core, way, piece(step + chips - 1, way))]
-        return pltpu.make_async_remote_copy(
-            src_ref=here, dst_ref=here, send_sem=side_send.at[which, way, step],
-            recv_sem=side_recv.at[which, way, step], device_id=other, device_id_type=MESH,
-        )
-
-    def incoming(which, way, step):
-        here = results[which].at[final_rows(which, way, step)]
-        return pltpu.make_async_remote_copy(
-            src_ref=here, dst_ref=here, send_sem=spread_send.at[which, way, step],
-            recv_sem=spread_recv.at[which, way, step - 1], device_id=targets[way], device_id_type=MESH,
-        )
-
-    both = [(which, way) for way in range(2) for which in range(2)]
-
-    def begin(step, carry):
-        for which, way in both:
-            load(which, way, step).start()
-        return carry
-
-    lax.fori_loop(0, chips, begin, 0)
-    pl.semaphore_wait(barrier, 4)
-
-    def begin_swap(step, carry):
-        for which, way in both:
-            swap(which, way, step).start()
-        return carry
-
-    lax.fori_loop(0, chips, begin_swap, 0)
-
-    for which, way in both:
-        load(which, way, 0).wait()
-        swap(which, way, 0).wait_recv()
-        run[which][way, 0] = own[which][way, 0] + pair[which][way, 0]
-        pass_on(which, way, 0).start()
-
-    def gather_step(step, carry):
-        for which, way in both:
-            load(which, way, step).wait()
-            swap(which, way, step).wait_recv()
-            pass_on(which, way, step - 1).wait_recv()
-            run[which][way, step] = run[which][way, step] + own[which][way, step] + pair[which][way, step]
-
-            @pl.when(step < chips - 1)
-            def _():
-                pass_on(which, way, step).start()
-
-        return carry
-
-    lax.fori_loop(1, chips, gather_step, 0)
-
-    for way in range(2):
-        cross(way).start()
-        keep(0, way).start()
-        spread(0, way, 0, True).start()
-        aside(0, way, 0, True).start()
-    for way in range(2):
-        cross(way).wait()
-        run_misc[way, chips - 1] = run_misc[way, chips - 1] + far_misc[way]
-        keep(1, way).start()
-        spread(1, way, 0, True).start()
-        aside(1, way, 0, True).start()
-
-    def spread_step(step, carry):
-        for which, way in both:
-            incoming(which, way, step).wait_recv()
-
-            @pl.when(step < chips - 1)
-            def _():
-                spread(which, way, step).start()
-
-            aside(which, way, step).start()
-        return carry
-
-    lax.fori_loop(1, chips, spread_step, 0)
-
-    def finish(step, carry):
-        for which, way in both:
-            swap(which, way, step).wait_send()
-            beside(which, way, step).wait_recv()
-            aside(which, way, step).wait_send()
-
-            @pl.when(step < chips - 1)
-            def _():
-                pass_on(which, way, step).wait_send()
-                spread(which, way, step).wait_send()
-
-        return carry
-
-    lax.fori_loop(0, chips, finish, 0)
-    for which, way in both:
-        keep(which, way).wait()
-
-
-def head_kernel(side, book, down, up, late, early, out):
-    encoder = side[0] == 0
-    out[...] = jnp.zeros_like(out)
-    size = book.shape[0]
+    encoder = lax.axis_index("section") == 0
+    ring = Ring((hidden,), (hidden_out,), FINISH_WAYS, None, scratch) if scratch else None
+    count, width = query.shape
     narrow = down.shape[0]
-    at = size + 2 * narrow
+    steps = count // TOKENS
+    pairs = width // 128
+    row = edges.shape[0] - 1
+    at = book.shape[0] + 2 * narrow
+    inputs = (
+        (query, query_in), (marks, marks_in), (key, key_in), (value, value_in), (context_grad, grad_in),
+        (context, context_in), (key_mark.at[row], key_mark_in), (edges.at[row], edge_in), (mid_grad, mid_in),
+        (weight, weight_in), (branch_low, branch_in), (n1, n1_in),
+    )
+    loads = [pltpu.make_async_copy(*pair, in_sems.at[number]) for number, pair in enumerate(inputs)]
+    part_load = pltpu.make_async_copy(attention, part, part_sem)
+
+    if ring:
+        ring.greet()
 
     @pl.when(encoder)
     def _():
-        out[:size, :] = book[...]
-        out[size : size + narrow, :] = down[...]
-        out[at : at + 16, :] = late[...]
-        out[at + 16 : at + 32, :] = early[...]
+        for load in loads:
+            load.start()
+        part_load.start()
+
+    if ring:
+        ring.begin()
+    misc[...] = jnp.zeros_like(misc)
+
+    @pl.when(encoder)
+    def _():
+        misc[: book.shape[0], :] = book[...]
+        misc[book.shape[0] : book.shape[0] + narrow, :] = down[...]
+        misc[at : at + 16, :] = late[...]
+        misc[at + 16 : at + 32, :] = early[...]
+        for load in loads:
+            load.wait()
+        part_load.wait()
+        mark_grads(grad_in, context_in, grad_mark)
+        key_total[...] = jnp.zeros_like(key_total)
+        value_total[...] = jnp.zeros_like(value_total)
 
     @pl.when(jnp.logical_not(encoder))
     def _():
-        out[size + narrow : at, :] = up[...]
-        out[at + 32 : at + 48, :] = late[...]
-        out[at + 48 : at + 64, :] = early[...]
-
-
-def gather_head(side, book, down, up, late, early):
-    rows = book.shape[0] + 2 * down.shape[0] + 64
+        misc[book.shape[0] + narrow : at, :] = up[...]
+        misc[at + 32 : at + 48, :] = late[...]
+        misc[at + 48 : at + 64, :] = early[...]
+
+    def attention_piece(turn):
+        attend_back_block(
+            turn // 2, 0, count, (turn % 2) * (width // 2), pairs // 2,
+            query_in, marks_in, key_in, value_in, grad_in, key_mark_in, grad_mark, query_grad, key_total, value_total,
+        )
+
+    def entry_piece(number):
+        rows = pl.ds(pl.multiple_of(number * TOKENS, TOKENS), TOKENS)
+        normed_grad = (
+            dot(query_grad[rows, :], weight_in[:, :width], NT)
+            + dot(key_grad[rows, :], weight_in[:, width : 2 * width], NT)
+            + dot(value_grad[rows, :], weight_in[:, 2 * width :], NT)
+        )
+        hat, inverse = norm_parts(edge_in[rows, :].astype(F32))
+        misc[at + 16 : at + 17, :] += column_sum(query_grad[rows, :].astype(F32))
+        misc[at + 17 : at + 18, :] += column_sum(value_grad[rows, :].astype(F32))
+        misc[at + 18 : at + 19, :] += column_sum(normed_grad * hat)
+        misc[at + 19 : at + 20, :] += column_sum(normed_grad)
+        mid_in[rows, :] = mid_in[rows, :] + norm_back(normed_grad, gains[0:1, :], hat, inverse)
+
+    def weight_piece(number):
+        def put(left, right):
+            rows = pl.ds(pl.multiple_of(number * width, width), width)
+            part[rows, :] = part[rows, :] + dot(left[...], right[...], TN)
+
+        for choice, (left, right) in enumerate(
+            ((context_in, branch_in), (n1_in, query_grad), (n1_in, key_grad), (n1_in, value_grad))
+        ):
+            pl.when(number == choice)(functools.partial(put, left, right))
+
+    def summing(step):
+        if ring:
+            ring.gather(step)
+
+        @pl.when(encoder)
+        def _():
+            attention_piece(step - 1)
+
+    chips = ring.chips if ring else 8
+    pieces = 2 * steps
+    inside = min(chips - 1, pieces)
+    loop(1, inside + 1, summing)
+    if ring:
+        loop(inside + 1, chips, ring.gather)
+        ring.turn()
+
+    @pl.when(encoder)
+    def _():
+        loop(inside, pieces, attention_piece)
+        key_grad[...] = (key_total[...] * (1.0 / LOG2E)).astype(BF)
+        value_grad[...] = value_total[...].astype(BF)
+
+    def spreading(step):
+        if ring:
+            ring.pass_out(step)
+
+        @pl.when(encoder)
+        def _():
+            entry_piece(step - 1)
+            weight_piece(step - 1)
+
+    loop(1, steps + 1, spreading)
+    stores = [
+        pltpu.make_async_copy(mid_in, entry, out_sems.at[0]),
+        pltpu.make_async_copy(part, attention_out, out_sems.at[1]),
+    ]
+
+    @pl.when(encoder)
+    def _():
+        for store in stores:
+            store.start()
+
+    if ring:
+        loop(steps + 1, chips, ring.pass_out)
+        ring.finish()
+
+    @pl.when(encoder)
+    def _():
+        for store in stores:
+            store.wait()
+
+
+def finish_row(work, kept, late, early, up, book, hidden, attention):
+    count, width = kept["n1"].shape
+    alone = lax.axis_size("dp") < LEAST_DEVICES
+    operands = [
+        hidden, attention, kept["query"], kept["marks"], kept["key"], kept["value"], late["context_grad"],
+        kept["context"], work.key_mark, work.edges, late["mid_grad"], work.attention_in, late["branch_low"], kept["n1"],
+        work.gains, book, late["head_late"], up, late["sums_late"], early,
+    ]
+    hbm, vmem = pl.BlockSpec(memory_space=pl.ANY), pl.BlockSpec(memory_space=pltpu.VMEM)
+    rows = book.shape[0] + 2 * work.narrow + 64
     unit = 16 * lax.axis_size("dp")
-    vmem = pl.BlockSpec(memory_space=pltpu.VMEM)
-    return pl.pallas_call(
-        head_kernel,
-        in_specs=[pl.BlockSpec(memory_space=pltpu.SMEM)] + [vmem] * 5,
-        out_specs=vmem,
-        out_shape=jax.ShapeDtypeStruct((rows + (-rows % unit), book.shape[1]), F32),
-        compiler_params=PARAMS,
-        name="gather_head",
-    )(side, book, down, up, late, early)
-
-
-def unpack_kernel(main, misc, hidden_out, hidden_in, attention_out, attention_in, book, sems):
-    width = main.shape[1]
+    low = pltpu.VMEM((count, width), BF)
+    wide = pltpu.VMEM((count, width), F32)
+    scratch = [low] * 6 + [pltpu.VMEM((count, 128), BF), low, wide, pltpu.VMEM(work.attention_in.shape, BF), low, low]
+    scratch += [pltpu.VMEM(attention.shape, F32), low, low, wide, wide, low, low]
+    scratch += [pltpu.SemaphoreType.DMA((12,)), pltpu.SemaphoreType.DMA, pltpu.SemaphoreType.DMA((2,))]
+    settings = {}
+    if not alone:
+        scratch += Ring.scratch((hidden,), FINISH_WAYS, None)
+        settings = dict(collective_id=1, has_side_effects=True)
+    outs = pl.pallas_call(
+        finish_kernel,
+        in_specs=[hbm] * 14 + [vmem] * 6,
+        out_specs=[hbm, hbm, vmem, hbm],
+        out_shape=(
+            jax.ShapeDtypeStruct(hidden.shape, F32),
+            jax.ShapeDtypeStruct(attention.shape, F32),
+            jax.ShapeDtypeStruct((rows + (-rows % unit), width), F32),
+            jax.ShapeDtypeStruct((count, width), F32),
+        ),
+        scratch_shapes=scratch,
+        input_output_aliases={1: 1},
+        compiler_params=pltpu.CompilerParams(vmem_limit_bytes=58 << 20, **settings),
+        name="finish_row",
+    )(*operands)
+    return (hidden,) + tuple(outs[1:]) if alone else outs
+
+
+def unpack_kernel(
+    side, hidden, attention, misc, first_entry, second_entry, first_result, second_result,
+    hidden_out, hidden_in, attention_out, attention_in, book, edge, held, head, rows, ins, outs, row_ins, row_outs,
+):
+    width = hidden.shape[1]
     narrow = book.shape[0]
     steps = hidden_out.shape[0] // width
-    copies = [(main.at[pl.ds(0, steps * width)], hidden_out)]
-    at = steps
-    for out, count in ((hidden_in, steps), (attention_out, 1), (attention_in, 3)):
-        for number in range(count):
-            copies.append((main.at[pl.ds((at + number) * width, width)], out.at[:, pl.ds(number * width, width)]))
-        at += count
+    targets = [hidden_out.at[pl.ds(number * width, width), :] for number in range(steps)]
+    targets += [hidden_in.at[:, pl.ds(number * width, width)] for number in range(steps)]
+    targets += [attention_out]
+    targets += [attention_in.at[:, pl.ds(number * width, width)] for number in range(3)]
+    sources = [hidden.at[pl.ds(number * width, width), :] for number in range(2 * steps)]
+    sources += [attention.at[pl.ds(number * width, width), :] for number in range(4)]
+    tiles = range(len(targets))
+    for mine, pair in ((0, (first_entry, second_entry)), (1, (first_result, second_result))):
+
+        @pl.when(side[0] == mine)
+        def _():
+            for row in range(2):
+                pltpu.make_async_copy(pair[row], rows.at[row], row_ins.at[row]).start()
+
+    loads = [pltpu.make_async_copy(sources[number], held.at[number], ins.at[number]) for number in tiles]
+    loads.append(pltpu.make_async_copy(misc.at[pl.ds(0, head.shape[0]), :], head, ins.at[len(targets)]))
+    for load in loads:
+        load.start()
+    stores = []
+    for row in range(2):
+        pltpu.make_async_copy(first_entry, rows.at[row], row_ins.at[row]).wait()
+        stores.append(pltpu.make_async_copy(rows.at[row], edge.at[row], row_outs.at[row]))
+        stores[-1].start()
+    for number in tiles:
+        loads[number].wait()
+        stores.append(pltpu.make_async_copy(held.at[number], targets[number], outs.at[number]))
+        stores[-1].start()
+    loads[-1].wait()
     for number in range(book.shape[1] // width):
-        copies.append((misc.at[pl.ds(number * narrow, narrow)], book.at[:, pl.ds(number * width, width)]))
-    copies = [pltpu.make_async_copy(*pair, sems.at[number]) for number, pair in enumerate(copies)]
-    for copy in copies:
-        copy.start()
-    for copy in copies:
-        copy.wait()
-
-
-def unpack(main, misc, hidden, table_turned):
-    width = main.shape[1]
-    shapes = ((hidden, width), (width, hidden), (width, width), (width, 3 * width), table_turned.shape)
-    count = 5 + hidden // width + table_turned.shape[1] // width
+        book[:, number * width : (number + 1) * width] = head[number * narrow : (number + 1) * narrow, :]
+    for store in stores:
+        store.wait()
+
+
+def unpack(side, hidden, attention, misc, ends, table_turned):
+    width = hidden.shape[1]
+    features = hidden.shape[0] // 2
+    tiles = (hidden.shape[0] + attention.shape[0]) // width
+    shapes = (
+        (features, width), (width, features), (width, width), (width, 3 * width), table_turned.shape,
+        (2,) + ends[0].shape,
+    )
+    hbm, vmem = pl.BlockSpec(memory_space=pl.ANY), pl.BlockSpec(memory_space=pltpu.VMEM)
     return pl.pallas_call(
         unpack_kernel,
-        in_specs=[pl.BlockSpec(memory_space=pl.ANY)] * 2,
-        out_specs=[pl.BlockSpec(memory_space=pl.ANY)] * 5,
+        in_specs=[pl.BlockSpec(memory_space=pltpu.SMEM)] + [hbm] * 7,
+        out_specs=[hbm] * 4 + [vmem, hbm],
         out_shape=tuple(jax.ShapeDtypeStruct(shape, F32) for shape in shapes),
-        scratch_shapes=[pltpu.SemaphoreType.DMA((count,))],
+        scratch_shapes=[
+            pltpu.VMEM((tiles, width, width), F32),
+            pltpu.VMEM((table_turned.size // width, width), F32),
+            pltpu.VMEM((2,) + ends[0].shape, F32),
+            pltpu.SemaphoreType.DMA((tiles + 1,)),
+            pltpu.SemaphoreType.DMA((tiles,)),
+            pltpu.SemaphoreType.DMA((2,)),
+            pltpu.SemaphoreType.DMA((2,)),
+        ],
         compiler_params=PARAMS,
         name="unpack",
-    )(main, misc)
-
-
-def sum_over_dp(main, misc):
-    chips = lax.axis_size("dp") // 2
-    width = main.shape[1]
-    sizes = (main.shape[0] // (4 * chips), misc.shape[0] // (4 * chips))
-    slots = lambda which: pltpu.VMEM((2, chips, sizes[which], width), F32)
-    sems = lambda *shape: pltpu.SemaphoreType.DMA(shape)
-    return pl.pallas_call(
-        functools.partial(sum_kernel, chips),
-        in_specs=[pl.BlockSpec(memory_space=pl.ANY)] * 2,
-        out_specs=[pl.BlockSpec(memory_space=pl.ANY)] * 2,
-        out_shape=(jax.ShapeDtypeStruct(main.shape, F32), jax.ShapeDtypeStruct(misc.shape, F32)),
-        scratch_shapes=[slots(0), slots(1)] * 3
-        + [pltpu.VMEM((2, sizes[1], width), F32)]
-        + [sems(2, 2, chips)] * 5
-        + [sems(2)] * 2
-        + [sems(2, 2)]
-        + [sems(2, 2, chips)] * 4,
-        compiler_params=pltpu.CompilerParams(
-            collective_id=0, has_side_effects=True, vmem_limit_bytes=48 << 20
-        ),
-        name="sum_over_dp",
-    )(main, misc)
+    )(side, hidden, attention, misc, *ends)
 
 
 def nothing_kernel(*refs):
@@ -829,7 +1080,7 @@
 
 KEPT = ("n1", "query", "key", "value", "context", "marks", "mid", "n2", "active", "slope", "result", "latent")
 BACK = (
-    "out_low", "preact_low", "mid_grad", "branch_low", "query_grad", "key_grad", "value_grad",
+    "out_low", "preact_low", "mid_grad", "branch_low", "context_grad", "query_grad", "key_grad", "value_grad",
     "entry", "latent_out", "sums_late", "sums_early", "head_late", "head_early",
 )
 
@@ -855,9 +1106,8 @@
             n1=(d, BF), query=(d, BF), key=(d, BF), value=(d, BF), context=(d, BF), marks=(d, BF),
             mid=(d, F32), n2=(d, BF), active=(f, BF), slope=(f, BF), latent=(self.narrow, F32),
         )
-        shapes = {name: jax.ShapeDtypeStruct((n, size), kind) for name, (size, kind) in table.items()}
-        shapes["result"] = jax.ShapeDtypeStruct((self.rows, n, d), F32)
-        return shapes
+        table["result"] = (d, F32)
+        return {name: jax.ShapeDtypeStruct((n, size), kind) for name, (size, kind) in table.items()}
 
     def back_shapes(self):
         n, d, f = self.count, self.width, self.hidden
@@ -867,9 +1117,9 @@
             latent_out=(self.narrow, n, F32), sums_late=(16, d, F32), sums_early=(16, d, F32),
             head_late=(self.narrow, d, F32), head_early=(self.narrow, d, F32),
         )
-        shapes = {name: jax.ShapeDtypeStruct((a, b), kind) for name, (a, b, kind) in table.items()}
-        shapes["entry"] = jax.ShapeDtypeStruct((self.rows, n, d), F32)
-        return shapes
+        table["entry"] = table["mid_grad"]
+        table["context_grad"] = table["out_low"]
+        return {name: jax.ShapeDtypeStruct((a, b), kind) for name, (a, b, kind) in table.items()}
 
     def turned(self, array):
         return pl.BlockSpec((array.shape[0], TOKENS), lambda step: (0, step))
@@ -892,26 +1142,13 @@
             self.whole(self.head_bias),
         ]
 
-    def row_spec(self, row):
-        return pl.BlockSpec((None, TOKENS, self.width), lambda step: (row, step, 0))
-
     def unit_spec(self, row):
         steps = self.count // TOKENS
         return pl.BlockSpec((TOKENS, self.narrow), lambda step: (row * steps + step, 0))
 
-    def call(self, kernel, in_specs, operands, outs, out_specs, name, scratch=(), rest=None, place=0):
-        aliases = {}
-        if rest is not None:
-            inner, number = kernel, len(operands)
-
-            def kernel(*refs):
-                inner(*refs[:number], *refs[number + 1 :])
-
-            in_specs, operands = in_specs + [pl.BlockSpec(memory_space=pl.ANY)], operands + (rest,)
-            aliases = {number: place}
+    def call(self, kernel, in_specs, operands, outs, out_specs, name, scratch=()):
         return pl.pallas_call(
             kernel,
-            input_output_aliases=aliases,
             grid=(self.count // TOKENS,),
             in_specs=in_specs,
             out_specs=out_specs,
@@ -943,7 +1180,7 @@
             name=name,
         )(self.windows, *operands)
 
-    def forward(self, row, rest=None):
+    def forward(self, row):
         shapes = self.kept_shapes()
         entry = (self.edges, self.wide, self.up, self.head_bias)
         kept = {}
@@ -977,26 +1214,27 @@
             + [self.whole(array) for array in consts],
             (self.side,) + entry + (kept["context"],) + consts,
             [shapes[name] for name in names],
-            [self.row_spec(row) if name == "result" else self.tokens(shapes[name]) for name in names],
+            [self.tokens(shapes[name]) for name in names],
             "hidden",
-            rest=rest,
-            place=names.index("result"),
         )
         kept.update(zip(names, outs))
         return kept
 
-    def backward(self, row, kept, latent_in, former=None, rest=None):
+    def backward(self, row, kept, latent_in, former=None):
+        back = self.backward_late(row, kept, latent_in, former)
+        back.update(self.backward_early(row, kept, back, former))
+        return back
+
+    def backward_late(self, row, kept, latent_in, former=None):
         shapes = self.back_shapes()
         prior = () if former is None else (former["sums_late"], former["head_late"])
         adding = int(former is not None)
-        back = {}
         names = ("out_low", "preact_low", "mid_grad", "branch_low", "context_grad", "sums_late", "head_late")
-        shapes["context_grad"] = shapes["out_low"]
         consts = (self.output_gain, self.head_bias, self.down, self.down_bias, self.hidden_out)
         late = (self.gains, self.biases, self.attention_out)
         outs = self.call(
             functools.partial(tail_back_kernel, adding=adding),
-            [self.side_spec(), self.row_spec(row), self.entry_specs(row)[0], self.unit_spec(row),
+            [self.side_spec(), self.tokens(kept["result"]), self.entry_specs(row)[0], self.unit_spec(row),
              self.turned(latent_in)]
             + [self.whole(array) for array in consts]
             + [self.tokens(kept["slope"]), self.whole(self.hidden_in), self.tokens(kept["mid"])]
@@ -1008,12 +1246,17 @@
             "tail_back",
             scratch=[pltpu.VMEM((TOKENS, self.width), F32)],
         )
-        back.update(zip(names, outs))
+        return dict(zip(names, outs))
+
+    def backward_early(self, row, kept, late, former=None):
+        shapes = self.back_shapes()
+        adding = int(former is not None)
+        back = {}
         names = ("query_grad", "key_grad", "value_grad")
         half = self.width // 2
         outs = self.attention_call(
             attend_back_kernel, row,
-            (kept["query"], kept["marks"], kept["key"], kept["value"], back.pop("context_grad"), kept["context"],
+            (kept["query"], kept["marks"], kept["key"], kept["value"], late["context_grad"], kept["context"],
              self.key_mark),
             [shapes[name] for name in names],
             "attend_back",
@@ -1032,13 +1275,12 @@
             [self.side_spec()] + self.entry_specs(row) + [self.unit_spec(row)]
             + [self.tokens(array) for array in grads]
             + [self.whole(self.attention_in), self.whole(self.gains), self.whole(self.biases),
-               self.tokens(back["mid_grad"])] + [self.whole(array) for array in prior],
+               self.tokens(late["mid_grad"])] + [self.whole(array) for array in prior],
             (self.side, self.edges, self.wide, self.up, self.head_bias, self.unit) + grads
-            + (self.attention_in, self.gains, self.biases, back["mid_grad"]) + prior,
+            + (self.attention_in, self.gains, self.biases, late["mid_grad"]) + prior,
             [shapes[name] for name in names],
-            [self.row_spec(row), self.turned(shapes["latent_out"])] + [self.whole(shapes[name]) for name in names[2:]],
+            [self.tokens(shapes["entry"]), self.turned(shapes["latent_out"])] + [self.whole(shapes[name]) for name in names[2:]],
             "entry_back",
-            rest=rest,
         )
         back.update(zip(names, outs))
         return back
@@ -1086,7 +1328,8 @@
     kept_shapes = as_list(work.kept_shapes(), KEPT)
     back_shapes = as_list(work.back_shapes(), BACK)
     book_out = book_shape(table_turned, width)
-    weight_out = jax.ShapeDtypeStruct((2 * hidden + 4 * width, width), F32)
+    hidden_out_shape = jax.ShapeDtypeStruct((2 * hidden, width), F32)
+    attention_shape = jax.ShapeDtypeStruct((4 * width, width), F32)
     quiet = jnp.zeros((unit.shape[1], count), F32)
     first_kept = work.forward(0)
 
@@ -1105,37 +1348,44 @@
         return list(unwritten(kept_shapes)), as_list(work.backward(0, first_kept, latent_in), BACK)
 
     def decoder_third():
-        return as_list(work.forward(1, first_kept["result"]), KEPT), list(unwritten(back_shapes))
+        return as_list(work.forward(1), KEPT), list(unwritten(back_shapes))
 
     kept_b, back_b = lax.cond(encoder, encoder_third, decoder_third)
     kept_b, back_b = dict(zip(KEPT, kept_b)), dict(zip(BACK, back_b))
 
     def encoder_fourth():
         book = scatter_codes(index, unit, (first_kept["latent"], kept_a["latent"]), table_turned, width)
-        return list(unwritten(back_shapes)), weight_grads(first_kept, back_b), book
+        weights = hidden_weights(first_kept, back_b), attention_weights(first_kept, back_b)
+        return list(unwritten(back_shapes)), weights, book
 
     def decoder_fourth():
-        weights, book = unwritten([weight_out, book_out])
-        return as_list(work.backward(1, kept_b, quiet, back_a), BACK), weights, book
+        *weights, book = unwritten([hidden_out_shape, attention_shape, book_out])
+        return as_list(work.backward(1, kept_b, quiet, back_a), BACK), tuple(weights), book
 
     back_c, weights_c, book = lax.cond(encoder, encoder_fourth, decoder_fourth)
     back_c = dict(zip(BACK, back_c))
     latent_in_second = lax.ppermute(back_c["latent_out"], "section", [(1, 0)])
+    late_names = ("branch_low", "mid_grad", "context_grad", "sums_late", "head_late")
 
     def encoder_fifth():
-        back = work.backward(1, kept_a, latent_in_second, back_b, back_b["entry"])
-        total = weight_grads(kept_a, back, weights_c)
-        return total, as_list(back, BACK[-4:]), back["entry"]
+        late = work.backward_late(1, kept_a, latent_in_second, back_b)
+        total = hidden_weights(kept_a, late, weights_c[0])
+        return total, weights_c[1], as_list(late, late_names), back_b["sums_early"]
 
     def decoder_fifth():
-        total = weight_grads(first_kept, back_a)
-        total = weight_grads(kept_b, back_c, total)
-        return total, as_list(back_c, BACK[-4:]), kept_b["result"]
-
-    totals, (late, early, down, up), edge = lax.cond(encoder, encoder_fifth, decoder_fifth)
-    totals, misc = sum_all(totals, gather_head(side, book, down, up, late, early))
-    hidden_out_grad, hidden_in_grad, attention_out_grad, attention_in_grad, book = unpack(
-        totals, misc, hidden, table_turned
+        total = hidden_weights(kept_b, back_c, hidden_weights(first_kept, back_a))
+        attention = attention_weights(kept_b, back_c, attention_weights(first_kept, back_a))
+        return total, attention, as_list(back_c, late_names), back_c["sums_early"]
+
+    hidden_total, attention_total, late, early = lax.cond(encoder, encoder_fifth, decoder_fifth)
+    late = dict(zip(late_names, late))
+    hidden_total, attention_total, misc, second_entry = finish_row(
+        work, kept_a, late, early, back_c["head_early"], book, hidden_total, attention_total
+    )
+    attention_total, misc = sum_all(attention_total, misc)
+    hidden_out_grad, hidden_in_grad, attention_out_grad, attention_in_grad, book, edge = unpack(
+        side, hidden_total, attention_total, misc,
+        (back_b["entry"], second_entry, first_kept["result"], kept_b["result"]), table_turned,
     )
     narrow = unit.shape[1]
     pieces, at = [], book_out.shape[0]
@@ -1163,12 +1413,6 @@
     )
 
 
-def sum_all(main, misc):
-    if lax.axis_size("dp") < 4:
-        return main, lax.psum(misc, "section")
-    return sum_over_dp(main, misc)
-
-
 def solution(mesh):
     return jax.shard_map(
         on_device,

time: 843 us -> 418 us (0.50)
  Pallas kernels: 784 us -> 357 us
    pallas_call x13, Pallas kernels: 701 us -> 288 us  [the longest x1 98.2 us: finish_row(): pl.pallas_call(finish_kernel, in_specs=[hbm] * 14 + [vmem] * 6, out_specs...]
    pallas_call x4 -> x3, Pallas kernels: 64.9 us -> 51.9 us  [attention_call(): pl.pallas_call(functools.partial(kernel, row=row), grid_spec=pltpu.Prefet...]
where the time goes in v4:
time: 418 us; the launch traced here: 410 us
  Pallas kernels  357 us (85%)
  loops' own time  21.3 us (5%)
  waiting for transfers between devices  15.8 us (4%)
  local copies, waits for them, and re-layouts  10.7 us (3%)
    pallas_call x1, Pallas kernels, finish_row(): pl.pallas_call(finish_kernel, in_specs=[hbm] * 14 + [vmem] * 6, out_specs...  98.2 us
    pallas_call x7, Pallas kernels, call(): pl.pallas_call(kernel, grid=(self.count // TOKENS,), in_specs=in_specs, o...  81.2 us
    pallas_call x1, Pallas kernels, sum_all(): pl.pallas_call(sum_kernel, in_specs=[pl.BlockSpec(memory_space=pl.ANY)] *...  68.7 us
    pallas_call x3, Pallas kernels, attention_call(): pl.pallas_call(functools.partial(kernel, row=row), grid_spec=pltpu.Prefet...  51.9 us
    pallas_call x3, Pallas kernels, weight_call(): pl.pallas_call(kernel, grid=(steps,), in_specs=in_specs, out_specs=out_sp...  28.2 us
    pallas_call x1, Pallas kernels, unpack(): pl.pallas_call(unpack_kernel, in_specs=[pl.BlockSpec(memory_space=pltpu.S...  11.7 us
    pallas_call x1, Pallas kernels, scatter_codes(): pl.pallas_call(scatter_kernel, in_specs=[pl.BlockSpec(memory_space=pltpu....  10.3 us
    ppermute x1, waiting for transfers between devices, on_device(): latent_in = lax.ppermute(back_a['latent_out'], 'section', [(1, 0)])  10.1 us
  transfers between devices with their start and end apart: 2, of which 2 were waited for; matrix products, arithmetic and copies ran while one was open for 0% of the time, Pallas kernels for 0%

profile of v4, /device:TPU:0, one launch (start us, length us, event | category | flops | bytes accessed | tf_op | source)
XLA Modules:
  0.0 410.3 jit_solution(7797574415232994466)
XLA Ops:
  0.7 0.7 copy.54
  1.4 0.7 reshape.59
  2.1 0.1 fusion.4
  2.1 0.1 copy.48
  2.2 0.1 copy.47
  2.3 0.2 select_reduce_fusion.1
  2.6 0.1 copy.44
  2.7 0.1 reshape.60.windows
  2.8 0.7 copy.53
  3.5 6.9 %gather_codes.1 = (f32[2048,32]{1,0:T(8,128)}, bf16[2048,128]{1,0:T(8,128)(2,1)S(1)}, bf16[2,1024,128]{2,1,0:T(8,128)(2,1)S(1)}, bf16[2,1024,128]{2,1,0:T(8,128)(2,1)S(1)}) custom-call(s32[2048]{0:T(1024)S(1)} %bitcast.112, f32[32,8192]{1,0:T(8,128)} %bitcast.79, s32[2,1024]{1,0:T(2,128)} %segments.1), custom_call_target="tpu_custom_call" | custom-call | tf_op jit(solution)/shard_map/gather_codes/pallas_call | solution.py:99
  10.4 0.0 copy-start.4
  10.5 0.0 copy-start.41
  10.5 0.0 copy-start.42
  10.5 7.0 %project.5 = (bf16[1024,512]{1,0:T(8,128)(2,1)}, bf16[1024,512]{1,0:T(8,128)(2,1)}, bf16[1024,512]{1,0:T(8,128)(2,1)}, bf16[1024,512]{1,0:T(8,128)(2,1)}) custom-call(s32[1]{0:T(128)} %bitcast.side, bf16[2,1024,512]{2,1,0:T(8,128)(2,1)} %bitcast.42, bf16[2048,128]{1,0:T(8,128)(2,1)S(1)} %get-tuple-element.775.wide, f32[32,512]{1,0:T(8,128)} %up.3, ...), custom_call_target="tpu_custom_call" | custom-call | tf_op jit(solution)/shard_map/project/pallas_call | solution.py:1150
  17.6 13.0 %attend.5 = (bf16[1024,512]{1,0:T(8,128)(2,1)}, bf16[1024,512]{1,0:T(8,128)(2,1)}) custom-call(s32[16]{0:T(128)S(1)} %reshape.60.windows, bf16[1024,512]{1,0:T(8,128)(2,1)} %get-tuple-element.776.query, bf16[1024,512]{1,0:T(8,128)(2,1)} %get-tuple-element.777.key, bf16[1024,512]{1,0:T(8,128)(2,1)} %get-tuple-element.778.value, ...), custom_call_target="tpu_custom_call" | custom-call | tf_op jit(solution)/shard_map/attend/pallas_call | solution.py:1169
  30.7 14.8 %hidden.5 = (f32[1024,512]{1,0:T(8,128)}, bf16[1024,512]{1,0:T(8,128)(2,1)}, bf16[1024,2048]{1,0:T(8,128)(2,1)}, bf16[1024,2048]{1,0:T(8,128)(2,1)}, f32[1024,512]{1,0:T(8,128)}, /*index=5*/f32[1024,32]{1,0:T(8,128)}) custom-call(s32[1]{0:T(128)} %bitcast.side, bf16[2,1024,512]{2,1,0:T(8,128)(2,1)S(1)} %bitcast.43, bf16[2048,128]{1,0:T(8,128)(2,1)} %copy-done.15, ...), custom_call_target="tpu_custom_call" | custom-call | tf_op jit(solution)/shard_map/hidden/pallas_call | solution.py:1150
  45.5 39.0 %conditional.4 = (bf16[1024,512]{1,0:T(8,128)(2,1)}, bf16[1024,512]{1,0:T(8,128)(2,1)}, bf16[1024,512]{1,0:T(8,128)(2,1)}, bf16[1024,512]{1,0:T(8,128)(2,1)}, bf...) conditional(s32[]{:T(128)} %convert_element_type.2, ...), branch_computations={%region_2.3_spmd, %region_3.4_spmd} | conditional | bytes 11665708 | solution.py:1342
  51.2 5.4 %project.3 = (bf16[1024,512]{1,0:T(8,128)(2,1)}, bf16[1024,512]{1,0:T(8,128)(2,1)}, bf16[1024,512]{1,0:T(8,128)(2,1)}, bf16[1024,512]{1,0:T(8,128)(2,1)}) custom-call(s32[1]{0:T(128)} %get-tuple-element.408.side, bf16[2,1024,512]{2,1,0:T(8,128)(2,1)S(1)} %get-tuple-element.409.edge, bf16[2048,128]{1,0:T(8,128)(2,1)} %get-tuple-element.410.wide, ...), custom_call_target="tpu_custom_call" | custom-call | tf_op jit(solution)/shard_map/cond/branch_1_fun/project/pallas_call | solution.py:1150
  56.7 13.4 %attend.3 = (bf16[1024,512]{1,0:T(8,128)(2,1)}, bf16[1024,512]{1,0:T(8,128)(2,1)}) custom-call(s32[16]{0:T(128)S(1)} %get-tuple-element.420.windows, bf16[1024,512]{1,0:T(8,128)(2,1)} %get-tuple-element.956.query, bf16[1024,512]{1,0:T(8,128)(2,1)} %get-tuple-element.957.key, bf16[1024,512]{1,0:T(8,128)(2,1)} %get-tuple-element.958.value, ...), custom_call_target="tpu_custom_call" | custom-call | tf_op jit(solution)/shard_map/cond/branch_1_fun/attend/pallas_call | solution.py:1169
  70.0 14.4 %hidden.3 = (f32[1024,512]{1,0:T(8,128)}, bf16[1024,512]{1,0:T(8,128)(2,1)}, bf16[1024,2048]{1,0:T(8,128)(2,1)}, bf16[1024,2048]{1,0:T(8,128)(2,1)}, f32[1024,512]{1,0:T(8,128)}, /*index=5*/f32[1024,32]{1,0:T(8,128)}) custom-call(s32[1]{0:T(128)} %get-tuple-element.408.side, bf16[2,1024,512]{2,1,0:T(8,128)(2,1)S(1)} %get-tuple-element.409.edge, ...), custom_call_target="tpu_custom_call" | custom-call | tf_op jit(solution)/shard_map/cond/branch_1_fun/hidden/pallas_call | solution.py:1150
  84.5 1.3 collective-permute-start
  85.8 10.1 %collective-permute-done = f32[32,1024]{1,0:T(8,128)S(1)} collective-permute-done((f32[32,1024]{1,0:T(8,128)}, f32[32,1024]{1,0:T(8,128)S(1)}, u32[]{:S(2)}, u32[]{:S(2)}) %collective-permute-start) | collective-permute-done | bytes 131104 | tf_op jit(solution)/shard_map/ppermute | solution.py:1345
  95.8 55.4 %conditional.5 = (bf16[1024,512]{1,0:T(8,128)(2,1)}, bf16[1024,512]{1,0:T(8,128)(2,1)}, bf16[1024,512]{1,0:T(8,128)(2,1)}, bf16[1024,512]{1,0:T(8,128)(2,1)}, bf...) conditional(s32[]{:T(128)} %convert_element_type.2, ...), branch_computations={%region_4.5_spmd, %region_5.6_spmd} | conditional | bytes 23069264 | solution.py:1353
  102.6 16.6 %tail_back.5 = (bf16[1024,512]{1,0:T(8,128)(2,1)}, bf16[1024,2048]{1,0:T(8,128)(2,1)}, f32[1024,512]{1,0:T(8,128)}, bf16[1024,512]{1,0:T(8,128)(2,1)}, bf16[1024...) custom-call(s32[1]{0:T(128)} %get-tuple-element.499.side, f32[1024,512]{1,0:T(8,128)} %get-tuple-element.500.result, ...), custom_call_target="tpu_custom_call" | custom-call | tf_op jit(solution)/shard_map/cond/branch_1_fun/tail_back/pallas_call | solution.py:1150
  119.3 25.5 %attend_back.4 = (bf16[1024,512]{1,0:T(8,128)(2,1)}, bf16[1024,512]{1,0:T(8,128)(2,1)}, bf16[1024,512]{1,0:T(8,128)(2,1)}) custom-call(s32[16]{0:T(128)S(1)} %copy-done.53, bf16[1024,512]{1,0:T(8,128)(2,1)S(1)} %copy-done.32, bf16[1024,512]{1,0:T(8,128)(2,1)} %get-tuple-element.520.marks, bf16[1024,512]{1,0:T(8,128)(2,1)} %get-tuple-element.521.key, ...), custom_call_target="tpu_custom_call" | custom-call | tf_op jit(solution)/shard_map/cond/branch_1_fun/attend_back/pallas_call | solution.py:1169
  144.8 6.4 %entry_back.4 = (f32[1024,512]{1,0:T(8,128)}, f32[32,1024]{1,0:T(8,128)}, f32[16,512]{1,0:T(8,128)}, f32[32,512]{1,0:T(8,128)}) custom-call(s32[1]{0:T(128)} %get-tuple-element.499.side, bf16[2,1024,512]{2,1,0:T(8,128)(2,1)S(1)} %get-tuple-element.501.cotangent.edge, bf16[2048,128]{1,0:T(8,128)(2,1)S(1)} %copy-done.19, f32[32,512]{1,0:T(8,128)S(1)} %get-tuple-element.530.up, ...), custom_call_target="tpu_custom_call" | custom-call | tf_op jit(solution)/shard_map/cond/branch_1_fun/entry_back/pallas_call | solution.py:1150
  151.2 35.8 %conditional.6 = (bf16[1024,512]{1,0:T(8,128)(2,1)}, bf16[1024,2048]{1,0:T(8,128)(2,1)}, f32[1024,512]{1,0:T(8,128)}, bf16[1024,512]{1,0:T(8,128)(2,1)}, bf16[10...) conditional(s32[]{:T(128)} %convert_element_type.2, ...), branch_computations={%region_6.7_spmd, %region_7.8_spmd} | conditional | bytes 20447872 | solution.py:1365
  159.8 10.7 %hidden_weights.4 = f32[4096,512]{1,0:T(8,128)} custom-call(bf16[1024,2048]{1,0:T(8,128)(2,1)} %get-tuple-element.595.active, bf16[1024,512]{1,0:T(8,128)(2,1)} %get-tuple-element.596.out_low, bf16[1024,512]{1,0:T(8,128)(2,1)} %get-tuple-element.597.n2, bf16[1024,2048]{1,0:T(8,128)(2,1)} %get-tuple-element.598.preact_low), custom_call_target="tpu_custom_call" | custom-call | tf_op jit(solution)/shard_map/cond/branch_1_fun/hidden_weights/pallas_call | solution.py:529
  170.6 10.3 %scatter_codes.1 = f32[512,512]{1,0:T(8,128)} custom-call(s32[2048]{0:T(1024)S(1)} %get-tuple-element.605.index, f32[2048,32]{1,0:T(8,128)S(1)} %copy-done.14, f32[1024,32]{1,0:T(8,128)S(1)} %copy-done.44, f32[1024,32]{1,0:T(8,128)} %get-tuple-element.608.latent_second, f32[32,8192]{1,0:T(8,128)S(1)} %copy-done.39), custom_call_target="tpu_custom_call" | custom-call | tf_op jit(solution)/shard_map/cond/branch_1_fun/scatter_codes/pallas_call | solution.py:152
  180.9 6.1 %attention_weights.3 = f32[2048,512]{1,0:T(8,128)} custom-call(bf16[1024,512]{1,0:T(8,128)(2,1)S(1)} %copy-done.23, bf16[1024,512]{1,0:T(8,128)(2,1)} %get-tuple-element.600.branch_low, bf16[1024,512]{1,0:T(8,128)(2,1)S(1)} %copy-done.36, bf16[1024,512]{1,0:T(8,128)(2,1)} %get-tuple-element.602.query_grad, bf16[1024,512]{1,0:T(8,128)(2,1)} %get-tuple-element.603.key_grad, ...), custom_call_target="tpu_custom_call" | custom-call | tf_op jit(solution)/shard_map/cond/branch_1_fun/attention_weights/pallas_call | solution.py:529
  187.0 1.3 collective-permute-start.1
  188.3 5.8 %collective-permute-done.1 = f32[32,1024]{1,0:T(8,128)S(1)} collective-permute-done((f32[32,1024]{1,0:T(8,128)}, f32[32,1024]{1,0:T(8,128)S(1)}, u32[]{:S(2)}, u32[]{:S(2)}) %collective-permute-start.1) | collective-permute-done | bytes 131104 | tf_op jit(solution)/shard_map/ppermute | solution.py:1367
  194.0 29.6 %conditional.7 = (f32[4096,512]{1,0:T(8,128)}, f32[2048,512]{1,0:T(8,128)}, bf16[1024,512]{1,0:T(8,128)(2,1)}, f32[1024,512]{1,0:T(8,128)}, bf16[1024,512]{1,0:T...) conditional(s32[]{:T(128)} %convert_element_type.2, (bf16[1024,2048]{1,0:T(8,128)(2,1)}, ...), branch_computations={%region_8.9_spmd, %region_9.10_spmd} | conditional | bytes 16842844 | solution.py:1380
  194.2 1.4 copy.193
  195.6 16.6 %tail_back.7 = (bf16[1024,512]{1,0:T(8,128)(2,1)}, bf16[1024,2048]{1,0:T(8,128)(2,1)}, f32[1024,512]{1,0:T(8,128)}, bf16[1024,512]{1,0:T(8,128)(2,1)}, bf16[1024...) custom-call(s32[1]{0:T(128)} %get-tuple-element.636.side, f32[1024,512]{1,0:T(8,128)} %get-tuple-element.637.result, ...), custom_call_target="tpu_custom_call" | custom-call | tf_op jit(solution)/shard_map/cond/branch_1_fun/tail_back/pallas_call | solution.py:1150
  212.3 11.4 %hidden_weights.7 = f32[4096,512]{1,0:T(8,128)} custom-call(bf16[1024,2048]{1,0:T(8,128)(2,1)S(1)} %copy-done.40, bf16[1024,512]{1,0:T(8,128)(2,1)} %get-tuple-element.654.out_low, bf16[1024,512]{1,0:T(8,128)(2,1)} %get-tuple-element.655.n2, bf16[1024,2048]{1,0:T(8,128)(2,1)} %get-tuple-element.656.preact_low, ...), custom_call_target="tpu_custom_call", output_to_operand_aliasing={{}: (4, {})} | custom-call | tf_op jit(solution)/shard_map/cond/branch_1_fun/hidden_weights/pallas_call | solution.py:529
  223.7 98.2 %finish_row.1 = (f32[4096,512]{1,0:T(8,128)}, f32[2048,512]{1,0:T(8,128)}, f32[768,512]{1,0:T(8,128)}, f32[1024,512]{1,0:T(8,128)}) custom-call(f32[4096,512]{1,0:T(8,128)} %get-tuple-element.842.hidden, f32[2048,512]{1,0:T(8,128)} %get-tuple-element.843.attention, bf16[1024,512]{1,0:T(8,128)(2,1)} %get-tuple-element.844.query, ...), custom_call_target="tpu_custom_call", output_to_operand_aliasing={{1}: (1, {})} | custom-call | tf_op jit(solution)/shard_map/finish_row/pallas_call | solution.py:981
  321.9 1.4 copy-done.2
  323.3 68.7 %sum_all.1 = (f32[2048,512]{1,0:T(8,128)S(1)}, f32[768,512]{1,0:T(8,128)S(1)}) custom-call(f32[2048,512]{1,0:T(8,128)} %get-tuple-element.859.main, f32[768,512]{1,0:T(8,128)S(1)} %copy-done.2), custom_call_target="tpu_custom_call" | custom-call | tf_op jit(solution)/shard_map/sum_all/pallas_call | solution.py:809
  392.0 2.1 copy-done
  394.1 0.6 slice_bitcast_fusion.2
  394.6 0.6 fusion.1
  395.2 0.7 fusion
  395.9 0.6 copy.50
  396.5 0.6 copy.45
  397.1 0.6 pad_maximum_fusion
  397.7 0.6 maximum_bitcast_fusion
  398.3 11.7 %unpack.1 = (f32[2048,512]{1,0:T(8,128)}, f32[512,2048]{1,0:T(8,128)}, f32[512,512]{1,0:T(8,128)}, f32[512,1536]{1,0:T(8,128)}, f32[32,8192]{1,0:T(8,128)}, /*index=5*/f32[2,1024,512]{2,1,0:T(8,128)}) custom-call(s32[1]{0:T(128)} %bitcast.side, f32[4096,512]{1,0:T(8,128)} %get-tuple-element.858.hidden, f32[2048,512]{1,0:T(8,128)} %copy-done, ...), custom_call_target="tpu_custom_call" | custom-call | tf_op jit(solution)/shard_map/unpack/pallas_call | solution.py:1049
  (75 shorter events, 0.2 us)
Async XLA Ops:
  2.8 42.7 %copy-start.51 = (s32[16]{0:T(128)}, s32[16]{0:T(128)S(1)}, u32[]{:S(2)}) copy-start(s32[16]{0:T(128)S(1)} %reshape.60.windows) | copy-start | bytes 196
  10.4 20.2 %copy-start.15 = (bf16[2048,128]{1,0:T(8,128)(2,1)}, bf16[2048,128]{1,0:T(8,128)(2,1)S(1)}, u32[]{:S(2)}) copy-start(bf16[2048,128]{1,0:T(8,128)(2,1)S(1)} %get-tuple-element.775.wide) | copy-start | bytes 1572868
  10.4 20.2 %copy-start.26 = (bf16[2,1024,128]{2,1,0:T(8,128)(2,1)}, bf16[2,1024,128]{2,1,0:T(8,128)(2,1)S(1)}, u32[]{:S(2)}) copy-start(bf16[2,1024,128]{2,1,0:T(8,128)(2,1)S(1)} %get-tuple-element.780.key_mark) | copy-start | bytes 1572868
  10.4 20.2 %copy-start.34 = (bf16[2,1024,128]{2,1,0:T(8,128)(2,1)}, bf16[2,1024,128]{2,1,0:T(8,128)(2,1)S(1)}, u32[]{:S(2)}) copy-start(bf16[2,1024,128]{2,1,0:T(8,128)(2,1)S(1)} %get-tuple-element.779.query_mark) | copy-start | bytes 1572868
  10.4 20.2 %copy-start.3 = (bf16[1,2,1024,512]{3,2,1,0:T(8,128)(2,1)S(1)}, bf16[1,2,1024,512]{3,2,1,0:T(8,128)(2,1)}, u32[]{:S(2)}) copy-start(bf16[1,2,1024,512]{3,2,1,0:T(8,128)(2,1)} %param.24) | copy-start | bytes 6291460
  10.4 20.2 %copy-start.4 = (bf16[1,512,2048]{2,1,0:T(8,128)(2,1)S(1)}, bf16[1,512,2048]{2,1,0:T(8,128)(2,1)}, u32[]{:S(2)}) copy-start(bf16[1,512,2048]{2,1,0:T(8,128)(2,1)} %param.29) | copy-start | bytes 6291460
  10.4 20.2 %copy-start.6 = (bf16[1,2048,512]{2,1,0:T(8,128)(2,1)S(1)}, bf16[1,2048,512]{2,1,0:T(8,128)(2,1)}, u32[]{:S(2)}) copy-start(bf16[1,2048,512]{2,1,0:T(8,128)(2,1)} %param.30) | copy-start | bytes 6291460
  10.5 20.2 %copy-start.33 = (f32[32,512]{1,0:T(8,128)S(1)}, f32[32,512]{1,0:T(8,128)}, u32[]{:S(2)}) copy-start(f32[32,512]{1,0:T(8,128)} %up.3) | copy-start | bytes 196612
  10.5 20.2 %copy-start.41 = (f32[512,32]{0,1:T(8,128)S(1)}, f32[512,32]{0,1:T(8,128)}, u32[]{:S(2)}) copy-start(f32[512,32]{0,1:T(8,128)} %param.36) | copy-start | bytes 196612
  10.5 20.2 %copy-start.42 = (f32[1,2,512]{2,1,0:T(2,128)S(1)}, f32[1,2,512]{2,1,0:T(2,128)}, u32[]{:S(2)}) copy-start(f32[1,2,512]{2,1,0:T(2,128)} %param.31) | copy-start | bytes 12292
  10.5 20.2 %copy-start.43 = (f32[2,512]{1,0:T(2,128)S(1)}, f32[2,512]{1,0:T(2,128)}, u32[]{:S(2)}) copy-start(f32[2,512]{1,0:T(2,128)} %head_bias.3) | copy-start | bytes 12292
  10.5 20.2 %copy-start.45 = (f32[512]{0:T(512)S(1)}, f32[512]{0:T(512)}, u32[]{:S(2)}) copy-start(f32[512]{0:T(512)} %param.34) | copy-start | bytes 6148
  10.5 20.2 %copy-start.46 = (f32[1,2048]{1,0:T(1,128)S(1)}, f32[1,2048]{1,0:T(1,128)}, u32[]{:S(2)}) copy-start(f32[1,2048]{1,0:T(1,128)} %hidden_bias.1) | copy-start | bytes 24580
  10.5 20.2 %copy-start.50 = (f32[32]{0:T(128)S(1)}, f32[32]{0:T(128)}, u32[]{:S(2)}) copy-start(f32[32]{0:T(128)} %param.37) | copy-start | bytes 388
  30.7 14.8 %copy-start.8 = (bf16[1,512,1536]{2,1,0:T(8,128)(2,1)S(1)}, bf16[1,512,1536]{2,1,0:T(8,128)(2,1)}, u32[]{:S(2)}) copy-start(bf16[1,512,1536]{2,1,0:T(8,128)(2,1)} %param.27) | copy-start | bytes 4718596
  56.6 13.4 %copy-start.17 = (bf16[2048,128]{1,0:T(8,128)(2,1)S(1)}, bf16[2048,128]{1,0:T(8,128)(2,1)}, u32[]{:S(2)}) copy-start(bf16[2048,128]{1,0:T(8,128)(2,1)} %get-tuple-element.410.wide) | copy-start | bytes 1572868 | tf_op jit(solution)/shard_map/cond
  56.7 13.4 %copy-start.24 = (bf16[512,512]{1,0:T(8,128)(2,1)S(1)}, bf16[512,512]{1,0:T(8,128)(2,1)}, u32[]{:S(2)}) copy-start(bf16[512,512]{1,0:T(8,128)(2,1)} %get-tuple-element.425.weight_out) | copy-start | bytes 1572868 | tf_op jit(solution)/shard_map/cond
  84.5 11.4 %collective-permute-start = (f32[32,1024]{1,0:T(8,128)}, f32[32,1024]{1,0:T(8,128)S(1)}, u32[]{:S(2)}, u32[]{:S(2)}) collective-permute-start(f32[32,1024]{1,0:T(8,128)} %get-tuple-element.791), channel_id=1, source_target_pairs={{16,0},{17,1},{18,2},{19,3},{20,4},{21,5},{22,6},{23,7},{24,8},{25... | collective-permute-start | bytes 393224 | tf_op jit(solution)/shard_map/ppermute | solution.py:1345
  102.6 16.7 %copy-start.22 = (bf16[1024,512]{1,0:T(8,128)(2,1)S(1)}, bf16[1024,512]{1,0:T(8,128)(2,1)}, u32[]{:S(2)}) copy-start(bf16[1024,512]{1,0:T(8,128)(2,1)} %get-tuple-element.524.context) | copy-start | bytes 3145732 | tf_op jit(solution)/shard_map/cond
  102.6 16.7 %copy-start.29 = (bf16[2,1024,128]{2,1,0:T(8,128)(2,1)S(1)}, bf16[2,1024,128]{2,1,0:T(8,128)(2,1)}, u32[]{:S(2)}) copy-start(bf16[2,1024,128]{2,1,0:T(8,128)(2,1)} %get-tuple-element.525.key_mark) | copy-start | bytes 1572868 | tf_op jit(solution)/shard_map/cond
  102.6 16.7 %copy-start.32 = (bf16[1024,512]{1,0:T(8,128)(2,1)S(1)}, bf16[1024,512]{1,0:T(8,128)(2,1)}, u32[]{:S(2)}) copy-start(bf16[1024,512]{1,0:T(8,128)(2,1)} %get-tuple-element.519.query) | copy-start | bytes 3145732 | tf_op jit(solution)/shard_map/cond
  102.6 16.7 %copy-start.53 = (s32[16]{0:T(128)S(1)}, s32[16]{0:T(128)}, u32[]{:S(2)}) copy-start(s32[16]{0:T(128)} %get-tuple-element.518.windows) | copy-start | bytes 196 | tf_op jit(solution)/shard_map/cond
  119.2 25.6 %copy-start.9 = (bf16[512,1536]{1,0:T(8,128)(2,1)S(1)}, bf16[512,1536]{1,0:T(8,128)(2,1)}, u32[]{:S(2)}) copy-start(bf16[512,1536]{1,0:T(8,128)(2,1)} %get-tuple-element.531.weight) | copy-start | bytes 4718596 | tf_op jit(solution)/shard_map/cond
  119.2 25.6 %copy-start.12 = (f32[2048,32]{1,0:T(8,128)S(1)}, f32[2048,32]{1,0:T(8,128)}, u32[]{:S(2)}) copy-start(f32[2048,32]{1,0:T(8,128)} %get-tuple-element.502.unit) | copy-start | bytes 786436 | tf_op jit(solution)/shard_map/cond
  119.2 25.6 %copy-start.19 = (bf16[2048,128]{1,0:T(8,128)(2,1)S(1)}, bf16[2048,128]{1,0:T(8,128)(2,1)}, u32[]{:S(2)}) copy-start(bf16[2048,128]{1,0:T(8,128)(2,1)} %get-tuple-element.529.wide) | copy-start | bytes 1572868 | tf_op jit(solution)/shard_map/cond
  151.2 42.8 %copy-start.48 = (f32[32,512]{1,0:T(8,128)S(1)}, f32[32,512]{1,0:T(8,128)}, u32[]{:S(2)}) copy-start(f32[32,512]{1,0:T(8,128)} %get-tuple-element.836) | copy-start | bytes 196612
  159.7 10.8 %copy-start.14 = (f32[2048,32]{1,0:T(8,128)S(1)}, f32[2048,32]{1,0:T(8,128)}, u32[]{:S(2)}) copy-start(f32[2048,32]{1,0:T(8,128)} %get-tuple-element.606.unit) | copy-start | bytes 786436 | tf_op jit(solution)/shard_map/cond
  159.8 10.8 %copy-start.39 = (f32[32,8192]{1,0:T(8,128)S(1)}, f32[32,8192]{1,0:T(8,128)}, u32[]{:S(2)}) copy-start(f32[32,8192]{1,0:T(8,128)} %get-tuple-element.609.table_turned) | copy-start | bytes 3145732 | tf_op jit(solution)/shard_map/cond
  159.8 10.8 %copy-start.44 = (f32[1024,32]{1,0:T(8,128)S(1)}, f32[1024,32]{1,0:T(8,128)}, u32[]{:S(2)}) copy-start(f32[1024,32]{1,0:T(8,128)} %get-tuple-element.607.latent_first) | copy-start | bytes 393220 | tf_op jit(solution)/shard_map/cond
  170.5 10.4 %copy-start.23 = (bf16[1024,512]{1,0:T(8,128)(2,1)S(1)}, bf16[1024,512]{1,0:T(8,128)(2,1)}, u32[]{:S(2)}) copy-start(bf16[1024,512]{1,0:T(8,128)(2,1)} %get-tuple-element.599.context) | copy-start | bytes 3145732 | tf_op jit(solution)/shard_map/cond
  170.5 10.4 %copy-start.36 = (bf16[1024,512]{1,0:T(8,128)(2,1)S(1)}, bf16[1024,512]{1,0:T(8,128)(2,1)}, u32[]{:S(2)}) copy-start(bf16[1024,512]{1,0:T(8,128)(2,1)} %get-tuple-element.601.n1) | copy-start | bytes 3145732 | tf_op jit(solution)/shard_map/cond
  187.0 7.1 %collective-permute-start.1 = (f32[32,1024]{1,0:T(8,128)}, f32[32,1024]{1,0:T(8,128)S(1)}, u32[]{:S(2)}, u32[]{:S(2)}) collective-permute-start(f32[32,1024]{1,0:T(8,128)} %get-tuple-element.832), channel_id=1, source_target_pairs={{16,0},{17,1},{18,2},{19,3},{20,4},{21,5},{22,6},{23,7},{24,8},{25... | collective-permute-start | bytes 393224 | tf_op jit(solution)/shard_map/ppermute | solution.py:1367
  194.0 29.6 %copy-start.27 = (bf16[2,1024,128]{2,1,0:T(8,128)(2,1)S(1)}, bf16[2,1024,128]{2,1,0:T(8,128)(2,1)}, u32[]{:S(2)}) copy-start(bf16[2,1024,128]{2,1,0:T(8,128)(2,1)} %copy-done.26) | copy-start | bytes 1572868
  195.6 16.7 %copy-start.40 = (bf16[1024,2048]{1,0:T(8,128)(2,1)S(1)}, bf16[1024,2048]{1,0:T(8,128)(2,1)}, u32[]{:S(2)}) copy-start(bf16[1024,2048]{1,0:T(8,128)(2,1)} %get-tuple-element.635.active) | copy-start | bytes 12582916 | tf_op jit(solution)/shard_map/cond
  321.9 1.4 copy-start.2
  392.0 2.1 copy-start
  394.1 4.3 %copy-start.1 = (f32[768,512]{1,0:T(8,128)}, f32[768,512]{1,0:T(8,128)S(1)}, u32[]{:S(2)}) copy-start(f32[768,512]{1,0:T(8,128)S(1)} %get-tuple-element.862.misc) | copy-start | bytes 4718596

commit v5 on v4

--- a/solution.py
+++ b/solution.py
@@ -1,5 +1,6 @@
 import functools
 import math
+from typing import Any, NamedTuple
 
 import jax
 import jax.numpy as jnp
@@ -9,6 +10,7 @@
 from jax.sharding import PartitionSpec as P
 
 HEAD = 64
+SECTION, DP = "section", "dp"
 BF = jnp.bfloat16
 F32 = jnp.float32
 LOG2E = math.log2(math.e)
@@ -41,6 +43,11 @@
     return dot(left[0], right[0], dims) + dot(left[0], right[1], dims) + dot(left[1], right[0], dims)
 
 
+def unit_of(values):
+    scale = lax.rsqrt(jnp.sum(values * values, -1, keepdims=True) + NORM_EPS)
+    return values * scale, scale
+
+
 def norm_parts(values):
     center = values - jnp.mean(values, -1, keepdims=True)
     inverse = lax.rsqrt(jnp.mean(center * center, -1, keepdims=True) + NORM_EPS)
@@ -71,19 +78,22 @@
 
     lax.fori_loop(0, table.shape[0] // block, turn, 0)
 
-    def some(step, carry):
-        for inner in range(16):
-            token = step * 16 + inner
-            raw[pl.ds(token, 1), :] = table[pl.ds(index[token], 1), :]
-        return carry
-
-    lax.fori_loop(0, count // 16, some, 0)
+    length = segments.shape[1]
+    for row in range(index.shape[0]):
+
+        def some(step, carry):
+            for inner in range(16):
+                token = step * 16 + inner
+                raw[pl.ds(row * length + token, 1), :] = table[pl.ds(index[row, token], 1), :]
+            return carry
+
+        lax.fori_loop(0, length // 16, some, 0)
+
     values = raw[...]
     values = values * lax.rsqrt(jnp.sum(values * values, -1, keepdims=True) + NORM_EPS)
     unit[...] = values
     high, low = split(values)
     wide[...] = jnp.concatenate([high, low, high, jnp.zeros_like(high)], 1)
-    length = segments.shape[1]
     lane = lanes((length, 128)) & 63
     for row in range(segments.shape[0]):
         owner = jnp.broadcast_to(segments[row : row + 1, :], (128, length)).T
@@ -93,7 +103,7 @@
 
 
 def gather_codes(index, table_turned, segments):
-    count, width = index.shape[0], table_turned.shape[0]
+    count, width = index.size, table_turned.shape[0]
     vmem = pl.BlockSpec(memory_space=pltpu.VMEM)
     mark = jax.ShapeDtypeStruct(segments.shape + (128,), BF)
     return pl.pallas_call(
@@ -108,7 +118,6 @@
         ),
         scratch_shapes=[pltpu.VMEM(table_turned.shape[::-1], F32), pltpu.VMEM((count, width), F32)],
         compiler_params=PARAMS,
-        name="gather_codes",
     )(index, table_turned, segments)
 
 
@@ -117,17 +126,19 @@
     width = unit.shape[1]
     half = count // 2
     total[...] = jnp.zeros_like(total)
-    rows[:half, :] = 2.0 * (unit[:half, :] - latent_first[...])
-    rows[half:, :] = 2.0 * (unit[half:, :] - latent_second[...])
-
-    def some(step, carry):
-        for inner in range(8):
-            token = step * 8 + inner
-            here = pl.ds(index[token], 1)
-            total[here, :] = total[here, :] + rows[pl.ds(token, 1), :]
-        return carry
-
-    lax.fori_loop(0, count // 8, some, 0)
+    for row, latent in enumerate((latent_first, latent_second)):
+        here = slice(row * half, (row + 1) * half)
+        code, unused = unit_of(latent[...])
+        rows[here, :] = 2.0 * (unit[here, :] - code)
+
+        def some(step, carry):
+            for inner in range(8):
+                token = step * 8 + inner
+                place = pl.ds(index[row, token], 1)
+                total[place, :] = total[place, :] + rows[pl.ds(row * half + token, 1), :]
+            return carry
+
+        lax.fori_loop(0, half // 8, some, 0)
     block = out.shape[1]
 
     def back(step, carry):
@@ -156,7 +167,6 @@
         out_shape=book_shape(table_turned, width),
         scratch_shapes=[pltpu.VMEM(table_turned.shape[::-1], F32), pltpu.VMEM(unit.shape, F32)],
         compiler_params=PARAMS,
-        name="scatter_codes",
     )(index, unit, *latents, table_turned)
 
 
@@ -282,9 +292,7 @@
     def _():
         last_hat, unused = norm_parts(total)
         code = last_hat * output_gain[0:1, :] + head_bias[0:1, :]
-        latent = code_product(code, down[...]) + down_bias[0:1, :]
-        scale = lax.rsqrt(jnp.sum(latent * latent, -1, keepdims=True) + NORM_EPS)
-        latent_out[...] = latent * scale
+        latent_out[...] = code_product(code, down[...]) + down_bias[0:1, :]
 
 
 def code_product(values, weight):
@@ -292,7 +300,7 @@
 
 
 def tail_back_kernel(
-    side, result, cotangent, unit, latent_in, output_gain, head_bias, down, down_bias,
+    side, result, cotangent, unit, latent_in, latent, output_gain, head_bias, down,
     weight_last, slope, weight_in, mid, gains, biases, weight_out, *refs, adding
 ):
     before, refs = refs[: 2 * adding], refs[2 * adding :]
@@ -310,9 +318,7 @@
     def _():
         hat, inverse = norm_parts(result[...])
         normed = hat * output_gain[0:1, :] + head_bias[0:1, :]
-        latent = code_product(normed, down[...]) + down_bias[0:1, :]
-        scale = lax.rsqrt(jnp.sum(latent * latent, -1, keepdims=True) + NORM_EPS)
-        code = latent * scale
+        code, scale = unit_of(latent[...])
         code_grad = latent_in[...].T + 0.5 * (code - unit[...])
         latent_grad = scale * (code_grad - code * jnp.sum(code * code_grad, -1, keepdims=True))
         pieces = split(latent_grad)
@@ -424,19 +430,19 @@
     value_total[...] = jnp.zeros_like(value_total)
 
     def one(turn, carry):
-        number, pair = turn // pairs, turn % pairs
+        number = turn
         at = (row * steps + number) * 2
 
         def run(start, extent):
             attend_back_block(
-                number, start, extent, pair * 128, 1,
+                number, start, extent, 0, pairs,
                 query, marks, key, value, context_grad, key_mark, grad_mark, query_grad, key_total, value_total,
             )
 
         for_windows(windows[at], windows[at + 1], count, run)
         return carry
 
-    lax.fori_loop(0, steps * pairs, one, 0)
+    lax.fori_loop(0, steps, one, 0)
     key_grad[...] = (key_total[...] * (1.0 / LOG2E)).astype(BF)
     value_grad[...] = value_total[...].astype(BF)
 
@@ -519,7 +525,7 @@
         put(dot(n1[...], value_grad[...], TN), 1)
 
 
-def weight_call(kernel, operands, in_specs, steps, before, name):
+def weight_call(kernel, operands, in_specs, steps, before):
     width = operands[1].shape[1]
     out_spec = pl.BlockSpec((2 * width, width), lambda step: (step, 0))
     aliases = {}
@@ -534,14 +540,13 @@
         out_shape=jax.ShapeDtypeStruct((2 * steps * width, width), F32),
         input_output_aliases=aliases,
         compiler_params=PARAMS,
-        name=name,
     )(*operands)
 
 
-def hidden_weights(kept, back, before=None):
-    operands = [kept["active"], back["out_low"], kept["n2"], back["preact_low"]]
-    count, width = kept["n2"].shape
-    first = kept["active"].shape[1] // (2 * width)
+def hidden_weights(kept, late, before=None):
+    operands = [kept.active, late.out_low, kept.n2, late.preact_low]
+    count, width = kept.n2.shape
+    first = kept.active.shape[1] // (2 * width)
     full = pl.BlockSpec((count, width), lambda step: (0, 0))
     in_specs = [
         pl.BlockSpec((count, 2 * width), lambda step: (0, jnp.minimum(step, first - 1))),
@@ -549,14 +554,14 @@
         full,
         pl.BlockSpec((count, 2 * width), lambda step: (0, jnp.maximum(step - first, 0))),
     ]
-    return weight_call(hidden_weight_kernel, operands, in_specs, 2 * first, before, "hidden_weights")
-
-
-def attention_weights(kept, back, before=None):
-    operands = [kept["context"], back["branch_low"], kept["n1"]]
-    operands += [back["query_grad"], back["key_grad"], back["value_grad"]]
-    full = pl.BlockSpec(kept["n1"].shape, lambda step: (0, 0))
-    return weight_call(attention_weight_kernel, operands, [full] * 6, 2, before, "attention_weights")
+    return weight_call(hidden_weight_kernel, operands, in_specs, 2 * first, before)
+
+
+def attention_weights(kept, late, early, before=None):
+    operands = [kept.context, late.branch_low, kept.n1]
+    operands += list(early[:3])
+    full = pl.BlockSpec(kept.n1.shape, lambda step: (0, 0))
+    return weight_call(attention_weight_kernel, operands, [full] * 6, 2, before)
 
 
 MESH = pl.DeviceIdType.MESH
@@ -571,7 +576,7 @@
 class Ring:
     @staticmethod
     def scratch(arrays, ways, crossing):
-        chips = lax.axis_size("dp") // 2
+        chips = lax.axis_size(DP) // 2
         sizes = [array.shape[0] // (2 * count * chips) for array, count in zip(arrays, ways)]
         shapes = [(count, chips, size, array.shape[1]) for array, count, size in zip(arrays, ways, sizes)]
         buffers = [pltpu.VMEM(shape, F32) for shape in shapes] * 3
@@ -585,7 +590,7 @@
     def __init__(self, sources, results, ways, crossing, scratch):
         number = len(sources)
         take = lambda at: scratch[at * number : (at + 1) * number]
-        self.chips = lax.axis_size("dp") // 2
+        self.chips = lax.axis_size(DP) // 2
         self.sources, self.results, self.ways, self.crossing = sources, results, ways, crossing
         self.own, self.pair, self.run = take(0), take(1), take(2)
         (
@@ -595,16 +600,16 @@
         self.far = scratch[13 * number :]
         self.sizes = [run.shape[2] for run in self.run]
         self.lanes = [(which, way) for way in range(max(ways)) for which in range(number) if way < ways[which]]
-        place = lax.axis_index("dp")
+        place = lax.axis_index(DP)
         chip, self.core = place // 2, place % 2
         column, odd = chip // 2, chip % 2
         chips = self.chips
         self.position = (1 - odd) * column + odd * (chips - 1 - column)
-        self.other = {"dp": chip * 2 + (1 - self.core)}
-        self.across = {"section": 1 - lax.axis_index("section")}
+        self.other = {DP: chip * 2 + (1 - self.core)}
+        self.across = {SECTION: 1 - lax.axis_index(SECTION)}
         self.targets = (
-            {"dp": ring_chip((self.position + 1) % chips, chips) * 2 + self.core},
-            {"dp": ring_chip((self.position + chips - 1) % chips, chips) * 2 + self.core},
+            {DP: ring_chip((self.position + 1) % chips, chips) * 2 + self.core},
+            {DP: ring_chip((self.position + chips - 1) % chips, chips) * 2 + self.core},
         )
 
     def greet(self):
@@ -721,8 +726,8 @@
             self.run[which][way, 0] = self.own[which][way, 0] + self.pair[which][way, 0]
             self.pass_on(which, way, 0).start()
 
-    def gather(self, step):
-        for which, way in self.lanes:
+    def gather(self, step, lanes=None):
+        for which, way in self.lanes if lanes is None else lanes:
             run, own, pair = self.run[which], self.own[which], self.pair[which]
             self.load(which, way, step).wait()
             self.swap(which, way, step).wait_recv()
@@ -752,8 +757,8 @@
         self.aside(which, way, 0, True).start()
         self.keep(which, way).start()
 
-    def pass_out(self, step):
-        for which, way in self.lanes:
+    def pass_out(self, step, lanes=None):
+        for which, way in self.lanes if lanes is None else lanes:
             self.incoming(which, way, step).wait_recv()
 
             @pl.when(step < self.chips - 1)
@@ -803,8 +808,8 @@
 
 
 def sum_all(main, misc):
-    if lax.axis_size("dp") < LEAST_DEVICES:
-        return main, lax.psum(misc, "section")
+    if lax.axis_size(DP) < LEAST_DEVICES:
+        return main, lax.psum(misc, SECTION)
     arrays = (main, misc)
     return pl.pallas_call(
         sum_kernel,
@@ -813,7 +818,6 @@
         out_shape=tuple(jax.ShapeDtypeStruct(array.shape, F32) for array in arrays),
         scratch_shapes=Ring.scratch(arrays, SUM_WAYS, 1),
         compiler_params=pltpu.CompilerParams(collective_id=0, has_side_effects=True, vmem_limit_bytes=40 << 20),
-        name="sum_all",
     )(*arrays)
 
 
@@ -828,7 +832,7 @@
     part, grad_mark, query_grad, key_total, value_total, key_grad, value_grad, in_sems, part_sem, out_sems,
     *scratch,
 ):
-    encoder = lax.axis_index("section") == 0
+    encoder = lax.axis_index(SECTION) == 0
     ring = Ring((hidden,), (hidden_out,), FINISH_WAYS, None, scratch) if scratch else None
     count, width = query.shape
     narrow = down.shape[0]
@@ -878,7 +882,7 @@
 
     def attention_piece(turn):
         attend_back_block(
-            turn // 2, 0, count, (turn % 2) * (width // 2), pairs // 2,
+            turn // pairs, 0, count, (turn % pairs) * 128, 1,
             query_in, marks_in, key_in, value_in, grad_in, key_mark_in, grad_mark, query_grad, key_total, value_total,
         )
 
@@ -906,17 +910,20 @@
         ):
             pl.when(number == choice)(functools.partial(put, left, right))
 
+    halves = (ring.lanes[:2], ring.lanes[2:]) if ring else (None, None)
+    chips = ring.chips if ring else 8
+    pieces = steps * pairs
+
     def summing(step):
-        if ring:
-            ring.gather(step)
-
-        @pl.when(encoder)
-        def _():
-            attention_piece(step - 1)
-
-    chips = ring.chips if ring else 8
-    pieces = 2 * steps
-    inside = min(chips - 1, pieces)
+        for half in range(2):
+            if ring:
+                ring.gather(step, halves[half])
+
+            @pl.when(encoder)
+            def _():
+                attention_piece(2 * (step - 1) + half)
+
+    inside = min(chips - 1, pieces // 2)
     loop(1, inside + 1, summing)
     if ring:
         loop(inside + 1, chips, ring.gather)
@@ -924,18 +931,18 @@
 
     @pl.when(encoder)
     def _():
-        loop(inside, pieces, attention_piece)
+        loop(2 * inside, pieces, attention_piece)
         key_grad[...] = (key_total[...] * (1.0 / LOG2E)).astype(BF)
         value_grad[...] = value_total[...].astype(BF)
 
     def spreading(step):
-        if ring:
-            ring.pass_out(step)
-
-        @pl.when(encoder)
-        def _():
-            entry_piece(step - 1)
-            weight_piece(step - 1)
+        for half, work in enumerate((entry_piece, weight_piece)):
+            if ring:
+                ring.pass_out(step, halves[half])
+
+            @pl.when(encoder)
+            def _():
+                work(step - 1)
 
     loop(1, steps + 1, spreading)
     stores = [
@@ -958,17 +965,17 @@
             store.wait()
 
 
-def finish_row(work, kept, late, early, up, book, hidden, attention):
-    count, width = kept["n1"].shape
-    alone = lax.axis_size("dp") < LEAST_DEVICES
+def finish_row(work, kept, late, early, book, hidden, attention):
+    count, width = kept.n1.shape
+    alone = lax.axis_size(DP) < LEAST_DEVICES
     operands = [
-        hidden, attention, kept["query"], kept["marks"], kept["key"], kept["value"], late["context_grad"],
-        kept["context"], work.key_mark, work.edges, late["mid_grad"], work.attention_in, late["branch_low"], kept["n1"],
-        work.gains, book, late["head_late"], up, late["sums_late"], early,
+        hidden, attention, kept.query, kept.marks, kept.key, kept.value, late.context_grad,
+        kept.context, work.key_mark, work.edges, late.mid_grad, work.attention_in, late.branch_low, kept.n1,
+        work.gains, book, late.head, early.head, late.sums, early.sums,
     ]
     hbm, vmem = pl.BlockSpec(memory_space=pl.ANY), pl.BlockSpec(memory_space=pltpu.VMEM)
     rows = book.shape[0] + 2 * work.narrow + 64
-    unit = 16 * lax.axis_size("dp")
+    unit = 16 * lax.axis_size(DP)
     low = pltpu.VMEM((count, width), BF)
     wide = pltpu.VMEM((count, width), F32)
     scratch = [low] * 6 + [pltpu.VMEM((count, 128), BF), low, wide, pltpu.VMEM(work.attention_in.shape, BF), low, low]
@@ -991,14 +998,14 @@
         scratch_shapes=scratch,
         input_output_aliases={1: 1},
         compiler_params=pltpu.CompilerParams(vmem_limit_bytes=58 << 20, **settings),
-        name="finish_row",
     )(*operands)
     return (hidden,) + tuple(outs[1:]) if alone else outs
 
 
 def unpack_kernel(
     side, hidden, attention, misc, first_entry, second_entry, first_result, second_result,
-    hidden_out, hidden_in, attention_out, attention_in, book, edge, held, head, rows, ins, outs, row_ins, row_outs,
+    hidden_out, hidden_in, attention_out, attention_in, edge, book, gains, biases, bias, last_gain, head_bias, down, down_last,
+    up, held, head, rows, ins, outs, row_ins, row_outs,
 ):
     width = hidden.shape[1]
     narrow = book.shape[0]
@@ -1033,6 +1040,19 @@
     loads[-1].wait()
     for number in range(book.shape[1] // width):
         book[:, number * width : (number + 1) * width] = head[number * narrow : (number + 1) * narrow, :]
+    at = book.shape[0] * book.shape[1] // width
+    down[...] = head[at : at + narrow, :]
+    up[...] = head[at + narrow : at + 2 * narrow, :]
+    at += 2 * narrow
+    last_gain[...] = head[at + 8 : at + 9, :]
+    head_bias[0:1, :] = head[at + 9 : at + 10, :]
+    head_bias[1:2, :] = head[at + 52 : at + 53, :]
+    down_last[...] = head[at + 10 : at + 11, :narrow]
+    mine = jnp.where(side[0] == 0, head[at : at + 32, :], head[at + 32 : at + 64, :])
+    bias[...] = mine[:steps, :]
+    for out, places in ((gains, (18, 6)), (biases, (16, 17, 5, 19, 7, 4))):
+        for number, place in enumerate(places):
+            out[number : number + 1, :] = mine[place : place + 1, :]
     for store in stores:
         store.wait()
 
@@ -1041,19 +1061,22 @@
     width = hidden.shape[1]
     features = hidden.shape[0] // 2
     tiles = (hidden.shape[0] + attention.shape[0]) // width
+    narrow = table_turned.shape[0]
+    rows = table_turned.size // width + 2 * narrow + 64
     shapes = (
-        (features, width), (width, features), (width, width), (width, 3 * width), table_turned.shape,
-        (2,) + ends[0].shape,
+        (features, width), (width, features), (width, width), (width, 3 * width), (2,) + ends[0].shape,
+        table_turned.shape, (2, width), (6, width), (features // width, width), (1, width), (2, width),
+        (narrow, width), (1, narrow), (narrow, width),
     )
     hbm, vmem = pl.BlockSpec(memory_space=pl.ANY), pl.BlockSpec(memory_space=pltpu.VMEM)
     return pl.pallas_call(
         unpack_kernel,
         in_specs=[pl.BlockSpec(memory_space=pltpu.SMEM)] + [hbm] * 7,
-        out_specs=[hbm] * 4 + [vmem, hbm],
+        out_specs=[hbm] * 5 + [vmem] * 9,
         out_shape=tuple(jax.ShapeDtypeStruct(shape, F32) for shape in shapes),
         scratch_shapes=[
             pltpu.VMEM((tiles, width, width), F32),
-            pltpu.VMEM((table_turned.size // width, width), F32),
+            pltpu.VMEM((rows, width), F32),
             pltpu.VMEM((2,) + ends[0].shape, F32),
             pltpu.SemaphoreType.DMA((tiles + 1,)),
             pltpu.SemaphoreType.DMA((tiles,)),
@@ -1061,7 +1084,6 @@
             pltpu.SemaphoreType.DMA((2,)),
         ],
         compiler_params=PARAMS,
-        name="unpack",
     )(side, hidden, attention, misc, *ends)
 
 
@@ -1070,19 +1092,48 @@
 
 
 def unwritten(shapes):
-    return pl.pallas_call(
+    leaves, tree = jax.tree.flatten(shapes)
+    arrays = pl.pallas_call(
         nothing_kernel,
-        out_specs=[pl.BlockSpec(memory_space=pl.ANY)] * len(shapes),
-        out_shape=tuple(shapes),
-        name="unwritten",
+        out_specs=[pl.BlockSpec(memory_space=pl.ANY)] * len(leaves),
+        out_shape=tuple(leaves),
     )()
-
-
-KEPT = ("n1", "query", "key", "value", "context", "marks", "mid", "n2", "active", "slope", "result", "latent")
-BACK = (
-    "out_low", "preact_low", "mid_grad", "branch_low", "context_grad", "query_grad", "key_grad", "value_grad",
-    "entry", "latent_out", "sums_late", "sums_early", "head_late", "head_early",
-)
+    return jax.tree.unflatten(tree, arrays)
+
+
+class Kept(NamedTuple):
+    n1: Any
+    query: Any
+    key: Any
+    value: Any
+    context: Any
+    marks: Any
+    mid: Any
+    n2: Any
+    active: Any
+    slope: Any
+    result: Any
+    latent: Any
+
+
+class Late(NamedTuple):
+    out_low: Any
+    preact_low: Any
+    mid_grad: Any
+    branch_low: Any
+    context_grad: Any
+    sums: Any
+    head: Any
+
+
+class Early(NamedTuple):
+    query_grad: Any
+    key_grad: Any
+    value_grad: Any
+    entry: Any
+    latent_out: Any
+    sums: Any
+    head: Any
 
 
 class Rows:
@@ -1099,36 +1150,22 @@
         self.rows, self.count, self.width = edges.shape
         self.hidden = self.hidden_in.shape[1]
         self.narrow = unit.shape[1]
-
-    def kept_shapes(self):
         n, d, f = self.count, self.width, self.hidden
-        table = dict(
-            n1=(d, BF), query=(d, BF), key=(d, BF), value=(d, BF), context=(d, BF), marks=(d, BF),
-            mid=(d, F32), n2=(d, BF), active=(f, BF), slope=(f, BF), latent=(self.narrow, F32),
-        )
-        table["result"] = (d, F32)
-        return {name: jax.ShapeDtypeStruct((n, size), kind) for name, (size, kind) in table.items()}
-
-    def back_shapes(self):
-        n, d, f = self.count, self.width, self.hidden
-        table = dict(
-            out_low=(n, d, BF), preact_low=(n, f, BF), mid_grad=(n, d, F32), branch_low=(n, d, BF),
-            query_grad=(n, d, BF), key_grad=(n, d, BF), value_grad=(n, d, BF),
-            latent_out=(self.narrow, n, F32), sums_late=(16, d, F32), sums_early=(16, d, F32),
-            head_late=(self.narrow, d, F32), head_early=(self.narrow, d, F32),
-        )
-        table["entry"] = table["mid_grad"]
-        table["context_grad"] = table["out_low"]
-        return {name: jax.ShapeDtypeStruct((a, b), kind) for name, (a, b, kind) in table.items()}
+        shape = jax.ShapeDtypeStruct
+        low, tall, wide = shape((n, d), BF), shape((n, f), BF), shape((n, d), F32)
+        sums, head = shape((16, d), F32), shape((self.narrow, d), F32)
+        self.kept = Kept(low, low, low, low, low, low, wide, low, tall, tall, wide, shape((n, self.narrow), F32))
+        self.late = Late(low, tall, wide, low, low, sums, head)
+        self.early = Early(low, low, low, wide, shape((self.narrow, n), F32), sums, head)
+
+    def side_spec(self):
+        return pl.BlockSpec(memory_space=pltpu.SMEM)
+
+    def tokens(self, array):
+        return pl.BlockSpec((TOKENS, array.shape[1]), lambda step: (step, 0))
 
     def turned(self, array):
         return pl.BlockSpec((array.shape[0], TOKENS), lambda step: (0, step))
-
-    def side_spec(self):
-        return pl.BlockSpec(memory_space=pltpu.SMEM)
-
-    def tokens(self, array):
-        return pl.BlockSpec((TOKENS, array.shape[1]), lambda step: (step, 0))
 
     def whole(self, array):
         return pl.BlockSpec(array.shape, lambda step: (0,) * len(array.shape))
@@ -1146,7 +1183,7 @@
         steps = self.count // TOKENS
         return pl.BlockSpec((TOKENS, self.narrow), lambda step: (row * steps + step, 0))
 
-    def call(self, kernel, in_specs, operands, outs, out_specs, name, scratch=()):
+    def call(self, kernel, in_specs, operands, outs, out_specs, scratch=()):
         return pl.pallas_call(
             kernel,
             grid=(self.count // TOKENS,),
@@ -1155,10 +1192,9 @@
             out_shape=tuple(outs),
             scratch_shapes=list(scratch),
             compiler_params=PARAMS,
-            name=name,
         )(*operands)
 
-    def attention_call(self, kernel, row, operands, outs, name, scratch=()):
+    def attention_call(self, kernel, row, operands, outs, scratch=()):
         half = self.width // 2
 
         def spec(array):
@@ -1177,117 +1213,89 @@
             ),
             out_shape=tuple(outs),
             compiler_params=PARAMS,
-            name=name,
         )(self.windows, *operands)
 
     def forward(self, row):
-        shapes = self.kept_shapes()
+        shapes = self.kept
         entry = (self.edges, self.wide, self.up, self.head_bias)
-        kept = {}
-        names = ("n1", "query", "key", "value")
-        outs = self.call(
+        outs = shapes[:4]
+        n1, query, key, value = self.call(
             project_kernel,
             [self.side_spec()] + self.entry_specs(row)
             + [self.whole(self.gains), self.whole(self.biases), self.whole(self.attention_in)],
             (self.side,) + entry + (self.gains, self.biases, self.attention_in),
-            [shapes[name] for name in names],
-            [self.tokens(shapes[name]) for name in names],
-            "project",
-        )
-        kept.update(zip(names, outs))
-        names = ("context", "marks")
-        outs = self.attention_call(
-            attend_kernel, row,
-            (kept["query"], kept["key"], kept["value"], self.query_mark, self.key_mark),
-            [shapes[name] for name in names],
-            "attend",
-        )
-        kept.update(zip(names, outs))
-        names = ("mid", "n2", "active", "slope", "result", "latent")
+            outs,
+            [self.tokens(array) for array in outs],
+        )
+        context, marks = self.attention_call(
+            attend_kernel, row, (query, key, value, self.query_mark, self.key_mark), shapes[4:6]
+        )
         consts = (
             self.attention_out, self.gains, self.biases, self.hidden_in, self.hidden_bias, self.hidden_out,
             self.output_gain, self.down, self.down_bias,
         )
+        outs = shapes[6:]
         outs = self.call(
             hidden_kernel,
-            [self.side_spec()] + self.entry_specs(row) + [self.tokens(kept["context"])]
+            [self.side_spec()] + self.entry_specs(row) + [self.tokens(context)]
             + [self.whole(array) for array in consts],
-            (self.side,) + entry + (kept["context"],) + consts,
-            [shapes[name] for name in names],
-            [self.tokens(shapes[name]) for name in names],
-            "hidden",
-        )
-        kept.update(zip(names, outs))
-        return kept
-
-    def backward(self, row, kept, latent_in, former=None):
-        back = self.backward_late(row, kept, latent_in, former)
-        back.update(self.backward_early(row, kept, back, former))
-        return back
+            (self.side,) + entry + (context,) + consts,
+            outs,
+            [self.tokens(array) for array in outs],
+        )
+        return Kept(n1, query, key, value, context, marks, *outs)
+
+    def backward(self, row, kept, latent_in, former=(None, None)):
+        late = self.backward_late(row, kept, latent_in, former[0])
+        return late, self.backward_early(row, kept, late, former[1])
 
     def backward_late(self, row, kept, latent_in, former=None):
-        shapes = self.back_shapes()
-        prior = () if former is None else (former["sums_late"], former["head_late"])
+        prior = () if former is None else (former.sums, former.head)
         adding = int(former is not None)
-        names = ("out_low", "preact_low", "mid_grad", "branch_low", "context_grad", "sums_late", "head_late")
-        consts = (self.output_gain, self.head_bias, self.down, self.down_bias, self.hidden_out)
+        consts = (self.output_gain, self.head_bias, self.down, self.hidden_out)
         late = (self.gains, self.biases, self.attention_out)
-        outs = self.call(
+        outs = self.late
+        return Late(*self.call(
             functools.partial(tail_back_kernel, adding=adding),
-            [self.side_spec(), self.tokens(kept["result"]), self.entry_specs(row)[0], self.unit_spec(row),
-             self.turned(latent_in)]
+            [self.side_spec(), self.tokens(kept.result), self.entry_specs(row)[0], self.unit_spec(row),
+             self.turned(latent_in), self.tokens(kept.latent)]
             + [self.whole(array) for array in consts]
-            + [self.tokens(kept["slope"]), self.whole(self.hidden_in), self.tokens(kept["mid"])]
+            + [self.tokens(kept.slope), self.whole(self.hidden_in), self.tokens(kept.mid)]
             + [self.whole(array) for array in late + prior],
-            (self.side, kept["result"], self.edges, self.unit, latent_in) + consts
-            + (kept["slope"], self.hidden_in, kept["mid"]) + late + prior,
-            [shapes[name] for name in names],
-            [self.tokens(shapes[name]) for name in names[:5]] + [self.whole(shapes[name]) for name in names[5:]],
-            "tail_back",
+            (self.side, kept.result, self.edges, self.unit, latent_in, kept.latent) + consts
+            + (kept.slope, self.hidden_in, kept.mid) + late + prior,
+            outs,
+            [self.tokens(array) for array in outs[:5]] + [self.whole(array) for array in outs[5:]],
             scratch=[pltpu.VMEM((TOKENS, self.width), F32)],
-        )
-        return dict(zip(names, outs))
+        ))
 
     def backward_early(self, row, kept, late, former=None):
-        shapes = self.back_shapes()
         adding = int(former is not None)
-        back = {}
-        names = ("query_grad", "key_grad", "value_grad")
         half = self.width // 2
-        outs = self.attention_call(
+        grads = tuple(self.attention_call(
             attend_back_kernel, row,
-            (kept["query"], kept["marks"], kept["key"], kept["value"], late["context_grad"], kept["context"],
-             self.key_mark),
-            [shapes[name] for name in names],
-            "attend_back",
+            (kept.query, kept.marks, kept.key, kept.value, late.context_grad, kept.context, self.key_mark),
+            self.early[:3],
             scratch=[
                 pltpu.VMEM((self.count, half), BF),
                 pltpu.VMEM((self.count, half), F32),
                 pltpu.VMEM((self.count, half), F32),
             ],
-        )
-        back.update(zip(names, outs))
-        names = ("entry", "latent_out", "sums_early", "head_early")
-        prior = () if former is None else (former["sums_early"], former["head_early"])
-        grads = (back["query_grad"], back["key_grad"], back["value_grad"])
+        ))
+        prior = () if former is None else (former.sums, former.head)
+        outs = self.early[3:]
         outs = self.call(
             functools.partial(entry_back_kernel, adding=adding),
             [self.side_spec()] + self.entry_specs(row) + [self.unit_spec(row)]
             + [self.tokens(array) for array in grads]
             + [self.whole(self.attention_in), self.whole(self.gains), self.whole(self.biases),
-               self.tokens(late["mid_grad"])] + [self.whole(array) for array in prior],
+               self.tokens(late.mid_grad)] + [self.whole(array) for array in prior],
             (self.side, self.edges, self.wide, self.up, self.head_bias, self.unit) + grads
-            + (self.attention_in, self.gains, self.biases, late["mid_grad"]) + prior,
-            [shapes[name] for name in names],
-            [self.tokens(shapes["entry"]), self.turned(shapes["latent_out"])] + [self.whole(shapes[name]) for name in names[2:]],
-            "entry_back",
-        )
-        back.update(zip(names, outs))
-        return back
-
-
-def as_list(table, names):
-    return [table[name] for name in names]
+            + (self.attention_in, self.gains, self.biases, late.mid_grad) + prior,
+            outs,
+            [self.tokens(outs[0]), self.turned(outs[1])] + [self.whole(array) for array in outs[2:]],
+        )
+        return Early(*grads, *outs)
 
 
 def windows_of(segments):
@@ -1306,127 +1314,99 @@
     boundary, segments, code_index, attention_in, attention_out, hidden_in, hidden_out, block_gains,
     block_biases, hidden_bias, output_gain, head_bias, down_weight, down_bias, up_weight, codebook,
 ):
-    section = lax.axis_index("section")
+    section = lax.axis_index(SECTION)
     encoder = section == 0
     side = section.astype(jnp.int32)[None]
     edges = boundary[0]
     rows, count, width = edges.shape
     hidden = hidden_in.shape[2]
-    index = code_index.reshape(-1)
     table_turned = codebook.T
-    unit, wide, query_mark, key_mark = gather_codes(index, table_turned, segments)
+    unit, wide, query_mark, key_mark = gather_codes(code_index, table_turned, segments)
     work = Rows(
         side, edges, wide, unit, windows_of(segments), query_mark, key_mark,
         (
             attention_in[0], attention_out[0], hidden_in[0], hidden_out[0], block_gains[0], block_biases[0],
             hidden_bias,
         ),
-        (
-            output_gain[None], head_bias, down_weight.T, down_bias[None], up_weight,
-        ),
+        (output_gain[None], head_bias, down_weight.T, down_bias[None], up_weight),
     )
-    kept_shapes = as_list(work.kept_shapes(), KEPT)
-    back_shapes = as_list(work.back_shapes(), BACK)
     book_out = book_shape(table_turned, width)
-    hidden_out_shape = jax.ShapeDtypeStruct((2 * hidden, width), F32)
+    hidden_shape = jax.ShapeDtypeStruct((2 * hidden, width), F32)
     attention_shape = jax.ShapeDtypeStruct((4 * width, width), F32)
     quiet = jnp.zeros((unit.shape[1], count), F32)
     first_kept = work.forward(0)
 
     def encoder_second():
-        return as_list(work.forward(1), KEPT), list(unwritten(back_shapes))
+        kept = work.forward(1)
+        book = scatter_codes(code_index, unit, (first_kept.latent, kept.latent), table_turned, width)
+        return (kept, *unwritten((work.late, work.early)), book)
 
     def decoder_first():
-        return list(unwritten(kept_shapes)), as_list(work.backward(0, first_kept, quiet), BACK)
-
-    kept_a, back_a = lax.cond(encoder, encoder_second, decoder_first)
-    back_a = dict(zip(BACK, back_a))
-    kept_a = dict(zip(KEPT, kept_a))
-    latent_in = lax.ppermute(back_a["latent_out"], "section", [(1, 0)])
+        kept, book = unwritten((work.kept, book_out))
+        return (kept, *work.backward(0, first_kept, quiet), book)
+
+    kept_a, late_a, early_a, book = lax.cond(encoder, encoder_second, decoder_first)
+    latent_in = lax.ppermute(early_a.latent_out, SECTION, [(1, 0)])
 
     def encoder_third():
-        return list(unwritten(kept_shapes)), as_list(work.backward(0, first_kept, latent_in), BACK)
+        late, early = work.backward(0, first_kept, latent_in)
+        weights = hidden_weights(first_kept, late), attention_weights(first_kept, late, early)
+        return unwritten(work.kept), late, early, weights
 
     def decoder_third():
-        return as_list(work.forward(1), KEPT), list(unwritten(back_shapes))
-
-    kept_b, back_b = lax.cond(encoder, encoder_third, decoder_third)
-    kept_b, back_b = dict(zip(KEPT, kept_b)), dict(zip(BACK, back_b))
-
-    def encoder_fourth():
-        book = scatter_codes(index, unit, (first_kept["latent"], kept_a["latent"]), table_turned, width)
-        weights = hidden_weights(first_kept, back_b), attention_weights(first_kept, back_b)
-        return list(unwritten(back_shapes)), weights, book
-
-    def decoder_fourth():
-        *weights, book = unwritten([hidden_out_shape, attention_shape, book_out])
-        return as_list(work.backward(1, kept_b, quiet, back_a), BACK), tuple(weights), book
-
-    back_c, weights_c, book = lax.cond(encoder, encoder_fourth, decoder_fourth)
-    back_c = dict(zip(BACK, back_c))
-    latent_in_second = lax.ppermute(back_c["latent_out"], "section", [(1, 0)])
-    late_names = ("branch_low", "mid_grad", "context_grad", "sums_late", "head_late")
+        kept = work.forward(1)
+        return (kept, *work.backward(1, kept, quiet, (late_a, early_a)), unwritten((hidden_shape, attention_shape)))
+
+    kept_b, late_b, early_b, weights_b = lax.cond(encoder, encoder_third, decoder_third)
+    latent_in_second = lax.ppermute(early_b.latent_out, SECTION, [(1, 0)])
 
     def encoder_fifth():
-        late = work.backward_late(1, kept_a, latent_in_second, back_b)
-        total = hidden_weights(kept_a, late, weights_c[0])
-        return total, weights_c[1], as_list(late, late_names), back_b["sums_early"]
+        late = work.backward_late(1, kept_a, latent_in_second, late_b)
+        return hidden_weights(kept_a, late, weights_b[0]), weights_b[1], late[2:]
 
     def decoder_fifth():
-        total = hidden_weights(kept_b, back_c, hidden_weights(first_kept, back_a))
-        attention = attention_weights(kept_b, back_c, attention_weights(first_kept, back_a))
-        return total, attention, as_list(back_c, late_names), back_c["sums_early"]
-
-    hidden_total, attention_total, late, early = lax.cond(encoder, encoder_fifth, decoder_fifth)
-    late = dict(zip(late_names, late))
+        total = hidden_weights(kept_b, late_b, hidden_weights(first_kept, late_a))
+        attention = attention_weights(kept_b, late_b, early_b, attention_weights(first_kept, late_a, early_a))
+        return total, attention, (*unwritten(work.late[2:5]), late_b.sums, late_b.head)
+
+    hidden_total, attention_total, late = lax.cond(encoder, encoder_fifth, decoder_fifth)
+    late = Late(None, None, *late)
     hidden_total, attention_total, misc, second_entry = finish_row(
-        work, kept_a, late, early, back_c["head_early"], book, hidden_total, attention_total
+        work, kept_a, late, early_b, book, hidden_total, attention_total
     )
     attention_total, misc = sum_all(attention_total, misc)
-    hidden_out_grad, hidden_in_grad, attention_out_grad, attention_in_grad, book, edge = unpack(
+    (
+        hidden_out_grad, hidden_in_grad, attention_out_grad, attention_in_grad, edge, book, gains, biases, bias,
+        last_gain, head, down_grad, down_last, up_grad,
+    ) = unpack(
         side, hidden_total, attention_total, misc,
-        (back_b["entry"], second_entry, first_kept["result"], kept_b["result"]), table_turned,
+        (early_b.entry, second_entry, first_kept.result, kept_b.result), table_turned,
     )
-    narrow = unit.shape[1]
-    pieces, at = [], book_out.shape[0]
-    for size in (narrow, narrow, 16, 16, 16, 16):
-        pieces.append(misc[at : at + size])
-        at += size
-    down_grad, up_grad, first_late, first_early, second_late, second_early = pieces
-    late = jnp.where(encoder, first_late, second_late)
-    early = jnp.where(encoder, first_early, second_early)
     return (
         edge[None],
         attention_in_grad[None],
         attention_out_grad[None],
         hidden_in_grad[None],
         hidden_out_grad[None],
-        jnp.stack([early[2], late[6]])[None],
-        jnp.stack([early[0], early[1], late[5], early[3], late[7], late[4]])[None],
-        late[: hidden // width].reshape(1, hidden),
-        first_late[8],
-        jnp.stack([first_late[9], second_early[4]]),
+        gains[None],
+        biases[None],
+        bias.reshape(1, hidden),
+        last_gain[0],
+        head,
         down_grad.T,
-        first_late[10, :narrow],
+        down_last[0],
         up_grad,
         book.T,
     )
 
 
 def solution(mesh):
+    wide, split_last, flat = P(SECTION, DP, None, None), P(SECTION, None, None), P(SECTION, None)
+    blocks = (split_last,) * 6 + (flat,)
     return jax.shard_map(
         on_device,
         mesh=mesh,
-        in_specs=(
-            P("section", "dp", None, None), P("dp", None), P("dp", None),
-            P("section", None, None), P("section", None, None), P("section", None, None),
-            P("section", None, None), P("section", None, None), P("section", None, None),
-            P("section", None), P(), P(), P(), P(), P(), P(),
-        ),
-        out_specs=(
-            P("section", "dp", None, None), P("section", None, None), P("section", None, None),
-            P("section", None, None), P("section", None, None), P("section", None, None),
-            P("section", None, None), P("section", None), P(), P(), P(), P(), P(), P(),
-        ),
+        in_specs=(wide, P(DP, None), P(DP, None)) + blocks + (P(),) * 6,
+        out_specs=(wide,) + blocks + (P(),) * 6,
         check_vma=False,
     )

time: 418 us -> 425 us (1.017)
  waiting for transfers between devices: 15.8 us -> 25.8 us
  loops' own time: 21.3 us -> 15.1 us
  Pallas kernels: 357 us -> 363 us
    ppermute x2, waiting for transfers between devices: 15.8 us -> 25.8 us  [the longest x1 20 us: on_device(): latent_in_second = lax.ppermute(early_b.latent_out, SECTION, [(1, 0)])]
    another operation x3 -> x2, loops' own time: 21.2 us -> 15.1 us  [the longest x1 8.52 us: on_device(): lax.cond(encoder, encoder_third, decoder_third)]
    pallas_call x1, Pallas kernels: 68.7 us -> 73.8 us  [sum_all(): pl.pallas_call(sum_kernel, in_specs=[pl.BlockSpec(memory_space=pl.ANY)] *...]
where the time goes in v5:
time: 425 us; the launch traced here: 418 us
  Pallas kernels  363 us (85%)
  waiting for transfers between devices  25.8 us (6%)
  loops' own time  15.1 us (4%)
  local copies, waits for them, and re-layouts  10.5 us (2%)
    pallas_call x1, Pallas kernels, finish_row(): pl.pallas_call(finish_kernel, in_specs=[hbm] * 14 + [vmem] * 6, out_specs...  97 us
    pallas_call x7, Pallas kernels, call(): pl.pallas_call(kernel, grid=(self.count // TOKENS,), in_specs=in_specs, o...  77.6 us
    pallas_call x1, Pallas kernels, sum_all(): pl.pallas_call(sum_kernel, in_specs=[pl.BlockSpec(memory_space=pl.ANY)] *...  73.8 us
    pallas_call x3, Pallas kernels, attention_call(): pl.pallas_call(functools.partial(kernel, row=row), grid_spec=pltpu.Prefet...  49.9 us
    pallas_call x3, Pallas kernels, weight_call(): pl.pallas_call(kernel, grid=(steps,), in_specs=in_specs, out_specs=out_sp...  28.2 us
    ppermute x1, waiting for transfers between devices, on_device(): latent_in_second = lax.ppermute(early_b.latent_out, SECTION, [(1, 0)])  20 us
    pallas_call x1, Pallas kernels, scatter_codes(): pl.pallas_call(scatter_kernel, in_specs=[pl.BlockSpec(memory_space=pltpu....  13.8 us
    pallas_call x1, Pallas kernels, unpack(): pl.pallas_call(unpack_kernel, in_specs=[pl.BlockSpec(memory_space=pltpu.S...  13.3 us
  transfers between devices with their start and end apart: 2, of which 2 were waited for; matrix products, arithmetic and copies ran while one was open for 0% of the time, Pallas kernels for 0%

profile of v5, /device:TPU:0, one launch (start us, length us, event | category | flops | bytes accessed | tf_op | source)
XLA Modules:
  0.0 418.4 jit_solution(15887761477327849236)
XLA Ops:
  0.7 0.7 reshape.55
  1.4 0.1 fusion
  1.4 0.1 copy.48
  1.5 0.1 copy.47
  1.6 0.2 select_reduce_fusion.1
  1.9 0.1 copy.44
  2.0 0.1 reshape.56.windows
  2.1 0.7 copy.51
  2.8 9.4 %shard_map.263 = (f32[2048,32]{1,0:T(8,128)}, bf16[2048,128]{1,0:T(8,128)(2,1)S(1)}, bf16[2,1024,128]{2,1,0:T(8,128)(2,1)S(1)}, bf16[2,1024,128]{2,1,0:T(8,128)(2,1)S(1)}) custom-call(s32[2,1024]{1,0:T(2,128)} %index.1, f32[32,8192]{1,0:T(8,128)} %bitcast.66, s32[2,1024]{1,0:T(2,128)} %segments.1), custom_call_target="tpu_custom_call" | custom-call | tf_op jit(solution)/shard_map/pallas_call | solution.py:109
  12.2 0.0 copy-start.4
  12.2 0.0 copy-start.37
  12.2 0.0 copy-start.38
  12.3 0.0 copy-start.41
  12.3 0.0 copy-start.47
  12.3 7.0 %shard_map.264 = (bf16[1024,512]{1,0:T(8,128)(2,1)}, bf16[1024,512]{1,0:T(8,128)(2,1)}, bf16[1024,512]{1,0:T(8,128)(2,1)}, bf16[1024,512]{1,0:T(8,128)(2,1)}) custom-call(s32[1]{0:T(128)} %bitcast.side, bf16[2,1024,512]{2,1,0:T(8,128)(2,1)} %bitcast.34, bf16[2048,128]{1,0:T(8,128)(2,1)S(1)} %get-tuple-element.635.wide, f32[32,512]{1,0:T(8,128)} %up.3, ...), custom_call_target="tpu_custom_call" | custom-call | tf_op jit(solution)/shard_map/pallas_call | solution.py:1187
  19.3 13.0 %shard_map.265 = (bf16[1024,512]{1,0:T(8,128)(2,1)}, bf16[1024,512]{1,0:T(8,128)(2,1)}) custom-call(s32[16]{0:T(128)S(1)} %reshape.56.windows, bf16[1024,512]{1,0:T(8,128)(2,1)} %get-tuple-element.636.query, bf16[1024,512]{1,0:T(8,128)(2,1)} %get-tuple-element.637.key, bf16[1024,512]{1,0:T(8,128)(2,1)} %get-tuple-element.638.value, ...), custom_call_target="tpu_custom_call" | custom-call | tf_op jit(solution)/shard_map/pallas_call | solution.py:1205
  32.4 0.0 copy-start.8
  32.4 0.0 copy-start.46
  32.4 14.4 %shard_map.266 = (f32[1024,512]{1,0:T(8,128)}, bf16[1024,512]{1,0:T(8,128)(2,1)}, bf16[1024,2048]{1,0:T(8,128)(2,1)}, bf16[1024,2048]{1,0:T(8,128)(2,1)}, f32[1024,512]{1,0:T(8,128)}, /*index=5*/f32[1024,32]{1,0:T(8,128)}) custom-call(s32[1]{0:T(128)} %bitcast.side, bf16[2,1024,512]{2,1,0:T(8,128)(2,1)S(1)} %bitcast.35, bf16[2048,128]{1,0:T(8,128)(2,1)} %copy-done.15, ...), custom_call_target="tpu_custom_call" | custom-call | tf_op jit(solution)/shard_map/pallas_call | solution.py:1187
  46.9 53.6 %conditional.3 = (bf16[1024,512]{1,0:T(8,128)(2,1)}, bf16[1024,512]{1,0:T(8,128)(2,1)}, bf16[1024,512]{1,0:T(8,128)(2,1)}, bf16[1024,512]{1,0:T(8,128)(2,1)}, bf...) conditional(s32[]{:T(128)} %convert_element_type.2, ...), branch_computations={%region_2.3_spmd, %region_3.4_spmd} | conditional | bytes 11665716 | solution.py:1348
  53.4 5.4 %branch_1_fun.13 = (bf16[1024,512]{1,0:T(8,128)(2,1)}, bf16[1024,512]{1,0:T(8,128)(2,1)}, bf16[1024,512]{1,0:T(8,128)(2,1)}, bf16[1024,512]{1,0:T(8,128)(2,1)}) custom-call(s32[1]{0:T(128)} %get-tuple-element.337.side, bf16[2,1024,512]{2,1,0:T(8,128)(2,1)S(1)} %get-tuple-element.338.edge, bf16[2048,128]{1,0:T(8,128)(2,1)} %get-tuple-element.339.wide, ...), custom_call_target="tpu_custom_call" | custom-call | tf_op jit(solution)/shard_map/cond/branch_1_fun/pallas_call | solution.py:1187
  58.8 13.4 %branch_1_fun.14 = (bf16[1024,512]{1,0:T(8,128)(2,1)}, bf16[1024,512]{1,0:T(8,128)(2,1)}) custom-call(s32[16]{0:T(128)S(1)} %get-tuple-element.349.windows, bf16[1024,512]{1,0:T(8,128)(2,1)} %get-tuple-element.792.query, bf16[1024,512]{1,0:T(8,128)(2,1)} %get-tuple-element.793.key, bf16[1024,512]{1,0:T(8,128)(2,1)} %get-tuple-element.794.value, ...), custom_call_target="tpu_custom_call" | custom-call | tf_op jit(solution)/shard_map/cond/branch_1_fun/pallas_call | solution.py:1205
  72.2 14.3 %branch_1_fun.15 = (f32[1024,512]{1,0:T(8,128)}, bf16[1024,512]{1,0:T(8,128)(2,1)}, bf16[1024,2048]{1,0:T(8,128)(2,1)}, bf16[1024,2048]{1,0:T(8,128)(2,1)}, f32[1024,512]{1,0:T(8,128)}, /*index=5*/f32[1024,32]{1,0:T(8,128)}) custom-call(s32[1]{0:T(128)} %get-tuple-element.337.side, bf16[2,1024,512]{2,1,0:T(8,128)(2,1)S(1)} %get-tuple-element.338.edge, ...), custom_call_target="tpu_custom_call" | custom-call | tf_op jit(solution)/shard_map/cond/branch_1_fun/pallas_call | solution.py:1187
  86.6 13.8 %branch_1_fun.17 = f32[512,512]{1,0:T(8,128)} custom-call(s32[2,1024]{1,0:T(2,128)S(1)} %get-tuple-element.378.index, f32[2048,32]{1,0:T(8,128)S(1)} %copy-done.12, f32[1024,32]{1,0:T(8,128)} %get-tuple-element.380.latent_first, f32[1024,32]{1,0:T(8,128)} %get-tuple-element.802.latent_second, f32[32,8192]{1,0:T(8,128)} %get-tuple-element.381.table_turned), custom_call_target="tpu_custom_call" | custom-call | tf_op jit(solution)/shard_map/cond/branch_1_fun/pallas_call | solution.py:163
  100.4 1.3 collective-permute-start
  101.7 5.8 %collective-permute-done = f32[32,1024]{1,0:T(8,128)S(1)} collective-permute-done((f32[32,1024]{1,0:T(8,128)}, f32[32,1024]{1,0:T(8,128)S(1)}, u32[]{:S(2)}, u32[]{:S(2)}) %collective-permute-start) | collective-permute-done | bytes 131104 | tf_op jit(solution)/shard_map/ppermute | solution.py:1349
  107.5 70.3 %conditional.4 = (bf16[1024,512]{1,0:T(8,128)(2,1)}, bf16[1024,512]{1,0:T(8,128)(2,1)}, bf16[1024,512]{1,0:T(8,128)(2,1)}, bf16[1024,2048]{1,0:T(8,128)(2,1)}, f...) conditional(s32[]{:T(128)} %convert_element_type.2, ...), branch_computations={%region_4.5_spmd, %region_5.6_spmd} | conditional | bytes 33423852 | solution.py:1360
  115.8 15.0 %branch_1_fun.19 = (bf16[1024,512]{1,0:T(8,128)(2,1)}, bf16[1024,2048]{1,0:T(8,128)(2,1)}, f32[1024,512]{1,0:T(8,128)}, bf16[1024,512]{1,0:T(8,128)(2,1)}, bf16[...) custom-call(s32[1]{0:T(128)} %get-tuple-element.438.side, ...), custom_call_target="tpu_custom_call" | custom-call | tf_op jit(solution)/shard_map/cond/branch_1_fun/pallas_call | solution.py:1187
  130.8 0.0 copy-start.14
  130.8 23.5 %branch_1_fun.20 = (bf16[1024,512]{1,0:T(8,128)(2,1)}, bf16[1024,512]{1,0:T(8,128)(2,1)}, bf16[1024,512]{1,0:T(8,128)(2,1)}) custom-call(s32[16]{0:T(128)S(1)} %get-tuple-element.459.windows, bf16[1024,512]{1,0:T(8,128)(2,1)S(1)} %copy-done.28, bf16[1024,512]{1,0:T(8,128)(2,1)} %get-tuple-element.461.marks, bf16[1024,512]{1,0:T(8,128)(2,1)} %get-tuple-element.462.key, ...), custom_call_target="tpu_custom_call" | custom-call | tf_op jit(solution)/shard_map/cond/branch_1_fun/pallas_call | solution.py:1205
  154.4 6.4 %branch_1_fun.21 = (f32[1024,512]{1,0:T(8,128)}, f32[32,1024]{1,0:T(8,128)}, f32[16,512]{1,0:T(8,128)}, f32[32,512]{1,0:T(8,128)S(1)}) custom-call(s32[1]{0:T(128)} %get-tuple-element.438.side, bf16[2,1024,512]{2,1,0:T(8,128)(2,1)S(1)} %get-tuple-element.440.cotangent.edge, bf16[2048,128]{1,0:T(8,128)(2,1)S(1)} %copy-done.19, ...), custom_call_target="tpu_custom_call" | custom-call | tf_op jit(solution)/shard_map/cond/branch_1_fun/pallas_call | solution.py:1187
  160.9 6.6 %branch_1_fun.23 = f32[2048,512]{1,0:T(8,128)} custom-call(bf16[1024,512]{1,0:T(8,128)(2,1)S(1)} %copy-done.20, bf16[1024,512]{1,0:T(8,128)(2,1)} %get-tuple-element.841.branch_low, bf16[1024,512]{1,0:T(8,128)(2,1)S(1)} %copy-done.32, bf16[1024,512]{1,0:T(8,128)(2,1)} %get-tuple-element.844.query_grad, bf16[1024,512]{1,0:T(8,128)(2,1)} %get-tuple-element.845.key_grad, ...), custom_call_target="tpu_custom_call" | custom-call | tf_op jit(solution)/shard_map/cond/branch_1_fun/pallas_call | solution.py:535
  167.4 10.2 %branch_1_fun.22 = f32[4096,512]{1,0:T(8,128)} custom-call(bf16[1024,2048]{1,0:T(8,128)(2,1)} %get-tuple-element.478.active, bf16[1024,512]{1,0:T(8,128)(2,1)} %get-tuple-element.839.out_low, bf16[1024,512]{1,0:T(8,128)(2,1)S(1)} %copy-done.33, bf16[1024,2048]{1,0:T(8,128)(2,1)} %get-tuple-element.840.preact_low), custom_call_target="tpu_custom_call" | custom-call | tf_op jit(solution)/shard_map/cond/branch_1_fun/pallas_call | solution.py:535
  177.8 1.3 collective-permute-start.1
  179.1 20.0 %collective-permute-done.1 = f32[32,1024]{1,0:T(8,128)S(1)} collective-permute-done((f32[32,1024]{1,0:T(8,128)}, f32[32,1024]{1,0:T(8,128)S(1)}, u32[]{:S(2)}, u32[]{:S(2)}) %collective-permute-start.1) | collective-permute-done | bytes 131104 | tf_op jit(solution)/shard_map/ppermute | solution.py:1361
  199.1 27.6 %conditional.5 = (f32[4096,512]{1,0:T(8,128)}, f32[2048,512]{1,0:T(8,128)}, f32[1024,512]{1,0:T(8,128)}, bf16[1024,512]{1,0:T(8,128)(2,1)}, bf16[1024,512]{1,0:T...) conditional(s32[]{:T(128)} %convert_element_type.2, (bf16[1024,2048]{1,0:T(8,128)(2,1)}, ...), branch_computations={%region_6.7_spmd, %region_7.8_spmd} | conditional | bytes 16973908 | solution.py:1372
  199.1 0.6 copy.159.refs_1_
  199.7 0.6 copy.158.refs_0_
  200.3 15.0 %branch_1_fun.24 = (bf16[1024,512]{1,0:T(8,128)(2,1)}, bf16[1024,2048]{1,0:T(8,128)(2,1)}, f32[1024,512]{1,0:T(8,128)}, bf16[1024,512]{1,0:T(8,128)(2,1)}, bf16[...) custom-call(s32[1]{0:T(128)} %get-tuple-element.507.side, ...), custom_call_target="tpu_custom_call" | custom-call | tf_op jit(solution)/shard_map/cond/branch_1_fun/pallas_call | solution.py:1187
  215.3 11.4 %branch_1_fun.25 = f32[4096,512]{1,0:T(8,128)} custom-call(bf16[1024,2048]{1,0:T(8,128)(2,1)S(1)} %copy-done.36, bf16[1024,512]{1,0:T(8,128)(2,1)} %get-tuple-element.525.out_low, bf16[1024,512]{1,0:T(8,128)(2,1)} %get-tuple-element.526.n2, bf16[1024,2048]{1,0:T(8,128)(2,1)} %get-tuple-element.527.preact_low, ...), custom_call_target="tpu_custom_call", output_to_operand_aliasing={{}: (4, {})} | custom-call | tf_op jit(solution)/shard_map/cond/branch_1_fun/pallas_call | solution.py:535
  226.7 97.0 %shard_map.267 = (f32[4096,512]{1,0:T(8,128)}, f32[2048,512]{1,0:T(8,128)}, f32[768,512]{1,0:T(8,128)}, f32[1024,512]{1,0:T(8,128)}) custom-call(f32[4096,512]{1,0:T(8,128)} %get-tuple-element.683.hidden, f32[2048,512]{1,0:T(8,128)} %get-tuple-element.684.attention, bf16[1024,512]{1,0:T(8,128)(2,1)} %get-tuple-element.685.query, ...), custom_call_target="tpu_custom_call", output_to_operand_aliasing={{1}: (1, {})} | custom-call | tf_op jit(solution)/shard_map/pallas_call | solution.py:988
  323.7 1.4 copy-done.2
  325.1 73.8 %shard_map.268 = (f32[2048,512]{1,0:T(8,128)S(1)}, f32[768,512]{1,0:T(8,128)S(1)}) custom-call(f32[2048,512]{1,0:T(8,128)} %get-tuple-element.700.main, f32[768,512]{1,0:T(8,128)S(1)} %copy-done.2), custom_call_target="tpu_custom_call" | custom-call | tf_op jit(solution)/shard_map/pallas_call | solution.py:814
  399.0 2.0 copy-done
  401.0 1.2 copy-done.1
  402.2 13.3 %shard_map.269 = (f32[2048,512]{1,0:T(8,128)}, f32[512,2048]{1,0:T(8,128)}, f32[512,512]{1,0:T(8,128)}, f32[512,1536]{1,0:T(8,128)}, f32[2,1024,512]{2,1,0:T(8,1...) custom-call(s32[1]{0:T(128)} %bitcast.side, ...), custom_call_target="tpu_custom_call" | custom-call | tf_op jit(solution)/shard_map/pallas_call | solution.py:1072
  415.5 1.3 copy.49
  416.8 1.3 copy.45
  (55 shorter events, 0.1 us)
Async XLA Ops:
  12.2 20.1 %copy-start.15 = (bf16[2048,128]{1,0:T(8,128)(2,1)}, bf16[2048,128]{1,0:T(8,128)(2,1)S(1)}, u32[]{:S(2)}) copy-start(bf16[2048,128]{1,0:T(8,128)(2,1)S(1)} %get-tuple-element.635.wide) | copy-start | bytes 1572868
  12.2 20.1 %copy-start.22 = (bf16[2,1024,128]{2,1,0:T(8,128)(2,1)}, bf16[2,1024,128]{2,1,0:T(8,128)(2,1)S(1)}, u32[]{:S(2)}) copy-start(bf16[2,1024,128]{2,1,0:T(8,128)(2,1)S(1)} %get-tuple-element.640.key_mark) | copy-start | bytes 1572868
  12.2 20.1 %copy-start.30 = (bf16[2,1024,128]{2,1,0:T(8,128)(2,1)}, bf16[2,1024,128]{2,1,0:T(8,128)(2,1)S(1)}, u32[]{:S(2)}) copy-start(bf16[2,1024,128]{2,1,0:T(8,128)(2,1)S(1)} %get-tuple-element.639.query_mark) | copy-start | bytes 1572868
  12.2 20.1 %copy-start.3 = (bf16[1,2,1024,512]{3,2,1,0:T(8,128)(2,1)S(1)}, bf16[1,2,1024,512]{3,2,1,0:T(8,128)(2,1)}, u32[]{:S(2)}) copy-start(bf16[1,2,1024,512]{3,2,1,0:T(8,128)(2,1)} %param.22) | copy-start | bytes 6291460
  12.2 20.1 %copy-start.4 = (bf16[1,512,2048]{2,1,0:T(8,128)(2,1)S(1)}, bf16[1,512,2048]{2,1,0:T(8,128)(2,1)}, u32[]{:S(2)}) copy-start(bf16[1,512,2048]{2,1,0:T(8,128)(2,1)} %param.27) | copy-start | bytes 6291460
  12.2 20.1 %copy-start.6 = (bf16[1,2048,512]{2,1,0:T(8,128)(2,1)S(1)}, bf16[1,2048,512]{2,1,0:T(8,128)(2,1)}, u32[]{:S(2)}) copy-start(bf16[1,2048,512]{2,1,0:T(8,128)(2,1)} %param.28) | copy-start | bytes 6291460
  12.2 20.1 %copy-start.29 = (f32[32,512]{1,0:T(8,128)S(1)}, f32[32,512]{1,0:T(8,128)}, u32[]{:S(2)}) copy-start(f32[32,512]{1,0:T(8,128)} %up.3) | copy-start | bytes 196612
  12.2 20.1 %copy-start.37 = (f32[512,32]{0,1:T(8,128)S(1)}, f32[512,32]{0,1:T(8,128)}, u32[]{:S(2)}) copy-start(f32[512,32]{0,1:T(8,128)} %param.34) | copy-start | bytes 196612
  12.2 20.1 %copy-start.38 = (f32[1,2,512]{2,1,0:T(2,128)S(1)}, f32[1,2,512]{2,1,0:T(2,128)}, u32[]{:S(2)}) copy-start(f32[1,2,512]{2,1,0:T(2,128)} %param.29) | copy-start | bytes 12292
  12.2 20.1 %copy-start.39 = (f32[2,512]{1,0:T(2,128)S(1)}, f32[2,512]{1,0:T(2,128)}, u32[]{:S(2)}) copy-start(f32[2,512]{1,0:T(2,128)} %head_bias.3) | copy-start | bytes 12292
  12.3 20.1 %copy-start.40 = (f32[512]{0:T(512)S(1)}, f32[512]{0:T(512)}, u32[]{:S(2)}) copy-start(f32[512]{0:T(512)} %param.32) | copy-start | bytes 6148
  12.3 20.1 %copy-start.41 = (f32[1,2048]{1,0:T(1,128)S(1)}, f32[1,2048]{1,0:T(1,128)}, u32[]{:S(2)}) copy-start(f32[1,2048]{1,0:T(1,128)} %hidden_bias.1) | copy-start | bytes 24580
  12.3 20.1 %copy-start.47 = (f32[32]{0:T(128)S(1)}, f32[32]{0:T(128)}, u32[]{:S(2)}) copy-start(f32[32]{0:T(128)} %param.35) | copy-start | bytes 388
  32.4 14.4 %copy-start.8 = (bf16[1,512,1536]{2,1,0:T(8,128)(2,1)S(1)}, bf16[1,512,1536]{2,1,0:T(8,128)(2,1)}, u32[]{:S(2)}) copy-start(bf16[1,512,1536]{2,1,0:T(8,128)(2,1)} %param.25) | copy-start | bytes 4718596
  32.4 14.4 %copy-start.46 = (s32[2,1024]{1,0:T(2,128)S(1)}, s32[2,1024]{1,0:T(2,128)}, u32[]{:S(2)}) copy-start(s32[2,1024]{1,0:T(2,128)} %index.1) | copy-start | bytes 24580
  58.8 13.4 %copy-start.17 = (bf16[2048,128]{1,0:T(8,128)(2,1)S(1)}, bf16[2048,128]{1,0:T(8,128)(2,1)}, u32[]{:S(2)}) copy-start(bf16[2048,128]{1,0:T(8,128)(2,1)} %get-tuple-element.339.wide) | copy-start | bytes 1572868 | tf_op jit(solution)/shard_map/cond
  72.2 14.4 %copy-start.12 = (f32[2048,32]{1,0:T(8,128)S(1)}, f32[2048,32]{1,0:T(8,128)}, u32[]{:S(2)}) copy-start(f32[2048,32]{1,0:T(8,128)} %get-tuple-element.379.unit) | copy-start | bytes 786436 | tf_op jit(solution)/shard_map/cond
  100.4 7.1 %collective-permute-start = (f32[32,1024]{1,0:T(8,128)}, f32[32,1024]{1,0:T(8,128)S(1)}, u32[]{:S(2)}, u32[]{:S(2)}) collective-permute-start(f32[32,1024]{1,0:T(8,128)} %get-tuple-element.656), channel_id=1, source_target_pairs={{16,0},{17,1},{18,2},{19,3},{20,4},{21,5},{22,6},{23,7},{24,8},{25... | collective-permute-start | bytes 393224 | tf_op jit(solution)/shard_map/ppermute | solution.py:1349
  115.7 15.1 %copy-start.20 = (bf16[1024,512]{1,0:T(8,128)(2,1)S(1)}, bf16[1024,512]{1,0:T(8,128)(2,1)}, u32[]{:S(2)}) copy-start(bf16[1024,512]{1,0:T(8,128)(2,1)} %get-tuple-element.465.context) | copy-start | bytes 3145732 | tf_op jit(solution)/shard_map/cond
  115.8 15.1 %copy-start.25 = (bf16[2,1024,128]{2,1,0:T(8,128)(2,1)S(1)}, bf16[2,1024,128]{2,1,0:T(8,128)(2,1)}, u32[]{:S(2)}) copy-start(bf16[2,1024,128]{2,1,0:T(8,128)(2,1)} %get-tuple-element.466.key_mark) | copy-start | bytes 1572868 | tf_op jit(solution)/shard_map/cond
  115.8 15.1 %copy-start.28 = (bf16[1024,512]{1,0:T(8,128)(2,1)S(1)}, bf16[1024,512]{1,0:T(8,128)(2,1)}, u32[]{:S(2)}) copy-start(bf16[1024,512]{1,0:T(8,128)(2,1)} %get-tuple-element.460.query) | copy-start | bytes 3145732 | tf_op jit(solution)/shard_map/cond
  130.8 23.6 %copy-start.10 = (bf16[512,1536]{1,0:T(8,128)(2,1)S(1)}, bf16[512,1536]{1,0:T(8,128)(2,1)}, u32[]{:S(2)}) copy-start(bf16[512,1536]{1,0:T(8,128)(2,1)} %get-tuple-element.472.weight) | copy-start | bytes 4718596 | tf_op jit(solution)/shard_map/cond
  130.8 23.6 %copy-start.14 = (f32[2048,32]{1,0:T(8,128)S(1)}, f32[2048,32]{1,0:T(8,128)}, u32[]{:S(2)}) copy-start(f32[2048,32]{1,0:T(8,128)} %get-tuple-element.441.unit) | copy-start | bytes 786436 | tf_op jit(solution)/shard_map/cond
  130.8 23.6 %copy-start.19 = (bf16[2048,128]{1,0:T(8,128)(2,1)S(1)}, bf16[2048,128]{1,0:T(8,128)(2,1)}, u32[]{:S(2)}) copy-start(bf16[2048,128]{1,0:T(8,128)(2,1)} %get-tuple-element.470.wide) | copy-start | bytes 1572868 | tf_op jit(solution)/shard_map/cond
  154.4 6.5 %copy-start.32 = (bf16[1024,512]{1,0:T(8,128)(2,1)S(1)}, bf16[1024,512]{1,0:T(8,128)(2,1)}, u32[]{:S(2)}) copy-start(bf16[1024,512]{1,0:T(8,128)(2,1)} %get-tuple-element.480.n1) | copy-start | bytes 3145732 | tf_op jit(solution)/shard_map/cond
  160.8 6.6 %copy-start.33 = (bf16[1024,512]{1,0:T(8,128)(2,1)S(1)}, bf16[1024,512]{1,0:T(8,128)(2,1)}, u32[]{:S(2)}) copy-start(bf16[1024,512]{1,0:T(8,128)(2,1)} %get-tuple-element.479.n2) | copy-start | bytes 3145732 | tf_op jit(solution)/shard_map/cond
  177.8 21.3 %collective-permute-start.1 = (f32[32,1024]{1,0:T(8,128)}, f32[32,1024]{1,0:T(8,128)S(1)}, u32[]{:S(2)}, u32[]{:S(2)}) collective-permute-start(f32[32,1024]{1,0:T(8,128)} %get-tuple-element.675), channel_id=1, source_target_pairs={{16,0},{17,1},{18,2},{19,3},{20,4},{21,5},{22,6},{23,7},{24,8},{25... | collective-permute-start | bytes 393224 | tf_op jit(solution)/shard_map/ppermute | solution.py:1361
  199.1 27.6 %copy-start.23 = (bf16[2,1024,128]{2,1,0:T(8,128)(2,1)S(1)}, bf16[2,1024,128]{2,1,0:T(8,128)(2,1)}, u32[]{:S(2)}) copy-start(bf16[2,1024,128]{2,1,0:T(8,128)(2,1)} %copy-done.22) | copy-start | bytes 1572868
  200.3 15.0 %copy-start.36 = (bf16[1024,2048]{1,0:T(8,128)(2,1)S(1)}, bf16[1024,2048]{1,0:T(8,128)(2,1)}, u32[]{:S(2)}) copy-start(bf16[1024,2048]{1,0:T(8,128)(2,1)} %get-tuple-element.506.active) | copy-start | bytes 12582916 | tf_op jit(solution)/shard_map/cond
  226.7 175.5 %copy-start.26 = (f32[1024,512]{1,0:T(8,128)S(1)}, f32[1024,512]{1,0:T(8,128)}, u32[]{:S(2)}) copy-start(f32[1024,512]{1,0:T(8,128)} %get-tuple-element.643.first_result) | copy-start | bytes 6291460
  323.7 1.4 copy-start.2
  399.0 2.0 copy-start
  401.0 1.2 copy-start.1

commit v6 on v5

--- a/solution.py
+++ b/solution.py
@@ -79,15 +79,14 @@
     lax.fori_loop(0, table.shape[0] // block, turn, 0)
 
     length = segments.shape[1]
-    for row in range(index.shape[0]):
-
-        def some(step, carry):
-            for inner in range(16):
-                token = step * 16 + inner
-                raw[pl.ds(row * length + token, 1), :] = table[pl.ds(index[row, token], 1), :]
-            return carry
-
-        lax.fori_loop(0, length // 16, some, 0)
+
+    def some(step, carry):
+        for inner in range(16):
+            token = step * 16 + inner
+            raw[pl.ds(token, 1), :] = table[pl.ds(index[token], 1), :]
+        return carry
+
+    lax.fori_loop(0, count // 16, some, 0)
 
     values = raw[...]
     values = values * lax.rsqrt(jnp.sum(values * values, -1, keepdims=True) + NORM_EPS)
@@ -103,7 +102,7 @@
 
 
 def gather_codes(index, table_turned, segments):
-    count, width = index.size, table_turned.shape[0]
+    count, width = index.shape[0], table_turned.shape[0]
     vmem = pl.BlockSpec(memory_space=pltpu.VMEM)
     mark = jax.ShapeDtypeStruct(segments.shape + (128,), BF)
     return pl.pallas_call(
@@ -131,14 +130,14 @@
         code, unused = unit_of(latent[...])
         rows[here, :] = 2.0 * (unit[here, :] - code)
 
-        def some(step, carry):
-            for inner in range(8):
-                token = step * 8 + inner
-                place = pl.ds(index[row, token], 1)
-                total[place, :] = total[place, :] + rows[pl.ds(row * half + token, 1), :]
-            return carry
-
-        lax.fori_loop(0, half // 8, some, 0)
+    def some(step, carry):
+        for inner in range(8):
+            token = step * 8 + inner
+            place = pl.ds(index[token], 1)
+            total[place, :] = total[place, :] + rows[pl.ds(token, 1), :]
+        return carry
+
+    lax.fori_loop(0, count // 8, some, 0)
     block = out.shape[1]
 
     def back(step, carry):
@@ -323,7 +322,7 @@
         latent_grad = scale * (code_grad - code * jnp.sum(code * code_grad, -1, keepdims=True))
         pieces = split(latent_grad)
         normed_grad = dot3(pieces, split(down[...]), NN)
-        head_weight[...] += dot3(pieces, split(normed), TN)
+        head_weight[...] += dot(pieces[0], normed.astype(BF), TN) + dot(pieces[1], normed.astype(BF), TN)
         sums[8:9, :] += column_sum(normed_grad * hat)
         sums[9:10, :] += column_sum(normed_grad)
         sums[10:11, :narrow] += column_sum(latent_grad)
@@ -826,12 +825,15 @@
 
 def finish_kernel(
     hidden, attention, query, marks, key, value, context_grad, context, key_mark, edges, mid_grad, weight, branch_low, n1,
-    gains, book, down, up, late, early,
-    hidden_out, attention_out, misc, entry,
-    query_in, marks_in, key_in, value_in, grad_in, context_in, key_mark_in, edge_in, mid_in, weight_in, branch_in, n1_in,
-    part, grad_mark, query_grad, key_total, value_total, key_grad, value_grad, in_sems, part_sem, out_sems,
-    *scratch,
+    *refs,
 ):
+    others, refs = refs[:12], refs[12:]
+    (
+        gains, book, down, up, late, early,
+        hidden_out, attention_out, misc, entry,
+        query_in, marks_in, key_in, value_in, grad_in, context_in, key_mark_in, edge_in, mid_in, weight_in, branch_in,
+        n1_in, part, grad_mark, query_grad, key_total, value_total, key_grad, value_grad, in_sems, part_sem, out_sems,
+    ), scratch = refs[:32], refs[32:]
     encoder = lax.axis_index(SECTION) == 0
     ring = Ring((hidden,), (hidden_out,), FINISH_WAYS, None, scratch) if scratch else None
     count, width = query.shape
@@ -847,6 +849,12 @@
     )
     loads = [pltpu.make_async_copy(*pair, in_sems.at[number]) for number, pair in enumerate(inputs)]
     part_load = pltpu.make_async_copy(attention, part, part_sem)
+    first_held = (query_in, marks_in, key_in, value_in, grad_in, grad_mark)
+    second_held = (context_in, branch_in, n1_in, query_grad, key_grad, value_grad)
+    other_loads = [
+        pltpu.make_async_copy(*pair, in_sems.at[number])
+        for number, pair in enumerate(zip(others, first_held + second_held))
+    ]
 
     if ring:
         ring.greet()
@@ -856,6 +864,11 @@
         for load in loads:
             load.start()
         part_load.start()
+
+    @pl.when(jnp.logical_not(encoder))
+    def _():
+        for load in other_loads:
+            load.start()
 
     if ring:
         ring.begin()
@@ -879,6 +892,8 @@
         misc[book.shape[0] + narrow : at, :] = up[...]
         misc[at + 32 : at + 48, :] = late[...]
         misc[at + 48 : at + 64, :] = early[...]
+        for load in other_loads:
+            load.wait()
 
     def attention_piece(turn):
         attend_back_block(
@@ -900,6 +915,15 @@
         misc[at + 19 : at + 20, :] += column_sum(normed_grad)
         mid_in[rows, :] = mid_in[rows, :] + norm_back(normed_grad, gains[0:1, :], hat, inverse)
 
+    def both_piece(number):
+        def put(first, second):
+            rows = pl.ds(pl.multiple_of(number * width, width), width)
+            part[rows, :] = dot(first[0][...], first[1][...], TN) + dot(second[0][...], second[1][...], TN)
+
+        for choice, places in enumerate(((0, 1), (2, 3), (2, 4), (2, 5))):
+            pairs_of = [[held[place] for place in places] for held in (first_held, second_held)]
+            pl.when(number == choice)(functools.partial(put, *pairs_of))
+
     def weight_piece(number):
         def put(left, right):
             rows = pl.ds(pl.multiple_of(number * width, width), width)
@@ -922,6 +946,10 @@
             @pl.when(encoder)
             def _():
                 attention_piece(2 * (step - 1) + half)
+
+        @pl.when(jnp.logical_not(encoder) & (step <= 4))
+        def _():
+            both_piece(step - 1)
 
     inside = min(chips - 1, pieces // 2)
     loop(1, inside + 1, summing)
@@ -952,27 +980,30 @@
 
     @pl.when(encoder)
     def _():
-        for store in stores:
-            store.start()
-
+        stores[0].start()
+
+    stores[1].start()
     if ring:
         loop(steps + 1, chips, ring.pass_out)
         ring.finish()
 
     @pl.when(encoder)
     def _():
-        for store in stores:
-            store.wait()
-
-
-def finish_row(work, kept, late, early, book, hidden, attention):
+        stores[0].wait()
+
+    stores[1].wait()
+
+
+def finish_row(work, kept, late, early, book, hidden, attention, others):
     count, width = kept.n1.shape
     alone = lax.axis_size(DP) < LEAST_DEVICES
     operands = [
         hidden, attention, kept.query, kept.marks, kept.key, kept.value, late.context_grad,
         kept.context, work.key_mark, work.edges, late.mid_grad, work.attention_in, late.branch_low, kept.n1,
-        work.gains, book, late.head, early.head, late.sums, early.sums,
     ]
+    for its_kept, its_late, its_early in others:
+        operands += [its_kept.context, its_late.branch_low, its_kept.n1, *its_early[:3]]
+    operands += [work.gains, book, late.head, early.head, late.sums, early.sums]
     hbm, vmem = pl.BlockSpec(memory_space=pl.ANY), pl.BlockSpec(memory_space=pltpu.VMEM)
     rows = book.shape[0] + 2 * work.narrow + 64
     unit = 16 * lax.axis_size(DP)
@@ -987,7 +1018,7 @@
         settings = dict(collective_id=1, has_side_effects=True)
     outs = pl.pallas_call(
         finish_kernel,
-        in_specs=[hbm] * 14 + [vmem] * 6,
+        in_specs=[hbm] * 26 + [vmem] * 6,
         out_specs=[hbm, hbm, vmem, hbm],
         out_shape=(
             jax.ShapeDtypeStruct(hidden.shape, F32),
@@ -1150,6 +1181,7 @@
         self.rows, self.count, self.width = edges.shape
         self.hidden = self.hidden_in.shape[1]
         self.narrow = unit.shape[1]
+        self.size = TOKENS
         n, d, f = self.count, self.width, self.hidden
         shape = jax.ShapeDtypeStruct
         low, tall, wide = shape((n, d), BF), shape((n, f), BF), shape((n, d), F32)
@@ -1162,31 +1194,31 @@
         return pl.BlockSpec(memory_space=pltpu.SMEM)
 
     def tokens(self, array):
-        return pl.BlockSpec((TOKENS, array.shape[1]), lambda step: (step, 0))
+        return pl.BlockSpec((self.size, array.shape[1]), lambda step: (step, 0))
 
     def turned(self, array):
-        return pl.BlockSpec((array.shape[0], TOKENS), lambda step: (0, step))
+        return pl.BlockSpec((array.shape[0], self.size), lambda step: (0, step))
 
     def whole(self, array):
         return pl.BlockSpec(array.shape, lambda step: (0,) * len(array.shape))
 
     def entry_specs(self, row):
-        steps = self.count // TOKENS
+        steps = self.count // self.size
         return [
-            pl.BlockSpec((None, TOKENS, self.width), lambda step: (row, step, 0)),
-            pl.BlockSpec((TOKENS, self.wide.shape[1]), lambda step: (row * steps + step, 0)),
+            pl.BlockSpec((None, self.size, self.width), lambda step: (row, step, 0)),
+            pl.BlockSpec((self.size, self.wide.shape[1]), lambda step: (row * steps + step, 0)),
             self.whole(self.up),
             self.whole(self.head_bias),
         ]
 
     def unit_spec(self, row):
-        steps = self.count // TOKENS
-        return pl.BlockSpec((TOKENS, self.narrow), lambda step: (row * steps + step, 0))
+        steps = self.count // self.size
+        return pl.BlockSpec((self.size, self.narrow), lambda step: (row * steps + step, 0))
 
     def call(self, kernel, in_specs, operands, outs, out_specs, scratch=()):
         return pl.pallas_call(
             kernel,
-            grid=(self.count // TOKENS,),
+            grid=(self.count // self.size,),
             in_specs=in_specs,
             out_specs=out_specs,
             out_shape=tuple(outs),
@@ -1219,6 +1251,7 @@
         shapes = self.kept
         entry = (self.edges, self.wide, self.up, self.head_bias)
         outs = shapes[:4]
+        self.size = 2 * TOKENS
         n1, query, key, value = self.call(
             project_kernel,
             [self.side_spec()] + self.entry_specs(row)
@@ -1227,6 +1260,7 @@
             outs,
             [self.tokens(array) for array in outs],
         )
+        self.size = TOKENS
         context, marks = self.attention_call(
             attend_kernel, row, (query, key, value, self.query_mark, self.key_mark), shapes[4:6]
         )
@@ -1266,7 +1300,7 @@
             + (kept.slope, self.hidden_in, kept.mid) + late + prior,
             outs,
             [self.tokens(array) for array in outs[:5]] + [self.whole(array) for array in outs[5:]],
-            scratch=[pltpu.VMEM((TOKENS, self.width), F32)],
+            scratch=[pltpu.VMEM((self.size, self.width), F32)],
         ))
 
     def backward_early(self, row, kept, late, former=None):
@@ -1321,6 +1355,7 @@
     rows, count, width = edges.shape
     hidden = hidden_in.shape[2]
     table_turned = codebook.T
+    code_index = code_index.reshape(-1)
     unit, wide, query_mark, key_mark = gather_codes(code_index, table_turned, segments)
     work = Rows(
         side, edges, wide, unit, windows_of(segments), query_mark, key_mark,
@@ -1337,42 +1372,41 @@
     first_kept = work.forward(0)
 
     def encoder_second():
-        kept = work.forward(1)
-        book = scatter_codes(code_index, unit, (first_kept.latent, kept.latent), table_turned, width)
-        return (kept, *unwritten((work.late, work.early)), book)
+        return (work.forward(1), *unwritten((work.late, work.early)))
 
     def decoder_first():
-        kept, book = unwritten((work.kept, book_out))
-        return (kept, *work.backward(0, first_kept, quiet), book)
-
-    kept_a, late_a, early_a, book = lax.cond(encoder, encoder_second, decoder_first)
+        return (unwritten(work.kept), *work.backward(0, first_kept, quiet))
+
+    kept_a, late_a, early_a = lax.cond(encoder, encoder_second, decoder_first)
     latent_in = lax.ppermute(early_a.latent_out, SECTION, [(1, 0)])
 
     def encoder_third():
         late, early = work.backward(0, first_kept, latent_in)
         weights = hidden_weights(first_kept, late), attention_weights(first_kept, late, early)
-        return unwritten(work.kept), late, early, weights
+        book = scatter_codes(code_index, unit, (first_kept.latent, kept_a.latent), table_turned, width)
+        return unwritten(work.kept), late, early, weights, book
 
     def decoder_third():
         kept = work.forward(1)
-        return (kept, *work.backward(1, kept, quiet, (late_a, early_a)), unwritten((hidden_shape, attention_shape)))
-
-    kept_b, late_b, early_b, weights_b = lax.cond(encoder, encoder_third, decoder_third)
+        weights, book = unwritten(((hidden_shape, attention_shape), book_out))
+        return (kept, *work.backward(1, kept, quiet, (late_a, early_a)), weights, book)
+
+    kept_b, late_b, early_b, weights_b, book = lax.cond(section == 1, decoder_third, encoder_third)
     latent_in_second = lax.ppermute(early_b.latent_out, SECTION, [(1, 0)])
 
     def encoder_fifth():
         late = work.backward_late(1, kept_a, latent_in_second, late_b)
-        return hidden_weights(kept_a, late, weights_b[0]), weights_b[1], late[2:]
+        return hidden_weights(kept_a, late, weights_b[0]), late[2:]
 
     def decoder_fifth():
         total = hidden_weights(kept_b, late_b, hidden_weights(first_kept, late_a))
-        attention = attention_weights(kept_b, late_b, early_b, attention_weights(first_kept, late_a, early_a))
-        return total, attention, (*unwritten(work.late[2:5]), late_b.sums, late_b.head)
-
-    hidden_total, attention_total, late = lax.cond(encoder, encoder_fifth, decoder_fifth)
+        return total, (*unwritten(work.late[2:5]), late_b.sums, late_b.head)
+
+    hidden_total, late = lax.cond(encoder, encoder_fifth, decoder_fifth)
     late = Late(None, None, *late)
     hidden_total, attention_total, misc, second_entry = finish_row(
-        work, kept_a, late, early_b, book, hidden_total, attention_total
+        work, kept_a, late, early_b, book, hidden_total, weights_b[1],
+        ((first_kept, late_a, early_a), (kept_b, late_b, early_b)),
     )
     attention_total, misc = sum_all(attention_total, misc)
     (

time: 425 us -> 408 us (0.960)
  Pallas kernels: 363 us -> 348 us
  waiting for transfers between devices: 25.8 us -> 15.2 us
  loops' own time: 15.1 us -> 20.9 us
    ppermute x1, waiting for transfers between devices: 20 us -> 5.77 us  [on_device(): latent_in_second = lax.ppermute(early_b.latent_out, SECTION, [(1, 0)])]
    another operation x3, loops' own time: 15.1 us -> 20.9 us  [the longest x1 14.7 us: on_device(): lax.cond(section == 1, decoder_third, encoder_third)]
    pallas_call x1, Pallas kernels: 73.8 us -> 68.7 us  [sum_all(): pl.pallas_call(sum_kernel, in_specs=[pl.BlockSpec(memory_space=pl.ANY)] *...]
    unnamed x45 -> x48, local copies, waits for them, and re-layouts: 8.26 us -> 8.98 us
where the time goes in v6:
time: 408 us; the launch traced here: 400 us
  Pallas kernels  348 us (85%)
  loops' own time  20.9 us (5%)
  waiting for transfers between devices  15.2 us (4%)
  local copies, waits for them, and re-layouts  11.3 us (3%)
    pallas_call x1, Pallas kernels, finish_row(): pl.pallas_call(finish_kernel, in_specs=[hbm] * 26 + [vmem] * 6, out_specs...  96 us
    pallas_call x7, Pallas kernels, call(): pl.pallas_call(kernel, grid=(self.count // self.size,), in_specs=in_specs...  75.4 us
    pallas_call x1, Pallas kernels, sum_all(): pl.pallas_call(sum_kernel, in_specs=[pl.BlockSpec(memory_space=pl.ANY)] *...  68.7 us
    pallas_call x3, Pallas kernels, attention_call(): pl.pallas_call(functools.partial(kernel, row=row), grid_spec=pltpu.Prefet...  49.7 us
    pallas_call x3, Pallas kernels, weight_call(): pl.pallas_call(kernel, grid=(steps,), in_specs=in_specs, out_specs=out_sp...  27.9 us
    another operation x1, loops' own time, on_device(): lax.cond(section == 1, decoder_third, encoder_third)  14.7 us
    pallas_call x1, Pallas kernels, unpack(): pl.pallas_call(unpack_kernel, in_specs=[pl.BlockSpec(memory_space=pltpu.S...  13.3 us
    pallas_call x1, Pallas kernels, scatter_codes(): pl.pallas_call(scatter_kernel, in_specs=[pl.BlockSpec(memory_space=pltpu....  10.6 us
  transfers between devices with their start and end apart: 2, of which 2 were waited for; matrix products, arithmetic and copies ran while one was open for 0% of the time, Pallas kernels for 0%

profile of v6, /device:TPU:0, one launch (start us, length us, event | category | flops | bytes accessed | tf_op | source)
XLA Modules:
  0.0 400.0 jit_solution(12319532957148214215)
XLA Ops:
  0.7 0.7 copy.53
  1.4 0.7 reshape.59
  2.1 0.1 fusion
  2.1 0.1 copy.47
  2.2 0.1 copy.46
  2.3 0.2 select_reduce_fusion.1
  2.6 0.1 copy.43
  2.7 0.1 reshape.60.windows
  2.8 0.7 copy.52
  3.5 6.9 %shard_map.263 = (f32[2048,32]{1,0:T(8,128)}, bf16[2048,128]{1,0:T(8,128)(2,1)S(1)}, bf16[2,1024,128]{2,1,0:T(8,128)(2,1)S(1)}, bf16[2,1024,128]{2,1,0:T(8,128)(2,1)S(1)}) custom-call(s32[2048]{0:T(1024)S(1)} %bitcast.99, f32[32,8192]{1,0:T(8,128)} %bitcast.70, s32[2,1024]{1,0:T(2,128)} %segments.1), custom_call_target="tpu_custom_call" | custom-call | tf_op jit(solution)/shard_map/pallas_call | solution.py:108
  10.4 0.0 copy-start.4
  10.5 0.0 copy-start.40
  10.5 0.0 copy-start.41
  10.5 0.0 copy-start.44
  10.5 0.0 copy-start.50
  10.5 6.0 %shard_map.264 = (bf16[1024,512]{1,0:T(8,128)(2,1)}, bf16[1024,512]{1,0:T(8,128)(2,1)}, bf16[1024,512]{1,0:T(8,128)(2,1)}, bf16[1024,512]{1,0:T(8,128)(2,1)}) custom-call(s32[1]{0:T(128)} %bitcast.side, bf16[2,1024,512]{2,1,0:T(8,128)(2,1)} %bitcast.38, bf16[2048,128]{1,0:T(8,128)(2,1)S(1)} %get-tuple-element.592.wide, f32[32,512]{1,0:T(8,128)} %up.3, ...), custom_call_target="tpu_custom_call" | custom-call | tf_op jit(solution)/shard_map/pallas_call | solution.py:1219
  16.5 13.0 %shard_map.265 = (bf16[1024,512]{1,0:T(8,128)(2,1)}, bf16[1024,512]{1,0:T(8,128)(2,1)}) custom-call(s32[16]{0:T(128)S(1)} %reshape.60.windows, bf16[1024,512]{1,0:T(8,128)(2,1)} %get-tuple-element.593.query, bf16[1024,512]{1,0:T(8,128)(2,1)} %get-tuple-element.594.key, bf16[1024,512]{1,0:T(8,128)(2,1)} %get-tuple-element.595.value, ...), custom_call_target="tpu_custom_call" | custom-call | tf_op jit(solution)/shard_map/pallas_call | solution.py:1237
  29.6 0.0 copy-start.8
  29.6 14.4 %shard_map.266 = (f32[1024,512]{1,0:T(8,128)}, bf16[1024,512]{1,0:T(8,128)(2,1)}, bf16[1024,2048]{1,0:T(8,128)(2,1)}, bf16[1024,2048]{1,0:T(8,128)(2,1)}, f32[1024,512]{1,0:T(8,128)}, /*index=5*/f32[1024,32]{1,0:T(8,128)}) custom-call(s32[1]{0:T(128)} %bitcast.side, bf16[2,1024,512]{2,1,0:T(8,128)(2,1)S(1)} %bitcast.39, bf16[2048,128]{1,0:T(8,128)(2,1)} %copy-done.14, ...), custom_call_target="tpu_custom_call" | custom-call | tf_op jit(solution)/shard_map/pallas_call | solution.py:1219
  44.1 38.3 %conditional.3 = (bf16[1024,512]{1,0:T(8,128)(2,1)}, bf16[1024,512]{1,0:T(8,128)(2,1)}, bf16[1024,512]{1,0:T(8,128)(2,1)}, bf16[1024,512]{1,0:T(8,128)(2,1)}, bf...) conditional(s32[]{:T(128)} %convert_element_type.7, ...), branch_computations={%region_2.3_spmd, %region_3.4_spmd} | conditional | bytes 11665708 | solution.py:1380
  50.3 4.7 %branch_1_fun.13 = (bf16[1024,512]{1,0:T(8,128)(2,1)}, bf16[1024,512]{1,0:T(8,128)(2,1)}, bf16[1024,512]{1,0:T(8,128)(2,1)}, bf16[1024,512]{1,0:T(8,128)(2,1)}) custom-call(s32[1]{0:T(128)} %get-tuple-element.308.side, bf16[2,1024,512]{2,1,0:T(8,128)(2,1)S(1)} %get-tuple-element.309.edge, bf16[2048,128]{1,0:T(8,128)(2,1)} %get-tuple-element.310.wide, ...), custom_call_target="tpu_custom_call" | custom-call | tf_op jit(solution)/shard_map/cond/branch_1_fun/pallas_call | solution.py:1219
  54.9 13.3 %branch_1_fun.14 = (bf16[1024,512]{1,0:T(8,128)(2,1)}, bf16[1024,512]{1,0:T(8,128)(2,1)}) custom-call(s32[16]{0:T(128)S(1)} %get-tuple-element.320.windows, bf16[1024,512]{1,0:T(8,128)(2,1)} %get-tuple-element.747.query, bf16[1024,512]{1,0:T(8,128)(2,1)} %get-tuple-element.748.key, bf16[1024,512]{1,0:T(8,128)(2,1)} %get-tuple-element.749.value, ...), custom_call_target="tpu_custom_call" | custom-call | tf_op jit(solution)/shard_map/cond/branch_1_fun/pallas_call | solution.py:1237
  68.2 14.1 %branch_1_fun.15 = (f32[1024,512]{1,0:T(8,128)}, bf16[1024,512]{1,0:T(8,128)(2,1)}, bf16[1024,2048]{1,0:T(8,128)(2,1)}, bf16[1024,2048]{1,0:T(8,128)(2,1)}, f32[1024,512]{1,0:T(8,128)}, /*index=5*/f32[1024,32]{1,0:T(8,128)}) custom-call(s32[1]{0:T(128)} %get-tuple-element.308.side, bf16[2,1024,512]{2,1,0:T(8,128)(2,1)S(1)} %get-tuple-element.309.edge, ...), custom_call_target="tpu_custom_call" | custom-call | tf_op jit(solution)/shard_map/cond/branch_1_fun/pallas_call | solution.py:1219
  82.4 1.3 collective-permute-start
  83.6 9.4 %collective-permute-done = f32[32,1024]{1,0:T(8,128)S(1)} collective-permute-done((f32[32,1024]{1,0:T(8,128)}, f32[32,1024]{1,0:T(8,128)S(1)}, u32[]{:S(2)}, u32[]{:S(2)}) %collective-permute-start) | collective-permute-done | bytes 131104 | tf_op jit(solution)/shard_map/ppermute | solution.py:1381
  93.0 86.5 %conditional.4 = (bf16[1024,512]{1,0:T(8,128)(2,1)}, bf16[1024,512]{1,0:T(8,128)(2,1)}, bf16[1024,512]{1,0:T(8,128)(2,1)}, bf16[1024,2048]{1,0:T(8,128)(2,1)}, f...) conditional(s32[]{:T(128)} %convert_element_type.8, ...), branch_computations={%region_4.5_spmd, %region_5.6_spmd} | conditional | bytes 37618192 | solution.py:1394
  93.2 0.0 copy-start.12
  93.3 14.8 %branch_0_fun.19 = (bf16[1024,512]{1,0:T(8,128)(2,1)}, bf16[1024,2048]{1,0:T(8,128)(2,1)}, f32[1024,512]{1,0:T(8,128)}, bf16[1024,512]{1,0:T(8,128)(2,1)}, bf16[...) custom-call(s32[1]{0:T(128)} %get-tuple-element.354.side, ...), custom_call_target="tpu_custom_call" | custom-call | tf_op jit(solution)/shard_map/cond/branch_0_fun/pallas_call | solution.py:1219
  108.2 10.6 %branch_0_fun.24 = f32[512,512]{1,0:T(8,128)} custom-call(s32[2048]{0:T(1024)S(1)} %get-tuple-element.397.index, f32[2048,32]{1,0:T(8,128)S(1)} %copy-done.12, f32[1024,32]{1,0:T(8,128)S(1)} %copy-done.34, f32[1024,32]{1,0:T(8,128)} %get-tuple-element.398.latent_second, f32[32,8192]{1,0:T(8,128)S(1)} %copy-done.36), custom_call_target="tpu_custom_call" | custom-call | tf_op jit(solution)/shard_map/cond/branch_0_fun/pallas_call | solution.py:162
  118.7 23.3 %branch_0_fun.20 = (bf16[1024,512]{1,0:T(8,128)(2,1)S(1)}, bf16[1024,512]{1,0:T(8,128)(2,1)}, bf16[1024,512]{1,0:T(8,128)(2,1)}) custom-call(s32[16]{0:T(128)S(1)} %get-tuple-element.375.windows, bf16[1024,512]{1,0:T(8,128)(2,1)} %get-tuple-element.376.query, bf16[1024,512]{1,0:T(8,128)(2,1)} %get-tuple-element.377.marks, ...), custom_call_target="tpu_custom_call" | custom-call | tf_op jit(solution)/shard_map/cond/branch_0_fun/pallas_call | solution.py:1237
  142.1 6.5 %branch_0_fun.21 = (f32[1024,512]{1,0:T(8,128)}, f32[32,1024]{1,0:T(8,128)}, f32[16,512]{1,0:T(8,128)}, f32[32,512]{1,0:T(8,128)}) custom-call(s32[1]{0:T(128)} %get-tuple-element.354.side, bf16[2,1024,512]{2,1,0:T(8,128)(2,1)S(1)} %get-tuple-element.356.cotangent.edge, bf16[2048,128]{1,0:T(8,128)(2,1)S(1)} %copy-done.17, ...), custom_call_target="tpu_custom_call" | custom-call | tf_op jit(solution)/shard_map/cond/branch_0_fun/pallas_call | solution.py:1219
  148.6 6.2 %branch_0_fun.23 = f32[2048,512]{1,0:T(8,128)} custom-call(bf16[1024,512]{1,0:T(8,128)(2,1)S(1)} %copy-done.20, bf16[1024,512]{1,0:T(8,128)(2,1)} %get-tuple-element.776.branch_low, bf16[1024,512]{1,0:T(8,128)(2,1)} %get-tuple-element.396.n1, bf16[1024,512]{1,0:T(8,128)(2,1)S(1)} %get-tuple-element.779.query_grad, ...), custom_call_target="tpu_custom_call" | custom-call | tf_op jit(solution)/shard_map/cond/branch_0_fun/pallas_call | solution.py:534
  154.9 10.2 %branch_0_fun.22 = f32[4096,512]{1,0:T(8,128)} custom-call(bf16[1024,2048]{1,0:T(8,128)(2,1)} %get-tuple-element.394.active, bf16[1024,512]{1,0:T(8,128)(2,1)} %get-tuple-element.774.out_low, bf16[1024,512]{1,0:T(8,128)(2,1)S(1)} %copy-done.35, bf16[1024,2048]{1,0:T(8,128)(2,1)} %get-tuple-element.775.preact_low), custom_call_target="tpu_custom_call" | custom-call | tf_op jit(solution)/shard_map/cond/branch_0_fun/pallas_call | solution.py:534
  179.6 1.3 collective-permute-start.1
  180.9 5.8 %collective-permute-done.1 = f32[32,1024]{1,0:T(8,128)S(1)} collective-permute-done((f32[32,1024]{1,0:T(8,128)}, f32[32,1024]{1,0:T(8,128)S(1)}, u32[]{:S(2)}, u32[]{:S(2)}) %collective-permute-start.1) | collective-permute-done | bytes 131104 | tf_op jit(solution)/shard_map/ppermute | solution.py:1395
  186.6 27.5 %conditional.5 = (f32[4096,512]{1,0:T(8,128)}, f32[1024,512]{1,0:T(8,128)}, bf16[1024,512]{1,0:T(8,128)(2,1)}, bf16[1024,512]{1,0:T(8,128)(2,1)}, f32[16,512]{1,0:T(8,128)S(1)}, /*index=5*/f32[32,512]{1,0:T(8,128)S(1)}) conditional(s32[]{:T(128)} %convert_element_type.7, (bf16[1024,2048]{1,0:T(8,128)(2,1)}, bf16[1024,512]{1,0:T(8,128)(2,1)}, ...), branch_computations={%region_6.7_spmd, %region_7.8_spmd} | conditional | bytes 16973900 | solution.py:1405
  186.6 0.6 copy.158.refs_1_
  187.3 0.6 copy.157.refs_0_
  187.9 14.9 %branch_1_fun.24 = (bf16[1024,512]{1,0:T(8,128)(2,1)}, bf16[1024,2048]{1,0:T(8,128)(2,1)}, f32[1024,512]{1,0:T(8,128)}, bf16[1024,512]{1,0:T(8,128)(2,1)}, bf16[...) custom-call(s32[1]{0:T(128)} %get-tuple-element.466.side, ...), custom_call_target="tpu_custom_call" | custom-call | tf_op jit(solution)/shard_map/cond/branch_1_fun/pallas_call | solution.py:1219
  202.8 11.4 %branch_1_fun.25 = f32[4096,512]{1,0:T(8,128)} custom-call(bf16[1024,2048]{1,0:T(8,128)(2,1)S(1)} %copy-done.37, bf16[1024,512]{1,0:T(8,128)(2,1)} %get-tuple-element.484.out_low, bf16[1024,512]{1,0:T(8,128)(2,1)} %get-tuple-element.485.n2, bf16[1024,2048]{1,0:T(8,128)(2,1)} %get-tuple-element.486.preact_low, ...), custom_call_target="tpu_custom_call", output_to_operand_aliasing={{}: (4, {})} | custom-call | tf_op jit(solution)/shard_map/cond/branch_1_fun/pallas_call | solution.py:534
  214.2 96.0 %shard_map.267 = (f32[4096,512]{1,0:T(8,128)}, f32[2048,512]{1,0:T(8,128)}, f32[768,512]{1,0:T(8,128)}, f32[1024,512]{1,0:T(8,128)}) custom-call(f32[4096,512]{1,0:T(8,128)} %get-tuple-element.629.hidden, f32[2048,512]{1,0:T(8,128)} %get-tuple-element.630.attention, bf16[1024,512]{1,0:T(8,128)(2,1)} %get-tuple-element.631.query, ...), custom_call_target="tpu_custom_call", output_to_operand_aliasing={{1}: (1, {})} | custom-call | tf_op jit(solution)/shard_map/pallas_call | solution.py:1019
  310.2 1.4 copy-done.2
  311.6 68.7 %shard_map.268 = (f32[2048,512]{1,0:T(8,128)S(1)}, f32[768,512]{1,0:T(8,128)S(1)}) custom-call(f32[2048,512]{1,0:T(8,128)} %get-tuple-element.656.main, f32[768,512]{1,0:T(8,128)S(1)} %copy-done.2), custom_call_target="tpu_custom_call" | custom-call | tf_op jit(solution)/shard_map/pallas_call | solution.py:813
  380.3 2.1 copy-done
  382.4 1.1 copy-done.1
  383.6 13.3 %shard_map.269 = (f32[2048,512]{1,0:T(8,128)}, f32[512,2048]{1,0:T(8,128)}, f32[512,512]{1,0:T(8,128)}, f32[512,1536]{1,0:T(8,128)}, f32[2,1024,512]{2,1,0:T(8,1...) custom-call(s32[1]{0:T(128)} %bitcast.side, ...), custom_call_target="tpu_custom_call" | custom-call | tf_op jit(solution)/shard_map/pallas_call | solution.py:1103
  396.9 1.3 copy.49
  398.2 1.3 copy.44
  (60 shorter events, 0.1 us)
Async XLA Ops:
  10.4 19.1 %copy-start.14 = (bf16[2048,128]{1,0:T(8,128)(2,1)}, bf16[2048,128]{1,0:T(8,128)(2,1)S(1)}, u32[]{:S(2)}) copy-start(bf16[2048,128]{1,0:T(8,128)(2,1)S(1)} %get-tuple-element.592.wide) | copy-start | bytes 1572868
  10.4 19.1 %copy-start.21 = (bf16[2,1024,128]{2,1,0:T(8,128)(2,1)}, bf16[2,1024,128]{2,1,0:T(8,128)(2,1)S(1)}, u32[]{:S(2)}) copy-start(bf16[2,1024,128]{2,1,0:T(8,128)(2,1)S(1)} %get-tuple-element.597.key_mark) | copy-start | bytes 1572868
  10.4 19.1 %copy-start.32 = (bf16[2,1024,128]{2,1,0:T(8,128)(2,1)}, bf16[2,1024,128]{2,1,0:T(8,128)(2,1)S(1)}, u32[]{:S(2)}) copy-start(bf16[2,1024,128]{2,1,0:T(8,128)(2,1)S(1)} %get-tuple-element.596.query_mark) | copy-start | bytes 1572868
  10.4 19.1 %copy-start.3 = (bf16[1,2,1024,512]{3,2,1,0:T(8,128)(2,1)S(1)}, bf16[1,2,1024,512]{3,2,1,0:T(8,128)(2,1)}, u32[]{:S(2)}) copy-start(bf16[1,2,1024,512]{3,2,1,0:T(8,128)(2,1)} %param.22) | copy-start | bytes 6291460
  10.4 19.1 %copy-start.4 = (bf16[1,512,2048]{2,1,0:T(8,128)(2,1)S(1)}, bf16[1,512,2048]{2,1,0:T(8,128)(2,1)}, u32[]{:S(2)}) copy-start(bf16[1,512,2048]{2,1,0:T(8,128)(2,1)} %param.27) | copy-start | bytes 6291460
  10.4 19.1 %copy-start.6 = (bf16[1,2048,512]{2,1,0:T(8,128)(2,1)S(1)}, bf16[1,2048,512]{2,1,0:T(8,128)(2,1)}, u32[]{:S(2)}) copy-start(bf16[1,2048,512]{2,1,0:T(8,128)(2,1)} %param.28) | copy-start | bytes 6291460
  10.4 19.1 %copy-start.31 = (f32[32,512]{1,0:T(8,128)S(1)}, f32[32,512]{1,0:T(8,128)}, u32[]{:S(2)}) copy-start(f32[32,512]{1,0:T(8,128)} %up.3) | copy-start | bytes 196612
  10.5 19.1 %copy-start.40 = (f32[512,32]{0,1:T(8,128)S(1)}, f32[512,32]{0,1:T(8,128)}, u32[]{:S(2)}) copy-start(f32[512,32]{0,1:T(8,128)} %param.34) | copy-start | bytes 196612
  10.5 19.1 %copy-start.41 = (f32[1,2,512]{2,1,0:T(2,128)S(1)}, f32[1,2,512]{2,1,0:T(2,128)}, u32[]{:S(2)}) copy-start(f32[1,2,512]{2,1,0:T(2,128)} %param.29) | copy-start | bytes 12292
  10.5 19.1 %copy-start.42 = (f32[2,512]{1,0:T(2,128)S(1)}, f32[2,512]{1,0:T(2,128)}, u32[]{:S(2)}) copy-start(f32[2,512]{1,0:T(2,128)} %head_bias.3) | copy-start | bytes 12292
  10.5 19.1 %copy-start.43 = (f32[512]{0:T(512)S(1)}, f32[512]{0:T(512)}, u32[]{:S(2)}) copy-start(f32[512]{0:T(512)} %param.32) | copy-start | bytes 6148
  10.5 19.1 %copy-start.44 = (f32[1,2048]{1,0:T(1,128)S(1)}, f32[1,2048]{1,0:T(1,128)}, u32[]{:S(2)}) copy-start(f32[1,2048]{1,0:T(1,128)} %hidden_bias.1) | copy-start | bytes 24580
  10.5 19.1 %copy-start.50 = (f32[32]{0:T(128)S(1)}, f32[32]{0:T(128)}, u32[]{:S(2)}) copy-start(f32[32]{0:T(128)} %param.35) | copy-start | bytes 388
  29.6 14.4 %copy-start.8 = (bf16[1,512,1536]{2,1,0:T(8,128)(2,1)S(1)}, bf16[1,512,1536]{2,1,0:T(8,128)(2,1)}, u32[]{:S(2)}) copy-start(bf16[1,512,1536]{2,1,0:T(8,128)(2,1)} %param.25) | copy-start | bytes 4718596
  54.9 13.3 %copy-start.16 = (bf16[2048,128]{1,0:T(8,128)(2,1)S(1)}, bf16[2048,128]{1,0:T(8,128)(2,1)}, u32[]{:S(2)}) copy-start(bf16[2048,128]{1,0:T(8,128)(2,1)} %get-tuple-element.310.wide) | copy-start | bytes 1572868 | tf_op jit(solution)/shard_map/cond
  54.9 13.3 %copy-start.25 = (bf16[512,512]{1,0:T(8,128)(2,1)S(1)}, bf16[512,512]{1,0:T(8,128)(2,1)}, u32[]{:S(2)}) copy-start(bf16[512,512]{1,0:T(8,128)(2,1)} %get-tuple-element.325.weight_out) | copy-start | bytes 1572868 | tf_op jit(solution)/shard_map/cond
  82.4 10.7 %collective-permute-start = (f32[32,1024]{1,0:T(8,128)}, f32[32,1024]{1,0:T(8,128)S(1)}, u32[]{:S(2)}, u32[]{:S(2)}) collective-permute-start(f32[32,1024]{1,0:T(8,128)} %get-tuple-element.609), channel_id=1, source_target_pairs={{16,0},{17,1},{18,2},{19,3},{20,4},{21,5},{22,6},{23,7},{24,8},{25... | collective-permute-start | bytes 393224 | tf_op jit(solution)/shard_map/ppermute | solution.py:1381
  93.2 14.9 %copy-start.12 = (f32[2048,32]{1,0:T(8,128)S(1)}, f32[2048,32]{1,0:T(8,128)}, u32[]{:S(2)}) copy-start(f32[2048,32]{1,0:T(8,128)} %get-tuple-element.357.unit) | copy-start | bytes 786436 | tf_op jit(solution)/shard_map/cond
  93.2 14.9 %copy-start.34 = (f32[1024,32]{1,0:T(8,128)S(1)}, f32[1024,32]{1,0:T(8,128)}, u32[]{:S(2)}) copy-start(f32[1024,32]{1,0:T(8,128)} %get-tuple-element.359.latent.latent_first) | copy-start | bytes 393220 | tf_op jit(solution)/shard_map/cond
  93.3 14.9 %copy-start.36 = (f32[32,8192]{1,0:T(8,128)S(1)}, f32[32,8192]{1,0:T(8,128)}, u32[]{:S(2)}) copy-start(f32[32,8192]{1,0:T(8,128)} %get-tuple-element.399.table_turned) | copy-start | bytes 3145732 | tf_op jit(solution)/shard_map/cond
  108.1 10.6 %copy-start.20 = (bf16[1024,512]{1,0:T(8,128)(2,1)S(1)}, bf16[1024,512]{1,0:T(8,128)(2,1)}, u32[]{:S(2)}) copy-start(bf16[1024,512]{1,0:T(8,128)(2,1)} %get-tuple-element.381.context) | copy-start | bytes 3145732 | tf_op jit(solution)/shard_map/cond
  108.1 10.6 %copy-start.22 = (bf16[2,1024,128]{2,1,0:T(8,128)(2,1)S(1)}, bf16[2,1024,128]{2,1,0:T(8,128)(2,1)}, u32[]{:S(2)}) copy-start(bf16[2,1024,128]{2,1,0:T(8,128)(2,1)} %get-tuple-element.382.key_mark) | copy-start | bytes 1572868 | tf_op jit(solution)/shard_map/cond
  118.7 23.4 %copy-start.9 = (bf16[512,1536]{1,0:T(8,128)(2,1)S(1)}, bf16[512,1536]{1,0:T(8,128)(2,1)}, u32[]{:S(2)}) copy-start(bf16[512,1536]{1,0:T(8,128)(2,1)} %get-tuple-element.388.weight) | copy-start | bytes 4718596 | tf_op jit(solution)/shard_map/cond
  118.7 23.4 %copy-start.17 = (bf16[2048,128]{1,0:T(8,128)(2,1)S(1)}, bf16[2048,128]{1,0:T(8,128)(2,1)}, u32[]{:S(2)}) copy-start(bf16[2048,128]{1,0:T(8,128)(2,1)} %get-tuple-element.386.wide) | copy-start | bytes 1572868 | tf_op jit(solution)/shard_map/cond
  142.1 12.8 %copy-start.28 = (bf16[1024,512]{1,0:T(8,128)(2,1)}, bf16[1024,512]{1,0:T(8,128)(2,1)S(1)}, u32[]{:S(2)}) copy-start(bf16[1024,512]{1,0:T(8,128)(2,1)S(1)} %get-tuple-element.779.query_grad) | copy-start | bytes 3145732 | tf_op jit(solution)/shard_map/cond
  148.6 6.2 %copy-start.35 = (bf16[1024,512]{1,0:T(8,128)(2,1)S(1)}, bf16[1024,512]{1,0:T(8,128)(2,1)}, u32[]{:S(2)}) copy-start(bf16[1024,512]{1,0:T(8,128)(2,1)} %get-tuple-element.395.n2) | copy-start | bytes 3145732 | tf_op jit(solution)/shard_map/cond
  179.6 7.1 %collective-permute-start.1 = (f32[32,1024]{1,0:T(8,128)}, f32[32,1024]{1,0:T(8,128)S(1)}, u32[]{:S(2)}, u32[]{:S(2)}) collective-permute-start(f32[32,1024]{1,0:T(8,128)} %get-tuple-element.623), channel_id=1, source_target_pairs={{16,0},{17,1},{18,2},{19,3},{20,4},{21,5},{22,6},{23,7},{24,8},{25... | collective-permute-start | bytes 393224 | tf_op jit(solution)/shard_map/ppermute | solution.py:1395
  186.6 27.5 %copy-start.19 = (bf16[1024,512]{1,0:T(8,128)(2,1)S(1)}, bf16[1024,512]{1,0:T(8,128)(2,1)}, u32[]{:S(2)}) copy-start(bf16[1024,512]{1,0:T(8,128)(2,1)} %get-tuple-element.598.context.refs_0_) | copy-start | bytes 3145732
  186.6 27.5 %copy-start.45 = (f32[32,512]{1,0:T(8,128)S(1)}, f32[32,512]{1,0:T(8,128)}, u32[]{:S(2)}) copy-start(f32[32,512]{1,0:T(8,128)} %get-tuple-element.652.refs_15_) | copy-start | bytes 196612
  187.9 14.9 %copy-start.37 = (bf16[1024,2048]{1,0:T(8,128)(2,1)S(1)}, bf16[1024,2048]{1,0:T(8,128)(2,1)}, u32[]{:S(2)}) copy-start(bf16[1024,2048]{1,0:T(8,128)(2,1)} %get-tuple-element.465.active) | copy-start | bytes 12582916 | tf_op jit(solution)/shard_map/cond
  214.2 169.4 %copy-start.26 = (f32[1024,512]{1,0:T(8,128)S(1)}, f32[1024,512]{1,0:T(8,128)}, u32[]{:S(2)}) copy-start(f32[1024,512]{1,0:T(8,128)} %get-tuple-element.600.first_result) | copy-start | bytes 6291460
  310.2 1.4 copy-start.2
  311.6 72.0 %copy-start.30 = (f32[1024,512]{1,0:T(8,128)S(1)}, f32[1024,512]{1,0:T(8,128)}, u32[]{:S(2)}) copy-start(f32[1024,512]{1,0:T(8,128)} %get-tuple-element.662.second_result) | copy-start | bytes 6291460
  380.3 2.1 copy-start
  382.4 1.1 copy-start.1

commit v7 on v6

--- a/solution.py
+++ b/solution.py
@@ -503,27 +503,6 @@
         put(value[:, width:], slice(width, 2 * width))
 
 
-def attention_weight_kernel(context, branch_low, n1, query_grad, key_grad, value_grad, *refs):
-    out = refs[-1]
-    before = refs[0] if len(refs) > 1 else None
-    step = pl.program_id(0)
-    width = n1.shape[1]
-
-    def put(value, number):
-        rows = slice(number * width, (number + 1) * width)
-        out[rows, :] = value if before is None else value + before[rows, :]
-
-    @pl.when(step == 0)
-    def _():
-        put(dot(context[...], branch_low[...], TN), 0)
-        put(dot(n1[...], query_grad[...], TN), 1)
-
-    @pl.when(step == 1)
-    def _():
-        put(dot(n1[...], key_grad[...], TN), 0)
-        put(dot(n1[...], value_grad[...], TN), 1)
-
-
 def weight_call(kernel, operands, in_specs, steps, before):
     width = operands[1].shape[1]
     out_spec = pl.BlockSpec((2 * width, width), lambda step: (step, 0))
@@ -554,13 +533,6 @@
         pl.BlockSpec((count, 2 * width), lambda step: (0, jnp.maximum(step - first, 0))),
     ]
     return weight_call(hidden_weight_kernel, operands, in_specs, 2 * first, before)
-
-
-def attention_weights(kept, late, early, before=None):
-    operands = [kept.context, late.branch_low, kept.n1]
-    operands += list(early[:3])
-    full = pl.BlockSpec(kept.n1.shape, lambda step: (0, 0))
-    return weight_call(attention_weight_kernel, operands, [full] * 6, 2, before)
 
 
 MESH = pl.DeviceIdType.MESH
@@ -613,7 +585,7 @@
 
     def greet(self):
         self.barrier = pltpu.get_barrier_semaphore()
-        devices = (self.other,) + self.targets + (() if self.crossing is None else (self.across,))
+        devices = (self.other, self.across) + self.targets
         for device in devices:
             pl.semaphore_signal(self.barrier, inc=1, device_id=device, device_id_type=MESH)
         self.greeted = len(devices)
@@ -705,7 +677,7 @@
             here, here, self.side_send[which].at[way, step], self.side_recv[which].at[way, step], self.other
         )
 
-    def begin(self):
+    def begin(self, waiting=True):
         def load(step, carry):
             for which, way in self.lanes:
                 self.load(which, way, step).start()
@@ -717,7 +689,8 @@
             return carry
 
         lax.fori_loop(0, self.chips, load, 0)
-        pl.semaphore_wait(self.barrier, self.greeted)
+        if waiting:
+            pl.semaphore_wait(self.barrier, self.greeted)
         lax.fori_loop(0, self.chips, swap, 0)
         for which, way in self.lanes:
             self.load(which, way, 0).wait()
@@ -793,49 +766,25 @@
     lax.fori_loop(start, stop, one, 0)
 
 
-SUM_WAYS = (4, 2)
-
-
-def sum_kernel(main, misc, main_out, misc_out, *scratch):
-    ring = Ring((main, misc), (main_out, misc_out), SUM_WAYS, 1, scratch)
-    ring.greet()
-    ring.begin()
-    loop(1, ring.chips, ring.gather)
-    ring.turn()
-    loop(1, ring.chips, ring.pass_out)
-    ring.finish()
-
-
-def sum_all(main, misc):
-    if lax.axis_size(DP) < LEAST_DEVICES:
-        return main, lax.psum(misc, SECTION)
-    arrays = (main, misc)
-    return pl.pallas_call(
-        sum_kernel,
-        in_specs=[pl.BlockSpec(memory_space=pl.ANY)] * 2,
-        out_specs=[pl.BlockSpec(memory_space=pl.ANY)] * 2,
-        out_shape=tuple(jax.ShapeDtypeStruct(array.shape, F32) for array in arrays),
-        scratch_shapes=Ring.scratch(arrays, SUM_WAYS, 1),
-        compiler_params=pltpu.CompilerParams(collective_id=0, has_side_effects=True, vmem_limit_bytes=40 << 20),
-    )(*arrays)
-
-
-FINISH_WAYS = (4,)
-
-
-def finish_kernel(
-    hidden, attention, query, marks, key, value, context_grad, context, key_mark, edges, mid_grad, weight, branch_low, n1,
-    *refs,
-):
-    others, refs = refs[:12], refs[12:]
+HIDDEN_WAYS = (4,)
+OTHER_WAYS = (4, 2)
+
+
+def finish_kernel(*refs, held):
+    (
+        hidden, query, marks, key, value, context_grad, context, key_mark, edges, mid_grad, weight, branch_low, n1,
+    ), refs = refs[:13], refs[13:]
+    mine, others, refs = refs[:6], refs[6:18], refs[18:]
     (
         gains, book, down, up, late, early,
-        hidden_out, attention_out, misc, entry,
+        hidden_out, attention_out, misc_out, entry,
         query_in, marks_in, key_in, value_in, grad_in, context_in, key_mark_in, edge_in, mid_in, weight_in, branch_in,
-        n1_in, part, grad_mark, query_grad, key_total, value_total, key_grad, value_grad, in_sems, part_sem, out_sems,
+        n1_in, part, misc, grad_mark, query_grad, key_total, value_total, key_grad, value_grad, in_sems, out_sems,
     ), scratch = refs[:32], refs[32:]
     encoder = lax.axis_index(SECTION) == 0
-    ring = Ring((hidden,), (hidden_out,), FINISH_WAYS, None, scratch) if scratch else None
+    decoder = jnp.logical_not(encoder)
+    ring = Ring((hidden,), (hidden_out,), HIDDEN_WAYS, None, scratch[:held]) if scratch else None
+    last = Ring((part, misc), (attention_out, misc_out), OTHER_WAYS, 1, scratch[held:]) if scratch else None
     count, width = query.shape
     narrow = down.shape[0]
     steps = count // TOKENS
@@ -847,29 +796,28 @@
         (context, context_in), (key_mark.at[row], key_mark_in), (edges.at[row], edge_in), (mid_grad, mid_in),
         (weight, weight_in), (branch_low, branch_in), (n1, n1_in),
     )
-    loads = [pltpu.make_async_copy(*pair, in_sems.at[number]) for number, pair in enumerate(inputs)]
-    part_load = pltpu.make_async_copy(attention, part, part_sem)
     first_held = (query_in, marks_in, key_in, value_in, grad_in, grad_mark)
     second_held = (context_in, branch_in, n1_in, query_grad, key_grad, value_grad)
-    other_loads = [
-        pltpu.make_async_copy(*pair, in_sems.at[number])
-        for number, pair in enumerate(zip(others, first_held + second_held))
-    ]
+
+    def copies(pairs):
+        return [pltpu.make_async_copy(*pair, in_sems.at[number]) for number, pair in enumerate(pairs)]
+
+    loads = copies(inputs)
+    other_loads = copies(zip(others, first_held + second_held))
+    first_loads = copies(zip(mine, first_held))
+
+    def start(copies):
+        for copy in copies:
+            copy.start()
+
+    def wait(copies):
+        for copy in copies:
+            copy.wait()
 
     if ring:
         ring.greet()
-
-    @pl.when(encoder)
-    def _():
-        for load in loads:
-            load.start()
-        part_load.start()
-
-    @pl.when(jnp.logical_not(encoder))
-    def _():
-        for load in other_loads:
-            load.start()
-
+    pl.when(encoder)(functools.partial(start, loads))
+    pl.when(decoder)(functools.partial(start, other_loads))
     if ring:
         ring.begin()
     misc[...] = jnp.zeros_like(misc)
@@ -880,20 +828,17 @@
         misc[book.shape[0] : book.shape[0] + narrow, :] = down[...]
         misc[at : at + 16, :] = late[...]
         misc[at + 16 : at + 32, :] = early[...]
-        for load in loads:
-            load.wait()
-        part_load.wait()
+        wait(loads)
         mark_grads(grad_in, context_in, grad_mark)
         key_total[...] = jnp.zeros_like(key_total)
         value_total[...] = jnp.zeros_like(value_total)
 
-    @pl.when(jnp.logical_not(encoder))
+    @pl.when(decoder)
     def _():
         misc[book.shape[0] + narrow : at, :] = up[...]
         misc[at + 32 : at + 48, :] = late[...]
         misc[at + 48 : at + 64, :] = early[...]
-        for load in other_loads:
-            load.wait()
+        wait(other_loads)
 
     def attention_piece(turn):
         attend_back_block(
@@ -915,24 +860,14 @@
         misc[at + 19 : at + 20, :] += column_sum(normed_grad)
         mid_in[rows, :] = mid_in[rows, :] + norm_back(normed_grad, gains[0:1, :], hat, inverse)
 
-    def both_piece(number):
+    def weight_piece(number):
         def put(first, second):
             rows = pl.ds(pl.multiple_of(number * width, width), width)
             part[rows, :] = dot(first[0][...], first[1][...], TN) + dot(second[0][...], second[1][...], TN)
 
         for choice, places in enumerate(((0, 1), (2, 3), (2, 4), (2, 5))):
-            pairs_of = [[held[place] for place in places] for held in (first_held, second_held)]
-            pl.when(number == choice)(functools.partial(put, *pairs_of))
-
-    def weight_piece(number):
-        def put(left, right):
-            rows = pl.ds(pl.multiple_of(number * width, width), width)
-            part[rows, :] = part[rows, :] + dot(left[...], right[...], TN)
-
-        for choice, (left, right) in enumerate(
-            ((context_in, branch_in), (n1_in, query_grad), (n1_in, key_grad), (n1_in, value_grad))
-        ):
-            pl.when(number == choice)(functools.partial(put, left, right))
+            both = [[held[place] for place in places] for held in (first_held, second_held)]
+            pl.when(number == choice)(functools.partial(put, *both))
 
     halves = (ring.lanes[:2], ring.lanes[2:]) if ring else (None, None)
     chips = ring.chips if ring else 8
@@ -946,10 +881,6 @@
             @pl.when(encoder)
             def _():
                 attention_piece(2 * (step - 1) + half)
-
-        @pl.when(jnp.logical_not(encoder) & (step <= 4))
-        def _():
-            both_piece(step - 1)
 
     inside = min(chips - 1, pieces // 2)
     loop(1, inside + 1, summing)
@@ -960,77 +891,97 @@
     @pl.when(encoder)
     def _():
         loop(2 * inside, pieces, attention_piece)
+        start(first_loads)
         key_grad[...] = (key_total[...] * (1.0 / LOG2E)).astype(BF)
         value_grad[...] = value_total[...].astype(BF)
+        wait(first_loads)
 
     def spreading(step):
-        for half, work in enumerate((entry_piece, weight_piece)):
-            if ring:
-                ring.pass_out(step, halves[half])
-
-            @pl.when(encoder)
-            def _():
-                work(step - 1)
+        if ring:
+            ring.pass_out(step, halves[0])
+
+        @pl.when(encoder)
+        def _():
+            entry_piece(step - 1)
+
+        if ring:
+            ring.pass_out(step, halves[1])
+        weight_piece(step - 1)
 
     loop(1, steps + 1, spreading)
-    stores = [
-        pltpu.make_async_copy(mid_in, entry, out_sems.at[0]),
-        pltpu.make_async_copy(part, attention_out, out_sems.at[1]),
-    ]
+    store = pltpu.make_async_copy(mid_in, entry, out_sems.at[0])
 
     @pl.when(encoder)
     def _():
-        stores[0].start()
-
-    stores[1].start()
+        store.start()
+
     if ring:
-        loop(steps + 1, chips, ring.pass_out)
+        last.begin(False)
+
+        def both(step):
+            ring.pass_out(step)
+            last.gather(step - steps)
+
+        loop(steps + 1, chips, both)
+        loop(chips - steps, chips, last.gather)
+        last.turn()
+        loop(1, chips, last.pass_out)
         ring.finish()
+        last.finish()
+    else:
+        stores = [
+            pltpu.make_async_copy(part, attention_out, out_sems.at[1]),
+            pltpu.make_async_copy(misc, misc_out, out_sems.at[2]),
+        ]
+        start(stores)
+        wait(stores)
 
     @pl.when(encoder)
     def _():
-        stores[0].wait()
-
-    stores[1].wait()
-
-
-def finish_row(work, kept, late, early, book, hidden, attention, others):
+        store.wait()
+
+
+def finish_row(work, first_kept, kept, late, mine, book, others, hidden):
     count, width = kept.n1.shape
     alone = lax.axis_size(DP) < LEAST_DEVICES
+    its_late, its_early = mine
     operands = [
-        hidden, attention, kept.query, kept.marks, kept.key, kept.value, late.context_grad,
+        hidden, kept.query, kept.marks, kept.key, kept.value, late.context_grad,
         kept.context, work.key_mark, work.edges, late.mid_grad, work.attention_in, late.branch_low, kept.n1,
     ]
-    for its_kept, its_late, its_early in others:
-        operands += [its_kept.context, its_late.branch_low, its_kept.n1, *its_early[:3]]
-    operands += [work.gains, book, late.head, early.head, late.sums, early.sums]
+    for a_kept, a_late, a_early in ((first_kept, its_late, its_early),) + others:
+        operands += [a_kept.context, a_late.branch_low, a_kept.n1, *a_early[:3]]
+    operands += [work.gains, book, late.head, its_early.head, late.sums, its_early.sums]
     hbm, vmem = pl.BlockSpec(memory_space=pl.ANY), pl.BlockSpec(memory_space=pltpu.VMEM)
     rows = book.shape[0] + 2 * work.narrow + 64
     unit = 16 * lax.axis_size(DP)
+    attention = jax.ShapeDtypeStruct((4 * width, width), F32)
+    misc = jax.ShapeDtypeStruct((rows + (-rows % unit), width), F32)
     low = pltpu.VMEM((count, width), BF)
     wide = pltpu.VMEM((count, width), F32)
     scratch = [low] * 6 + [pltpu.VMEM((count, 128), BF), low, wide, pltpu.VMEM(work.attention_in.shape, BF), low, low]
-    scratch += [pltpu.VMEM(attention.shape, F32), low, low, wide, wide, low, low]
-    scratch += [pltpu.SemaphoreType.DMA((12,)), pltpu.SemaphoreType.DMA, pltpu.SemaphoreType.DMA((2,))]
+    scratch += [pltpu.VMEM(attention.shape, F32), pltpu.VMEM(misc.shape, F32), low, low, wide, wide, low, low]
+    scratch += [pltpu.SemaphoreType.DMA((12,)), pltpu.SemaphoreType.DMA((3,))]
     settings = {}
+    held = 0
     if not alone:
-        scratch += Ring.scratch((hidden,), FINISH_WAYS, None)
-        settings = dict(collective_id=1, has_side_effects=True)
+        rings = Ring.scratch((hidden,), HIDDEN_WAYS, None)
+        held = len(rings)
+        scratch += rings + Ring.scratch((attention, misc), OTHER_WAYS, 1)
+        settings = dict(collective_id=0, has_side_effects=True)
     outs = pl.pallas_call(
-        finish_kernel,
-        in_specs=[hbm] * 26 + [vmem] * 6,
-        out_specs=[hbm, hbm, vmem, hbm],
+        functools.partial(finish_kernel, held=held),
+        in_specs=[hbm] * 31 + [vmem] * 6,
+        out_specs=[hbm] * 4,
         out_shape=(
-            jax.ShapeDtypeStruct(hidden.shape, F32),
-            jax.ShapeDtypeStruct(attention.shape, F32),
-            jax.ShapeDtypeStruct((rows + (-rows % unit), width), F32),
-            jax.ShapeDtypeStruct((count, width), F32),
+            jax.ShapeDtypeStruct(hidden.shape, F32), attention, misc, jax.ShapeDtypeStruct((count, width), F32),
         ),
         scratch_shapes=scratch,
-        input_output_aliases={1: 1},
-        compiler_params=pltpu.CompilerParams(vmem_limit_bytes=58 << 20, **settings),
+        compiler_params=pltpu.CompilerParams(vmem_limit_bytes=60 << 20, **settings),
     )(*operands)
-    return (hidden,) + tuple(outs[1:]) if alone else outs
+    if alone:
+        return hidden, outs[1], lax.psum(outs[2], SECTION), outs[3]
+    return outs
 
 
 def unpack_kernel(
@@ -1367,48 +1318,45 @@
     )
     book_out = book_shape(table_turned, width)
     hidden_shape = jax.ShapeDtypeStruct((2 * hidden, width), F32)
-    attention_shape = jax.ShapeDtypeStruct((4 * width, width), F32)
     quiet = jnp.zeros((unit.shape[1], count), F32)
     first_kept = work.forward(0)
 
-    def encoder_second():
+    def encoder_first():
         return (work.forward(1), *unwritten((work.late, work.early)))
 
     def decoder_first():
         return (unwritten(work.kept), *work.backward(0, first_kept, quiet))
 
-    kept_a, late_a, early_a = lax.cond(encoder, encoder_second, decoder_first)
+    kept_a, late_a, early_a = lax.cond(encoder, encoder_first, decoder_first)
     latent_in = lax.ppermute(early_a.latent_out, SECTION, [(1, 0)])
 
-    def encoder_third():
+    def encoder_second():
         late, early = work.backward(0, first_kept, latent_in)
-        weights = hidden_weights(first_kept, late), attention_weights(first_kept, late, early)
         book = scatter_codes(code_index, unit, (first_kept.latent, kept_a.latent), table_turned, width)
-        return unwritten(work.kept), late, early, weights, book
-
-    def decoder_third():
+        return unwritten(work.kept), late, early, hidden_weights(first_kept, late), book
+
+    def decoder_second():
         kept = work.forward(1)
-        weights, book = unwritten(((hidden_shape, attention_shape), book_out))
+        weights, book = unwritten((hidden_shape, book_out))
         return (kept, *work.backward(1, kept, quiet, (late_a, early_a)), weights, book)
 
-    kept_b, late_b, early_b, weights_b, book = lax.cond(section == 1, decoder_third, encoder_third)
+    kept_b, late_b, early_b, weights_b, book = lax.cond(encoder, encoder_second, decoder_second)
     latent_in_second = lax.ppermute(early_b.latent_out, SECTION, [(1, 0)])
 
-    def encoder_fifth():
-        late = work.backward_late(1, kept_a, latent_in_second, late_b)
-        return hidden_weights(kept_a, late, weights_b[0]), late[2:]
-
-    def decoder_fifth():
+    def decoder_fourth():
         total = hidden_weights(kept_b, late_b, hidden_weights(first_kept, late_a))
         return total, (*unwritten(work.late[2:5]), late_b.sums, late_b.head)
 
-    hidden_total, late = lax.cond(encoder, encoder_fifth, decoder_fifth)
+    def encoder_fourth():
+        late = work.backward_late(1, kept_a, latent_in_second, late_b)
+        return hidden_weights(kept_a, late, weights_b), late[2:]
+
+    hidden_total, late = lax.cond(encoder, encoder_fourth, decoder_fourth)
     late = Late(None, None, *late)
     hidden_total, attention_total, misc, second_entry = finish_row(
-        work, kept_a, late, early_b, book, hidden_total, weights_b[1],
-        ((first_kept, late_a, early_a), (kept_b, late_b, early_b)),
+        work, first_kept, kept_a, late, (late_b, early_b), book,
+        ((first_kept, late_a, early_a), (kept_b, late_b, early_b)), hidden_total,
     )
-    attention_total, misc = sum_all(attention_total, misc)
     (
         hidden_out_grad, hidden_in_grad, attention_out_grad, attention_in_grad, edge, book, gains, biases, bias,
         last_gain, head, down_grad, down_last, up_grad,

time: 408 us -> 397 us (0.973)
  waiting for transfers between devices: 15.2 us -> 22.1 us
  loops' own time: 20.9 us -> 14.5 us
  Pallas kernels: 348 us -> 343 us
  local copies, waits for them, and re-layouts: 11.3 us -> 6.57 us
    another operation x3, loops' own time: 20.9 us -> 14.5 us  [the longest x1 8.68 us: on_device(): lax.cond(encoder, encoder_second, decoder_second)]
    pallas_call x3 -> x2, Pallas kernels: 27.9 us -> 21.8 us  [weight_call(): pl.pallas_call(kernel, grid=(steps,), in_specs=in_specs, out_specs=out_sp...]
    pallas_call x2 -> x1, Pallas kernels: 165 us -> 170 us  [finish_row(): pl.pallas_call(functools.partial(finish_kernel, held=held), in_specs=[hbm...]
    unnamed x48 -> x30, local copies, waits for them, and re-layouts: 8.98 us -> 4.31 us
    ppermute x1, waiting for transfers between devices: 5.77 us -> 10 us  [on_device(): latent_in_second = lax.ppermute(early_b.latent_out, SECTION, [(1, 0)])]
where the time goes in v7:
time: 397 us; the launch traced here: 390 us
  Pallas kernels  343 us (86%)
  waiting for transfers between devices  22.1 us (6%)
  loops' own time  14.5 us (4%)
  local copies, waits for them, and re-layouts  6.57 us (2%)
    pallas_call x1, Pallas kernels, finish_row(): pl.pallas_call(functools.partial(finish_kernel, held=held), in_specs=[hbm...  170 us
    pallas_call x7, Pallas kernels, call(): pl.pallas_call(kernel, grid=(self.count // self.size,), in_specs=in_specs...  75.6 us
    pallas_call x3, Pallas kernels, attention_call(): pl.pallas_call(functools.partial(kernel, row=row), grid_spec=pltpu.Prefet...  46.9 us
    pallas_call x2, Pallas kernels, weight_call(): pl.pallas_call(kernel, grid=(steps,), in_specs=in_specs, out_specs=out_sp...  21.8 us
    ppermute x1, waiting for transfers between devices, on_device(): latent_in = lax.ppermute(early_a.latent_out, SECTION, [(1, 0)])  12.1 us
    pallas_call x1, Pallas kernels, unpack(): pl.pallas_call(unpack_kernel, in_specs=[pl.BlockSpec(memory_space=pltpu.S...  11.8 us
    ppermute x1, waiting for transfers between devices, on_device(): latent_in_second = lax.ppermute(early_b.latent_out, SECTION, [(1, 0)])  10 us
    pallas_call x1, Pallas kernels, scatter_codes(): pl.pallas_call(scatter_kernel, in_specs=[pl.BlockSpec(memory_space=pltpu....  9.98 us
  transfers between devices with their start and end apart: 2, of which 2 were waited for; matrix products, arithmetic and copies ran while one was open for 0% of the time, Pallas kernels for 0%

profile of v7, /device:TPU:0, one launch (start us, length us, event | category | flops | bytes accessed | tf_op | source)
XLA Modules:
  0.0 390.4 jit_solution(6134983470415032346)
XLA Ops:
  0.7 0.7 copy.52
  1.4 0.7 reshape.59
  2.1 0.1 fusion
  2.1 0.1 copy.46
  2.2 0.1 copy.45
  2.3 0.2 select_reduce_fusion.1
  2.6 0.1 copy.42
  2.7 0.1 reshape.60.windows
  2.8 0.7 copy.51
  3.5 7.5 %shard_map.263 = (f32[2048,32]{1,0:T(8,128)S(1)}, bf16[2048,128]{1,0:T(8,128)(2,1)S(1)}, bf16[2,1024,128]{2,1,0:T(8,128)(2,1)}, bf16[2,1024,128]{2,1,0:T(8,128)(2,1)}) custom-call(s32[2048]{0:T(1024)S(1)} %bitcast.99, f32[32,8192]{1,0:T(8,128)} %bitcast.70, s32[2,1024]{1,0:T(2,128)} %segments.1), custom_call_target="tpu_custom_call" | custom-call | tf_op jit(solution)/shard_map/pallas_call | solution.py:108
  11.0 0.0 copy-start.3
  11.0 0.0 copy-start.17
  11.1 0.0 copy-start.25
  11.1 0.0 copy-start.28
  11.1 0.0 copy-start.29
  11.1 0.0 copy-start.30
  11.1 0.0 copy-start.31
  11.1 0.0 copy-start.37
  11.1 5.6 %shard_map.264 = (bf16[1024,512]{1,0:T(8,128)(2,1)}, bf16[1024,512]{1,0:T(8,128)(2,1)}, bf16[1024,512]{1,0:T(8,128)(2,1)}, bf16[1024,512]{1,0:T(8,128)(2,1)}) custom-call(s32[1]{0:T(128)} %bitcast.side, bf16[2,1024,512]{2,1,0:T(8,128)(2,1)} %bitcast.38, bf16[2048,128]{1,0:T(8,128)(2,1)S(1)} %get-tuple-element.585.wide, f32[32,512]{1,0:T(8,128)} %up.3, ...), custom_call_target="tpu_custom_call" | custom-call | tf_op jit(solution)/shard_map/pallas_call | solution.py:1170
  16.7 13.3 %shard_map.265 = (bf16[1024,512]{1,0:T(8,128)(2,1)}, bf16[1024,512]{1,0:T(8,128)(2,1)}) custom-call(s32[16]{0:T(128)S(1)} %reshape.60.windows, bf16[1024,512]{1,0:T(8,128)(2,1)} %get-tuple-element.586.query, bf16[1024,512]{1,0:T(8,128)(2,1)} %get-tuple-element.587.key, bf16[1024,512]{1,0:T(8,128)(2,1)} %get-tuple-element.588.value, ...), custom_call_target="tpu_custom_call" | custom-call | tf_op jit(solution)/shard_map/pallas_call | solution.py:1188
  30.1 14.3 %shard_map.266 = (f32[1024,512]{1,0:T(8,128)}, bf16[1024,512]{1,0:T(8,128)(2,1)}, bf16[1024,2048]{1,0:T(8,128)(2,1)}, bf16[1024,2048]{1,0:T(8,128)(2,1)}, f32[1024,512]{1,0:T(8,128)}, /*index=5*/f32[1024,32]{1,0:T(8,128)}) custom-call(s32[1]{0:T(128)} %bitcast.side, bf16[2,1024,512]{2,1,0:T(8,128)(2,1)S(1)} %bitcast.39, ...), custom_call_target="tpu_custom_call" | custom-call | tf_op jit(solution)/shard_map/pallas_call | solution.py:1170
  44.4 35.5 %conditional.3 = (bf16[1024,512]{1,0:T(8,128)(2,1)}, bf16[1024,512]{1,0:T(8,128)(2,1)}, bf16[1024,512]{1,0:T(8,128)(2,1)}, bf16[1024,512]{1,0:T(8,128)(2,1)}, bf...) conditional(s32[]{:T(128)} %convert_element_type.2, ...), branch_computations={%region_2.3_spmd, %region_3.4_spmd} | conditional | bytes 14811408 | solution.py:1330
  50.2 5.2 %branch_1_fun.12 = (bf16[1024,512]{1,0:T(8,128)(2,1)}, bf16[1024,512]{1,0:T(8,128)(2,1)}, bf16[1024,512]{1,0:T(8,128)(2,1)}, bf16[1024,512]{1,0:T(8,128)(2,1)}) custom-call(s32[1]{0:T(128)} %get-tuple-element.306.side, bf16[2,1024,512]{2,1,0:T(8,128)(2,1)S(1)} %get-tuple-element.307.edge, bf16[2048,128]{1,0:T(8,128)(2,1)S(1)} %get-tuple-element.308.wide, ...), custom_call_target="tpu_custom_call" | custom-call | tf_op jit(solution)/shard_map/cond/branch_1_fun/pallas_call | solution.py:1170
  55.4 10.2 %branch_1_fun.13 = (bf16[1024,512]{1,0:T(8,128)(2,1)}, bf16[1024,512]{1,0:T(8,128)(2,1)}) custom-call(s32[16]{0:T(128)S(1)} %get-tuple-element.318.windows, bf16[1024,512]{1,0:T(8,128)(2,1)} %get-tuple-element.737.query, bf16[1024,512]{1,0:T(8,128)(2,1)} %get-tuple-element.738.key, bf16[1024,512]{1,0:T(8,128)(2,1)} %get-tuple-element.739.value, ...), custom_call_target="tpu_custom_call" | custom-call | tf_op jit(solution)/shard_map/cond/branch_1_fun/pallas_call | solution.py:1188
  65.7 14.3 %branch_1_fun.14 = (f32[1024,512]{1,0:T(8,128)}, bf16[1024,512]{1,0:T(8,128)(2,1)}, bf16[1024,2048]{1,0:T(8,128)(2,1)}, bf16[1024,2048]{1,0:T(8,128)(2,1)}, f32[1024,512]{1,0:T(8,128)}, /*index=5*/f32[1024,32]{1,0:T(8,128)}) custom-call(s32[1]{0:T(128)} %get-tuple-element.306.side, bf16[2,1024,512]{2,1,0:T(8,128)(2,1)S(1)} %get-tuple-element.307.edge, ...), custom_call_target="tpu_custom_call" | custom-call | tf_op jit(solution)/shard_map/cond/branch_1_fun/pallas_call | solution.py:1170
  79.9 1.3 collective-permute-start
  81.2 12.1 %collective-permute-done = f32[32,1024]{1,0:T(8,128)S(1)} collective-permute-done((f32[32,1024]{1,0:T(8,128)}, f32[32,1024]{1,0:T(8,128)S(1)}, u32[]{:S(2)}, u32[]{:S(2)}) %collective-permute-start) | collective-permute-done | bytes 131104 | tf_op jit(solution)/shard_map/ppermute | solution.py:1331
  93.3 73.9 %conditional.4 = (bf16[1024,512]{1,0:T(8,128)(2,1)}, bf16[1024,512]{1,0:T(8,128)(2,1)}, bf16[1024,512]{1,0:T(8,128)(2,1)}, bf16[1024,2048]{1,0:T(8,128)(2,1)}, f...) conditional(s32[]{:T(128)} %convert_element_type.2, ...), branch_computations={%region_4.5_spmd, %region_5.6_spmd} | conditional | bytes 32375248 | solution.py:1343
  101.5 0.0 copy-start.23
  101.5 14.8 %branch_1_fun.17 = (bf16[1024,512]{1,0:T(8,128)(2,1)}, bf16[1024,2048]{1,0:T(8,128)(2,1)}, f32[1024,512]{1,0:T(8,128)}, bf16[1024,512]{1,0:T(8,128)(2,1)}, bf16[...) custom-call(s32[1]{0:T(128)} %get-tuple-element.403.side, ...), custom_call_target="tpu_custom_call" | custom-call | tf_op jit(solution)/shard_map/cond/branch_1_fun/pallas_call | solution.py:1170
  116.4 0.0 copy-start.16
  116.4 10.0 %branch_1_fun.21 = f32[512,512]{1,0:T(8,128)} custom-call(s32[2048]{0:T(1024)S(1)} %get-tuple-element.445.index, f32[2048,32]{1,0:T(8,128)S(1)} %get-tuple-element.406.unit, f32[1024,32]{1,0:T(8,128)S(1)} %copy-done.19, f32[1024,32]{1,0:T(8,128)S(1)} %copy-done.26, f32[32,8192]{1,0:T(8,128)S(1)} %copy-done.23), custom_call_target="tpu_custom_call" | custom-call | tf_op jit(solution)/shard_map/cond/branch_1_fun/pallas_call | solution.py:162
  126.4 0.0 copy-done.14
  126.4 23.3 %branch_1_fun.18 = (bf16[1024,512]{1,0:T(8,128)(2,1)}, bf16[1024,512]{1,0:T(8,128)(2,1)}, bf16[1024,512]{1,0:T(8,128)(2,1)}) custom-call(s32[16]{0:T(128)S(1)} %get-tuple-element.424.windows, bf16[1024,512]{1,0:T(8,128)(2,1)S(1)} %copy-done.16, bf16[1024,512]{1,0:T(8,128)(2,1)} %get-tuple-element.426.marks, bf16[1024,512]{1,0:T(8,128)(2,1)} %get-tuple-element.427.key, ...), custom_call_target="tpu_custom_call" | custom-call | tf_op jit(solution)/shard_map/cond/branch_1_fun/pallas_call | solution.py:1188
  149.7 6.7 %branch_1_fun.19 = (f32[1024,512]{1,0:T(8,128)}, f32[32,1024]{1,0:T(8,128)}, f32[16,512]{1,0:T(8,128)}, f32[32,512]{1,0:T(8,128)}) custom-call(s32[1]{0:T(128)} %get-tuple-element.403.side, bf16[2,1024,512]{2,1,0:T(8,128)(2,1)S(1)} %get-tuple-element.405.cotangent.edge, bf16[2048,128]{1,0:T(8,128)(2,1)S(1)} %copy-done.10, ...), custom_call_target="tpu_custom_call" | custom-call | tf_op jit(solution)/shard_map/cond/branch_1_fun/pallas_call | solution.py:1170
  156.5 10.3 %branch_1_fun.20 = f32[4096,512]{1,0:T(8,128)} custom-call(bf16[1024,2048]{1,0:T(8,128)(2,1)} %get-tuple-element.443.active, bf16[1024,512]{1,0:T(8,128)(2,1)} %get-tuple-element.783.out_low, bf16[1024,512]{1,0:T(8,128)(2,1)S(1)} %copy-done.20, bf16[1024,2048]{1,0:T(8,128)(2,1)} %get-tuple-element.784.preact_low), custom_call_target="tpu_custom_call" | custom-call | tf_op jit(solution)/shard_map/cond/branch_1_fun/pallas_call | solution.py:513
  167.2 1.3 collective-permute-start.1
  168.5 10.0 %collective-permute-done.1 = f32[32,1024]{1,0:T(8,128)S(1)} collective-permute-done((f32[32,1024]{1,0:T(8,128)}, f32[32,1024]{1,0:T(8,128)S(1)}, u32[]{:S(2)}, u32[]{:S(2)}) %collective-permute-start.1) | collective-permute-done | bytes 131104 | tf_op jit(solution)/shard_map/ppermute | solution.py:1344
  178.5 27.6 %conditional.5 = (f32[4096,512]{1,0:T(8,128)}, f32[1024,512]{1,0:T(8,128)}, bf16[1024,512]{1,0:T(8,128)(2,1)S(1)}, bf16[1024,512]{1,0:T(8,128)(2,1)}, f32[16,512]{1,0:T(8,128)S(1)}, /*index=5*/f32[32,512]{1,0:T(8,128)S(1)}) conditional(s32[]{:T(128)} %convert_element_type.2, (bf16[1024,2048]{1,0:T(8,128)(2,1)}, bf16[1024,512]{1,0:T(8,128)(2,1)}, ...), branch_computations={%region_6.7_spmd, %region_7.8_spmd} | conditional | bytes 21168232 | solution.py:1354
  178.5 0.6 copy.154.refs_1_
  179.1 0.6 copy.153.refs_0_
  179.8 14.8 %branch_1_fun.22 = (bf16[1024,512]{1,0:T(8,128)(2,1)}, bf16[1024,2048]{1,0:T(8,128)(2,1)}, f32[1024,512]{1,0:T(8,128)}, bf16[1024,512]{1,0:T(8,128)(2,1)}, bf16[...) custom-call(s32[1]{0:T(128)} %get-tuple-element.462.side, ...), custom_call_target="tpu_custom_call" | custom-call | tf_op jit(solution)/shard_map/cond/branch_1_fun/pallas_call | solution.py:1170
  194.6 11.5 %branch_1_fun.23 = f32[4096,512]{1,0:T(8,128)} custom-call(bf16[1024,2048]{1,0:T(8,128)(2,1)S(1)} %copy-done.24, bf16[1024,512]{1,0:T(8,128)(2,1)} %get-tuple-element.480.out_low, bf16[1024,512]{1,0:T(8,128)(2,1)} %get-tuple-element.481.n2, bf16[1024,2048]{1,0:T(8,128)(2,1)} %get-tuple-element.482.preact_low, ...), custom_call_target="tpu_custom_call", output_to_operand_aliasing={{}: (4, {})} | custom-call | tf_op jit(solution)/shard_map/cond/branch_1_fun/pallas_call | solution.py:513
  206.1 0.0 copy-done.27
  206.1 169.6 %shard_map.267 = (f32[4096,512]{1,0:T(8,128)}, f32[2048,512]{1,0:T(8,128)}, f32[768,512]{1,0:T(8,128)}, f32[1024,512]{1,0:T(8,128)}) custom-call(f32[4096,512]{1,0:T(8,128)} %get-tuple-element.621.refs_0_, bf16[1024,512]{1,0:T(8,128)(2,1)} %get-tuple-element.622.refs_1_, bf16[1024,512]{1,0:T(8,128)(2,1)} %get-tuple-element.623.refs_2_, ...), custom_call_target="tpu_custom_call" | custom-call | tf_op jit(solution)/shard_map/pallas_call | solution.py:972
  375.7 11.8 %shard_map.268 = (f32[2048,512]{1,0:T(8,128)}, f32[512,2048]{1,0:T(8,128)}, f32[512,512]{1,0:T(8,128)}, f32[512,1536]{1,0:T(8,128)}, f32[2,1024,512]{2,1,0:T(8,1...) custom-call(s32[1]{0:T(128)} %bitcast.side, ...), custom_call_target="tpu_custom_call" | custom-call | tf_op jit(solution)/shard_map/pallas_call | solution.py:1054
  387.5 1.3 copy.48
  388.8 1.3 copy.43
  (38 shorter events, 0.1 us)
Async XLA Ops:
  11.0 33.4 %copy-start.8 = (bf16[2048,128]{1,0:T(8,128)(2,1)}, bf16[2048,128]{1,0:T(8,128)(2,1)S(1)}, u32[]{:S(2)}) copy-start(bf16[2048,128]{1,0:T(8,128)(2,1)S(1)} %get-tuple-element.585.wide) | copy-start | bytes 1572868
  11.0 19.0 %copy-start = (bf16[1,2,1024,512]{3,2,1,0:T(8,128)(2,1)S(1)}, bf16[1,2,1024,512]{3,2,1,0:T(8,128)(2,1)}, u32[]{:S(2)}) copy-start(bf16[1,2,1024,512]{3,2,1,0:T(8,128)(2,1)} %param.22) | copy-start | bytes 6291460
  11.0 19.0 %copy-start.1 = (bf16[1,512,2048]{2,1,0:T(8,128)(2,1)S(1)}, bf16[1,512,2048]{2,1,0:T(8,128)(2,1)}, u32[]{:S(2)}) copy-start(bf16[1,512,2048]{2,1,0:T(8,128)(2,1)} %param.27) | copy-start | bytes 6291460
  11.0 19.0 %copy-start.3 = (bf16[1,2048,512]{2,1,0:T(8,128)(2,1)S(1)}, bf16[1,2048,512]{2,1,0:T(8,128)(2,1)}, u32[]{:S(2)}) copy-start(bf16[1,2048,512]{2,1,0:T(8,128)(2,1)} %param.28) | copy-start | bytes 6291460
  11.0 19.0 %copy-start.17 = (f32[32,512]{1,0:T(8,128)S(1)}, f32[32,512]{1,0:T(8,128)}, u32[]{:S(2)}) copy-start(f32[32,512]{1,0:T(8,128)} %up.3) | copy-start | bytes 196612
  11.1 19.0 %copy-start.25 = (f32[512,32]{0,1:T(8,128)S(1)}, f32[512,32]{0,1:T(8,128)}, u32[]{:S(2)}) copy-start(f32[512,32]{0,1:T(8,128)} %param.34) | copy-start | bytes 196612
  11.1 19.0 %copy-start.28 = (f32[1,2,512]{2,1,0:T(2,128)S(1)}, f32[1,2,512]{2,1,0:T(2,128)}, u32[]{:S(2)}) copy-start(f32[1,2,512]{2,1,0:T(2,128)} %param.29) | copy-start | bytes 12292
  11.1 19.0 %copy-start.29 = (f32[2,512]{1,0:T(2,128)S(1)}, f32[2,512]{1,0:T(2,128)}, u32[]{:S(2)}) copy-start(f32[2,512]{1,0:T(2,128)} %head_bias.3) | copy-start | bytes 12292
  11.1 19.0 %copy-start.30 = (f32[512]{0:T(512)S(1)}, f32[512]{0:T(512)}, u32[]{:S(2)}) copy-start(f32[512]{0:T(512)} %param.32) | copy-start | bytes 6148
  11.1 19.0 %copy-start.31 = (f32[1,2048]{1,0:T(1,128)S(1)}, f32[1,2048]{1,0:T(1,128)}, u32[]{:S(2)}) copy-start(f32[1,2048]{1,0:T(1,128)} %hidden_bias.1) | copy-start | bytes 24580
  11.1 19.0 %copy-start.37 = (f32[32]{0:T(128)S(1)}, f32[32]{0:T(128)}, u32[]{:S(2)}) copy-start(f32[32]{0:T(128)} %param.35) | copy-start | bytes 388
  79.9 13.4 %collective-permute-start = (f32[32,1024]{1,0:T(8,128)}, f32[32,1024]{1,0:T(8,128)S(1)}, u32[]{:S(2)}, u32[]{:S(2)}) collective-permute-start(f32[32,1024]{1,0:T(8,128)} %get-tuple-element.606), channel_id=1, source_target_pairs={{16,0},{17,1},{18,2},{19,3},{20,4},{21,5},{22,6},{23,7},{24,8},{25... | collective-permute-start | bytes 393224 | tf_op jit(solution)/shard_map/ppermute | solution.py:1331
  101.5 14.8 %copy-start.19 = (f32[1024,32]{1,0:T(8,128)S(1)}, f32[1024,32]{1,0:T(8,128)}, u32[]{:S(2)}) copy-start(f32[1024,32]{1,0:T(8,128)} %get-tuple-element.408.latent.latent_first) | copy-start | bytes 393220 | tf_op jit(solution)/shard_map/cond
  101.5 14.8 %copy-start.23 = (f32[32,8192]{1,0:T(8,128)S(1)}, f32[32,8192]{1,0:T(8,128)}, u32[]{:S(2)}) copy-start(f32[32,8192]{1,0:T(8,128)} %get-tuple-element.447.table_turned) | copy-start | bytes 3145732 | tf_op jit(solution)/shard_map/cond
  101.5 14.8 %copy-start.26 = (f32[1024,32]{1,0:T(8,128)S(1)}, f32[1024,32]{1,0:T(8,128)}, u32[]{:S(2)}) copy-start(f32[1024,32]{1,0:T(8,128)} %get-tuple-element.446.latent_second) | copy-start | bytes 393220 | tf_op jit(solution)/shard_map/cond
  116.3 10.0 %copy-start.11 = (bf16[1024,512]{1,0:T(8,128)(2,1)S(1)}, bf16[1024,512]{1,0:T(8,128)(2,1)}, u32[]{:S(2)}) copy-start(bf16[1024,512]{1,0:T(8,128)(2,1)} %get-tuple-element.430.context) | copy-start | bytes 3145732 | tf_op jit(solution)/shard_map/cond
  116.3 10.0 %copy-start.14 = (bf16[2,1024,128]{2,1,0:T(8,128)(2,1)S(1)}, bf16[2,1024,128]{2,1,0:T(8,128)(2,1)}, u32[]{:S(2)}) copy-start(bf16[2,1024,128]{2,1,0:T(8,128)(2,1)} %get-tuple-element.431.key_mark) | copy-start | bytes 1572868 | tf_op jit(solution)/shard_map/cond
  116.4 10.0 %copy-start.16 = (bf16[1024,512]{1,0:T(8,128)(2,1)S(1)}, bf16[1024,512]{1,0:T(8,128)(2,1)}, u32[]{:S(2)}) copy-start(bf16[1024,512]{1,0:T(8,128)(2,1)} %get-tuple-element.425.query) | copy-start | bytes 3145732 | tf_op jit(solution)/shard_map/cond
  126.3 23.4 %copy-start.7 = (bf16[512,1536]{1,0:T(8,128)(2,1)S(1)}, bf16[512,1536]{1,0:T(8,128)(2,1)}, u32[]{:S(2)}) copy-start(bf16[512,1536]{1,0:T(8,128)(2,1)} %get-tuple-element.437.weight) | copy-start | bytes 4718596 | tf_op jit(solution)/shard_map/cond
  126.4 23.4 %copy-start.10 = (bf16[2048,128]{1,0:T(8,128)(2,1)S(1)}, bf16[2048,128]{1,0:T(8,128)(2,1)}, u32[]{:S(2)}) copy-start(bf16[2048,128]{1,0:T(8,128)(2,1)} %get-tuple-element.435.wide) | copy-start | bytes 1572868 | tf_op jit(solution)/shard_map/cond
  149.7 6.7 %copy-start.20 = (bf16[1024,512]{1,0:T(8,128)(2,1)S(1)}, bf16[1024,512]{1,0:T(8,128)(2,1)}, u32[]{:S(2)}) copy-start(bf16[1024,512]{1,0:T(8,128)(2,1)} %get-tuple-element.444.n2) | copy-start | bytes 3145732 | tf_op jit(solution)/shard_map/cond
  167.2 11.3 %collective-permute-start.1 = (f32[32,1024]{1,0:T(8,128)}, f32[32,1024]{1,0:T(8,128)S(1)}, u32[]{:S(2)}, u32[]{:S(2)}) collective-permute-start(f32[32,1024]{1,0:T(8,128)} %get-tuple-element.615), channel_id=1, source_target_pairs={{16,0},{17,1},{18,2},{19,3},{20,4},{21,5},{22,6},{23,7},{24,8},{25... | collective-permute-start | bytes 393224 | tf_op jit(solution)/shard_map/ppermute | solution.py:1344
  178.5 27.6 %copy-start.34 = (f32[32,512]{1,0:T(8,128)S(1)}, f32[32,512]{1,0:T(8,128)}, u32[]{:S(2)}) copy-start(f32[32,512]{1,0:T(8,128)} %get-tuple-element.644.refs_34_) | copy-start | bytes 196612
  179.8 14.8 %copy-start.24 = (bf16[1024,2048]{1,0:T(8,128)(2,1)S(1)}, bf16[1024,2048]{1,0:T(8,128)(2,1)}, u32[]{:S(2)}) copy-start(bf16[1024,2048]{1,0:T(8,128)(2,1)} %get-tuple-element.461.active) | copy-start | bytes 12582916 | tf_op jit(solution)/shard_map/cond
  194.6 11.5 %copy-start.27 = (bf16[1024,512]{1,0:T(8,128)(2,1)S(1)}, bf16[1024,512]{1,0:T(8,128)(2,1)}, u32[]{:S(2)}) copy-start(bf16[1024,512]{1,0:T(8,128)(2,1)} %get-tuple-element.805) | copy-start | bytes 3145732 | tf_op jit(solution)/shard_map/cond

commit v8 on v7

--- a/solution.py
+++ b/solution.py
@@ -180,13 +180,13 @@
     encoder = side[0] == 0
     values = entry_values(encoder, edge[...], wide[...], up[...], head_bias[...])
     hat, unused = norm_parts(values)
-    normed = (hat * gains[0:1, :] + biases[3:4, :]).astype(BF)
+    normed = (hat * gains[0:1, :] + biases[3]).astype(BF)
     n1[...] = normed
     query[...] = (
-        (dot(normed, weight[:, :width], NN) + biases[0:1, :]) * (LOG2E * HEAD ** (-0.5))
+        (dot(normed, weight[:, :width], NN) + biases[0]) * (LOG2E * HEAD ** (-0.5))
     ).astype(BF)
     key[...] = dot(normed, weight[:, width : 2 * width], NN).astype(BF)
-    value[...] = (dot(normed, weight[:, 2 * width :], NN) + biases[1:2, :]).astype(BF)
+    value[...] = (dot(normed, weight[:, 2 * width :], NN) + biases[1]).astype(BF)
 
 
 def merge(low_half, left, right):
@@ -271,12 +271,12 @@
     encoder = side[0] == 0
     width = edge.shape[1]
     values = entry_values(encoder, edge[...], wide[...], up[...], head_bias[...])
-    midway = values + (dot(context[...], weight_out[...], NN) + biases[2:3, :])
+    midway = values + (dot(context[...], weight_out[...], NN) + biases[2])
     mid[...] = midway
     hat, unused = norm_parts(midway)
-    normed = (hat * gains[1:2, :] + biases[4:5, :]).astype(BF)
+    normed = (hat * gains[1:2, :] + biases[4]).astype(BF)
     n2[...] = normed
-    total = midway + biases[5:6, :]
+    total = midway + biases[5]
     chunk = 256
     for start in range(0, weight_in.shape[1], chunk):
         here = slice(start, start + chunk)
@@ -822,6 +822,12 @@
         ring.begin()
     misc[...] = jnp.zeros_like(misc)
 
+    def attention_piece(turn):
+        attend_back_block(
+            turn // pairs, 0, count, (turn % pairs) * 128, 1,
+            query_in, marks_in, key_in, value_in, grad_in, key_mark_in, grad_mark, query_grad, key_total, value_total,
+        )
+
     @pl.when(encoder)
     def _():
         misc[: book.shape[0], :] = book[...]
@@ -832,6 +838,7 @@
         mark_grads(grad_in, context_in, grad_mark)
         key_total[...] = jnp.zeros_like(key_total)
         value_total[...] = jnp.zeros_like(value_total)
+        loop(0, 2, attention_piece)
 
     @pl.when(decoder)
     def _():
@@ -840,12 +847,6 @@
         misc[at + 48 : at + 64, :] = early[...]
         wait(other_loads)
 
-    def attention_piece(turn):
-        attend_back_block(
-            turn // pairs, 0, count, (turn % pairs) * 128, 1,
-            query_in, marks_in, key_in, value_in, grad_in, key_mark_in, grad_mark, query_grad, key_total, value_total,
-        )
-
     def entry_piece(number):
         rows = pl.ds(pl.multiple_of(number * TOKENS, TOKENS), TOKENS)
         normed_grad = (
@@ -880,9 +881,9 @@
 
             @pl.when(encoder)
             def _():
-                attention_piece(2 * (step - 1) + half)
-
-    inside = min(chips - 1, pieces // 2)
+                attention_piece(2 * step + half)
+
+    inside = min(chips - 1, pieces // 2 - 1)
     loop(1, inside + 1, summing)
     if ring:
         loop(inside + 1, chips, ring.gather)
@@ -890,11 +891,10 @@
 
     @pl.when(encoder)
     def _():
-        loop(2 * inside, pieces, attention_piece)
+        loop(2 * inside + 2, pieces, attention_piece)
         start(first_loads)
         key_grad[...] = (key_total[...] * (1.0 / LOG2E)).astype(BF)
         value_grad[...] = value_total[...].astype(BF)
-        wait(first_loads)
 
     def spreading(step):
         if ring:
@@ -906,6 +906,7 @@
 
         if ring:
             ring.pass_out(step, halves[1])
+        pl.when(encoder & (step == 1))(functools.partial(wait, first_loads))
         weight_piece(step - 1)
 
     loop(1, steps + 1, spreading)
@@ -1031,10 +1032,12 @@
     head_bias[1:2, :] = head[at + 52 : at + 53, :]
     down_last[...] = head[at + 10 : at + 11, :narrow]
     mine = jnp.where(side[0] == 0, head[at : at + 32, :], head[at + 32 : at + 64, :])
-    bias[...] = mine[:steps, :]
-    for out, places in ((gains, (18, 6)), (biases, (16, 17, 5, 19, 7, 4))):
-        for number, place in enumerate(places):
-            out[number : number + 1, :] = mine[place : place + 1, :]
+    for number in range(steps):
+        bias[:, number * width : (number + 1) * width] = mine[number : number + 1, :]
+    for number, place in enumerate((18, 6)):
+        gains[number : number + 1, :] = mine[place : place + 1, :]
+    for number, place in enumerate((16, 17, 5, 19, 7, 4)):
+        biases[number] = mine[place : place + 1, :]
     for store in stores:
         store.wait()
 
@@ -1047,7 +1050,7 @@
     rows = table_turned.size // width + 2 * narrow + 64
     shapes = (
         (features, width), (width, features), (width, width), (width, 3 * width), (2,) + ends[0].shape,
-        table_turned.shape, (2, width), (6, width), (features // width, width), (1, width), (2, width),
+        table_turned.shape, (2, width), (6, 1, width), (1, features), (1, width), (2, width),
         (narrow, width), (1, narrow), (narrow, width),
     )
     hbm, vmem = pl.BlockSpec(memory_space=pl.ANY), pl.BlockSpec(memory_space=pltpu.VMEM)
@@ -1311,14 +1314,14 @@
     work = Rows(
         side, edges, wide, unit, windows_of(segments), query_mark, key_mark,
         (
-            attention_in[0], attention_out[0], hidden_in[0], hidden_out[0], block_gains[0], block_biases[0],
+            attention_in[0], attention_out[0], hidden_in[0], hidden_out[0], block_gains[0], block_biases.transpose(1, 0, 2),
             hidden_bias,
         ),
         (output_gain[None], head_bias, down_weight.T, down_bias[None], up_weight),
     )
     book_out = book_shape(table_turned, width)
     hidden_shape = jax.ShapeDtypeStruct((2 * hidden, width), F32)
-    quiet = jnp.zeros((unit.shape[1], count), F32)
+    quiet = unwritten(work.early.latent_out)
     first_kept = work.forward(0)
 
     def encoder_first():
@@ -1371,8 +1374,8 @@
         hidden_in_grad[None],
         hidden_out_grad[None],
         gains[None],
-        biases[None],
-        bias.reshape(1, hidden),
+        biases.transpose(1, 0, 2),
+        bias,
         last_gain[0],
         head,
         down_grad.T,

time: 397 us -> 394 us (level)
    pallas_call x1, Pallas kernels: 170 us -> 181 us  [finish_row(): pl.pallas_call(functools.partial(finish_kernel, held=held), in_specs=[hbm...]
    pallas_call x3, Pallas kernels: 46.9 us -> 38.2 us  [attention_call(): pl.pallas_call(functools.partial(kernel, row=row), grid_spec=pltpu.Prefet...]
    ppermute x1, waiting for transfers between devices: 12.1 us -> 6.37 us  [on_device(): latent_in = lax.ppermute(early_a.latent_out, SECTION, [(1, 0)])]
where the time goes in v8:
time: 394 us; the launch traced here: 388 us
  Pallas kernels  346 us (88%)
  waiting for transfers between devices  19.8 us (5%)
  loops' own time  14.6 us (4%)
    pallas_call x1, Pallas kernels, finish_row(): pl.pallas_call(functools.partial(finish_kernel, held=held), in_specs=[hbm...  181 us
    pallas_call x7, Pallas kernels, call(): pl.pallas_call(kernel, grid=(self.count // self.size,), in_specs=in_specs...  75.7 us
    pallas_call x3, Pallas kernels, attention_call(): pl.pallas_call(functools.partial(kernel, row=row), grid_spec=pltpu.Prefet...  38.2 us
    pallas_call x2, Pallas kernels, weight_call(): pl.pallas_call(kernel, grid=(steps,), in_specs=in_specs, out_specs=out_sp...  21.6 us
    ppermute x1, waiting for transfers between devices, on_device(): latent_in_second = lax.ppermute(early_b.latent_out, SECTION, [(1, 0)])  13.4 us
    pallas_call x1, Pallas kernels, unpack(): pl.pallas_call(unpack_kernel, in_specs=[pl.BlockSpec(memory_space=pltpu.S...  11.8 us
    pallas_call x1, Pallas kernels, scatter_codes(): pl.pallas_call(scatter_kernel, in_specs=[pl.BlockSpec(memory_space=pltpu....  10.5 us
    another operation x1, loops' own time, on_device(): lax.cond(encoder, encoder_second, decoder_second)  8.68 us
  transfers between devices with their start and end apart: 2, of which 2 were waited for; matrix products, arithmetic and copies ran while one was open for 0% of the time, Pallas kernels for 0%

profile of v8, /device:TPU:0, one launch (start us, length us, event | category | flops | bytes accessed | tf_op | source)
XLA Modules:
  0.0 387.7 jit_solution(15660301959790504036)
XLA Ops:
  0.7 0.7 copy.45
  1.4 0.7 reshape.56
  2.1 0.1 fusion
  2.2 0.1 copy.42
  2.3 0.1 copy.41
  2.4 0.2 select_reduce_fusion.1
  2.6 0.1 copy.40
  2.7 0.1 reshape.57.windows
  2.8 6.9 %shard_map.263 = (f32[2048,32]{1,0:T(8,128)}, bf16[2048,128]{1,0:T(8,128)(2,1)S(1)}, bf16[2,1024,128]{2,1,0:T(8,128)(2,1)S(1)}, bf16[2,1024,128]{2,1,0:T(8,128)(2,1)S(1)}) custom-call(s32[2048]{0:T(1024)S(1)} %bitcast.94, f32[32,8192]{1,0:T(8,128)} %bitcast.65, s32[2,1024]{1,0:T(2,128)} %segments.1), custom_call_target="tpu_custom_call" | custom-call | tf_op jit(solution)/shard_map/pallas_call | solution.py:108
  9.7 0.0 copy-start.1
  9.7 0.0 copy-start.3
  9.8 0.0 copy-start.25
  9.8 0.0 copy-start.34
  9.8 0.0 copy-start.35
  9.8 0.0 copy-start.36
  9.8 0.0 copy-start.37
  9.8 0.0 copy-start.39
  9.8 0.0 copy-start.40
  9.8 0.0 copy-start.45
  9.8 5.9 %shard_map.264 = (bf16[1024,512]{1,0:T(8,128)(2,1)}, bf16[1024,512]{1,0:T(8,128)(2,1)}, bf16[1024,512]{1,0:T(8,128)(2,1)}, bf16[1024,512]{1,0:T(8,128)(2,1)}) custom-call(s32[1]{0:T(128)} %bitcast.side, bf16[2,1024,512]{2,1,0:T(8,128)(2,1)} %bitcast.33, bf16[2048,128]{1,0:T(8,128)(2,1)S(1)} %get-tuple-element.591.wide, f32[32,512]{1,0:T(8,128)} %up.3, ...), custom_call_target="tpu_custom_call" | custom-call | tf_op jit(solution)/shard_map/pallas_call | solution.py:1173
  15.8 10.0 %shard_map.265 = (bf16[1024,512]{1,0:T(8,128)(2,1)}, bf16[1024,512]{1,0:T(8,128)(2,1)}) custom-call(s32[16]{0:T(128)S(1)} %reshape.57.windows, bf16[1024,512]{1,0:T(8,128)(2,1)} %get-tuple-element.592.query, bf16[1024,512]{1,0:T(8,128)(2,1)} %get-tuple-element.593.key, bf16[1024,512]{1,0:T(8,128)(2,1)} %get-tuple-element.594.value, ...), custom_call_target="tpu_custom_call" | custom-call | tf_op jit(solution)/shard_map/pallas_call | solution.py:1191
  25.8 0.0 copy-done.26
  25.8 0.0 copy-done
  25.8 0.0 copy-done.1
  25.9 0.0 copy-start.5
  25.9 14.4 %shard_map.266 = (f32[1024,512]{1,0:T(8,128)}, bf16[1024,512]{1,0:T(8,128)(2,1)}, bf16[1024,2048]{1,0:T(8,128)(2,1)}, bf16[1024,2048]{1,0:T(8,128)(2,1)}, f32[1024,512]{1,0:T(8,128)}, /*index=5*/f32[1024,32]{1,0:T(8,128)}) custom-call(s32[1]{0:T(128)} %bitcast.side, bf16[2,1024,512]{2,1,0:T(8,128)(2,1)S(1)} %bitcast.34, bf16[2048,128]{1,0:T(8,128)(2,1)} %copy-done.11, ...), custom_call_target="tpu_custom_call" | custom-call | tf_op jit(solution)/shard_map/pallas_call | solution.py:1173
  40.4 34.9 %conditional.3 = (bf16[1024,512]{1,0:T(8,128)(2,1)}, bf16[1024,512]{1,0:T(8,128)(2,1)}, bf16[1024,512]{1,0:T(8,128)(2,1)}, bf16[1024,512]{1,0:T(8,128)(2,1)}, bf...) conditional(s32[]{:T(128)} %convert_element_type.2, ...), branch_computations={%region_2.3_spmd, %region_3.4_spmd} | conditional | bytes 11534632 | solution.py:1333
  46.2 4.7 %branch_1_fun.12 = (bf16[1024,512]{1,0:T(8,128)(2,1)}, bf16[1024,512]{1,0:T(8,128)(2,1)}, bf16[1024,512]{1,0:T(8,128)(2,1)}, bf16[1024,512]{1,0:T(8,128)(2,1)}) custom-call(s32[1]{0:T(128)} %get-tuple-element.311.side, bf16[2,1024,512]{2,1,0:T(8,128)(2,1)S(1)} %get-tuple-element.312.edge, bf16[2048,128]{1,0:T(8,128)(2,1)} %get-tuple-element.313.wide, ...), custom_call_target="tpu_custom_call" | custom-call | tf_op jit(solution)/shard_map/cond/branch_1_fun/pallas_call | solution.py:1173
  50.9 10.2 %branch_1_fun.13 = (bf16[1024,512]{1,0:T(8,128)(2,1)}, bf16[1024,512]{1,0:T(8,128)(2,1)}) custom-call(s32[16]{0:T(128)S(1)} %get-tuple-element.323.windows, bf16[1024,512]{1,0:T(8,128)(2,1)} %get-tuple-element.701.query, bf16[1024,512]{1,0:T(8,128)(2,1)} %get-tuple-element.702.key, bf16[1024,512]{1,0:T(8,128)(2,1)} %get-tuple-element.703.value, ...), custom_call_target="tpu_custom_call" | custom-call | tf_op jit(solution)/shard_map/cond/branch_1_fun/pallas_call | solution.py:1191
  61.2 14.1 %branch_1_fun.14 = (f32[1024,512]{1,0:T(8,128)}, bf16[1024,512]{1,0:T(8,128)(2,1)}, bf16[1024,2048]{1,0:T(8,128)(2,1)}, bf16[1024,2048]{1,0:T(8,128)(2,1)}, f32[1024,512]{1,0:T(8,128)}, /*index=5*/f32[1024,32]{1,0:T(8,128)}) custom-call(s32[1]{0:T(128)} %get-tuple-element.311.side, bf16[2,1024,512]{2,1,0:T(8,128)(2,1)S(1)} %get-tuple-element.312.edge, ...), custom_call_target="tpu_custom_call" | custom-call | tf_op jit(solution)/shard_map/cond/branch_1_fun/pallas_call | solution.py:1173
  75.3 1.3 collective-permute-start
  76.6 6.4 %collective-permute-done = f32[32,1024]{1,0:T(8,128)S(1)} collective-permute-done((f32[32,1024]{1,0:T(8,128)}, f32[32,1024]{1,0:T(8,128)S(1)}, u32[]{:S(2)}, u32[]{:S(2)}) %collective-permute-start) | collective-permute-done | bytes 131104 | tf_op jit(solution)/shard_map/ppermute | solution.py:1334
  82.9 69.7 %conditional.4 = (bf16[1024,512]{1,0:T(8,128)(2,1)}, bf16[1024,512]{1,0:T(8,128)(2,1)}, bf16[1024,512]{1,0:T(8,128)(2,1)}, bf16[1024,2048]{1,0:T(8,128)(2,1)}, f...) conditional(s32[]{:T(128)} %convert_element_type.2, ...), branch_computations={%region_4.5_spmd, %region_5.6_spmd} | conditional | bytes 33030604 | solution.py:1346
  91.2 0.6 copy-done.38
  91.8 15.0 %branch_1_fun.17 = (bf16[1024,512]{1,0:T(8,128)(2,1)}, bf16[1024,2048]{1,0:T(8,128)(2,1)}, f32[1024,512]{1,0:T(8,128)}, bf16[1024,512]{1,0:T(8,128)(2,1)}, bf16[...) custom-call(s32[1]{0:T(128)} %get-tuple-element.409.side, ...), custom_call_target="tpu_custom_call" | custom-call | tf_op jit(solution)/shard_map/cond/branch_1_fun/pallas_call | solution.py:1173
  106.8 10.5 %branch_1_fun.21 = f32[512,512]{1,0:T(8,128)} custom-call(s32[2048]{0:T(1024)S(1)} %get-tuple-element.451.index, f32[2048,32]{1,0:T(8,128)S(1)} %copy-done.10, f32[1024,32]{1,0:T(8,128)S(1)} %copy-done.28, f32[1024,32]{1,0:T(8,128)} %get-tuple-element.452.latent_second, f32[32,8192]{1,0:T(8,128)S(1)} %copy-done.32), custom_call_target="tpu_custom_call" | custom-call | tf_op jit(solution)/shard_map/cond/branch_1_fun/pallas_call | solution.py:162
  117.4 17.9 %branch_1_fun.18 = (bf16[1024,512]{1,0:T(8,128)(2,1)}, bf16[1024,512]{1,0:T(8,128)(2,1)}, bf16[1024,512]{1,0:T(8,128)(2,1)}) custom-call(s32[16]{0:T(128)S(1)} %get-tuple-element.430.windows, bf16[1024,512]{1,0:T(8,128)(2,1)S(1)} %copy-done.24, bf16[1024,512]{1,0:T(8,128)(2,1)} %get-tuple-element.432.marks, bf16[1024,512]{1,0:T(8,128)(2,1)} %get-tuple-element.433.key, ...), custom_call_target="tpu_custom_call" | custom-call | tf_op jit(solution)/shard_map/cond/branch_1_fun/pallas_call | solution.py:1191
  135.3 6.7 %branch_1_fun.19 = (f32[1024,512]{1,0:T(8,128)}, f32[32,1024]{1,0:T(8,128)}, f32[16,512]{1,0:T(8,128)}, f32[32,512]{1,0:T(8,128)}) custom-call(s32[1]{0:T(128)} %get-tuple-element.409.side, bf16[2,1024,512]{2,1,0:T(8,128)(2,1)S(1)} %get-tuple-element.411.cotangent.edge, bf16[2048,128]{1,0:T(8,128)(2,1)S(1)} %copy-done.15, ...), custom_call_target="tpu_custom_call" | custom-call | tf_op jit(solution)/shard_map/cond/branch_1_fun/pallas_call | solution.py:1173
  142.0 10.2 %branch_1_fun.20 = f32[4096,512]{1,0:T(8,128)} custom-call(bf16[1024,2048]{1,0:T(8,128)(2,1)} %get-tuple-element.449.active, bf16[1024,512]{1,0:T(8,128)(2,1)} %get-tuple-element.747.out_low, bf16[1024,512]{1,0:T(8,128)(2,1)S(1)} %copy-done.29, bf16[1024,2048]{1,0:T(8,128)(2,1)} %get-tuple-element.748.preact_low), custom_call_target="tpu_custom_call" | custom-call | tf_op jit(solution)/shard_map/cond/branch_1_fun/pallas_call | solution.py:513
  152.6 1.3 collective-permute-start.1
  153.9 13.4 %collective-permute-done.1 = f32[32,1024]{1,0:T(8,128)S(1)} collective-permute-done((f32[32,1024]{1,0:T(8,128)}, f32[32,1024]{1,0:T(8,128)S(1)}, u32[]{:S(2)}, u32[]{:S(2)}) %collective-permute-start.1) | collective-permute-done | bytes 131104 | tf_op jit(solution)/shard_map/ppermute | solution.py:1347
  167.3 27.5 %conditional.5 = (f32[4096,512]{1,0:T(8,128)}, f32[1024,512]{1,0:T(8,128)}, bf16[1024,512]{1,0:T(8,128)(2,1)}, bf16[1024,512]{1,0:T(8,128)(2,1)}, f32[16,512]{1,0:T(8,128)S(1)}, /*index=5*/f32[32,512]{1,0:T(8,128)S(1)}) conditional(s32[]{:T(128)} %convert_element_type.2, (bf16[1024,2048]{1,0:T(8,128)(2,1)}, bf16[1024,512]{1,0:T(8,128)(2,1)}, ...), branch_computations={%region_6.7_spmd, %region_7.8_spmd} | conditional | bytes 16973900 | solution.py:1357
  167.3 0.6 copy.147.refs_1_
  168.0 0.6 copy.146.refs_0_
  168.6 14.9 %branch_1_fun.22 = (bf16[1024,512]{1,0:T(8,128)(2,1)}, bf16[1024,2048]{1,0:T(8,128)(2,1)}, f32[1024,512]{1,0:T(8,128)}, bf16[1024,512]{1,0:T(8,128)(2,1)}, bf16[...) custom-call(s32[1]{0:T(128)} %get-tuple-element.468.side, ...), custom_call_target="tpu_custom_call" | custom-call | tf_op jit(solution)/shard_map/cond/branch_1_fun/pallas_call | solution.py:1173
  183.5 11.4 %branch_1_fun.23 = f32[4096,512]{1,0:T(8,128)} custom-call(bf16[1024,2048]{1,0:T(8,128)(2,1)S(1)} %copy-done.33, bf16[1024,512]{1,0:T(8,128)(2,1)} %get-tuple-element.486.out_low, bf16[1024,512]{1,0:T(8,128)(2,1)} %get-tuple-element.487.n2, bf16[1024,2048]{1,0:T(8,128)(2,1)} %get-tuple-element.488.preact_low, ...), custom_call_target="tpu_custom_call", output_to_operand_aliasing={{}: (4, {})} | custom-call | tf_op jit(solution)/shard_map/cond/branch_1_fun/pallas_call | solution.py:513
  194.8 180.9 %shard_map.268 = (f32[4096,512]{1,0:T(8,128)}, f32[2048,512]{1,0:T(8,128)}, f32[768,512]{1,0:T(8,128)}, f32[1024,512]{1,0:T(8,128)}) custom-call(f32[4096,512]{1,0:T(8,128)} %get-tuple-element.627.refs_0_, bf16[1024,512]{1,0:T(8,128)(2,1)} %get-tuple-element.628.refs_1_, bf16[1024,512]{1,0:T(8,128)(2,1)} %get-tuple-element.629.refs_2_, ...), custom_call_target="tpu_custom_call" | custom-call | tf_op jit(solution)/shard_map/pallas_call | solution.py:973
  375.7 11.8 %shard_map.269 = (f32[2048,512]{1,0:T(8,128)}, f32[512,2048]{1,0:T(8,128)}, f32[512,512]{1,0:T(8,128)}, f32[512,1536]{1,0:T(8,128)}, f32[2,1024,512]{2,1,0:T(8,1...) custom-call(s32[1]{0:T(128)} %bitcast.side, ...), custom_call_target="tpu_custom_call" | custom-call | tf_op jit(solution)/shard_map/pallas_call | solution.py:1057
  (50 shorter events, 0.1 us)
Async XLA Ops:
  9.7 16.1 %copy-start.11 = (bf16[2048,128]{1,0:T(8,128)(2,1)}, bf16[2048,128]{1,0:T(8,128)(2,1)S(1)}, u32[]{:S(2)}) copy-start(bf16[2048,128]{1,0:T(8,128)(2,1)S(1)} %get-tuple-element.591.wide) | copy-start | bytes 1572868
  9.7 16.1 %copy-start.18 = (bf16[2,1024,128]{2,1,0:T(8,128)(2,1)}, bf16[2,1024,128]{2,1,0:T(8,128)(2,1)S(1)}, u32[]{:S(2)}) copy-start(bf16[2,1024,128]{2,1,0:T(8,128)(2,1)S(1)} %get-tuple-element.596.key_mark.refs_7_) | copy-start | bytes 1572868
  9.7 16.1 %copy-start.26 = (bf16[2,1024,128]{2,1,0:T(8,128)(2,1)}, bf16[2,1024,128]{2,1,0:T(8,128)(2,1)S(1)}, u32[]{:S(2)}) copy-start(bf16[2,1024,128]{2,1,0:T(8,128)(2,1)S(1)} %get-tuple-element.595.query_mark) | copy-start | bytes 1572868
  9.7 16.1 %copy-start = (bf16[1,2,1024,512]{3,2,1,0:T(8,128)(2,1)S(1)}, bf16[1,2,1024,512]{3,2,1,0:T(8,128)(2,1)}, u32[]{:S(2)}) copy-start(bf16[1,2,1024,512]{3,2,1,0:T(8,128)(2,1)} %param.22) | copy-start | bytes 6291460
  9.7 16.1 %copy-start.1 = (bf16[1,512,2048]{2,1,0:T(8,128)(2,1)S(1)}, bf16[1,512,2048]{2,1,0:T(8,128)(2,1)}, u32[]{:S(2)}) copy-start(bf16[1,512,2048]{2,1,0:T(8,128)(2,1)} %param.27) | copy-start | bytes 6291460
  9.7 16.1 %copy-start.3 = (bf16[1,2048,512]{2,1,0:T(8,128)(2,1)S(1)}, bf16[1,2048,512]{2,1,0:T(8,128)(2,1)}, u32[]{:S(2)}) copy-start(bf16[1,2048,512]{2,1,0:T(8,128)(2,1)} %param.28) | copy-start | bytes 6291460
  9.8 16.1 %copy-start.25 = (f32[32,512]{1,0:T(8,128)S(1)}, f32[32,512]{1,0:T(8,128)}, u32[]{:S(2)}) copy-start(f32[32,512]{1,0:T(8,128)} %up.3) | copy-start | bytes 196612
  9.8 16.1 %copy-start.34 = (f32[512,32]{0,1:T(8,128)S(1)}, f32[512,32]{0,1:T(8,128)}, u32[]{:S(2)}) copy-start(f32[512,32]{0,1:T(8,128)} %param.34) | copy-start | bytes 196612
  9.8 16.1 %copy-start.35 = (f32[1,6,512]{2,0,1:T(1,128)S(1)}, f32[1,6,512]{2,0,1:T(1,128)}, u32[]{:S(2)}) copy-start(f32[1,6,512]{2,0,1:T(1,128)} %param.30) | copy-start | bytes 36868
  9.8 16.1 %copy-start.36 = (f32[1,2,512]{2,1,0:T(2,128)S(1)}, f32[1,2,512]{2,1,0:T(2,128)}, u32[]{:S(2)}) copy-start(f32[1,2,512]{2,1,0:T(2,128)} %param.29) | copy-start | bytes 12292
  9.8 16.1 %copy-start.37 = (f32[2,512]{1,0:T(2,128)S(1)}, f32[2,512]{1,0:T(2,128)}, u32[]{:S(2)}) copy-start(f32[2,512]{1,0:T(2,128)} %head_bias.3) | copy-start | bytes 12292
  9.8 16.1 %copy-start.39 = (f32[512]{0:T(512)S(1)}, f32[512]{0:T(512)}, u32[]{:S(2)}) copy-start(f32[512]{0:T(512)} %param.32) | copy-start | bytes 6148
  9.8 16.1 %copy-start.40 = (f32[1,2048]{1,0:T(1,128)S(1)}, f32[1,2048]{1,0:T(1,128)}, u32[]{:S(2)}) copy-start(f32[1,2048]{1,0:T(1,128)} %hidden_bias.1) | copy-start | bytes 24580
  9.8 16.1 %copy-start.45 = (f32[32]{0:T(128)S(1)}, f32[32]{0:T(128)}, u32[]{:S(2)}) copy-start(f32[32]{0:T(128)} %param.35) | copy-start | bytes 388
  25.9 14.4 %copy-start.5 = (bf16[1,512,1536]{2,1,0:T(8,128)(2,1)S(1)}, bf16[1,512,1536]{2,1,0:T(8,128)(2,1)}, u32[]{:S(2)}) copy-start(bf16[1,512,1536]{2,1,0:T(8,128)(2,1)} %param.25) | copy-start | bytes 4718596
  50.9 10.2 %copy-start.13 = (bf16[2048,128]{1,0:T(8,128)(2,1)S(1)}, bf16[2048,128]{1,0:T(8,128)(2,1)}, u32[]{:S(2)}) copy-start(bf16[2048,128]{1,0:T(8,128)(2,1)} %get-tuple-element.313.wide) | copy-start | bytes 1572868 | tf_op jit(solution)/shard_map/cond
  50.9 10.2 %copy-start.22 = (bf16[512,512]{1,0:T(8,128)(2,1)S(1)}, bf16[512,512]{1,0:T(8,128)(2,1)}, u32[]{:S(2)}) copy-start(bf16[512,512]{1,0:T(8,128)(2,1)} %get-tuple-element.328.weight_out) | copy-start | bytes 1572868 | tf_op jit(solution)/shard_map/cond
  75.3 7.7 %collective-permute-start = (f32[32,1024]{1,0:T(8,128)}, f32[32,1024]{1,0:T(8,128)S(1)}, u32[]{:S(2)}, u32[]{:S(2)}) collective-permute-start(f32[32,1024]{1,0:T(8,128)} %get-tuple-element.612), channel_id=1, source_target_pairs={{16,0},{17,1},{18,2},{19,3},{20,4},{21,5},{22,6},{23,7},{24,8},{25... | collective-permute-start | bytes 393224 | tf_op jit(solution)/shard_map/ppermute | solution.py:1334
  91.2 0.7 copy-start.38
  91.8 15.0 %copy-start.10 = (f32[2048,32]{1,0:T(8,128)S(1)}, f32[2048,32]{1,0:T(8,128)}, u32[]{:S(2)}) copy-start(f32[2048,32]{1,0:T(8,128)} %get-tuple-element.412.unit) | copy-start | bytes 786436 | tf_op jit(solution)/shard_map/cond
  91.8 15.0 %copy-start.28 = (f32[1024,32]{1,0:T(8,128)S(1)}, f32[1024,32]{1,0:T(8,128)}, u32[]{:S(2)}) copy-start(f32[1024,32]{1,0:T(8,128)} %get-tuple-element.414.latent.latent_first) | copy-start | bytes 393220 | tf_op jit(solution)/shard_map/cond
  91.8 15.0 %copy-start.32 = (f32[32,8192]{1,0:T(8,128)S(1)}, f32[32,8192]{1,0:T(8,128)}, u32[]{:S(2)}) copy-start(f32[32,8192]{1,0:T(8,128)} %get-tuple-element.453.table_turned) | copy-start | bytes 3145732 | tf_op jit(solution)/shard_map/cond
  106.8 10.6 %copy-start.17 = (bf16[1024,512]{1,0:T(8,128)(2,1)S(1)}, bf16[1024,512]{1,0:T(8,128)(2,1)}, u32[]{:S(2)}) copy-start(bf16[1024,512]{1,0:T(8,128)(2,1)} %get-tuple-element.436.context) | copy-start | bytes 3145732 | tf_op jit(solution)/shard_map/cond
  106.8 10.6 %copy-start.21 = (bf16[2,1024,128]{2,1,0:T(8,128)(2,1)S(1)}, bf16[2,1024,128]{2,1,0:T(8,128)(2,1)}, u32[]{:S(2)}) copy-start(bf16[2,1024,128]{2,1,0:T(8,128)(2,1)} %get-tuple-element.437.key_mark) | copy-start | bytes 1572868 | tf_op jit(solution)/shard_map/cond
  106.8 10.5 %copy-start.24 = (bf16[1024,512]{1,0:T(8,128)(2,1)S(1)}, bf16[1024,512]{1,0:T(8,128)(2,1)}, u32[]{:S(2)}) copy-start(bf16[1024,512]{1,0:T(8,128)(2,1)} %get-tuple-element.431.query) | copy-start | bytes 3145732 | tf_op jit(solution)/shard_map/cond
  117.4 18.0 %copy-start.7 = (bf16[512,1536]{1,0:T(8,128)(2,1)S(1)}, bf16[512,1536]{1,0:T(8,128)(2,1)}, u32[]{:S(2)}) copy-start(bf16[512,1536]{1,0:T(8,128)(2,1)} %get-tuple-element.443.weight) | copy-start | bytes 4718596 | tf_op jit(solution)/shard_map/cond
  117.4 18.0 %copy-start.15 = (bf16[2048,128]{1,0:T(8,128)(2,1)S(1)}, bf16[2048,128]{1,0:T(8,128)(2,1)}, u32[]{:S(2)}) copy-start(bf16[2048,128]{1,0:T(8,128)(2,1)} %get-tuple-element.441.wide) | copy-start | bytes 1572868 | tf_op jit(solution)/shard_map/cond
  135.3 6.7 %copy-start.29 = (bf16[1024,512]{1,0:T(8,128)(2,1)S(1)}, bf16[1024,512]{1,0:T(8,128)(2,1)}, u32[]{:S(2)}) copy-start(bf16[1024,512]{1,0:T(8,128)(2,1)} %get-tuple-element.450.n2) | copy-start | bytes 3145732 | tf_op jit(solution)/shard_map/cond
  152.6 14.7 %collective-permute-start.1 = (f32[32,1024]{1,0:T(8,128)}, f32[32,1024]{1,0:T(8,128)S(1)}, u32[]{:S(2)}, u32[]{:S(2)}) collective-permute-start(f32[32,1024]{1,0:T(8,128)} %get-tuple-element.621), channel_id=1, source_target_pairs={{16,0},{17,1},{18,2},{19,3},{20,4},{21,5},{22,6},{23,7},{24,8},{25... | collective-permute-start | bytes 393224 | tf_op jit(solution)/shard_map/ppermute | solution.py:1347
  167.3 27.5 %copy-start.16 = (bf16[1024,512]{1,0:T(8,128)(2,1)S(1)}, bf16[1024,512]{1,0:T(8,128)(2,1)}, u32[]{:S(2)}) copy-start(bf16[1024,512]{1,0:T(8,128)(2,1)} %get-tuple-element.597.context.refs_13_.refs_19_) | copy-start | bytes 3145732
  167.3 27.5 %copy-start.42 = (f32[32,512]{1,0:T(8,128)S(1)}, f32[32,512]{1,0:T(8,128)}, u32[]{:S(2)}) copy-start(f32[32,512]{1,0:T(8,128)} %get-tuple-element.650.refs_34_) | copy-start | bytes 196612
  168.6 14.9 %copy-start.33 = (bf16[1024,2048]{1,0:T(8,128)(2,1)S(1)}, bf16[1024,2048]{1,0:T(8,128)(2,1)}, u32[]{:S(2)}) copy-start(bf16[1024,2048]{1,0:T(8,128)(2,1)} %get-tuple-element.467.active) | copy-start | bytes 12582916 | tf_op jit(solution)/shard_map/cond

commit v9 on v8

--- a/solution.py
+++ b/solution.py
@@ -22,7 +22,7 @@
 NT = (((1,), (1,)), ((), ()))
 TN = (((0,), (0,)), ((), ()))
 TOKENS = 256
-WINDOW = 256
+WINDOW = 128
 PARAMS = pltpu.CompilerParams(vmem_limit_bytes=56 << 20)
 
 
@@ -237,14 +237,14 @@
 
     def one(number, carry):
         base = (row * (count // size) + number) * 2
-        for_windows(windows[base], windows[base + 1], count, functools.partial(block, number))
+        for_windows(windows[base], windows[base + 1], count, (768,), functools.partial(block, number))
         return carry
 
     lax.fori_loop(0, count // size, one, 0)
 
 
-def for_windows(start, steps, count, run):
-    extents = list(range(2 * WINDOW, count + 1, WINDOW))
+def for_windows(start, steps, count, extents, run):
+    extents = [extent for extent in extents if extent < count] + [count]
     for position, extent in enumerate(extents):
         take = steps * WINDOW <= extent
         if position:
@@ -438,7 +438,7 @@
                 query, marks, key, value, context_grad, key_mark, grad_mark, query_grad, key_total, value_total,
             )
 
-        for_windows(windows[at], windows[at + 1], count, run)
+        for_windows(windows[at], windows[at + 1], count, (640, 768), run)
         return carry
 
     lax.fori_loop(0, steps, one, 0)
@@ -479,7 +479,8 @@
     def _():
         sums[4:5, :] += column_sum(total)
         latent_out[...] = code_product(total, up[...]).T
-        head_weight[...] += dot3(split(unit[...]), split(total), TN)
+        codes, low_total = split(unit[...]), total.astype(BF)
+        head_weight[...] += dot(codes[0], low_total, TN) + dot(codes[1], low_total, TN)
 
 
 def hidden_weight_kernel(active, out_low, n2, preact_low, *refs):
@@ -1289,9 +1290,8 @@
 def windows_of(segments):
     rows, count = segments.shape
     steps = count // WINDOW
-    blocks = segments.reshape(rows, steps, WINDOW)
-    least, most = blocks[:, :, 0], blocks[:, :, -1]
-    meets = (most[:, :, None] >= least[:, None, :]) & (least[:, :, None] <= most[:, None, :])
+    wide, blocks = (segments.reshape(rows, -1, size) for size in (TOKENS, WINDOW))
+    meets = (wide[:, :, None, -1] >= blocks[:, None, :, 0]) & (wide[:, :, None, 0] <= blocks[:, None, :, -1])
     place = jnp.arange(steps)
     start = jnp.min(jnp.where(meets, place, steps), -1)
     stop = jnp.max(jnp.where(meets, place, -1), -1) + 1

time: 394 us -> 395 us (level)
  Pallas kernels: 346 us -> 342 us
    pallas_call x1, Pallas kernels: 181 us -> 168 us  [finish_row(): pl.pallas_call(functools.partial(finish_kernel, held=held), in_specs=[hbm...]
    pallas_call x3, Pallas kernels: 38.2 us -> 47.1 us  [attention_call(): pl.pallas_call(functools.partial(kernel, row=row), grid_spec=pltpu.Prefet...]
where the time goes in v9:
time: 395 us; the launch traced here: 387 us
  Pallas kernels  342 us (87%)
  waiting for transfers between devices  22.3 us (6%)
  loops' own time  14.2 us (4%)
  local copies, waits for them, and re-layouts  4.83 us (1%)
    pallas_call x1, Pallas kernels, finish_row(): pl.pallas_call(functools.partial(finish_kernel, held=held), in_specs=[hbm...  168 us
    pallas_call x7, Pallas kernels, call(): pl.pallas_call(kernel, grid=(self.count // self.size,), in_specs=in_specs...  75.7 us
    pallas_call x3, Pallas kernels, attention_call(): pl.pallas_call(functools.partial(kernel, row=row), grid_spec=pltpu.Prefet...  47.1 us
    pallas_call x2, Pallas kernels, weight_call(): pl.pallas_call(kernel, grid=(steps,), in_specs=in_specs, out_specs=out_sp...  21.6 us
    ppermute x1, waiting for transfers between devices, on_device(): latent_in_second = lax.ppermute(early_b.latent_out, SECTION, [(1, 0)])  15.6 us
    pallas_call x1, Pallas kernels, unpack(): pl.pallas_call(unpack_kernel, in_specs=[pl.BlockSpec(memory_space=pltpu.S...  11.8 us
    pallas_call x1, Pallas kernels, scatter_codes(): pl.pallas_call(scatter_kernel, in_specs=[pl.BlockSpec(memory_space=pltpu....  10.5 us
    another operation x1, loops' own time, on_device(): lax.cond(encoder, encoder_second, decoder_second)  8.91 us
  transfers between devices with their start and end apart: 2, of which 2 were waited for; matrix products, arithmetic and copies ran while one was open for 0% of the time, Pallas kernels for 0%

profile of v9, /device:TPU:0, one launch (start us, length us, event | category | flops | bytes accessed | tf_op | source)
XLA Modules:
  0.0 387.2 jit_solution(18055661738214739333)
XLA Ops:
  0.7 0.7 copy.56
  1.4 0.7 reshape.59
  2.1 0.7 copy.55
  2.8 0.1 fusion
  2.8 0.1 copy.47
  3.0 0.1 copy.49
  3.0 0.1 fusion.1
  3.1 0.1 copy.48
  3.2 0.1 copy.50
  3.3 0.2 select_reduce_fusion.1
  3.5 0.1 copy.46
  3.6 0.1 reshape.61.windows
  3.7 6.9 %shard_map.263 = (f32[2048,32]{1,0:T(8,128)}, bf16[2048,128]{1,0:T(8,128)(2,1)S(1)}, bf16[2,1024,128]{2,1,0:T(8,128)(2,1)S(1)}, bf16[2,1024,128]{2,1,0:T(8,128)(2,1)S(1)}) custom-call(s32[2048]{0:T(1024)S(1)} %bitcast.100, f32[32,8192]{1,0:T(8,128)} %bitcast.71, s32[2,1024]{1,0:T(2,128)} %segments.1), custom_call_target="tpu_custom_call" | custom-call | tf_op jit(solution)/shard_map/pallas_call | solution.py:108
  10.7 0.0 copy-start.1
  10.7 0.0 copy-start.3
  10.7 0.0 copy-start.25
  10.7 0.0 copy-start.34
  10.7 0.0 copy-start.35
  10.7 0.0 copy-start.36
  10.7 0.0 copy-start.37
  10.8 0.0 copy-start.39
  10.8 0.0 copy-start.45
  10.8 6.0 %shard_map.264 = (bf16[1024,512]{1,0:T(8,128)(2,1)}, bf16[1024,512]{1,0:T(8,128)(2,1)}, bf16[1024,512]{1,0:T(8,128)(2,1)}, bf16[1024,512]{1,0:T(8,128)(2,1)}) custom-call(s32[1]{0:T(128)} %bitcast.side, bf16[2,1024,512]{2,1,0:T(8,128)(2,1)} %bitcast.39, bf16[2048,128]{1,0:T(8,128)(2,1)S(1)} %get-tuple-element.591.wide, f32[32,512]{1,0:T(8,128)} %up.3, ...), custom_call_target="tpu_custom_call" | custom-call | tf_op jit(solution)/shard_map/pallas_call | solution.py:1174
  16.7 13.1 %shard_map.265 = (bf16[1024,512]{1,0:T(8,128)(2,1)}, bf16[1024,512]{1,0:T(8,128)(2,1)}) custom-call(s32[16]{0:T(128)S(1)} %reshape.61.windows, bf16[1024,512]{1,0:T(8,128)(2,1)} %get-tuple-element.592.query, bf16[1024,512]{1,0:T(8,128)(2,1)} %get-tuple-element.593.key, bf16[1024,512]{1,0:T(8,128)(2,1)} %get-tuple-element.594.value, ...), custom_call_target="tpu_custom_call" | custom-call | tf_op jit(solution)/shard_map/pallas_call | solution.py:1192
  30.0 0.0 copy-start.5
  30.0 14.4 %shard_map.266 = (f32[1024,512]{1,0:T(8,128)}, bf16[1024,512]{1,0:T(8,128)(2,1)}, bf16[1024,2048]{1,0:T(8,128)(2,1)}, bf16[1024,2048]{1,0:T(8,128)(2,1)}, f32[1024,512]{1,0:T(8,128)}, /*index=5*/f32[1024,32]{1,0:T(8,128)}) custom-call(s32[1]{0:T(128)} %bitcast.side, bf16[2,1024,512]{2,1,0:T(8,128)(2,1)S(1)} %bitcast.40, bf16[2048,128]{1,0:T(8,128)(2,1)} %copy-done.11, ...), custom_call_target="tpu_custom_call" | custom-call | tf_op jit(solution)/shard_map/pallas_call | solution.py:1174
  44.4 37.6 %conditional.3 = (bf16[1024,512]{1,0:T(8,128)(2,1)}, bf16[1024,512]{1,0:T(8,128)(2,1)}, bf16[1024,512]{1,0:T(8,128)(2,1)}, bf16[1024,512]{1,0:T(8,128)(2,1)}, bf...) conditional(s32[]{:T(128)} %convert_element_type.2, ...), branch_computations={%region_2.3_spmd, %region_3.4_spmd} | conditional | bytes 11534632 | solution.py:1333
  49.8 4.7 %branch_1_fun.12 = (bf16[1024,512]{1,0:T(8,128)(2,1)}, bf16[1024,512]{1,0:T(8,128)(2,1)}, bf16[1024,512]{1,0:T(8,128)(2,1)}, bf16[1024,512]{1,0:T(8,128)(2,1)}) custom-call(s32[1]{0:T(128)} %get-tuple-element.311.side, bf16[2,1024,512]{2,1,0:T(8,128)(2,1)S(1)} %get-tuple-element.312.edge, bf16[2048,128]{1,0:T(8,128)(2,1)} %get-tuple-element.313.wide, ...), custom_call_target="tpu_custom_call" | custom-call | tf_op jit(solution)/shard_map/cond/branch_1_fun/pallas_call | solution.py:1174
  54.5 13.4 %branch_1_fun.13 = (bf16[1024,512]{1,0:T(8,128)(2,1)}, bf16[1024,512]{1,0:T(8,128)(2,1)}) custom-call(s32[16]{0:T(128)S(1)} %get-tuple-element.323.windows, bf16[1024,512]{1,0:T(8,128)(2,1)} %get-tuple-element.703.query, bf16[1024,512]{1,0:T(8,128)(2,1)} %get-tuple-element.704.key, bf16[1024,512]{1,0:T(8,128)(2,1)} %get-tuple-element.705.value, ...), custom_call_target="tpu_custom_call" | custom-call | tf_op jit(solution)/shard_map/cond/branch_1_fun/pallas_call | solution.py:1192
  67.9 14.1 %branch_1_fun.14 = (f32[1024,512]{1,0:T(8,128)}, bf16[1024,512]{1,0:T(8,128)(2,1)}, bf16[1024,2048]{1,0:T(8,128)(2,1)}, bf16[1024,2048]{1,0:T(8,128)(2,1)}, f32[1024,512]{1,0:T(8,128)}, /*index=5*/f32[1024,32]{1,0:T(8,128)}) custom-call(s32[1]{0:T(128)} %get-tuple-element.311.side, bf16[2,1024,512]{2,1,0:T(8,128)(2,1)S(1)} %get-tuple-element.312.edge, ...), custom_call_target="tpu_custom_call" | custom-call | tf_op jit(solution)/shard_map/cond/branch_1_fun/pallas_call | solution.py:1174
  82.0 1.3 collective-permute-start
  83.3 6.7 %collective-permute-done = f32[32,1024]{1,0:T(8,128)S(1)} collective-permute-done((f32[32,1024]{1,0:T(8,128)}, f32[32,1024]{1,0:T(8,128)S(1)}, u32[]{:S(2)}, u32[]{:S(2)}) %collective-permute-start) | collective-permute-done | bytes 131104 | tf_op jit(solution)/shard_map/ppermute | solution.py:1334
  90.0 72.5 %conditional.4 = (bf16[1024,512]{1,0:T(8,128)(2,1)}, bf16[1024,512]{1,0:T(8,128)(2,1)}, bf16[1024,512]{1,0:T(8,128)(2,1)}, bf16[1024,2048]{1,0:T(8,128)(2,1)}, f...) conditional(s32[]{:T(128)} %convert_element_type.2, ...), branch_computations={%region_4.5_spmd, %region_5.6_spmd} | conditional | bytes 33030604 | solution.py:1346
  98.5 0.6 copy-done.38
  99.1 15.0 %branch_1_fun.17 = (bf16[1024,512]{1,0:T(8,128)(2,1)}, bf16[1024,2048]{1,0:T(8,128)(2,1)}, f32[1024,512]{1,0:T(8,128)}, bf16[1024,512]{1,0:T(8,128)(2,1)}, bf16[...) custom-call(s32[1]{0:T(128)} %get-tuple-element.409.side, ...), custom_call_target="tpu_custom_call" | custom-call | tf_op jit(solution)/shard_map/cond/branch_1_fun/pallas_call | solution.py:1174
  114.1 10.5 %branch_1_fun.21 = f32[512,512]{1,0:T(8,128)} custom-call(s32[2048]{0:T(1024)S(1)} %get-tuple-element.451.index, f32[2048,32]{1,0:T(8,128)S(1)} %copy-done.10, f32[1024,32]{1,0:T(8,128)S(1)} %copy-done.28, f32[1024,32]{1,0:T(8,128)} %get-tuple-element.452.latent_second, f32[32,8192]{1,0:T(8,128)S(1)} %copy-done.32), custom_call_target="tpu_custom_call" | custom-call | tf_op jit(solution)/shard_map/cond/branch_1_fun/pallas_call | solution.py:162
  124.7 20.5 %branch_1_fun.18 = (bf16[1024,512]{1,0:T(8,128)(2,1)}, bf16[1024,512]{1,0:T(8,128)(2,1)}, bf16[1024,512]{1,0:T(8,128)(2,1)}) custom-call(s32[16]{0:T(128)S(1)} %get-tuple-element.430.windows, bf16[1024,512]{1,0:T(8,128)(2,1)S(1)} %copy-done.24, bf16[1024,512]{1,0:T(8,128)(2,1)} %get-tuple-element.432.marks, bf16[1024,512]{1,0:T(8,128)(2,1)} %get-tuple-element.433.key, ...), custom_call_target="tpu_custom_call" | custom-call | tf_op jit(solution)/shard_map/cond/branch_1_fun/pallas_call | solution.py:1192
  145.2 6.7 %branch_1_fun.19 = (f32[1024,512]{1,0:T(8,128)}, f32[32,1024]{1,0:T(8,128)}, f32[16,512]{1,0:T(8,128)}, f32[32,512]{1,0:T(8,128)}) custom-call(s32[1]{0:T(128)} %get-tuple-element.409.side, bf16[2,1024,512]{2,1,0:T(8,128)(2,1)S(1)} %get-tuple-element.411.cotangent.edge, bf16[2048,128]{1,0:T(8,128)(2,1)S(1)} %copy-done.15, ...), custom_call_target="tpu_custom_call" | custom-call | tf_op jit(solution)/shard_map/cond/branch_1_fun/pallas_call | solution.py:1174
  151.9 10.3 %branch_1_fun.20 = f32[4096,512]{1,0:T(8,128)} custom-call(bf16[1024,2048]{1,0:T(8,128)(2,1)} %get-tuple-element.449.active, bf16[1024,512]{1,0:T(8,128)(2,1)} %get-tuple-element.749.out_low, bf16[1024,512]{1,0:T(8,128)(2,1)S(1)} %copy-done.29, bf16[1024,2048]{1,0:T(8,128)(2,1)} %get-tuple-element.750.preact_low), custom_call_target="tpu_custom_call" | custom-call | tf_op jit(solution)/shard_map/cond/branch_1_fun/pallas_call | solution.py:514
  162.5 1.3 collective-permute-start.1
  163.8 15.6 %collective-permute-done.1 = f32[32,1024]{1,0:T(8,128)S(1)} collective-permute-done((f32[32,1024]{1,0:T(8,128)}, f32[32,1024]{1,0:T(8,128)S(1)}, u32[]{:S(2)}, u32[]{:S(2)}) %collective-permute-start.1) | collective-permute-done | bytes 131104 | tf_op jit(solution)/shard_map/ppermute | solution.py:1347
  179.4 27.5 %conditional.5 = (f32[4096,512]{1,0:T(8,128)}, f32[1024,512]{1,0:T(8,128)}, bf16[1024,512]{1,0:T(8,128)(2,1)}, bf16[1024,512]{1,0:T(8,128)(2,1)}, f32[16,512]{1,0:T(8,128)S(1)}, /*index=5*/f32[32,512]{1,0:T(8,128)S(1)}) conditional(s32[]{:T(128)} %convert_element_type.2, (bf16[1024,2048]{1,0:T(8,128)(2,1)}, bf16[1024,512]{1,0:T(8,128)(2,1)}, ...), branch_computations={%region_6.7_spmd, %region_7.8_spmd} | conditional | bytes 16973900 | solution.py:1357
  179.4 0.6 copy.158.refs_1_
  180.1 0.6 copy.157.refs_0_
  180.7 14.9 %branch_1_fun.22 = (bf16[1024,512]{1,0:T(8,128)(2,1)}, bf16[1024,2048]{1,0:T(8,128)(2,1)}, f32[1024,512]{1,0:T(8,128)}, bf16[1024,512]{1,0:T(8,128)(2,1)}, bf16[...) custom-call(s32[1]{0:T(128)} %get-tuple-element.468.side, ...), custom_call_target="tpu_custom_call" | custom-call | tf_op jit(solution)/shard_map/cond/branch_1_fun/pallas_call | solution.py:1174
  195.6 11.4 %branch_1_fun.23 = f32[4096,512]{1,0:T(8,128)} custom-call(bf16[1024,2048]{1,0:T(8,128)(2,1)S(1)} %copy-done.33, bf16[1024,512]{1,0:T(8,128)(2,1)} %get-tuple-element.486.out_low, bf16[1024,512]{1,0:T(8,128)(2,1)} %get-tuple-element.487.n2, bf16[1024,2048]{1,0:T(8,128)(2,1)} %get-tuple-element.488.preact_low, ...), custom_call_target="tpu_custom_call", output_to_operand_aliasing={{}: (4, {})} | custom-call | tf_op jit(solution)/shard_map/cond/branch_1_fun/pallas_call | solution.py:514
  207.0 168.2 %shard_map.268 = (f32[4096,512]{1,0:T(8,128)}, f32[2048,512]{1,0:T(8,128)}, f32[768,512]{1,0:T(8,128)}, f32[1024,512]{1,0:T(8,128)}) custom-call(f32[4096,512]{1,0:T(8,128)} %get-tuple-element.627.refs_0_, bf16[1024,512]{1,0:T(8,128)(2,1)} %get-tuple-element.628.refs_1_, bf16[1024,512]{1,0:T(8,128)(2,1)} %get-tuple-element.629.refs_2_, ...), custom_call_target="tpu_custom_call" | custom-call | tf_op jit(solution)/shard_map/pallas_call | solution.py:974
  375.2 11.8 %shard_map.269 = (f32[2048,512]{1,0:T(8,128)}, f32[512,2048]{1,0:T(8,128)}, f32[512,512]{1,0:T(8,128)}, f32[512,1536]{1,0:T(8,128)}, f32[2,1024,512]{2,1,0:T(8,1...) custom-call(s32[1]{0:T(128)} %bitcast.side, ...), custom_call_target="tpu_custom_call" | custom-call | tf_op jit(solution)/shard_map/pallas_call | solution.py:1058
  (54 shorter events, 0.1 us)
Async XLA Ops:
  10.7 19.2 %copy-start.11 = (bf16[2048,128]{1,0:T(8,128)(2,1)}, bf16[2048,128]{1,0:T(8,128)(2,1)S(1)}, u32[]{:S(2)}) copy-start(bf16[2048,128]{1,0:T(8,128)(2,1)S(1)} %get-tuple-element.591.wide) | copy-start | bytes 1572868
  10.7 19.2 %copy-start.18 = (bf16[2,1024,128]{2,1,0:T(8,128)(2,1)}, bf16[2,1024,128]{2,1,0:T(8,128)(2,1)S(1)}, u32[]{:S(2)}) copy-start(bf16[2,1024,128]{2,1,0:T(8,128)(2,1)S(1)} %get-tuple-element.596.key_mark.refs_7_) | copy-start | bytes 1572868
  10.7 19.2 %copy-start.26 = (bf16[2,1024,128]{2,1,0:T(8,128)(2,1)}, bf16[2,1024,128]{2,1,0:T(8,128)(2,1)S(1)}, u32[]{:S(2)}) copy-start(bf16[2,1024,128]{2,1,0:T(8,128)(2,1)S(1)} %get-tuple-element.595.query_mark) | copy-start | bytes 1572868
  10.7 19.2 %copy-start = (bf16[1,2,1024,512]{3,2,1,0:T(8,128)(2,1)S(1)}, bf16[1,2,1024,512]{3,2,1,0:T(8,128)(2,1)}, u32[]{:S(2)}) copy-start(bf16[1,2,1024,512]{3,2,1,0:T(8,128)(2,1)} %param.22) | copy-start | bytes 6291460
  10.7 19.2 %copy-start.1 = (bf16[1,512,2048]{2,1,0:T(8,128)(2,1)S(1)}, bf16[1,512,2048]{2,1,0:T(8,128)(2,1)}, u32[]{:S(2)}) copy-start(bf16[1,512,2048]{2,1,0:T(8,128)(2,1)} %param.27) | copy-start | bytes 6291460
  10.7 19.2 %copy-start.3 = (bf16[1,2048,512]{2,1,0:T(8,128)(2,1)S(1)}, bf16[1,2048,512]{2,1,0:T(8,128)(2,1)}, u32[]{:S(2)}) copy-start(bf16[1,2048,512]{2,1,0:T(8,128)(2,1)} %param.28) | copy-start | bytes 6291460
  10.7 19.2 %copy-start.25 = (f32[32,512]{1,0:T(8,128)S(1)}, f32[32,512]{1,0:T(8,128)}, u32[]{:S(2)}) copy-start(f32[32,512]{1,0:T(8,128)} %up.3) | copy-start | bytes 196612
  10.7 19.2 %copy-start.34 = (f32[512,32]{0,1:T(8,128)S(1)}, f32[512,32]{0,1:T(8,128)}, u32[]{:S(2)}) copy-start(f32[512,32]{0,1:T(8,128)} %param.34) | copy-start | bytes 196612
  10.7 19.2 %copy-start.35 = (f32[1,6,512]{2,0,1:T(1,128)S(1)}, f32[1,6,512]{2,0,1:T(1,128)}, u32[]{:S(2)}) copy-start(f32[1,6,512]{2,0,1:T(1,128)} %param.30) | copy-start | bytes 36868
  10.7 19.2 %copy-start.36 = (f32[1,2,512]{2,1,0:T(2,128)S(1)}, f32[1,2,512]{2,1,0:T(2,128)}, u32[]{:S(2)}) copy-start(f32[1,2,512]{2,1,0:T(2,128)} %param.29) | copy-start | bytes 12292
  10.7 19.2 %copy-start.37 = (f32[2,512]{1,0:T(2,128)S(1)}, f32[2,512]{1,0:T(2,128)}, u32[]{:S(2)}) copy-start(f32[2,512]{1,0:T(2,128)} %head_bias.3) | copy-start | bytes 12292
  10.8 19.2 %copy-start.39 = (f32[512]{0:T(512)S(1)}, f32[512]{0:T(512)}, u32[]{:S(2)}) copy-start(f32[512]{0:T(512)} %param.32) | copy-start | bytes 6148
  10.8 19.2 %copy-start.40 = (f32[1,2048]{1,0:T(1,128)S(1)}, f32[1,2048]{1,0:T(1,128)}, u32[]{:S(2)}) copy-start(f32[1,2048]{1,0:T(1,128)} %hidden_bias.1) | copy-start | bytes 24580
  10.8 19.2 %copy-start.45 = (f32[32]{0:T(128)S(1)}, f32[32]{0:T(128)}, u32[]{:S(2)}) copy-start(f32[32]{0:T(128)} %param.35) | copy-start | bytes 388
  30.0 14.4 %copy-start.5 = (bf16[1,512,1536]{2,1,0:T(8,128)(2,1)S(1)}, bf16[1,512,1536]{2,1,0:T(8,128)(2,1)}, u32[]{:S(2)}) copy-start(bf16[1,512,1536]{2,1,0:T(8,128)(2,1)} %param.25) | copy-start | bytes 4718596
  54.5 13.4 %copy-start.13 = (bf16[2048,128]{1,0:T(8,128)(2,1)S(1)}, bf16[2048,128]{1,0:T(8,128)(2,1)}, u32[]{:S(2)}) copy-start(bf16[2048,128]{1,0:T(8,128)(2,1)} %get-tuple-element.313.wide) | copy-start | bytes 1572868 | tf_op jit(solution)/shard_map/cond
  54.5 13.4 %copy-start.22 = (bf16[512,512]{1,0:T(8,128)(2,1)S(1)}, bf16[512,512]{1,0:T(8,128)(2,1)}, u32[]{:S(2)}) copy-start(bf16[512,512]{1,0:T(8,128)(2,1)} %get-tuple-element.328.weight_out) | copy-start | bytes 1572868 | tf_op jit(solution)/shard_map/cond
  82.0 8.0 %collective-permute-start = (f32[32,1024]{1,0:T(8,128)}, f32[32,1024]{1,0:T(8,128)S(1)}, u32[]{:S(2)}, u32[]{:S(2)}) collective-permute-start(f32[32,1024]{1,0:T(8,128)} %get-tuple-element.612), channel_id=1, source_target_pairs={{16,0},{17,1},{18,2},{19,3},{20,4},{21,5},{22,6},{23,7},{24,8},{25... | collective-permute-start | bytes 393224 | tf_op jit(solution)/shard_map/ppermute | solution.py:1334
  98.4 0.6 copy-start.38
  99.1 15.0 %copy-start.10 = (f32[2048,32]{1,0:T(8,128)S(1)}, f32[2048,32]{1,0:T(8,128)}, u32[]{:S(2)}) copy-start(f32[2048,32]{1,0:T(8,128)} %get-tuple-element.412.unit) | copy-start | bytes 786436 | tf_op jit(solution)/shard_map/cond
  99.1 15.0 %copy-start.28 = (f32[1024,32]{1,0:T(8,128)S(1)}, f32[1024,32]{1,0:T(8,128)}, u32[]{:S(2)}) copy-start(f32[1024,32]{1,0:T(8,128)} %get-tuple-element.414.latent.latent_first) | copy-start | bytes 393220 | tf_op jit(solution)/shard_map/cond
  99.1 15.0 %copy-start.32 = (f32[32,8192]{1,0:T(8,128)S(1)}, f32[32,8192]{1,0:T(8,128)}, u32[]{:S(2)}) copy-start(f32[32,8192]{1,0:T(8,128)} %get-tuple-element.453.table_turned) | copy-start | bytes 3145732 | tf_op jit(solution)/shard_map/cond
  114.1 10.6 %copy-start.17 = (bf16[1024,512]{1,0:T(8,128)(2,1)S(1)}, bf16[1024,512]{1,0:T(8,128)(2,1)}, u32[]{:S(2)}) copy-start(bf16[1024,512]{1,0:T(8,128)(2,1)} %get-tuple-element.436.context) | copy-start | bytes 3145732 | tf_op jit(solution)/shard_map/cond
  114.1 10.5 %copy-start.21 = (bf16[2,1024,128]{2,1,0:T(8,128)(2,1)S(1)}, bf16[2,1024,128]{2,1,0:T(8,128)(2,1)}, u32[]{:S(2)}) copy-start(bf16[2,1024,128]{2,1,0:T(8,128)(2,1)} %get-tuple-element.437.key_mark) | copy-start | bytes 1572868 | tf_op jit(solution)/shard_map/cond
  114.1 10.5 %copy-start.24 = (bf16[1024,512]{1,0:T(8,128)(2,1)S(1)}, bf16[1024,512]{1,0:T(8,128)(2,1)}, u32[]{:S(2)}) copy-start(bf16[1024,512]{1,0:T(8,128)(2,1)} %get-tuple-element.431.query) | copy-start | bytes 3145732 | tf_op jit(solution)/shard_map/cond
  124.6 20.5 %copy-start.7 = (bf16[512,1536]{1,0:T(8,128)(2,1)S(1)}, bf16[512,1536]{1,0:T(8,128)(2,1)}, u32[]{:S(2)}) copy-start(bf16[512,1536]{1,0:T(8,128)(2,1)} %get-tuple-element.443.weight) | copy-start | bytes 4718596 | tf_op jit(solution)/shard_map/cond
  124.6 20.5 %copy-start.15 = (bf16[2048,128]{1,0:T(8,128)(2,1)S(1)}, bf16[2048,128]{1,0:T(8,128)(2,1)}, u32[]{:S(2)}) copy-start(bf16[2048,128]{1,0:T(8,128)(2,1)} %get-tuple-element.441.wide) | copy-start | bytes 1572868 | tf_op jit(solution)/shard_map/cond
  145.2 6.7 %copy-start.29 = (bf16[1024,512]{1,0:T(8,128)(2,1)S(1)}, bf16[1024,512]{1,0:T(8,128)(2,1)}, u32[]{:S(2)}) copy-start(bf16[1024,512]{1,0:T(8,128)(2,1)} %get-tuple-element.450.n2) | copy-start | bytes 3145732 | tf_op jit(solution)/shard_map/cond
  162.5 16.9 %collective-permute-start.1 = (f32[32,1024]{1,0:T(8,128)}, f32[32,1024]{1,0:T(8,128)S(1)}, u32[]{:S(2)}, u32[]{:S(2)}) collective-permute-start(f32[32,1024]{1,0:T(8,128)} %get-tuple-element.621), channel_id=1, source_target_pairs={{16,0},{17,1},{18,2},{19,3},{20,4},{21,5},{22,6},{23,7},{24,8},{25... | collective-permute-start | bytes 393224 | tf_op jit(solution)/shard_map/ppermute | solution.py:1347
  179.4 27.5 %copy-start.16 = (bf16[1024,512]{1,0:T(8,128)(2,1)S(1)}, bf16[1024,512]{1,0:T(8,128)(2,1)}, u32[]{:S(2)}) copy-start(bf16[1024,512]{1,0:T(8,128)(2,1)} %get-tuple-element.597.context.refs_13_.refs_19_) | copy-start | bytes 3145732
  179.4 27.5 %copy-start.42 = (f32[32,512]{1,0:T(8,128)S(1)}, f32[32,512]{1,0:T(8,128)}, u32[]{:S(2)}) copy-start(f32[32,512]{1,0:T(8,128)} %get-tuple-element.650.refs_34_) | copy-start | bytes 196612
  180.7 14.9 %copy-start.33 = (bf16[1024,2048]{1,0:T(8,128)(2,1)S(1)}, bf16[1024,2048]{1,0:T(8,128)(2,1)}, u32[]{:S(2)}) copy-start(bf16[1024,2048]{1,0:T(8,128)(2,1)} %get-tuple-element.467.active) | copy-start | bytes 12582916 | tf_op jit(solution)/shard_map/cond

commit v10 on v9

--- a/solution.py
+++ b/solution.py
@@ -321,7 +321,8 @@
         code_grad = latent_in[...].T + 0.5 * (code - unit[...])
         latent_grad = scale * (code_grad - code * jnp.sum(code * code_grad, -1, keepdims=True))
         pieces = split(latent_grad)
-        normed_grad = dot3(pieces, split(down[...]), NN)
+        low_down = down[...].astype(BF)
+        normed_grad = dot(pieces[0], low_down, NN) + dot(pieces[1], low_down, NN)
         head_weight[...] += dot(pieces[0], normed.astype(BF), TN) + dot(pieces[1], normed.astype(BF), TN)
         sums[8:9, :] += column_sum(normed_grad * hat)
         sums[9:10, :] += column_sum(normed_grad)
@@ -764,7 +765,8 @@
         run(step)
         return carry
 
-    lax.fori_loop(start, stop, one, 0)
+    if start < stop:
+        lax.fori_loop(start, stop, one, 0)
 
 
 HIDDEN_WAYS = (4,)

time: 395 us -> 393 us (level)
  no operation moved by 1% of the time
where the time goes in v10:
time: 393 us; the launch traced here: 387 us
  Pallas kernels  342 us (87%)
  waiting for transfers between devices  21.9 us (6%)
  loops' own time  14.2 us (4%)
  local copies, waits for them, and re-layouts  4.83 us (1%)
    pallas_call x1, Pallas kernels, finish_row(): pl.pallas_call(functools.partial(finish_kernel, held=held), in_specs=[hbm...  166 us
    pallas_call x7, Pallas kernels, call(): pl.pallas_call(kernel, grid=(self.count // self.size,), in_specs=in_specs...  75.3 us
    pallas_call x3, Pallas kernels, attention_call(): pl.pallas_call(functools.partial(kernel, row=row), grid_spec=pltpu.Prefet...  50.4 us
    pallas_call x2, Pallas kernels, weight_call(): pl.pallas_call(kernel, grid=(steps,), in_specs=in_specs, out_specs=out_sp...  21.6 us
    ppermute x1, waiting for transfers between devices, on_device(): latent_in_second = lax.ppermute(early_b.latent_out, SECTION, [(1, 0)])  13.1 us
    pallas_call x1, Pallas kernels, unpack(): pl.pallas_call(unpack_kernel, in_specs=[pl.BlockSpec(memory_space=pltpu.S...  11.8 us
    pallas_call x1, Pallas kernels, scatter_codes(): pl.pallas_call(scatter_kernel, in_specs=[pl.BlockSpec(memory_space=pltpu....  10.5 us
    ppermute x1, waiting for transfers between devices, on_device(): latent_in = lax.ppermute(early_a.latent_out, SECTION, [(1, 0)])  8.9 us
  transfers between devices with their start and end apart: 2, of which 2 were waited for; matrix products, arithmetic and copies ran while one was open for 0% of the time, Pallas kernels for 0%

profile of v10, /device:TPU:0, one launch (start us, length us, event | category | flops | bytes accessed | tf_op | source)
XLA Modules:
  0.0 387.1 jit_solution(8893325195015007525)
XLA Ops:
  0.7 0.7 copy.56
  1.4 0.7 reshape.59
  2.1 0.7 copy.55
  2.8 0.1 fusion
  2.8 0.1 copy.47
  3.0 0.1 copy.49
  3.0 0.1 fusion.1
  3.1 0.1 copy.48
  3.2 0.1 copy.50
  3.3 0.2 select_reduce_fusion.1
  3.5 0.1 copy.46
  3.6 0.1 reshape.61.windows
  3.7 6.9 %shard_map.263 = (f32[2048,32]{1,0:T(8,128)}, bf16[2048,128]{1,0:T(8,128)(2,1)S(1)}, bf16[2,1024,128]{2,1,0:T(8,128)(2,1)S(1)}, bf16[2,1024,128]{2,1,0:T(8,128)(2,1)S(1)}) custom-call(s32[2048]{0:T(1024)S(1)} %bitcast.100, f32[32,8192]{1,0:T(8,128)} %bitcast.71, s32[2,1024]{1,0:T(2,128)} %segments.1), custom_call_target="tpu_custom_call" | custom-call | tf_op jit(solution)/shard_map/pallas_call | solution.py:108
  10.7 0.0 copy-start.1
  10.7 0.0 copy-start.3
  10.7 0.0 copy-start.25
  10.7 0.0 copy-start.34
  10.7 0.0 copy-start.35
  10.7 0.0 copy-start.36
  10.7 0.0 copy-start.37
  10.8 0.0 copy-start.39
  10.8 0.0 copy-start.40
  10.8 6.0 %shard_map.264 = (bf16[1024,512]{1,0:T(8,128)(2,1)}, bf16[1024,512]{1,0:T(8,128)(2,1)}, bf16[1024,512]{1,0:T(8,128)(2,1)}, bf16[1024,512]{1,0:T(8,128)(2,1)}) custom-call(s32[1]{0:T(128)} %bitcast.side, bf16[2,1024,512]{2,1,0:T(8,128)(2,1)} %bitcast.39, bf16[2048,128]{1,0:T(8,128)(2,1)S(1)} %get-tuple-element.591.wide, f32[32,512]{1,0:T(8,128)} %up.3, ...), custom_call_target="tpu_custom_call" | custom-call | tf_op jit(solution)/shard_map/pallas_call | solution.py:1176
  16.7 13.8 %shard_map.265 = (bf16[1024,512]{1,0:T(8,128)(2,1)}, bf16[1024,512]{1,0:T(8,128)(2,1)}) custom-call(s32[16]{0:T(128)S(1)} %reshape.61.windows, bf16[1024,512]{1,0:T(8,128)(2,1)} %get-tuple-element.592.query, bf16[1024,512]{1,0:T(8,128)(2,1)} %get-tuple-element.593.key, bf16[1024,512]{1,0:T(8,128)(2,1)} %get-tuple-element.594.value, ...), custom_call_target="tpu_custom_call" | custom-call | tf_op jit(solution)/shard_map/pallas_call | solution.py:1194
  30.7 0.0 copy-start.5
  30.7 14.4 %shard_map.266 = (f32[1024,512]{1,0:T(8,128)}, bf16[1024,512]{1,0:T(8,128)(2,1)}, bf16[1024,2048]{1,0:T(8,128)(2,1)}, bf16[1024,2048]{1,0:T(8,128)(2,1)}, f32[1024,512]{1,0:T(8,128)}, /*index=5*/f32[1024,32]{1,0:T(8,128)}) custom-call(s32[1]{0:T(128)} %bitcast.side, bf16[2,1024,512]{2,1,0:T(8,128)(2,1)S(1)} %bitcast.40, bf16[2048,128]{1,0:T(8,128)(2,1)} %copy-done.11, ...), custom_call_target="tpu_custom_call" | custom-call | tf_op jit(solution)/shard_map/pallas_call | solution.py:1176
  45.1 37.6 %conditional.3 = (bf16[1024,512]{1,0:T(8,128)(2,1)}, bf16[1024,512]{1,0:T(8,128)(2,1)}, bf16[1024,512]{1,0:T(8,128)(2,1)}, bf16[1024,512]{1,0:T(8,128)(2,1)}, bf...) conditional(s32[]{:T(128)} %convert_element_type.2, ...), branch_computations={%region_2.3_spmd, %region_3.4_spmd} | conditional | bytes 11534632 | solution.py:1335
  50.4 4.7 %branch_1_fun.12 = (bf16[1024,512]{1,0:T(8,128)(2,1)}, bf16[1024,512]{1,0:T(8,128)(2,1)}, bf16[1024,512]{1,0:T(8,128)(2,1)}, bf16[1024,512]{1,0:T(8,128)(2,1)}) custom-call(s32[1]{0:T(128)} %get-tuple-element.311.side, bf16[2,1024,512]{2,1,0:T(8,128)(2,1)S(1)} %get-tuple-element.312.edge, bf16[2048,128]{1,0:T(8,128)(2,1)} %get-tuple-element.313.wide, ...), custom_call_target="tpu_custom_call" | custom-call | tf_op jit(solution)/shard_map/cond/branch_1_fun/pallas_call | solution.py:1176
  55.1 13.4 %branch_1_fun.13 = (bf16[1024,512]{1,0:T(8,128)(2,1)}, bf16[1024,512]{1,0:T(8,128)(2,1)}) custom-call(s32[16]{0:T(128)S(1)} %get-tuple-element.323.windows, bf16[1024,512]{1,0:T(8,128)(2,1)} %get-tuple-element.703.query, bf16[1024,512]{1,0:T(8,128)(2,1)} %get-tuple-element.704.key, bf16[1024,512]{1,0:T(8,128)(2,1)} %get-tuple-element.705.value, ...), custom_call_target="tpu_custom_call" | custom-call | tf_op jit(solution)/shard_map/cond/branch_1_fun/pallas_call | solution.py:1194
  68.5 14.1 %branch_1_fun.14 = (f32[1024,512]{1,0:T(8,128)}, bf16[1024,512]{1,0:T(8,128)(2,1)}, bf16[1024,2048]{1,0:T(8,128)(2,1)}, bf16[1024,2048]{1,0:T(8,128)(2,1)}, f32[1024,512]{1,0:T(8,128)}, /*index=5*/f32[1024,32]{1,0:T(8,128)}) custom-call(s32[1]{0:T(128)} %get-tuple-element.311.side, bf16[2,1024,512]{2,1,0:T(8,128)(2,1)S(1)} %get-tuple-element.312.edge, ...), custom_call_target="tpu_custom_call" | custom-call | tf_op jit(solution)/shard_map/cond/branch_1_fun/pallas_call | solution.py:1176
  82.7 1.3 collective-permute-start
  83.9 8.9 %collective-permute-done = f32[32,1024]{1,0:T(8,128)S(1)} collective-permute-done((f32[32,1024]{1,0:T(8,128)}, f32[32,1024]{1,0:T(8,128)S(1)}, u32[]{:S(2)}, u32[]{:S(2)}) %collective-permute-start) | collective-permute-done | bytes 131104 | tf_op jit(solution)/shard_map/ppermute | solution.py:1336
  92.8 75.0 %conditional.4 = (bf16[1024,512]{1,0:T(8,128)(2,1)}, bf16[1024,512]{1,0:T(8,128)(2,1)}, bf16[1024,512]{1,0:T(8,128)(2,1)}, bf16[1024,2048]{1,0:T(8,128)(2,1)}, f...) conditional(s32[]{:T(128)} %convert_element_type.2, ...), branch_computations={%region_4.5_spmd, %region_5.6_spmd} | conditional | bytes 33030604 | solution.py:1348
  101.3 0.6 copy-done.38
  101.9 14.8 %branch_1_fun.17 = (bf16[1024,512]{1,0:T(8,128)(2,1)}, bf16[1024,2048]{1,0:T(8,128)(2,1)}, f32[1024,512]{1,0:T(8,128)}, bf16[1024,512]{1,0:T(8,128)(2,1)}, bf16[...) custom-call(s32[1]{0:T(128)} %get-tuple-element.409.side, ...), custom_call_target="tpu_custom_call" | custom-call | tf_op jit(solution)/shard_map/cond/branch_1_fun/pallas_call | solution.py:1176
  116.7 10.5 %branch_1_fun.21 = f32[512,512]{1,0:T(8,128)} custom-call(s32[2048]{0:T(1024)S(1)} %get-tuple-element.451.index, f32[2048,32]{1,0:T(8,128)S(1)} %copy-done.10, f32[1024,32]{1,0:T(8,128)S(1)} %copy-done.28, f32[1024,32]{1,0:T(8,128)} %get-tuple-element.452.latent_second, f32[32,8192]{1,0:T(8,128)S(1)} %copy-done.32), custom_call_target="tpu_custom_call" | custom-call | tf_op jit(solution)/shard_map/cond/branch_1_fun/pallas_call | solution.py:162
  127.3 23.2 %branch_1_fun.18 = (bf16[1024,512]{1,0:T(8,128)(2,1)}, bf16[1024,512]{1,0:T(8,128)(2,1)}, bf16[1024,512]{1,0:T(8,128)(2,1)}) custom-call(s32[16]{0:T(128)S(1)} %get-tuple-element.430.windows, bf16[1024,512]{1,0:T(8,128)(2,1)S(1)} %copy-done.24, bf16[1024,512]{1,0:T(8,128)(2,1)} %get-tuple-element.432.marks, bf16[1024,512]{1,0:T(8,128)(2,1)} %get-tuple-element.433.key, ...), custom_call_target="tpu_custom_call" | custom-call | tf_op jit(solution)/shard_map/cond/branch_1_fun/pallas_call | solution.py:1194
  150.5 6.7 %branch_1_fun.19 = (f32[1024,512]{1,0:T(8,128)}, f32[32,1024]{1,0:T(8,128)}, f32[16,512]{1,0:T(8,128)}, f32[32,512]{1,0:T(8,128)}) custom-call(s32[1]{0:T(128)} %get-tuple-element.409.side, bf16[2,1024,512]{2,1,0:T(8,128)(2,1)S(1)} %get-tuple-element.411.cotangent.edge, bf16[2048,128]{1,0:T(8,128)(2,1)S(1)} %copy-done.15, ...), custom_call_target="tpu_custom_call" | custom-call | tf_op jit(solution)/shard_map/cond/branch_1_fun/pallas_call | solution.py:1176
  157.2 10.3 %branch_1_fun.20 = f32[4096,512]{1,0:T(8,128)} custom-call(bf16[1024,2048]{1,0:T(8,128)(2,1)} %get-tuple-element.449.active, bf16[1024,512]{1,0:T(8,128)(2,1)} %get-tuple-element.749.out_low, bf16[1024,512]{1,0:T(8,128)(2,1)S(1)} %copy-done.29, bf16[1024,2048]{1,0:T(8,128)(2,1)} %get-tuple-element.750.preact_low), custom_call_target="tpu_custom_call" | custom-call | tf_op jit(solution)/shard_map/cond/branch_1_fun/pallas_call | solution.py:515
  167.9 1.3 collective-permute-start.1
  169.2 13.1 %collective-permute-done.1 = f32[32,1024]{1,0:T(8,128)S(1)} collective-permute-done((f32[32,1024]{1,0:T(8,128)}, f32[32,1024]{1,0:T(8,128)S(1)}, u32[]{:S(2)}, u32[]{:S(2)}) %collective-permute-start.1) | collective-permute-done | bytes 131104 | tf_op jit(solution)/shard_map/ppermute | solution.py:1349
  182.2 27.3 %conditional.5 = (f32[4096,512]{1,0:T(8,128)}, f32[1024,512]{1,0:T(8,128)}, bf16[1024,512]{1,0:T(8,128)(2,1)}, bf16[1024,512]{1,0:T(8,128)(2,1)}, f32[16,512]{1,0:T(8,128)S(1)}, /*index=5*/f32[32,512]{1,0:T(8,128)S(1)}) conditional(s32[]{:T(128)} %convert_element_type.2, (bf16[1024,2048]{1,0:T(8,128)(2,1)}, bf16[1024,512]{1,0:T(8,128)(2,1)}, ...), branch_computations={%region_6.7_spmd, %region_7.8_spmd} | conditional | bytes 16973900 | solution.py:1359
  182.2 0.6 copy.158.refs_1_
  182.8 0.6 copy.157.refs_0_
  183.5 14.7 %branch_1_fun.22 = (bf16[1024,512]{1,0:T(8,128)(2,1)}, bf16[1024,2048]{1,0:T(8,128)(2,1)}, f32[1024,512]{1,0:T(8,128)}, bf16[1024,512]{1,0:T(8,128)(2,1)}, bf16[...) custom-call(s32[1]{0:T(128)} %get-tuple-element.468.side, ...), custom_call_target="tpu_custom_call" | custom-call | tf_op jit(solution)/shard_map/cond/branch_1_fun/pallas_call | solution.py:1176
  198.2 11.4 %branch_1_fun.23 = f32[4096,512]{1,0:T(8,128)} custom-call(bf16[1024,2048]{1,0:T(8,128)(2,1)S(1)} %copy-done.33, bf16[1024,512]{1,0:T(8,128)(2,1)} %get-tuple-element.486.out_low, bf16[1024,512]{1,0:T(8,128)(2,1)} %get-tuple-element.487.n2, bf16[1024,2048]{1,0:T(8,128)(2,1)} %get-tuple-element.488.preact_low, ...), custom_call_target="tpu_custom_call", output_to_operand_aliasing={{}: (4, {})} | custom-call | tf_op jit(solution)/shard_map/cond/branch_1_fun/pallas_call | solution.py:515
  209.6 165.5 %shard_map.268 = (f32[4096,512]{1,0:T(8,128)}, f32[2048,512]{1,0:T(8,128)}, f32[768,512]{1,0:T(8,128)}, f32[1024,512]{1,0:T(8,128)}) custom-call(f32[4096,512]{1,0:T(8,128)} %get-tuple-element.627.refs_0_, bf16[1024,512]{1,0:T(8,128)(2,1)} %get-tuple-element.628.refs_1_, bf16[1024,512]{1,0:T(8,128)(2,1)} %get-tuple-element.629.refs_2_, ...), custom_call_target="tpu_custom_call" | custom-call | tf_op jit(solution)/shard_map/pallas_call | solution.py:976
  375.1 11.8 %shard_map.269 = (f32[2048,512]{1,0:T(8,128)}, f32[512,2048]{1,0:T(8,128)}, f32[512,512]{1,0:T(8,128)}, f32[512,1536]{1,0:T(8,128)}, f32[2,1024,512]{2,1,0:T(8,1...) custom-call(s32[1]{0:T(128)} %bitcast.side, ...), custom_call_target="tpu_custom_call" | custom-call | tf_op jit(solution)/shard_map/pallas_call | solution.py:1060
  (54 shorter events, 0.1 us)
Async XLA Ops:
  10.7 19.9 %copy-start.11 = (bf16[2048,128]{1,0:T(8,128)(2,1)}, bf16[2048,128]{1,0:T(8,128)(2,1)S(1)}, u32[]{:S(2)}) copy-start(bf16[2048,128]{1,0:T(8,128)(2,1)S(1)} %get-tuple-element.591.wide) | copy-start | bytes 1572868
  10.7 19.9 %copy-start.18 = (bf16[2,1024,128]{2,1,0:T(8,128)(2,1)}, bf16[2,1024,128]{2,1,0:T(8,128)(2,1)S(1)}, u32[]{:S(2)}) copy-start(bf16[2,1024,128]{2,1,0:T(8,128)(2,1)S(1)} %get-tuple-element.596.key_mark.refs_7_) | copy-start | bytes 1572868
  10.7 19.9 %copy-start.26 = (bf16[2,1024,128]{2,1,0:T(8,128)(2,1)}, bf16[2,1024,128]{2,1,0:T(8,128)(2,1)S(1)}, u32[]{:S(2)}) copy-start(bf16[2,1024,128]{2,1,0:T(8,128)(2,1)S(1)} %get-tuple-element.595.query_mark) | copy-start | bytes 1572868
  10.7 19.9 %copy-start = (bf16[1,2,1024,512]{3,2,1,0:T(8,128)(2,1)S(1)}, bf16[1,2,1024,512]{3,2,1,0:T(8,128)(2,1)}, u32[]{:S(2)}) copy-start(bf16[1,2,1024,512]{3,2,1,0:T(8,128)(2,1)} %param.22) | copy-start | bytes 6291460
  10.7 19.9 %copy-start.1 = (bf16[1,512,2048]{2,1,0:T(8,128)(2,1)S(1)}, bf16[1,512,2048]{2,1,0:T(8,128)(2,1)}, u32[]{:S(2)}) copy-start(bf16[1,512,2048]{2,1,0:T(8,128)(2,1)} %param.27) | copy-start | bytes 6291460
  10.7 19.9 %copy-start.3 = (bf16[1,2048,512]{2,1,0:T(8,128)(2,1)S(1)}, bf16[1,2048,512]{2,1,0:T(8,128)(2,1)}, u32[]{:S(2)}) copy-start(bf16[1,2048,512]{2,1,0:T(8,128)(2,1)} %param.28) | copy-start | bytes 6291460
  10.7 19.9 %copy-start.25 = (f32[32,512]{1,0:T(8,128)S(1)}, f32[32,512]{1,0:T(8,128)}, u32[]{:S(2)}) copy-start(f32[32,512]{1,0:T(8,128)} %up.3) | copy-start | bytes 196612
  10.7 19.9 %copy-start.34 = (f32[512,32]{0,1:T(8,128)S(1)}, f32[512,32]{0,1:T(8,128)}, u32[]{:S(2)}) copy-start(f32[512,32]{0,1:T(8,128)} %param.34) | copy-start | bytes 196612
  10.7 19.9 %copy-start.35 = (f32[1,6,512]{2,0,1:T(1,128)S(1)}, f32[1,6,512]{2,0,1:T(1,128)}, u32[]{:S(2)}) copy-start(f32[1,6,512]{2,0,1:T(1,128)} %param.30) | copy-start | bytes 36868
  10.7 19.9 %copy-start.36 = (f32[1,2,512]{2,1,0:T(2,128)S(1)}, f32[1,2,512]{2,1,0:T(2,128)}, u32[]{:S(2)}) copy-start(f32[1,2,512]{2,1,0:T(2,128)} %param.29) | copy-start | bytes 12292
  10.7 19.9 %copy-start.37 = (f32[2,512]{1,0:T(2,128)S(1)}, f32[2,512]{1,0:T(2,128)}, u32[]{:S(2)}) copy-start(f32[2,512]{1,0:T(2,128)} %head_bias.3) | copy-start | bytes 12292
  10.8 19.9 %copy-start.39 = (f32[512]{0:T(512)S(1)}, f32[512]{0:T(512)}, u32[]{:S(2)}) copy-start(f32[512]{0:T(512)} %param.32) | copy-start | bytes 6148
  10.8 19.9 %copy-start.40 = (f32[1,2048]{1,0:T(1,128)S(1)}, f32[1,2048]{1,0:T(1,128)}, u32[]{:S(2)}) copy-start(f32[1,2048]{1,0:T(1,128)} %hidden_bias.1) | copy-start | bytes 24580
  10.8 19.9 %copy-start.45 = (f32[32]{0:T(128)S(1)}, f32[32]{0:T(128)}, u32[]{:S(2)}) copy-start(f32[32]{0:T(128)} %param.35) | copy-start | bytes 388
  30.7 14.4 %copy-start.5 = (bf16[1,512,1536]{2,1,0:T(8,128)(2,1)S(1)}, bf16[1,512,1536]{2,1,0:T(8,128)(2,1)}, u32[]{:S(2)}) copy-start(bf16[1,512,1536]{2,1,0:T(8,128)(2,1)} %param.25) | copy-start | bytes 4718596
  55.1 13.4 %copy-start.13 = (bf16[2048,128]{1,0:T(8,128)(2,1)S(1)}, bf16[2048,128]{1,0:T(8,128)(2,1)}, u32[]{:S(2)}) copy-start(bf16[2048,128]{1,0:T(8,128)(2,1)} %get-tuple-element.313.wide) | copy-start | bytes 1572868 | tf_op jit(solution)/shard_map/cond
  55.1 13.4 %copy-start.22 = (bf16[512,512]{1,0:T(8,128)(2,1)S(1)}, bf16[512,512]{1,0:T(8,128)(2,1)}, u32[]{:S(2)}) copy-start(bf16[512,512]{1,0:T(8,128)(2,1)} %get-tuple-element.328.weight_out) | copy-start | bytes 1572868 | tf_op jit(solution)/shard_map/cond
  82.7 10.2 %collective-permute-start = (f32[32,1024]{1,0:T(8,128)}, f32[32,1024]{1,0:T(8,128)S(1)}, u32[]{:S(2)}, u32[]{:S(2)}) collective-permute-start(f32[32,1024]{1,0:T(8,128)} %get-tuple-element.612), channel_id=1, source_target_pairs={{16,0},{17,1},{18,2},{19,3},{20,4},{21,5},{22,6},{23,7},{24,8},{25... | collective-permute-start | bytes 393224 | tf_op jit(solution)/shard_map/ppermute | solution.py:1336
  101.2 0.6 copy-start.38
  101.9 14.8 %copy-start.10 = (f32[2048,32]{1,0:T(8,128)S(1)}, f32[2048,32]{1,0:T(8,128)}, u32[]{:S(2)}) copy-start(f32[2048,32]{1,0:T(8,128)} %get-tuple-element.412.unit) | copy-start | bytes 786436 | tf_op jit(solution)/shard_map/cond
  101.9 14.8 %copy-start.28 = (f32[1024,32]{1,0:T(8,128)S(1)}, f32[1024,32]{1,0:T(8,128)}, u32[]{:S(2)}) copy-start(f32[1024,32]{1,0:T(8,128)} %get-tuple-element.414.latent.latent_first) | copy-start | bytes 393220 | tf_op jit(solution)/shard_map/cond
  101.9 14.8 %copy-start.32 = (f32[32,8192]{1,0:T(8,128)S(1)}, f32[32,8192]{1,0:T(8,128)}, u32[]{:S(2)}) copy-start(f32[32,8192]{1,0:T(8,128)} %get-tuple-element.453.table_turned) | copy-start | bytes 3145732 | tf_op jit(solution)/shard_map/cond
  116.7 10.6 %copy-start.17 = (bf16[1024,512]{1,0:T(8,128)(2,1)S(1)}, bf16[1024,512]{1,0:T(8,128)(2,1)}, u32[]{:S(2)}) copy-start(bf16[1024,512]{1,0:T(8,128)(2,1)} %get-tuple-element.436.context) | copy-start | bytes 3145732 | tf_op jit(solution)/shard_map/cond
  116.7 10.5 %copy-start.21 = (bf16[2,1024,128]{2,1,0:T(8,128)(2,1)S(1)}, bf16[2,1024,128]{2,1,0:T(8,128)(2,1)}, u32[]{:S(2)}) copy-start(bf16[2,1024,128]{2,1,0:T(8,128)(2,1)} %get-tuple-element.437.key_mark) | copy-start | bytes 1572868 | tf_op jit(solution)/shard_map/cond
  116.7 10.5 %copy-start.24 = (bf16[1024,512]{1,0:T(8,128)(2,1)S(1)}, bf16[1024,512]{1,0:T(8,128)(2,1)}, u32[]{:S(2)}) copy-start(bf16[1024,512]{1,0:T(8,128)(2,1)} %get-tuple-element.431.query) | copy-start | bytes 3145732 | tf_op jit(solution)/shard_map/cond
  127.2 23.3 %copy-start.7 = (bf16[512,1536]{1,0:T(8,128)(2,1)S(1)}, bf16[512,1536]{1,0:T(8,128)(2,1)}, u32[]{:S(2)}) copy-start(bf16[512,1536]{1,0:T(8,128)(2,1)} %get-tuple-element.443.weight) | copy-start | bytes 4718596 | tf_op jit(solution)/shard_map/cond
  127.2 23.3 %copy-start.15 = (bf16[2048,128]{1,0:T(8,128)(2,1)S(1)}, bf16[2048,128]{1,0:T(8,128)(2,1)}, u32[]{:S(2)}) copy-start(bf16[2048,128]{1,0:T(8,128)(2,1)} %get-tuple-element.441.wide) | copy-start | bytes 1572868 | tf_op jit(solution)/shard_map/cond
  150.5 6.7 %copy-start.29 = (bf16[1024,512]{1,0:T(8,128)(2,1)S(1)}, bf16[1024,512]{1,0:T(8,128)(2,1)}, u32[]{:S(2)}) copy-start(bf16[1024,512]{1,0:T(8,128)(2,1)} %get-tuple-element.450.n2) | copy-start | bytes 3145732 | tf_op jit(solution)/shard_map/cond
  167.9 14.4 %collective-permute-start.1 = (f32[32,1024]{1,0:T(8,128)}, f32[32,1024]{1,0:T(8,128)S(1)}, u32[]{:S(2)}, u32[]{:S(2)}) collective-permute-start(f32[32,1024]{1,0:T(8,128)} %get-tuple-element.621), channel_id=1, source_target_pairs={{16,0},{17,1},{18,2},{19,3},{20,4},{21,5},{22,6},{23,7},{24,8},{25... | collective-permute-start | bytes 393224 | tf_op jit(solution)/shard_map/ppermute | solution.py:1349
  182.2 27.3 %copy-start.16 = (bf16[1024,512]{1,0:T(8,128)(2,1)S(1)}, bf16[1024,512]{1,0:T(8,128)(2,1)}, u32[]{:S(2)}) copy-start(bf16[1024,512]{1,0:T(8,128)(2,1)} %get-tuple-element.597.context.refs_13_.refs_19_) | copy-start | bytes 3145732
  182.2 27.3 %copy-start.42 = (f32[32,512]{1,0:T(8,128)S(1)}, f32[32,512]{1,0:T(8,128)}, u32[]{:S(2)}) copy-start(f32[32,512]{1,0:T(8,128)} %get-tuple-element.650.refs_34_) | copy-start | bytes 196612
  183.5 14.7 %copy-start.33 = (bf16[1024,2048]{1,0:T(8,128)(2,1)S(1)}, bf16[1024,2048]{1,0:T(8,128)(2,1)}, u32[]{:S(2)}) copy-start(bf16[1024,2048]{1,0:T(8,128)(2,1)} %get-tuple-element.467.active) | copy-start | bytes 12582916 | tf_op jit(solution)/shard_map/cond
